TPU v7x, 32 devices: a whole 2x2x4 slice. The times are simulated.
32 devices in a mesh: dp: 32 (over z, y, x, core), refl: 1.
Axes of the slice: x: 2, y: 2, z: 4, core: 2. Of those that a mesh axis runs over, the one named last changes fastest.
Arguments:
- intensities: bfloat16 [1024, 16384], P('dp', 'refl'), may hold values from -12 to 12
- observed: int32 [1024, 16384], P('dp', 'refl'), may hold values 0 or 1
- qweights: bfloat16 [1024, 16384], P('dp', 'refl'), may hold values from 0.25 to 4
- ops: int32 [4, 16384], P(None, 'refl'), may hold values from 0 to 16383, as said below
- pick: int32 [32, 32], P(None, 'dp'), may hold values from 0 to 7
Outputs:
- corr: float32 [4, 1024, 128], P(None, ('dp', 'refl'))
- returned: float32 [4, 32, 32, 4, 32], P(None, 'dp', None, None, 'refl')
Inputs may be any that keep to these rules, and one draw needn't show every extreme that they name: Each row of ops is a permutation of the reflections that maps every aligned block of 16384 reflections onto itself.
All inputs are finite; a program needn't handle non-finite values. No bound on the sum of `observed` on one device may be relied on, other than what follows from the above.
Results may differ from a plain program's by a relative error of at most 0.0084.
Values may be sent and summed in bfloat16 or wider, within the bound.
No kernel may reach another device: no remote copies, remote signals or barrier semaphores. Data moves between devices by JAX's collectives and lax.ppermute only.
A program may use at most 128 MiB of HBM per device.

v0:
```python
import jax
import jax.numpy as jnp
from jax import lax
from jax.sharding import PartitionSpec as P

SUB = 4
NOPS = 4


def gram(left, right):
    return lax.dot_general(
        left, right, (((1,), (1,)), ((), ())), preferred_element_type=jnp.float32
    )


def collect(stacked_own, blk, part_w, part_wy, part_wyy):
    first = gram(stacked_own, part_w).reshape(3, blk, -1)
    second = gram(stacked_own[: 2 * blk], part_wy).reshape(2, blk, -1)
    third = gram(stacked_own[:blk], part_wyy)[None]
    return jnp.concatenate([first, second, third], 0)


def pearson(share):
    total_w, sum_x, sum_xx = (share[:, 0], share[:, 1], share[:, 2])
    sum_y, sum_xy, sum_yy = (share[:, 3], share[:, 4], share[:, 5])
    numer = total_w * sum_xy - sum_x * sum_y
    var_x = jnp.maximum(total_w * sum_xx - sum_x * sum_x, 0.05 * total_w * sum_xx)
    var_y = jnp.maximum(total_w * sum_yy - sum_y * sum_y, 0.05 * total_w * sum_yy)
    return numer / jnp.sqrt(var_x * var_y)


def shards(intensities, observed, qweights, ops, pick):
    blk = intensities.shape[0]
    width = intensities.shape[1]
    groups = lax.axis_size("dp")
    shares = lax.axis_size("refl")
    weights = observed.astype(jnp.float32) * qweights.astype(jnp.float32)
    values = intensities.astype(jnp.float32)
    own_w = weights.astype(jnp.bfloat16)
    own_wx = (weights * values).astype(jnp.bfloat16)
    own_wxx = (weights * values * values).astype(jnp.bfloat16)
    stacked_own = jnp.concatenate([own_w, own_wx, own_wxx], 0)
    local_ops = ops - lax.axis_index("refl") * width
    request = pick[:, 0][:, None] * SUB + jnp.arange(SUB, dtype=jnp.int32)[None, :]
    send_x = intensities[request]
    send_w = own_w[request]
    got_x = lax.all_to_all(send_x, "dp", split_axis=0, concat_axis=0, tiled=True)
    got_w = lax.all_to_all(send_w, "dp", split_axis=0, concat_axis=0, tiled=True)
    count = got_x.shape[1]
    flat_x = got_x.reshape(-1, width)
    flat_w = got_w.reshape(-1, width)
    per_op = []
    wide_w = flat_w.astype(jnp.float32)
    wide_x = flat_x.astype(jnp.float32)
    part_wy = (wide_w * wide_x).astype(jnp.bfloat16)
    part_wyy = (wide_w * wide_x * wide_x).astype(jnp.bfloat16)
    positions = jnp.arange(width, dtype=jnp.int32)
    for k in range(NOPS):
        inverse = jnp.zeros((width,), jnp.int32).at[local_ops[k]].set(positions)
        moved_own = jnp.take(stacked_own, inverse, axis=1)
        per_op.append(collect(moved_own, blk, flat_w, part_wy, part_wyy))
    stats = jnp.stack(per_op, 0)
    stats = stats.reshape(NOPS, 6, blk, groups, count)
    flat_stats = stats.reshape(NOPS, 6, blk, -1)
    rows = blk // shares
    totals = lax.psum(flat_stats, "refl")
    share = lax.dynamic_slice_in_dim(totals, lax.axis_index("refl") * rows, rows, 2)
    corr = pearson(share)
    outgoing = jnp.transpose(corr.reshape(NOPS, rows, groups, SUB), (0, 2, 3, 1))[:, :, None]
    returned = lax.all_to_all(outgoing, "dp", split_axis=1, concat_axis=2, tiled=True)
    return (corr, returned)


def solution(mesh):
    return jax.shard_map(
        shards,
        mesh=mesh,
        in_specs=(
            P("dp", "refl"),
            P("dp", "refl"),
            P("dp", "refl"),
            P(None, "refl"),
            P(None, "dp"),
        ),
        out_specs=(P(None, ("dp", "refl"), None), P(None, "dp", None, None, "refl")),
        check_vma=False,
    )
```

profile of v0, /device:TPU:0, one launch (start us, length us, event | category | flops | bytes accessed | tf_op | source)
XLA Modules:
  0.0 705.6 jit_solution(7291780774419484248)
XLA Ops:
  0.6 0.7 multiply_bitcast_fusion.1
  1.5 10.2 %gather_fusion.1 = bf16[128,16384]{1,0:T(8,128)(2,1)} fusion(bf16[32,16384]{1,0:T(8,128)(2,1)} %param.7, s32[1024]{0:T(1024)S(1)} %pad_clamp_fusion), kind=kCustom, calls=%fused_computation.5 | custom fusion | bytes 8389120 | tf_op jit(solution)/shard_map/gather | solution.py:45
  11.7 7.2 %reshape.248 = bf16[32,4,16384]{2,1,0:T(4,128)(2,1)} reshape(bf16[128,16384]{1,0:T(8,128)(2,1)} %gather_fusion.1) | data formatting | bytes 8388608 | tf_op jit(solution)/shard_map/gather | solution.py:45
  18.9 7.4 %all-to-all-start.1 = ((bf16[32,4,16384]{2,1,0:T(4,128)(2,1)}), bf16[32,4,16384]{2,1,0:T(4,128)(2,1)}, u32[]{:S(2)}, u32[]{:S(2)}) async-start(bf16[32,4,16384]{2,1,0:T(4,128)(2,1)} %reshape.248), calls=%async_computation.1 | async-start | bytes 8388608 | tf_op jit(solution)/shard_map/all_to_all | solution.py:47
  26.3 0.3 compare_select_fusion.3
  26.6 60.5 %scatter_custom_fusion.2 = s32[16384]{0:T(1024)S(1)} fusion(s32[16384]{0:T(1024)S(1)} %bitcast.184, s32[16384]{0:T(1024)S(1)} %iota.17, s32[]{:T(128)} %constant.13.clone.1), kind=kCustom, calls=%fused_computation.83 | custom fusion | bytes 65540 | tf_op jit(solution)/shard_map/scatter | solution.py:59
  87.2 3.5 fusion.10
  90.7 5.2 gather_fusion
  95.9 7.3 %reshape.240 = bf16[32,4,16384]{2,1,0:T(4,128)(2,1)} reshape(bf16[128,16384]{1,0:T(8,128)(2,1)} %gather_fusion) | data formatting | bytes 8388608 | tf_op jit(solution)/shard_map/gather | solution.py:46
  103.2 1.7 pad_maximum_fusion
  104.9 5.9 copy.87
  110.8 57.6 %gather_fusion.4 = bf16[16384,96]{1,0:T(8,128)(2,1)} fusion(bf16[96,16384]{0,1:T(8,128)(2,1)} %copy.87, s32[16384]{0:T(1024)S(1)} %fusion.38), kind=kCustom, calls=%fused_computation.2.clone | custom fusion | bytes 6356992 | tf_op jit(solution)/shard_map/jit(_take)/gather | solution.py:60
  168.5 11.5 %select_bitcast_fusion.1 = bf16[96,16384]{0,1:T(8,128)(2,1)} fusion(bf16[16384,96]{1,0:T(8,128)(2,1)} %gather_fusion.4, pred[16384]{0:T(1024)(128)(4,1)S(1)} %compare_and_fusion.1), kind=kLoop, calls=%fused_computation.22 | loop fusion | flops 1572864 | bytes 6307840 | tf_op jit(solution)/shard_map/jit(_take)/select_n | solution.py:60
  180.0 6.1 copy.94
  186.0 3.5 copy.95
  189.6 60.3 %scatter_custom_fusion.3 = s32[16384]{0:T(1024)S(1)} fusion(s32[16384]{0:T(1024)S(1)} %bitcast.183, s32[16384]{0:T(1024)S(1)} %iota.18, s32[]{:T(128)} %constant.13.clone.1), kind=kCustom, calls=%fused_computation.81 | custom fusion | bytes 65540 | tf_op jit(solution)/shard_map/scatter | solution.py:59
  250.0 57.7 %gather_fusion.5 = bf16[16384,96]{1,0:T(8,128)(2,1)} fusion(bf16[96,16384]{0,1:T(8,128)(2,1)} %copy.87, s32[16384]{0:T(1024)S(1)} %fusion.39), kind=kCustom, calls=%fused_computation.3.clone | custom fusion | bytes 6356992 | tf_op jit(solution)/shard_map/jit(_take)/gather | solution.py:60
  307.7 11.5 %select_bitcast_fusion = bf16[96,16384]{0,1:T(8,128)(2,1)} fusion(bf16[16384,96]{1,0:T(8,128)(2,1)} %gather_fusion.5, pred[16384]{0:T(1024)(128)(4,1)S(1)} %compare_and_fusion), kind=kLoop, calls=%fused_computation.21 | loop fusion | flops 1572864 | bytes 6307840 | tf_op jit(solution)/shard_map/jit(_take)/select_n | solution.py:60
  319.2 6.0 copy.97
  325.2 4.8 copy.98
  329.9 60.3 %scatter_custom_fusion = s32[16384]{0:T(1024)S(1)} fusion(s32[16384]{0:T(1024)S(1)} %bitcast.182, s32[16384]{0:T(1024)S(1)} %iota.15, s32[]{:T(128)} %constant.13.clone.1), kind=kCustom, calls=%fused_computation.87 | custom fusion | bytes 65540 | tf_op jit(solution)/shard_map/scatter | solution.py:59
  390.3 57.7 %gather_fusion.2 = bf16[16384,96]{1,0:T(8,128)(2,1)} fusion(bf16[96,16384]{0,1:T(8,128)(2,1)} %copy.87, s32[16384]{0:T(1024)S(1)} %fusion.36), kind=kCustom, calls=%fused_computation.clone | custom fusion | bytes 6356992 | tf_op jit(solution)/shard_map/jit(_take)/gather | solution.py:60
  448.0 6.1 all-to-all-start
  454.1 11.6 %select_bitcast_fusion.3 = bf16[96,16384]{0,1:T(8,128)(2,1)} fusion(bf16[16384,96]{1,0:T(8,128)(2,1)} %gather_fusion.2, pred[16384]{0:T(1024)(128)(4,1)S(1)} %compare_and_fusion.3), kind=kLoop, calls=%fused_computation.24 | loop fusion | flops 1572864 | bytes 6307840 | tf_op jit(solution)/shard_map/jit(_take)/select_n | solution.py:60
  465.7 5.9 copy.88
  471.6 4.8 copy.89
  476.4 60.3 %scatter_custom_fusion.1 = s32[16384]{0:T(1024)S(1)} fusion(s32[16384]{0:T(1024)S(1)} %bitcast.181, s32[16384]{0:T(1024)S(1)} %iota.16, s32[]{:T(128)} %constant.13.clone.1), kind=kCustom, calls=%fused_computation.85 | custom fusion | bytes 65540 | tf_op jit(solution)/shard_map/scatter | solution.py:59
  536.8 57.7 %gather_fusion.3 = bf16[16384,96]{1,0:T(8,128)(2,1)} fusion(bf16[96,16384]{0,1:T(8,128)(2,1)} %copy.87, s32[16384]{0:T(1024)S(1)} %fusion.37), kind=kCustom, calls=%fused_computation.1.clone | custom fusion | bytes 6356992 | tf_op jit(solution)/shard_map/jit(_take)/gather | solution.py:60
  594.5 11.5 %select_bitcast_fusion.2 = bf16[96,16384]{0,1:T(8,128)(2,1)} fusion(bf16[16384,96]{1,0:T(8,128)(2,1)} %gather_fusion.3, pred[16384]{0:T(1024)(128)(4,1)S(1)} %compare_and_fusion.2), kind=kLoop, calls=%fused_computation.23 | loop fusion | flops 1572864 | bytes 6307840 | tf_op jit(solution)/shard_map/jit(_take)/select_n | solution.py:60
  606.0 6.0 copy.91
  612.0 4.7 copy.92
  616.7 7.3 %reshape.206 = f32[128,16384]{1,0:T(8,128)} reshape(bf16[32,4,16384]{2,1,0:T(4,128)(2,1)} %all-to-all-done.1) | data formatting | bytes 12582912 | tf_op jit(solution)/shard_map/convert_element_type | solution.py:54
  624.0 6.9 reshape.205
  631.0 5.8 fusion
  636.8 1.2 fusion.17
  638.0 1.0 copy-done.5
  638.9 1.3 fusion.20
  640.3 0.9 copy-done.6
  641.1 1.3 fusion.11
  642.4 0.9 copy-done.7
  643.3 1.3 fusion.14
  644.6 9.5 %multiply_convert_fusion = bf16[32,4,16384]{2,1,0:T(4,128)(2,1)} fusion(bf16[32,4,16384]{2,1,0:T(4,128)(2,1)} %all-to-all-done, bf16[32,4,16384]{2,1,0:T(4,128)(2,1)} %all-to-all-done.1), kind=kLoop, calls=%fused_computation.12 | loop fusion | flops 8388608 | bytes 12582912 | tf_op jit(solution)/shard_map/convert_element_type | solution.py:55
  654.1 7.1 %reshape.302 = bf16[128,16384,1]{1,0,2:T(8,128)(2,1)} reshape(bf16[32,4,16384]{2,1,0:T(4,128)(2,1)} %multiply_convert_fusion) | data formatting | bytes 8388608 | tf_op jit(solution)/shard_map/convert_element_type | solution.py:55
  661.3 3.9 fusion.54
  665.4 1.6 fusion.56
  667.0 7.1 %reshape.301 = bf16[128,16384,1]{1,0,2:T(8,128)(2,1)} reshape(bf16[32,4,16384]{2,1,0:T(4,128)(2,1)} %all-to-all-done) | data formatting | bytes 8388608 | tf_op jit(solution)/shard_map/reshape | solution.py:51
  674.1 3.8 fusion.53
  677.9 0.6 copy-done.12
  678.5 1.5 fusion.55
  680.0 0.3 copy-done.2
  680.2 0.6 copy-done.9
  680.8 1.6 fusion.50
  682.4 0.3 copy-done.13
  682.7 1.5 fusion.49
  684.2 1.6 fusion.52
  685.8 0.3 copy-done.14
  686.1 1.5 fusion.51
  687.6 0.7 fusion.28
  689.3 0.2 copy_bitcast_fusion
  689.5 0.2 reshape.313
  689.8 13.2 %all_to_all.22 = f32[32,1,512]{2,1,0:T(1,128)S(1)} all-to-all(f32[32,1,512]{2,1,0:T(1,128)S(1)} %reshape.313), channel_id=1, replica_groups=mesh['dp'=32,'refl'=1] {'dp'}, dimensions={0} | all-to-all | bytes 131072 | tf_op jit(solution)/shard_map/all_to_all | solution.py:70
  702.9 0.5 broadcast.200
  703.4 0.8 reduce
  704.4 0.7 copy.112
  (57 shorter events, 1.8 us)
Async XLA Ops:
  18.8 7.4 %copy-start.16 = (s32[4,16384]{1,0:T(4,128)S(1)}, s32[4,16384]{1,0:T(4,128)}, u32[]{:S(2)}) copy-start(s32[4,16384]{1,0:T(4,128)} %param.10) | copy-start | bytes 786436
  18.8 68.4 %copy-start = (bf16[32,16384]{1,0:T(8,128)(2,1)S(1)}, bf16[32,16384]{1,0:T(8,128)(2,1)}, u32[]{:S(2)}) copy-start(bf16[32,16384]{1,0:T(8,128)(2,1)} %param.7) | copy-start | bytes 3145732
  18.9 429.2 %all-to-all-start.1 = ((bf16[32,4,16384]{2,1,0:T(4,128)(2,1)}), bf16[32,4,16384]{2,1,0:T(4,128)(2,1)}, u32[]{:S(2)}, u32[]{:S(2)}) async-start(bf16[32,4,16384]{2,1,0:T(4,128)(2,1)} %reshape.248), calls=%async_computation.1 | async-start | bytes 8388608 | tf_op jit(solution)/shard_map/all_to_all | solution.py:47
  95.9 7.3 %copy-start.15 = (bf16[32,16384]{1,0:T(8,128)(2,1)S(1)}, bf16[32,16384]{1,0:T(8,128)(2,1)}, u32[]{:S(2)}) copy-start(bf16[32,16384]{1,0:T(8,128)(2,1)} %get-tuple-element.12) | copy-start | bytes 3145732
  448.0 176.0 %all-to-all-start = ((bf16[32,4,16384]{2,1,0:T(4,128)(2,1)}), bf16[32,4,16384]{2,1,0:T(4,128)(2,1)}, u32[]{:S(2)}, u32[]{:S(2)}) async-start(bf16[32,4,16384]{2,1,0:T(4,128)(2,1)} %reshape.240), calls=%async_computation | async-start | bytes 8388608 | tf_op jit(solution)/shard_map/all_to_all | solution.py:48
  631.0 5.8 copy-start.4
  636.7 2.2 copy-start.5
  638.9 2.2 copy-start.6
  641.1 2.2 copy-start.7
  661.2 3.9 copy-start.1
  661.3 4.1 copy-start.8
  666.9 7.2 %copy-start.11 = (bf16[96,16384]{1,0:T(8,128)(2,1)S(1)}, bf16[96,16384]{1,0:T(8,128)(2,1)}, u32[]{:S(2)}) copy-start(bf16[96,16384]{1,0:T(8,128)(2,1)} %copy.94) | copy-start | bytes 9437188
  674.1 3.8 copy-start.3
  674.1 4.4 copy-start.12
  677.9 2.3 copy-start.2
  677.9 2.9 copy-start.9
  680.8 1.9 copy-start.13
  682.4 1.8 copy-start.10
  684.2 1.9 copy-start.14
where the time goes:
time: 715 us; the launch traced here: 706 us
  local copies, waits for them, and re-layouts  586 us (82%)
  other arithmetic  69.5 us (10%)
  matrix products  21.9 us (3%)
  starting transfers between devices  13.5 us (2%)
  blocking collectives  13.2 us (2%)
    scatter x4, local copies, waits for them, and re-layouts, shards(): inverse = jnp.zeros((width,), jnp.int32).at[local_ops[k]].set(positions)  242 us
    gather x4, local copies, waits for them, and re-layouts, shards(): moved_own = jnp.take(stacked_own, inverse, axis=1)  231 us
    select_n x4, other arithmetic, shards(): moved_own = jnp.take(stacked_own, inverse, axis=1)  46.1 us
    select_n x4, local copies, waits for them, and re-layouts, shards(): moved_own = jnp.take(stacked_own, inverse, axis=1)  23.9 us
    dot_general x12, matrix products, gram(): lax.dot_general(left, right, (((1,), (1,)), ((), ())), preferred_element_...  21.9 us
    slice x4, local copies, waits for them, and re-layouts, collect(): second = gram(stacked_own[:2 * blk], part_wy).reshape(2, blk, -1)  17.8 us
    gather x2, local copies, waits for them, and re-layouts, shards(): send_x = intensities[request]  17.4 us
  transfers between devices with their start and end apart: 2, of which 0 were waited for; matrix products, arithmetic and copies ran while one was open for 84% of the time, Pallas kernels for 0%

commit v1 on v0

v1 whole, which is shorter than its diff:
```python
import functools

import jax
import jax.numpy as jnp
from jax import lax
from jax.experimental import pallas as pl
from jax.experimental.pallas import tpu as pltpu
from jax.sharding import PartitionSpec as P

SUB = 4
NOPS = 4
LANES = 128
SLAB = 2 * SUB
VMEM_LIMIT = 56 * 1024 * 1024


def params():
    return pltpu.CompilerParams(vmem_limit_bytes=VMEM_LIMIT)


def pack_kernel(pick_ref, x_ref, obs_ref, qw_ref, send_ref, w_ref, slabs, sems):
    blk, width = x_ref.shape
    step = min(512, width)

    @pl.loop(0, width // step)
    def _(i):
        cols = pl.ds(pl.multiple_of(i * step, step), step)
        wide_w = obs_ref[:, cols].astype(jnp.float32) * qw_ref[:, cols].astype(jnp.float32)
        wide_x = x_ref[:, cols].astype(jnp.float32)
        w_ref[:, cols] = wide_w.astype(jnp.bfloat16)
        for g in range(blk // SUB):
            rows = slice(g * SUB, (g + 1) * SUB)
            slab = jnp.concatenate([wide_x[rows], wide_w[rows]], 0)
            slabs[g, :, cols] = slab.astype(jnp.bfloat16)

    groups = send_ref.shape[0]

    def copy(d):
        return pltpu.make_async_copy(slabs.at[pick_ref[d]], send_ref.at[d], sems.at[d])

    @pl.loop(0, groups)
    def _(d):
        copy(d).start()

    @pl.loop(0, groups)
    def _(d):
        copy(d).wait()


def pack(pick, intensities, observed, qweights):
    blk, width = intensities.shape
    groups = pick.shape[0]
    whole = pl.BlockSpec(memory_space=pltpu.VMEM)
    return pl.pallas_call(
        pack_kernel,
        out_shape=(
            jax.ShapeDtypeStruct((groups, SLAB, width), jnp.bfloat16),
            jax.ShapeDtypeStruct((blk, width), jnp.bfloat16),
        ),
        in_specs=[pl.BlockSpec(memory_space=pltpu.SMEM), whole, whole, whole],
        out_specs=(pl.BlockSpec(memory_space=pl.ANY), whole),
        scratch_shapes=[
            pltpu.VMEM((blk // SUB, SLAB, width), jnp.bfloat16),
            pltpu.SemaphoreType.DMA((groups,)),
        ],
        compiler_params=params(),
        cost_estimate=pl.CostEstimate(
            flops=blk * width * 4, bytes_accessed=(groups * SLAB * 2 + blk * 10) * width, transcendentals=0
        ),
        name="pack",
    )(pick, intensities, observed, qweights)


def move_kernel(ops_ref, x_ref, w_ref, moved_ref, table, target):
    blk, width = x_ref.shape

    @pl.when(pl.program_id(0) == 0)
    def _():
        @pl.loop(0, width // LANES)
        def _(i):
            cols = pl.ds(pl.multiple_of(i * LANES, LANES), LANES)
            wide_x = x_ref[:, cols].astype(jnp.float32)
            wide_w = w_ref[:, cols].astype(jnp.float32)
            wx = (wide_w * wide_x).astype(jnp.bfloat16).astype(jnp.float32)
            wxx = (wide_w * wide_x * wide_x).astype(jnp.bfloat16).astype(jnp.float32)
            stacked = jnp.concatenate([wide_w, wx, wxx, jnp.zeros((LANES - 3 * blk, LANES), jnp.float32)], 0)
            table[cols, :] = stacked.T

    unroll = 16

    @pl.loop(0, width // unroll)
    def _(i):
        base = pl.multiple_of(i * unroll, unroll)
        for j in range(unroll):
            to = ops_ref[0, 0, base + j]
            target[pl.ds(to, 1), :] = table[pl.ds(base + j, 1), :]

    step = min(512, width)

    @pl.loop(0, width // step)
    def _(i):
        rows = pl.ds(pl.multiple_of(i * step, step), step)
        moved_ref[rows, :] = target[rows, :].astype(jnp.bfloat16)


def move(local_ops, intensities, own_w):
    blk, width = intensities.shape
    whole = pl.BlockSpec(memory_space=pltpu.VMEM)
    return pl.pallas_call(
        move_kernel,
        grid=(NOPS,),
        out_shape=jax.ShapeDtypeStruct((width, NOPS * LANES), jnp.bfloat16),
        in_specs=[
            pl.BlockSpec((1, 1, width), lambda k: (k, 0, 0), memory_space=pltpu.SMEM),
            whole,
            whole,
        ],
        out_specs=pl.BlockSpec((width, LANES), lambda k: (0, k)),
        scratch_shapes=[
            pltpu.VMEM((width, LANES), jnp.float32),
            pltpu.VMEM((width, LANES), jnp.float32),
        ],
        compiler_params=params(),
        cost_estimate=pl.CostEstimate(
            flops=0, bytes_accessed=NOPS * width * LANES * 100, transcendentals=0
        ),
        name="move",
    )(local_ops[:, None, :], intensities, own_w)


def sums_kernel(got_ref, moved_ref, out_ref):
    rows, depth = got_ref.shape
    step = min(512, depth)

    @pl.when(pl.program_id(0) == 0)
    def _():
        out_ref[...] = jnp.zeros_like(out_ref)

    is_x = lax.broadcasted_iota(jnp.int32, (rows // SLAB, SLAB, step), 1) < SUB

    @pl.loop(0, depth // step)
    def _(i):
        cols = pl.ds(pl.multiple_of(i * step, step), step)
        raw = got_ref[:, cols]
        wide = raw.astype(jnp.float32).reshape(rows // SLAB, SLAB, step)
        product = wide * pltpu.roll(wide, SUB, 1)
        second = jnp.where(is_x, product * wide, product)
        second = second.reshape(rows, step).astype(jnp.bfloat16)
        right = moved_ref[cols, :]
        out_ref[0] += jnp.dot(raw, right, preferred_element_type=jnp.float32)
        out_ref[1] += jnp.dot(second, right, preferred_element_type=jnp.float32)


def sums(got, moved):
    rows, width = got.shape
    depth = min(2048, width)
    return pl.pallas_call(
        sums_kernel,
        grid=(width // depth,),
        out_shape=jax.ShapeDtypeStruct((2, rows, moved.shape[1]), jnp.float32),
        in_specs=[
            pl.BlockSpec((rows, depth), lambda i: (0, i)),
            pl.BlockSpec((depth, moved.shape[1]), lambda i: (i, 0)),
        ],
        out_specs=pl.BlockSpec((2, rows, moved.shape[1]), lambda i: (0, 0, 0)),
        compiler_params=params(),
        cost_estimate=pl.CostEstimate(
            flops=4 * rows * width * moved.shape[1],
            bytes_accessed=2 * width * (rows + moved.shape[1]),
            transcendentals=0,
        ),
        name="sums",
    )(got, moved)


def pearson(share, blk):
    first, second = share[0], share[1]
    total_w = first[:, SUB:, :, :blk]
    sum_x = first[:, SUB:, :, blk : 2 * blk]
    sum_xx = first[:, SUB:, :, 2 * blk : 3 * blk]
    sum_y = second[:, SUB:, :, :blk]
    sum_xy = second[:, SUB:, :, blk : 2 * blk]
    sum_yy = second[:, :SUB, :, :blk]
    numer = total_w * sum_xy - sum_x * sum_y
    var_x = jnp.maximum(total_w * sum_xx - sum_x * sum_x, 0.05 * total_w * sum_xx)
    var_y = jnp.maximum(total_w * sum_yy - sum_y * sum_y, 0.05 * total_w * sum_yy)
    return numer / jnp.sqrt(var_x * var_y)


def shards(intensities, observed, qweights, ops, pick):
    blk, width = intensities.shape
    groups = lax.axis_size("dp")
    shares = lax.axis_size("refl")
    local_ops = ops - lax.axis_index("refl") * width
    send, own_w = pack(pick[:, 0], intensities, observed, qweights)
    got = lax.all_to_all(send, "dp", split_axis=0, concat_axis=0, tiled=True)
    moved = move(local_ops, intensities, own_w)
    stats = sums(got.reshape(groups * SLAB, width), moved)
    if shares > 1:
        stats = lax.psum(stats, "refl")
    stats = stats.reshape(2, groups, SLAB, NOPS, LANES)
    full = pearson(stats, blk)
    rows = blk // shares
    if shares > 1:
        full = lax.dynamic_slice_in_dim(full, lax.axis_index("refl") * rows, rows, 3)
    corr = jnp.transpose(full, (2, 3, 0, 1)).reshape(NOPS, rows, groups * SUB)
    back = lax.all_to_all(full, "dp", split_axis=0, concat_axis=0, tiled=True)
    returned = jnp.transpose(back, (2, 0, 1, 3))[:, None]
    return (corr, returned)


def solution(mesh):
    return jax.shard_map(
        shards,
        mesh=mesh,
        in_specs=(
            P("dp", "refl"),
            P("dp", "refl"),
            P("dp", "refl"),
            P(None, "refl"),
            P(None, "dp"),
        ),
        out_specs=(P(None, ("dp", "refl"), None), P(None, "dp", None, None, "refl")),
        check_vma=False,
    )
```

time: 715 us -> 235 us (0.33); the launches traced: 706 us -> 234 us
  local copies, waits for them, and re-layouts: 586 us -> 5.23 us
  Pallas kernels: 0 us -> 115 us
  waiting for transfers between devices: 0.01 us -> 101 us
  other arithmetic: 69.5 us -> 1.88 us
  matrix products: 21.9 us -> 0 us
  blocking collectives: 13.2 us -> 0 us
    gather x8 -> x0, local copies, waits for them, and re-layouts: 260 us -> none  [the longest x4 231 us: shards(): moved_own = jnp.take(stacked_own, inverse, axis=1)]
    scatter x4 -> x0, local copies, waits for them, and re-layouts: 242 us -> none  [shards(): inverse = jnp.zeros((width,), jnp.int32).at[local_ops[k]].set(positions)]
    pallas_call x0 -> x3, Pallas kernels: none -> 115 us  [the longest x1 90.2 us: move(): pl.pallas_call(move_kernel, grid=(NOPS,), out_shape=jax.ShapeDtypeStruct(...]
    all_to_all x2, waiting for transfers between devices: 0.01 us -> 101 us  [the longest x1 94.9 us: shards(): got = lax.all_to_all(send, 'dp', split_axis=0, concat_axis=0, tiled=True)]
    select_n x6 -> x0, other arithmetic: 46.5 us -> none  [the longest x4 46.1 us: shards(): moved_own = jnp.take(stacked_own, inverse, axis=1)]
    select_n x5 -> x0, local copies, waits for them, and re-layouts: 24 us -> none  [the longest x4 23.9 us: shards(): moved_own = jnp.take(stacked_own, inverse, axis=1)]
    dot_general x12 -> x0, matrix products: 21.9 us -> none  [gram(): lax.dot_general(left, right, (((1,), (1,)), ((), ())), preferred_element_...]
    convert_element_type x3 -> x0, other arithmetic: 18.7 us -> none  [the longest x1 9.45 us: shards(): part_wy = (wide_w * wide_x).astype(jnp.bfloat16)]
  transfers between devices with their start and end apart: 2 -> 2, of which waited for: 0 -> 2; matrix products, arithmetic and copies ran while one was open for 84% -> 1% of each run, Pallas kernels for 0% -> 39%
where the time goes in v1:
time: 235 us; the launch traced here: 234 us
  Pallas kernels  115 us (49%)
  waiting for transfers between devices  101 us (43%)
  starting transfers between devices  10 us (4%)
  local copies, waits for them, and re-layouts  5.23 us (2%)
    all_to_all x1, waiting for transfers between devices, shards(): got = lax.all_to_all(send, 'dp', split_axis=0, concat_axis=0, tiled=True)  94.9 us
    pallas_call x1, Pallas kernels, move(): pl.pallas_call(move_kernel, grid=(NOPS,), out_shape=jax.ShapeDtypeStruct(...  90.2 us
    pallas_call x1, Pallas kernels, sums(): pl.pallas_call(sums_kernel, grid=(width // depth,), out_shape=jax.ShapeDt...  17.8 us
    pallas_call x1, Pallas kernels, pack(): pl.pallas_call(pack_kernel, out_shape=(jax.ShapeDtypeStruct((groups, SLAB...  7.44 us
    all_to_all x1, starting transfers between devices, shards(): got = lax.all_to_all(send, 'dp', split_axis=0, concat_axis=0, tiled=True)  7.43 us
    all_to_all x1, waiting for transfers between devices, shards(): back = lax.all_to_all(full, 'dp', split_axis=0, concat_axis=0, tiled=True)  6.07 us
  transfers between devices with their start and end apart: 2, of which 2 were waited for; matrix products, arithmetic and copies ran while one was open for 1% of the time, Pallas kernels for 39%

profile of v1, /device:TPU:0, one launch (start us, length us, event | category | flops | bytes accessed | tf_op | source)
XLA Modules:
  0.0 234.3 jit_solution(2170565092194234565)
XLA Ops:
  0.6 7.4 %pack.1 = (bf16[32,8,16384]{2,1,0:T(8,128)(2,1)}, bf16[32,16384]{1,0:T(8,128)(2,1)}) custom-call(s32[32]{0:T(128)} %bitcast.18, bf16[32,16384]{1,0:T(8,128)(2,1)} %x_ref.3, s32[32,16384]{1,0:T(8,128)} %obs_ref.1, bf16[32,16384]{1,0:T(8,128)(2,1)} %qw_ref.1), custom_call_target="tpu_custom_call" | custom-call | flops 2097152 | bytes 13631488 | tf_op jit(solution)/shard_map/pack/pallas_call | solution.py:54
  8.1 0.0 copy-start
  8.1 7.4 %all-to-all-start = ((bf16[32,8,16384]{2,1,0:T(8,128)(2,1)}), bf16[32,8,16384]{2,1,0:T(8,128)(2,1)}, u32[]{:S(2)}, u32[]{:S(2)}) async-start(bf16[32,8,16384]{2,1,0:T(8,128)(2,1)} %get-tuple-element.4), calls=%async_computation | async-start | bytes 16777216 | tf_op jit(solution)/shard_map/all_to_all | solution.py:196
  15.5 0.0 copy-done
  15.5 0.9 broadcast_in_dim.6.ops_ref
  16.4 90.2 %move.1.moved_ref = bf16[16384,512]{1,0:T(8,128)(2,1)} custom-call(s32[4,1,16384]{2,1,0:T(1,128)} %broadcast_in_dim.6.ops_ref, bf16[32,16384]{1,0:T(8,128)(2,1)} %x_ref.3, bf16[32,16384]{1,0:T(8,128)(2,1)} %get-tuple-element.5.w_ref), custom_call_target="tpu_custom_call" | custom-call | bytes 838860800 | tf_op jit(solution)/shard_map/move/pallas_call | solution.py:109
  106.6 94.9 %all-to-all-done = bf16[32,8,16384]{2,1,0:T(8,128)(2,1)} async-done(((bf16[32,8,16384]{2,1,0:T(8,128)(2,1)}), bf16[32,8,16384]{2,1,0:T(8,128)(2,1)}, u32[]{:S(2)}, u32[]{:S(2)}) %all-to-all-start) | async-done | bytes 8388640 | tf_op jit(solution)/shard_map/all_to_all | solution.py:196
  201.6 17.8 %sums.1 = f32[2,256,512]{2,1,0:T(8,128)} custom-call(bf16[256,16384]{1,0:T(8,128)(2,1)} %bitcast.1.got_ref, bf16[16384,512]{1,0:T(8,128)(2,1)} %move.1.moved_ref), custom_call_target="tpu_custom_call" | custom-call | flops 8589934592 | bytes 25165824 | tf_op jit(solution)/shard_map/sums/pallas_call | solution.py:157
  219.3 1.3 slice_bitcast_fusion.1
  220.6 0.5 fusion.2
  221.2 0.8 reshape.17
  222.0 2.6 %all-to-all-start.1 = ((f32[32,1,512]{2,1,0:T(1,128)}), f32[32,1,512]{2,1,0:T(1,128)S(1)}, u32[]{:S(2)}, u32[]{:S(2)}) async-start(f32[32,1,512]{2,1,0:T(1,128)} %reshape.17), calls=%async_computation.1 | async-start | bytes 131072 | tf_op jit(solution)/shard_map/all_to_all | solution.py:207
  224.6 0.5 fusion.3
  225.2 0.7 copy.21
  225.9 6.1 %all-to-all-done.1 = f32[32,1,512]{2,1,0:T(1,128)S(1)} async-done(((f32[32,1,512]{2,1,0:T(1,128)}), f32[32,1,512]{2,1,0:T(1,128)S(1)}, u32[]{:S(2)}, u32[]{:S(2)}) %all-to-all-start.1) | async-done | bytes 65568 | tf_op jit(solution)/shard_map/all_to_all | solution.py:207
  232.0 0.5 broadcast.9
  232.5 0.8 reduce
  233.3 0.2 reshape.18
  233.5 0.7 copy.22
  (2 shorter events, 0.1 us)
Async XLA Ops:
  8.1 7.5 %copy-start = (s32[4,16384]{1,0:T(4,128)S(1)}, s32[4,16384]{1,0:T(4,128)}, u32[]{:S(2)}) copy-start(s32[4,16384]{1,0:T(4,128)} %param.8) | copy-start | bytes 786436
  8.1 193.5 %all-to-all-start = ((bf16[32,8,16384]{2,1,0:T(8,128)(2,1)}), bf16[32,8,16384]{2,1,0:T(8,128)(2,1)}, u32[]{:S(2)}, u32[]{:S(2)}) async-start(bf16[32,8,16384]{2,1,0:T(8,128)(2,1)} %get-tuple-element.4), calls=%async_computation | async-start | bytes 16777216 | tf_op jit(solution)/shard_map/all_to_all | solution.py:196
  222.0 10.0 %all-to-all-start.1 = ((f32[32,1,512]{2,1,0:T(1,128)}), f32[32,1,512]{2,1,0:T(1,128)S(1)}, u32[]{:S(2)}, u32[]{:S(2)}) async-start(f32[32,1,512]{2,1,0:T(1,128)} %reshape.17), calls=%async_computation.1 | async-start | bytes 131072 | tf_op jit(solution)/shard_map/all_to_all | solution.py:207

commit v2 on v1

--- a/solution.py
+++ b/solution.py
@@ -12,6 +12,9 @@
 LANES = 128
 SLAB = 2 * SUB
 VMEM_LIMIT = 56 * 1024 * 1024
+PLANES = 4
+PLANE = 8
+UNROLL = 64
 
 
 def params():
@@ -187,7 +190,272 @@
     return numer / jnp.sqrt(var_x * var_y)
 
 
+def plane_pack_kernel(pick_ref, x_ref, w_ref, send_ref, slabs, sems):
+    blk, width = x_ref.shape
+    step = min(512, width)
+
+    @pl.loop(0, width // step)
+    def _(i):
+        cols = pl.ds(pl.multiple_of(i * step, step), step)
+        wide_x = x_ref[:, cols].astype(jnp.float32)
+        wide_w = w_ref[:, cols].astype(jnp.float32)
+        for g in range(blk // SUB):
+            rows = slice(g * SUB, (g + 1) * SUB)
+            slab = jnp.concatenate([wide_x[rows], wide_w[rows]], 0)
+            slabs[g, :, cols] = slab.astype(jnp.bfloat16)
+
+    me = lax.axis_index("dp")
+    mine = lax.div(me, PLANE)
+    partner = mine + 1 - 2 * lax.rem(mine, 2)
+
+    def copies(c):
+        first = pick_ref[mine * PLANE + c]
+        second = pick_ref[partner * PLANE + c]
+        return (
+            pltpu.make_async_copy(slabs.at[first], send_ref.at[c, 0], sems.at[c, 0]),
+            pltpu.make_async_copy(slabs.at[second], send_ref.at[c, 1], sems.at[c, 1]),
+        )
+
+    for c in range(PLANE):
+        for copy in copies(c):
+            copy.start()
+    for c in range(PLANE):
+        for copy in copies(c):
+            copy.wait()
+
+
+def plane_pack(pick, x, w):
+    blk, width = x.shape
+    whole = pl.BlockSpec(memory_space=pltpu.VMEM)
+    return pl.pallas_call(
+        plane_pack_kernel,
+        out_shape=jax.ShapeDtypeStruct((PLANE, 2, SLAB, width), jnp.bfloat16),
+        in_specs=[pl.BlockSpec(memory_space=pltpu.SMEM), whole, whole],
+        out_specs=pl.BlockSpec(memory_space=pl.ANY),
+        scratch_shapes=[
+            pltpu.VMEM((blk // SUB, SLAB, width), jnp.bfloat16),
+            pltpu.SemaphoreType.DMA((PLANE, 2)),
+        ],
+        compiler_params=params(),
+        cost_estimate=pl.CostEstimate(
+            flops=blk * width * 4, bytes_accessed=(PLANE * 2 * SLAB * 2 + blk * 4) * width, transcendentals=0
+        ),
+        name="plane_pack",
+    )(pick, x, w)
+
+
+def table_kernel(x_ref, x1_ref, w_ref, w1_ref, table_ref):
+    width = x_ref.shape[1]
+
+    @pl.loop(0, width // LANES)
+    def _(i):
+        cols = pl.ds(pl.multiple_of(i * LANES, LANES), LANES)
+        parts = [ref[:, cols].astype(jnp.float32) for ref in (x_ref, x1_ref, w_ref, w1_ref)]
+        table_ref[cols, :] = jnp.concatenate(parts, 0).T
+
+
+def make_table(x, x1, w, w1):
+    blk, width = x.shape
+    step = min(2048, width)
+    spec = pl.BlockSpec((blk, step), lambda i: (0, i))
+    return pl.pallas_call(
+        table_kernel,
+        grid=(width // step,),
+        out_shape=jax.ShapeDtypeStruct((width, LANES), jnp.float32),
+        in_specs=[spec] * 4,
+        out_specs=pl.BlockSpec((step, LANES), lambda i: (i, 0)),
+        compiler_params=params(),
+        cost_estimate=pl.CostEstimate(flops=0, bytes_accessed=width * LANES * 8, transcendentals=0),
+        name="table",
+    )(x, x1, w, w1)
+
+
+def place_kernel(ops_ref, table_ref, after_ref, moved_ref, target):
+    depth = table_ref.shape[0]
+    width = target.shape[0]
+
+    @pl.loop(0, depth // UNROLL)
+    def _(i):
+        base = pl.multiple_of(i * UNROLL, UNROLL)
+        for j in range(UNROLL):
+            to = ops_ref[0, 0, base + j]
+            target[pl.ds(to, 1), :] = table_ref[pl.ds(base + j, 1), :]
+
+    @pl.when(pl.program_id(1) == pl.num_programs(1) - 1)
+    def _():
+        step = min(512, width)
+
+        @pl.loop(0, width // step)
+        def _(i):
+            rows = pl.ds(pl.multiple_of(i * step, step), step)
+            moved_ref[rows, :] = target[rows, :].astype(jnp.bfloat16)
+
+
+def place(ops, table, after):
+    count = ops.shape[0]
+    width = table.shape[0]
+    depth = min(2048, width)
+    return pl.pallas_call(
+        place_kernel,
+        grid=(count, width // depth),
+        out_shape=jax.ShapeDtypeStruct((width, count * LANES), jnp.bfloat16),
+        in_specs=[
+            pl.BlockSpec((1, 1, depth), lambda k, i: (k, 0, i), memory_space=pltpu.SMEM),
+            pl.BlockSpec((depth, LANES), lambda k, i: (i, 0)),
+            pl.BlockSpec(memory_space=pl.ANY),
+        ],
+        out_specs=pl.BlockSpec((width, LANES), lambda k, i: (0, k)),
+        scratch_shapes=[pltpu.VMEM((width, LANES), jnp.float32)],
+        compiler_params=params(),
+        cost_estimate=pl.CostEstimate(
+            flops=0, bytes_accessed=count * width * LANES * 64, transcendentals=0
+        ),
+        name="place",
+    )(ops[:, None, :], table, after)
+
+
+def plane_sums_kernel(own_ref, far_ref, first_ref, second_ref, out_ref):
+    rows, depth = own_ref.shape
+    step = min(512, depth)
+    half = LANES // 2
+
+    @pl.when(pl.program_id(0) == 0)
+    def _():
+        out_ref[...] = jnp.zeros_like(out_ref)
+
+    is_x = lax.broadcasted_iota(jnp.int32, (rows // SLAB, SLAB, step), 1) < SUB
+    low = lax.broadcasted_iota(jnp.int32, (step, LANES), 1) < half
+
+    @pl.loop(0, depth // step)
+    def _(i):
+        cols = pl.ds(pl.multiple_of(i * step, step), step)
+        raws, products = [], []
+        for ref in (own_ref, far_ref):
+            raw = ref[:, cols]
+            wide = raw.astype(jnp.float32).reshape(rows // SLAB, SLAB, step)
+            product = wide * pltpu.roll(wide, SUB, 1)
+            both = jnp.where(is_x, product * wide, product)
+            raws.append(raw)
+            products.append(both.reshape(rows, step).astype(jnp.bfloat16))
+        linear, square = [], []
+        for ref in (first_ref, second_ref):
+            even, odd = None, None
+            for k in range(2):
+                values = ref[cols, k * LANES : (k + 1) * LANES].astype(jnp.float32)
+                swapped = pltpu.roll(values, half, 1)
+                product = values * swapped
+                linear.append(jnp.where(low, product, values).astype(jnp.bfloat16))
+                if k == 0:
+                    even = product * values
+                else:
+                    odd = product * swapped
+            square.append(jnp.where(low, even, odd).astype(jnp.bfloat16))
+        right = jnp.concatenate(linear + square, 1)
+        out_ref[0] += jnp.dot(jnp.concatenate(raws, 0), right, preferred_element_type=jnp.float32)
+        out_ref[1] += jnp.dot(jnp.concatenate(products, 0), right, preferred_element_type=jnp.float32)
+
+
+def plane_sums(own, far, first, second):
+    rows, width = own.shape
+    depth = min(2048, width)
+    lanes = (NOPS + NOPS // 2) * LANES
+    part = pl.BlockSpec((rows, depth), lambda i: (0, i))
+    moved = pl.BlockSpec((depth, 2 * LANES), lambda i: (i, 0))
+    return pl.pallas_call(
+        plane_sums_kernel,
+        grid=(width // depth,),
+        out_shape=jax.ShapeDtypeStruct((2, 2 * rows, lanes), jnp.float32),
+        in_specs=[part, part, moved, moved],
+        out_specs=pl.BlockSpec((2, 2 * rows, lanes), lambda i: (0, 0, 0)),
+        compiler_params=params(),
+        cost_estimate=pl.CostEstimate(
+            flops=8 * rows * width * lanes,
+            bytes_accessed=width * (4 * rows + 8 * LANES),
+            transcendentals=0,
+        ),
+        name="plane_sums",
+    )(own, far, first, second)
+
+
+def ratio(total_w, sum_x, sum_xx, sum_y, sum_xy, sum_yy):
+    numer = total_w * sum_xy - sum_x * sum_y
+    var_x = jnp.maximum(total_w * sum_xx - sum_x * sum_x, 0.05 * total_w * sum_xx)
+    var_y = jnp.maximum(total_w * sum_yy - sum_y * sum_y, 0.05 * total_w * sum_yy)
+    return numer / jnp.sqrt(var_x * var_y)
+
+
+def plane_pearson(stats, blk, which):
+    stats = stats.reshape(2, 2, PLANE, 2, SLAB, -1)[:, :, :, which]
+    lead = (2, PLANE, SUB)
+    straight = NOPS * LANES
+
+    def linear(part, rows, offset):
+        picked = part[:, :, rows, :straight].reshape(*lead, NOPS, 4, blk)
+        return picked[:, :, :, :, offset + which]
+
+    total_w = linear(stats[0], slice(SUB, None), 2)
+    sum_x = linear(stats[0], slice(SUB, None), 0)
+    sum_y = linear(stats[1], slice(SUB, None), 2)
+    sum_xy = linear(stats[1], slice(SUB, None), 0)
+    sum_yy = linear(stats[1], slice(None, SUB), 2)
+    sum_xx = stats[0][:, :, SUB:, straight:].reshape(*lead, NOPS, 2, blk)[:, :, :, :, which]
+    return ratio(total_w, sum_x, sum_xx, sum_y, sum_xy, sum_yy)
+
+
+def shards_by_plane(intensities, observed, qweights, ops, pick):
+    blk, width = intensities.shape
+    groups = PLANES * PLANE
+    near = [(i, i ^ PLANE) for i in range(groups)]
+    far = [(i, i ^ (2 * PLANE)) for i in range(groups)]
+    rings = [[z * PLANE + c for c in range(PLANE)] for z in range(PLANES)]
+    plane = lax.axis_index("dp") // PLANE
+    odd, upper = plane % 2 == 1, plane >= 2
+
+    def spread(send):
+        got = lax.all_to_all(send, "dp", split_axis=0, concat_axis=0, axis_index_groups=rings, tiled=True)
+        return got.reshape(PLANE * 2 * SLAB, width)
+
+    own_pick = pick[:, 0]
+    own_w = (observed.astype(jnp.float32) * qweights.astype(jnp.float32)).astype(jnp.bfloat16)
+    near_x = lax.ppermute(intensities, "dp", near)
+    near_w = lax.ppermute(own_w, "dp", near)
+    far_pick = lax.ppermute(own_pick, "dp", far)
+    own_got = spread(plane_pack(own_pick, intensities, own_w))
+    later_x, later_w, near_x, near_w = lax.optimization_barrier((intensities, own_w, near_x, near_w))
+    far_x = lax.ppermute(later_x, "dp", far)
+    far_w = lax.ppermute(later_w, "dp", far)
+    table = make_table(intensities, near_x, own_w, near_w)
+    first = place(ops[:2], table, own_pick)
+    far_send = plane_pack(far_pick, far_x, far_w)
+    far_got = spread(far_send)
+    second = place(ops[2:], table, far_send)
+    stats = plane_sums(own_got, far_got, first, second)
+    mine = plane_pearson(stats, blk, 0)
+    other = plane_pearson(stats, blk, 1)
+
+    from_near = lax.ppermute(other, "dp", near)
+    pair = jnp.stack([mine, from_near], 1)
+    pair = jnp.where(odd, pair[:, ::-1], pair)
+    pair = jnp.where(upper, pair[::-1], pair)
+    corr = jnp.transpose(pair.reshape(groups, SUB, NOPS, blk), (2, 3, 0, 1)).reshape(NOPS, blk, groups * SUB)
+
+    both = jnp.stack([mine, other], 2)
+    both = jnp.where(upper, both[::-1], both)
+    back = jnp.repeat(both, 2, 0).reshape(groups, 2, SUB, NOPS, blk)
+    back = lax.all_to_all(back, "dp", split_axis=0, concat_axis=0, tiled=True)
+    back = back.reshape(2, 2, PLANE, 2, SUB, NOPS, blk)
+    back = jnp.where(odd, back[:, 1, :, ::-1], back[:, 0])
+    returned = jnp.transpose(back, (4, 0, 2, 1, 3, 5)).reshape(NOPS, 1, groups, SUB, blk)
+    return (corr, returned)
+
+
 def shards(intensities, observed, qweights, ops, pick):
+    if lax.axis_size("dp") == PLANES * PLANE and lax.axis_size("refl") == 1:
+        return shards_by_plane(intensities, observed, qweights, ops, pick)
+    return shards_direct(intensities, observed, qweights, ops, pick)
+
+
+def shards_direct(intensities, observed, qweights, ops, pick):
     blk, width = intensities.shape
     groups = lax.axis_size("dp")
     shares = lax.axis_size("refl")

time: 235 us -> 305 us (1.30)
  waiting for transfers between devices: 101 us -> 141 us
  starting transfers between devices: 10 us -> 24.9 us
  local copies, waits for them, and re-layouts: 5.23 us -> 13 us
  Pallas kernels: 115 us -> 120 us
  other arithmetic: 1.88 us -> 5.06 us
    ppermute x0 -> x6, waiting for transfers between devices: none -> 134 us  [the longest x1 87.7 us: shards_by_plane(): far_pick = lax.ppermute(own_pick, 'dp', far)]
    all_to_all x2 -> x3, waiting for transfers between devices: 101 us -> 7.29 us  [the longest x1 7.28 us: shards_by_plane(): back = lax.all_to_all(back, 'dp', split_axis=0, concat_axis=0, tiled=True)]
    ppermute x0 -> x6, starting transfers between devices: none -> 8.84 us  [the longest x1 2.76 us: shards_by_plane(): far_x = lax.ppermute(later_x, 'dp', far)]
    all_to_all x2 -> x3, starting transfers between devices: 10 us -> 16 us  [the longest x2 9.99 us: spread(): lax.all_to_all(send, 'dp', split_axis=0, concat_axis=0, axis_index_groups...]
    pallas_call x3 -> x6, Pallas kernels: 115 us -> 120 us  [the longest x2 67.7 us: place(): pl.pallas_call(place_kernel, grid=(count, width // depth), out_shape=jax....]
    convert_element_type x0 -> x1, other arithmetic: none -> 3.17 us  [shards_by_plane(): (observed.astype(jnp.float32) * qweights.astype(jnp.float32)).astype(jnp....]
  transfers between devices with their start and end apart: 2 -> 9, of which waited for: 2 -> 4; matrix products, arithmetic and copies ran while one was open for 1% -> 1% of each run, Pallas kernels for 39% -> 29%
where the time goes in v2:
time: 305 us
  waiting for transfers between devices  141 us (46%)
  Pallas kernels  120 us (39%)
  starting transfers between devices  24.9 us (8%)
  local copies, waits for them, and re-layouts  13 us (4%)
  other arithmetic  5.06 us (2%)
    ppermute x1, waiting for transfers between devices, shards_by_plane(): far_pick = lax.ppermute(own_pick, 'dp', far)  87.7 us
    pallas_call x2, Pallas kernels, place(): pl.pallas_call(place_kernel, grid=(count, width // depth), out_shape=jax....  67.7 us
    pallas_call x1, Pallas kernels, plane_sums(): pl.pallas_call(plane_sums_kernel, grid=(width // depth,), out_shape=jax.S...  28.2 us
    ppermute x1, waiting for transfers between devices, shards_by_plane(): near_w = lax.ppermute(own_w, 'dp', near)  23.8 us
    ppermute x1, waiting for transfers between devices, shards_by_plane(): near_x = lax.ppermute(intensities, 'dp', near)  22.2 us
    pallas_call x1, Pallas kernels, make_table(): pl.pallas_call(table_kernel, grid=(width // step,), out_shape=jax.ShapeDt...  15.3 us
    all_to_all x2, starting transfers between devices, spread(): lax.all_to_all(send, 'dp', split_axis=0, concat_axis=0, axis_index_groups...  9.99 us
    pallas_call x2, Pallas kernels, plane_pack(): pl.pallas_call(plane_pack_kernel, out_shape=jax.ShapeDtypeStruct((PLANE,...  8.54 us
  transfers between devices with their start and end apart: 9, of which 4 were waited for; matrix products, arithmetic and copies ran while one was open for 1% of the time, Pallas kernels for 29%

profile of v2, /device:TPU:0, one launch (start us, length us, event | category | flops | bytes accessed | tf_op | source)
XLA Modules:
  0.0 304.7 jit_solution(14344898874094503428)
XLA Ops:
  0.6 3.2 %multiply_convert_fusion.w_ref = bf16[32,16384]{1,0:T(8,128)(2,1)} fusion(bf16[32,16384]{1,0:T(8,128)(2,1)} %param.7, s32[32,16384]{1,0:T(8,128)} %param.6), kind=kLoop, calls=%fused_computation | loop fusion | flops 2097152 | bytes 4194304 | tf_op jit(solution)/shard_map/convert_element_type | solution.py:419
  3.8 4.3 %plane_pack.2 = bf16[8,2,8,16384]{3,2,1,0:T(8,128)(2,1)} custom-call(s32[32]{0:T(128)} %bitcast.196, bf16[32,16384]{1,0:T(8,128)(2,1)} %x_ref.3, bf16[32,16384]{1,0:T(8,128)(2,1)} %multiply_convert_fusion.w_ref), custom_call_target="tpu_custom_call" | custom-call | flops 2097152 | bytes 6291456 | tf_op jit(solution)/shard_map/plane_pack/pallas_call | solution.py:230
  8.1 0.0 copy-start.1
  8.1 0.0 copy-start.7
  8.1 5.3 %all-to-all-start = ((bf16[8,2,8,16384]{3,2,1,0:T(8,128)(2,1)}), bf16[8,2,8,16384]{3,2,1,0:T(8,128)(2,1)}, u32[]{:S(2)}, u32[]{:S(2)}) async-start(bf16[8,2,8,16384]{3,2,1,0:T(8,128)(2,1)} %plane_pack.2), calls=%async_computation | async-start | bytes 8388608 | tf_op jit(solution)/shard_map/all_to_all | solution.py:415
  13.4 2.6 collective-permute-start.2
  16.0 0.1 collective-permute-start.1
  16.1 23.8 %collective-permute-done.2.w1_ref = bf16[32,16384]{1,0:T(8,128)(2,1)S(1)} collective-permute-done((bf16[32,16384]{1,0:T(8,128)(2,1)S(1)}, bf16[32,16384]{1,0:T(8,128)(2,1)S(1)}, u32[]{:S(2)}, u32[]{:S(2)}) %collective-permute-start.2) | collective-permute-done | bytes 1048608 | tf_op jit(solution)/shard_map/ppermute | solution.py:421
  39.9 22.2 %collective-permute-done.1.x1_ref = bf16[32,16384]{1,0:T(8,128)(2,1)S(1)} collective-permute-done((bf16[32,16384]{1,0:T(8,128)(2,1)S(1)}, bf16[32,16384]{1,0:T(8,128)(2,1)S(1)}, u32[]{:S(2)}, u32[]{:S(2)}) %collective-permute-start.1) | collective-permute-done | bytes 1048608 | tf_op jit(solution)/shard_map/ppermute | solution.py:420
  62.1 2.8 collective-permute-start.3
  64.8 0.2 collective-permute-start.4
  65.0 2.8 collective-permute-start
  67.7 87.7 %collective-permute-done.pick_ref = s32[32]{0:T(128)S(1)} collective-permute-done((s32[32]{0:T(128)S(1)}, s32[32]{0:T(128)S(1)}, u32[]{:S(2)}, u32[]{:S(2)}) %collective-permute-start) | collective-permute-done | bytes 160 | tf_op jit(solution)/shard_map/ppermute | solution.py:422
  155.4 0.0 collective-permute-done.3.x_ref
  155.5 0.0 collective-permute-done.4.w_ref
  155.5 0.5 copy-done.8
  155.9 0.6 copy-done.4
  156.5 1.1 copy-done.5
  157.6 4.3 %plane_pack.3.after_ref = bf16[8,2,8,16384]{3,2,1,0:T(8,128)(2,1)} custom-call(s32[32]{0:T(128)} %copy-done.8, bf16[32,16384]{1,0:T(8,128)(2,1)} %copy-done.4, bf16[32,16384]{1,0:T(8,128)(2,1)} %copy-done.5), custom_call_target="tpu_custom_call" | custom-call | flops 2097152 | bytes 6291456 | tf_op jit(solution)/shard_map/plane_pack/pallas_call | solution.py:230
  161.9 0.0 copy-start.6
  161.9 4.7 %all-to-all-start.1 = ((bf16[8,2,8,16384]{3,2,1,0:T(8,128)(2,1)}), bf16[8,2,8,16384]{3,2,1,0:T(8,128)(2,1)}, u32[]{:S(2)}, u32[]{:S(2)}) async-start(bf16[8,2,8,16384]{3,2,1,0:T(8,128)(2,1)} %plane_pack.3.after_ref), calls=%async_computation.1 | async-start | bytes 8388608 | tf_op jit(solution)/shard_map/all_to_all | solution.py:415
  166.6 0.1 fusion.28
  166.8 0.7 broadcast_in_dim.10.ops_ref
  167.5 0.7 broadcast_in_dim.9.ops_ref
  168.2 15.3 %table.1.table_ref = f32[16384,128]{1,0:T(8,128)} custom-call(bf16[32,16384]{1,0:T(8,128)(2,1)} %x_ref.3, bf16[32,16384]{1,0:T(8,128)(2,1)} %copy-done.3, bf16[32,16384]{1,0:T(8,128)(2,1)} %multiply_convert_fusion.w_ref, bf16[32,16384]{1,0:T(8,128)(2,1)} %copy-done.2), custom_call_target="tpu_custom_call" | custom-call | bytes 16777216 | tf_op jit(solution)/shard_map/table/pallas_call | solution.py:261
  183.5 33.9 %place.2.first_ref = bf16[16384,256]{1,0:T(8,128)(2,1)} custom-call(s32[2,1,16384]{2,1,0:T(1,128)} %broadcast_in_dim.9.ops_ref, f32[16384,128]{1,0:T(8,128)} %table.1.table_ref, s32[32]{0:T(128)} %bitcast.197), custom_call_target="tpu_custom_call" | custom-call | bytes 268435456 | tf_op jit(solution)/shard_map/place/pallas_call | solution.py:298
  217.4 33.9 %place.3.second_ref = bf16[16384,256]{1,0:T(8,128)(2,1)} custom-call(s32[2,1,16384]{2,1,0:T(1,128)} %broadcast_in_dim.10.ops_ref, f32[16384,128]{1,0:T(8,128)} %table.1.table_ref, bf16[8,2,8,16384]{3,2,1,0:T(8,128)(2,1)} %plane_pack.3.after_ref), custom_call_target="tpu_custom_call" | custom-call | bytes 268435456 | tf_op jit(solution)/shard_map/place/pallas_call | solution.py:298
  251.3 28.2 %plane_sums.1 = f32[2,256,768]{2,1,0:T(8,128)} custom-call(bf16[128,16384]{1,0:T(8,128)(2,1)} %bitcast.1.own_ref, bf16[128,16384]{1,0:T(8,128)(2,1)} %bitcast.2.far_ref, bf16[16384,256]{1,0:T(8,128)(2,1)} %place.2.first_ref, bf16[16384,256]{1,0:T(8,128)(2,1)} %place.3.second_ref), custom_call_target="tpu_custom_call" | custom-call | flops 12884901888 | bytes 25165824 | tf_op jit(solution)/shard_map/plane_sums/pallas_call | solution.py:364
  279.4 1.5 slice_bitcast_fusion.3
  281.1 0.1 fusion.26
  281.2 0.3 reshape.485
  281.4 0.2 fusion.22
  281.7 0.3 reshape.487
  281.9 0.1 slice.145
  282.1 0.3 reshape.484
  282.4 0.2 fusion.23
  282.6 0.2 reshape.486
  282.8 0.1 slice.143
  282.9 0.2 fusion.9
  283.1 0.2 fusion.20
  283.3 0.3 reshape.489
  283.6 0.2 fusion.24
  283.8 0.3 reshape.491
  284.1 0.1 slice.157
  284.2 0.3 reshape.488
  284.5 0.2 fusion.25
  284.8 0.2 reshape.490
  285.0 0.1 slice.155
  285.2 0.2 fusion.4
  285.3 0.2 fusion.14
  285.5 0.5 collective-permute-start.5
  286.0 0.1 pad_maximum_fusion.1
  286.1 0.2 copy.65
  286.3 0.1 broadcast_in_dim.11
  286.4 1.0 reshape.496
  287.4 6.0 %all-to-all-start.2 = ((f32[32,1,1024]{2,1,0:T(1,128)}), f32[32,1,1024]{2,1,0:T(1,128)S(1)}, u32[]{:S(2)}, u32[]{:S(2)}) async-start(f32[32,1,1024]{2,1,0:T(1,128)} %reshape.496), calls=%async_computation.2 | async-start | bytes 262144 | tf_op jit(solution)/shard_map/all_to_all | solution.py:445
  293.5 0.1 pad_maximum_fusion
  293.7 0.7 copy.68
  294.4 7.3 %all-to-all-done.2 = f32[32,1,1024]{2,1,0:T(1,128)S(1)} async-done(((f32[32,1,1024]{2,1,0:T(1,128)}), f32[32,1,1024]{2,1,0:T(1,128)S(1)}, u32[]{:S(2)}, u32[]{:S(2)}) %all-to-all-start.2) | async-done | bytes 131104 | tf_op jit(solution)/shard_map/all_to_all | solution.py:445
  301.7 0.5 broadcast.39
  302.2 0.9 reduce
  303.2 0.3 reshape.497
  303.4 0.3 copy.66
  303.8 0.9 copy.69
  (25 shorter events, 0.3 us)
Async XLA Ops:
  8.1 5.4 %copy-start = (bf16[32,16384]{1,0:T(8,128)(2,1)S(1)}, bf16[32,16384]{1,0:T(8,128)(2,1)}, u32[]{:S(2)}) copy-start(bf16[32,16384]{1,0:T(8,128)(2,1)} %multiply_convert_fusion.w_ref) | copy-start | bytes 3145732
  8.1 7.9 %copy-start.1 = (bf16[32,16384]{1,0:T(8,128)(2,1)S(1)}, bf16[32,16384]{1,0:T(8,128)(2,1)}, u32[]{:S(2)}) copy-start(bf16[32,16384]{1,0:T(8,128)(2,1)} %x_ref.3) | copy-start | bytes 3145732
  8.1 56.9 %copy-start.7 = (s32[32,1]{0,1:T(1,128)S(1)}, s32[32,1]{0,1:T(1,128)}, u32[]{:S(2)}) copy-start(s32[32,1]{0,1:T(1,128)} %param.9) | copy-start | bytes 388
  8.1 153.8 %all-to-all-start = ((bf16[8,2,8,16384]{3,2,1,0:T(8,128)(2,1)}), bf16[8,2,8,16384]{3,2,1,0:T(8,128)(2,1)}, u32[]{:S(2)}, u32[]{:S(2)}) async-start(bf16[8,2,8,16384]{3,2,1,0:T(8,128)(2,1)} %plane_pack.2), calls=%async_computation | async-start | bytes 8388608 | tf_op jit(solution)/shard_map/all_to_all | solution.py:415
  13.4 26.5 %collective-permute-start.2 = (bf16[32,16384]{1,0:T(8,128)(2,1)S(1)}, bf16[32,16384]{1,0:T(8,128)(2,1)S(1)}, u32[]{:S(2)}, u32[]{:S(2)}) collective-permute-start(bf16[32,16384]{1,0:T(8,128)(2,1)S(1)} %copy-done), channel_id=1, source_target_pairs={{0,8},{1,9},{2,10},{3,11},{4,12},{5,13},{6,14},{7,15},{8,0},{9,1},... | collective-permute-start | bytes 3145736 | tf_op jit(solution)/shard_map/ppermute | solution.py:421
  16.0 46.1 %collective-permute-start.1 = (bf16[32,16384]{1,0:T(8,128)(2,1)S(1)}, bf16[32,16384]{1,0:T(8,128)(2,1)S(1)}, u32[]{:S(2)}, u32[]{:S(2)}) collective-permute-start(bf16[32,16384]{1,0:T(8,128)(2,1)S(1)} %copy-done.1), channel_id=1, source_target_pairs={{0,8},{1,9},{2,10},{3,11},{4,12},{5,13},{6,14},{7,15},{8,0},{9,1},... | collective-permute-start | bytes 3145736 | tf_op jit(solution)/shard_map/ppermute | solution.py:420
  39.9 122.0 %copy-start.2 = (bf16[32,16384]{1,0:T(8,128)(2,1)}, bf16[32,16384]{1,0:T(8,128)(2,1)S(1)}, u32[]{:S(2)}) copy-start(bf16[32,16384]{1,0:T(8,128)(2,1)S(1)} %collective-permute-done.2.w1_ref) | copy-start | bytes 3145732
  62.1 93.4 %copy-start.3 = (bf16[32,16384]{1,0:T(8,128)(2,1)}, bf16[32,16384]{1,0:T(8,128)(2,1)S(1)}, u32[]{:S(2)}) copy-start(bf16[32,16384]{1,0:T(8,128)(2,1)S(1)} %collective-permute-done.1.x1_ref) | copy-start | bytes 3145732
  62.1 93.4 %collective-permute-start.3 = (bf16[32,16384]{1,0:T(8,128)(2,1)S(1)}, bf16[32,16384]{1,0:T(8,128)(2,1)S(1)}, u32[]{:S(2)}, u32[]{:S(2)}) collective-permute-start(bf16[32,16384]{1,0:T(8,128)(2,1)S(1)} %copy-done.1), channel_id=1, source_target_pairs={{0,16},{1,17},{2,18},{3,19},{4,20},{5,21},{6,22},{7,23},{8,24},{9,... | collective-permute-start | bytes 3145736 | tf_op jit(solution)/shard_map/ppermute | solution.py:425
  64.8 90.6 %collective-permute-start.4 = (bf16[32,16384]{1,0:T(8,128)(2,1)S(1)}, bf16[32,16384]{1,0:T(8,128)(2,1)S(1)}, u32[]{:S(2)}, u32[]{:S(2)}) collective-permute-start(bf16[32,16384]{1,0:T(8,128)(2,1)S(1)} %copy-done), channel_id=1, source_target_pairs={{0,16},{1,17},{2,18},{3,19},{4,20},{5,21},{6,22},{7,23},{8,24},{9,... | collective-permute-start | bytes 3145736 | tf_op jit(solution)/shard_map/ppermute | solution.py:426
  65.0 90.4 %collective-permute-start = (s32[32]{0:T(128)S(1)}, s32[32]{0:T(128)S(1)}, u32[]{:S(2)}, u32[]{:S(2)}) collective-permute-start(s32[32]{0:T(128)S(1)} %bitcast.198), channel_id=1, source_target_pairs={{0,16},{1,17},{2,18},{3,19},{4,20},{5,21},{6,22},{7,23},{8,24},{9,... | collective-permute-start | bytes 392 | tf_op jit(solution)/shard_map/ppermute | solution.py:422
  155.4 0.5 copy-start.8
  155.4 1.1 copy-start.4
  156.5 1.1 copy-start.5
  161.9 4.8 %copy-start.6 = (s32[4,16384]{1,0:T(4,128)S(1)}, s32[4,16384]{1,0:T(4,128)}, u32[]{:S(2)}) copy-start(s32[4,16384]{1,0:T(4,128)} %param.8) | copy-start | bytes 786436
  161.9 89.3 %all-to-all-start.1 = ((bf16[8,2,8,16384]{3,2,1,0:T(8,128)(2,1)}), bf16[8,2,8,16384]{3,2,1,0:T(8,128)(2,1)}, u32[]{:S(2)}, u32[]{:S(2)}) async-start(bf16[8,2,8,16384]{3,2,1,0:T(8,128)(2,1)} %plane_pack.3.after_ref), calls=%async_computation.1 | async-start | bytes 8388608 | tf_op jit(solution)/shard_map/all_to_all | solution.py:415
  285.5 8.0 %collective-permute-start.5 = (f32[2,8,4,4,32]{4,2,1,0,3:T(4,128)S(1)}, f32[2,8,4,4,32]{4,2,1,0,3:T(4,128)S(1)}, u32[]{:S(2)}, u32[]{:S(2)}) collective-permute-start(f32[2,8,4,4,32]{4,2,1,0,3:T(4,128)S(1)} %fusion.14), channel_id=1, source_target_pairs={{0,8},{1,9},{2,10},{3,11},{4,12},{5,13},{6,14},{7,15},{8,0},{9,1},... | collective-permute-start | bytes 98312 | tf_op jit(solution)/shard_map/ppermute | solution.py:436
  287.4 14.3 %all-to-all-start.2 = ((f32[32,1,1024]{2,1,0:T(1,128)}), f32[32,1,1024]{2,1,0:T(1,128)S(1)}, u32[]{:S(2)}, u32[]{:S(2)}) async-start(f32[32,1,1024]{2,1,0:T(1,128)} %reshape.496), calls=%async_computation.2 | async-start | bytes 262144 | tf_op jit(solution)/shard_map/all_to_all | solution.py:445

commit v3 on v2

--- a/solution.py
+++ b/solution.py
@@ -190,7 +190,7 @@
     return numer / jnp.sqrt(var_x * var_y)
 
 
-def plane_pack_kernel(pick_ref, x_ref, w_ref, send_ref, slabs, sems):
+def fill_slabs(slabs, x_ref, w_ref):
     blk, width = x_ref.shape
     step = min(512, width)
 
@@ -204,82 +204,113 @@
             slab = jnp.concatenate([wide_x[rows], wide_w[rows]], 0)
             slabs[g, :, cols] = slab.astype(jnp.bfloat16)
 
-    me = lax.axis_index("dp")
-    mine = lax.div(me, PLANE)
+
+def send_slabs(slabs, pick_ref, send_ref, sems):
+    mine = lax.div(lax.axis_index("dp"), PLANE)
     partner = mine + 1 - 2 * lax.rem(mine, 2)
-
-    def copies(c):
-        first = pick_ref[mine * PLANE + c]
-        second = pick_ref[partner * PLANE + c]
-        return (
-            pltpu.make_async_copy(slabs.at[first], send_ref.at[c, 0], sems.at[c, 0]),
-            pltpu.make_async_copy(slabs.at[second], send_ref.at[c, 1], sems.at[c, 1]),
+    copies = []
+    for c in range(PLANE):
+        for t, plane in enumerate((mine, partner)):
+            group = pick_ref[plane * PLANE + c]
+            copies.append(pltpu.make_async_copy(slabs.at[group], send_ref.at[c, t], sems.at[c, t]))
+    for copy in copies:
+        copy.start()
+    for copy in copies:
+        copy.wait()
+
+
+def own_pack_kernel(pick_ref, x_ref, w_ref, send_ref, slabs, sems):
+    fill_slabs(slabs, x_ref, w_ref)
+    send_slabs(slabs, pick_ref, send_ref, sems)
+
+
+def far_pack_kernel(pick_ref, xo_ref, wo_ref, xi_ref, wi_ref, after_ref, send_ref, x_buf, w_buf, slabs, sems, in_sems):
+    plane = lax.div(lax.axis_index("dp"), PLANE)
+    inner = (plane == 1) | (plane == 2)
+
+    def fetch(x_ref, w_ref):
+        copies = (
+            pltpu.make_async_copy(x_ref, x_buf, in_sems.at[0]),
+            pltpu.make_async_copy(w_ref, w_buf, in_sems.at[1]),
         )
-
-    for c in range(PLANE):
-        for copy in copies(c):
+        for copy in copies:
             copy.start()
-    for c in range(PLANE):
-        for copy in copies(c):
+        for copy in copies:
             copy.wait()
 
-
-def plane_pack(pick, x, w):
-    blk, width = x.shape
-    whole = pl.BlockSpec(memory_space=pltpu.VMEM)
+    @pl.when(inner)
+    def _():
+        fetch(xi_ref, wi_ref)
+
+    @pl.when(jnp.logical_not(inner))
+    def _():
+        fetch(xo_ref, wo_ref)
+
+    fill_slabs(slabs, x_buf, w_buf)
+    send_slabs(slabs, pick_ref, send_ref, sems)
+
+
+def pack_call(kernel, name, specs, scratch, blk, width, *operands):
     return pl.pallas_call(
-        plane_pack_kernel,
+        kernel,
         out_shape=jax.ShapeDtypeStruct((PLANE, 2, SLAB, width), jnp.bfloat16),
-        in_specs=[pl.BlockSpec(memory_space=pltpu.SMEM), whole, whole],
+        in_specs=[pl.BlockSpec(memory_space=pltpu.SMEM)] + specs,
         out_specs=pl.BlockSpec(memory_space=pl.ANY),
-        scratch_shapes=[
-            pltpu.VMEM((blk // SUB, SLAB, width), jnp.bfloat16),
-            pltpu.SemaphoreType.DMA((PLANE, 2)),
-        ],
+        scratch_shapes=scratch
+        + [pltpu.VMEM((blk // SUB, SLAB, width), jnp.bfloat16), pltpu.SemaphoreType.DMA((PLANE, 2))],
         compiler_params=params(),
         cost_estimate=pl.CostEstimate(
             flops=blk * width * 4, bytes_accessed=(PLANE * 2 * SLAB * 2 + blk * 4) * width, transcendentals=0
         ),
-        name="plane_pack",
-    )(pick, x, w)
-
-
-def table_kernel(x_ref, x1_ref, w_ref, w1_ref, table_ref):
-    width = x_ref.shape[1]
-
-    @pl.loop(0, width // LANES)
-    def _(i):
-        cols = pl.ds(pl.multiple_of(i * LANES, LANES), LANES)
-        parts = [ref[:, cols].astype(jnp.float32) for ref in (x_ref, x1_ref, w_ref, w1_ref)]
-        table_ref[cols, :] = jnp.concatenate(parts, 0).T
-
-
-def make_table(x, x1, w, w1):
-    blk, width = x.shape
-    step = min(2048, width)
-    spec = pl.BlockSpec((blk, step), lambda i: (0, i))
-    return pl.pallas_call(
-        table_kernel,
-        grid=(width // step,),
-        out_shape=jax.ShapeDtypeStruct((width, LANES), jnp.float32),
-        in_specs=[spec] * 4,
-        out_specs=pl.BlockSpec((step, LANES), lambda i: (i, 0)),
-        compiler_params=params(),
-        cost_estimate=pl.CostEstimate(flops=0, bytes_accessed=width * LANES * 8, transcendentals=0),
-        name="table",
-    )(x, x1, w, w1)
-
-
-def place_kernel(ops_ref, table_ref, after_ref, moved_ref, target):
-    depth = table_ref.shape[0]
+        name=name,
+    )(*operands)
+
+
+def own_pack(pick, x, w):
+    specs = [pl.BlockSpec(memory_space=pltpu.VMEM)] * 2
+    return pack_call(own_pack_kernel, "own_pack", specs, [], *x.shape, pick, x, w)
+
+
+def far_pack(pick, x_outer, w_outer, x_inner, w_inner, after):
+    blk, width = x_outer.shape
+    buf = pltpu.VMEM((blk, width), jnp.bfloat16)
+
+    def kernel(pick_ref, xo, wo, xi, wi, after_ref, send_ref, x_buf, w_buf, in_sems, slabs, sems):
+        far_pack_kernel(pick_ref, xo, wo, xi, wi, after_ref, send_ref, x_buf, w_buf, slabs, sems, in_sems)
+
+    return pack_call(
+        kernel, "far_pack", [pl.BlockSpec(memory_space=pl.ANY)] * 5,
+        [buf, buf, pltpu.SemaphoreType.DMA((2,))], blk, width,
+        pick, x_outer, w_outer, x_inner, w_inner, after,
+    )
+
+
+def place_kernel(ops_ref, x_ref, x1_ref, w_ref, w1_ref, after_ref, moved_ref, table, target):
+    depth = x_ref.shape[1]
     width = target.shape[0]
+    part = pl.multiple_of(pl.program_id(1) * depth, depth)
+
+    @pl.when(pl.program_id(0) == 0)
+    def _():
+        step = min(256, depth)
+        diagonal = lax.broadcasted_iota(jnp.int32, (step, step), 0) == lax.broadcasted_iota(
+            jnp.int32, (step, step), 1
+        )
+        identity = jnp.where(diagonal, 1.0, 0.0).astype(jnp.bfloat16)
+        for i in range(depth // step):
+            cols = slice(i * step, (i + 1) * step)
+            rows = jnp.concatenate([x_ref[:, cols], x1_ref[:, cols], w_ref[:, cols], w1_ref[:, cols]], 0)
+            table[pl.ds(part + i * step, step), :] = lax.dot_general(
+                identity, rows, (((1,), (1,)), ((), ())), preferred_element_type=jnp.float32
+            )
 
     @pl.loop(0, depth // UNROLL)
     def _(i):
         base = pl.multiple_of(i * UNROLL, UNROLL)
+        row = pl.multiple_of(part + base, UNROLL)
         for j in range(UNROLL):
             to = ops_ref[0, 0, base + j]
-            target[pl.ds(to, 1), :] = table_ref[pl.ds(base + j, 1), :]
+            target[pl.ds(to, 1), :] = table[pl.ds(row + j, 1), :]
 
     @pl.when(pl.program_id(1) == pl.num_programs(1) - 1)
     def _():
@@ -291,52 +322,68 @@
             moved_ref[rows, :] = target[rows, :].astype(jnp.bfloat16)
 
 
-def place(ops, table, after):
+def place(ops, x, x1, w, w1, after):
     count = ops.shape[0]
-    width = table.shape[0]
+    blk, width = x.shape
     depth = min(2048, width)
+    last = width // depth - 1
+    part = pl.BlockSpec((blk, depth), lambda k, i: (0, jnp.where(k == 0, i, last)))
     return pl.pallas_call(
         place_kernel,
         grid=(count, width // depth),
         out_shape=jax.ShapeDtypeStruct((width, count * LANES), jnp.bfloat16),
         in_specs=[
             pl.BlockSpec((1, 1, depth), lambda k, i: (k, 0, i), memory_space=pltpu.SMEM),
-            pl.BlockSpec((depth, LANES), lambda k, i: (i, 0)),
+            part,
+            part,
+            part,
+            part,
             pl.BlockSpec(memory_space=pl.ANY),
         ],
         out_specs=pl.BlockSpec((width, LANES), lambda k, i: (0, k)),
-        scratch_shapes=[pltpu.VMEM((width, LANES), jnp.float32)],
+        scratch_shapes=[pltpu.VMEM((width, LANES), jnp.float32)] * 2,
         compiler_params=params(),
         cost_estimate=pl.CostEstimate(
             flops=0, bytes_accessed=count * width * LANES * 64, transcendentals=0
         ),
         name="place",
-    )(ops[:, None, :], table, after)
-
-
-def plane_sums_kernel(own_ref, far_ref, first_ref, second_ref, out_ref):
+    )(ops[:, None, :], x, x1, w, w1, after)
+
+
+def ratio(total_w, sum_x, sum_xx, sum_y, sum_xy, sum_yy):
+    numer = total_w * sum_xy - sum_x * sum_y
+    var_x = jnp.maximum(total_w * sum_xx - sum_x * sum_x, 0.05 * total_w * sum_xx)
+    var_y = jnp.maximum(total_w * sum_yy - sum_y * sum_y, 0.05 * total_w * sum_yy)
+    return numer / jnp.sqrt(var_x * var_y)
+
+
+def plane_sums_kernel(own_ref, far_ref, first_ref, second_ref, out_ref, acc):
     rows, depth = own_ref.shape
-    step = min(512, depth)
+    step = min(1024, depth)
     half = LANES // 2
+    slabs = rows // SLAB
+    blk = half // 2
 
     @pl.when(pl.program_id(0) == 0)
     def _():
-        out_ref[...] = jnp.zeros_like(out_ref)
-
-    is_x = lax.broadcasted_iota(jnp.int32, (rows // SLAB, SLAB, step), 1) < SUB
-    low = lax.broadcasted_iota(jnp.int32, (step, LANES), 1) < half
+        acc[...] = jnp.zeros_like(acc)
 
     @pl.loop(0, depth // step)
     def _(i):
         cols = pl.ds(pl.multiple_of(i * step, step), step)
-        raws, products = [], []
+        is_x = lax.broadcasted_iota(jnp.int32, (slabs, SLAB, step), 1) < SUB
+        weights, products = [], []
         for ref in (own_ref, far_ref):
-            raw = ref[:, cols]
-            wide = raw.astype(jnp.float32).reshape(rows // SLAB, SLAB, step)
-            product = wide * pltpu.roll(wide, SUB, 1)
+            wide = ref[:, cols].astype(jnp.float32).reshape(slabs, SLAB, step)
+            rolled = pltpu.roll(wide, SUB, 1)
+            product = wide * rolled
             both = jnp.where(is_x, product * wide, product)
-            raws.append(raw)
             products.append(both.reshape(rows, step).astype(jnp.bfloat16))
+            mine = rolled.reshape(slabs // 2, 2, SLAB, step)[:, 0]
+            partner = wide.reshape(slabs // 2, 2, SLAB, step)[:, 1]
+            pair = jnp.where(is_x[: slabs // 2], mine, partner)
+            weights.append(pair.reshape(rows // 2, step).astype(jnp.bfloat16))
+        low = lax.broadcasted_iota(jnp.int32, (step, LANES), 1) < half
         linear, square = [], []
         for ref in (first_ref, second_ref):
             even, odd = None, None
@@ -350,9 +397,36 @@
                 else:
                     odd = product * swapped
             square.append(jnp.where(low, even, odd).astype(jnp.bfloat16))
+        left = jnp.concatenate(weights + products, 0)
         right = jnp.concatenate(linear + square, 1)
-        out_ref[0] += jnp.dot(jnp.concatenate(raws, 0), right, preferred_element_type=jnp.float32)
-        out_ref[1] += jnp.dot(jnp.concatenate(products, 0), right, preferred_element_type=jnp.float32)
+        acc[...] += jnp.dot(left, right, preferred_element_type=jnp.float32)
+
+    @pl.when(pl.program_id(0) == pl.num_programs(0) - 1)
+    def _():
+        tiles = slabs
+        top = lax.broadcasted_iota(jnp.int32, (tiles, SLAB, LANES), 1) < SUB
+        lane = lax.broadcasted_iota(jnp.int32, (tiles * SLAB, LANES), 1)
+        result = jnp.zeros((tiles * SLAB, LANES), jnp.float32)
+        for k in range(NOPS):
+            lanes = slice(k * LANES, (k + 1) * LANES)
+            squares = slice((NOPS + k // 2) * LANES, (NOPS + k // 2 + 1) * LANES)
+            with_w = acc[:rows, lanes]
+            with_y = acc[rows:, lanes].reshape(tiles, 2, SLAB, LANES)
+            mine, partner = with_y[:, 0], with_y[:, 1]
+            y = jnp.where(top, pltpu.roll(mine, SUB, 1), partner).reshape(tiles * SLAB, LANES)
+            yy = jnp.where(top, mine, pltpu.roll(partner, SUB, 1)).reshape(tiles * SLAB, LANES)
+            sum_xx = acc[:rows, squares]
+            if k % 2 == 1:
+                sum_xx = pltpu.roll(sum_xx, half, 1)
+            both = ratio(
+                pltpu.roll(with_w, half, 1), with_w, sum_xx, pltpu.roll(y, half, 1), y, pltpu.roll(yy, half, 1)
+            )
+            both = jnp.where(
+                top.reshape(tiles * SLAB, LANES), both, pltpu.roll(both, LANES - blk, 1)
+            )
+            moved = both if k == 0 else pltpu.roll(both, k * blk, 1)
+            result = jnp.where((lane >= k * blk) & (lane < (k + 1) * blk), moved, result)
+        out_ref[...] = result
 
 
 def plane_sums(own, far, first, second):
@@ -364,42 +438,18 @@
     return pl.pallas_call(
         plane_sums_kernel,
         grid=(width // depth,),
-        out_shape=jax.ShapeDtypeStruct((2, 2 * rows, lanes), jnp.float32),
+        out_shape=jax.ShapeDtypeStruct((rows, LANES), jnp.float32),
         in_specs=[part, part, moved, moved],
-        out_specs=pl.BlockSpec((2, 2 * rows, lanes), lambda i: (0, 0, 0)),
+        out_specs=pl.BlockSpec((rows, LANES), lambda i: (0, 0)),
+        scratch_shapes=[pltpu.VMEM((3 * rows, lanes), jnp.float32)],
         compiler_params=params(),
         cost_estimate=pl.CostEstimate(
-            flops=8 * rows * width * lanes,
+            flops=6 * rows * width * lanes,
             bytes_accessed=width * (4 * rows + 8 * LANES),
             transcendentals=0,
         ),
         name="plane_sums",
     )(own, far, first, second)
-
-
-def ratio(total_w, sum_x, sum_xx, sum_y, sum_xy, sum_yy):
-    numer = total_w * sum_xy - sum_x * sum_y
-    var_x = jnp.maximum(total_w * sum_xx - sum_x * sum_x, 0.05 * total_w * sum_xx)
-    var_y = jnp.maximum(total_w * sum_yy - sum_y * sum_y, 0.05 * total_w * sum_yy)
-    return numer / jnp.sqrt(var_x * var_y)
-
-
-def plane_pearson(stats, blk, which):
-    stats = stats.reshape(2, 2, PLANE, 2, SLAB, -1)[:, :, :, which]
-    lead = (2, PLANE, SUB)
-    straight = NOPS * LANES
-
-    def linear(part, rows, offset):
-        picked = part[:, :, rows, :straight].reshape(*lead, NOPS, 4, blk)
-        return picked[:, :, :, :, offset + which]
-
-    total_w = linear(stats[0], slice(SUB, None), 2)
-    sum_x = linear(stats[0], slice(SUB, None), 0)
-    sum_y = linear(stats[1], slice(SUB, None), 2)
-    sum_xy = linear(stats[1], slice(SUB, None), 0)
-    sum_yy = linear(stats[1], slice(None, SUB), 2)
-    sum_xx = stats[0][:, :, SUB:, straight:].reshape(*lead, NOPS, 2, blk)[:, :, :, :, which]
-    return ratio(total_w, sum_x, sum_xx, sum_y, sum_xy, sum_yy)
 
 
 def shards_by_plane(intensities, observed, qweights, ops, pick):
@@ -407,6 +457,8 @@
     groups = PLANES * PLANE
     near = [(i, i ^ PLANE) for i in range(groups)]
     far = [(i, i ^ (2 * PLANE)) for i in range(groups)]
+    middle = [(i, 3 * PLANE + 2 * (i % PLANE) - i) for i in range(PLANE, 3 * PLANE)]
+    outward = [(i, i - PLANE if i < 2 * PLANE else i + PLANE) for i in range(PLANE, 3 * PLANE)]
     rings = [[z * PLANE + c for c in range(PLANE)] for z in range(PLANES)]
     plane = lax.axis_index("dp") // PLANE
     odd, upper = plane % 2 == 1, plane >= 2
@@ -416,32 +468,34 @@
         return got.reshape(PLANE * 2 * SLAB, width)
 
     own_pick = pick[:, 0]
+    near_x = lax.ppermute(intensities, "dp", near)
+    mid_x = lax.ppermute(intensities, "dp", middle)
+    far_pick = lax.ppermute(own_pick, "dp", far)
     own_w = (observed.astype(jnp.float32) * qweights.astype(jnp.float32)).astype(jnp.bfloat16)
-    near_x = lax.ppermute(intensities, "dp", near)
     near_w = lax.ppermute(own_w, "dp", near)
-    far_pick = lax.ppermute(own_pick, "dp", far)
-    own_got = spread(plane_pack(own_pick, intensities, own_w))
-    later_x, later_w, near_x, near_w = lax.optimization_barrier((intensities, own_w, near_x, near_w))
-    far_x = lax.ppermute(later_x, "dp", far)
-    far_w = lax.ppermute(later_w, "dp", far)
-    table = make_table(intensities, near_x, own_w, near_w)
-    first = place(ops[:2], table, own_pick)
-    far_send = plane_pack(far_pick, far_x, far_w)
+    mid_w = lax.ppermute(own_w, "dp", middle)
+    own_got = spread(own_pack(own_pick, intensities, own_w))
+    near_x, mid_x, near_w, mid_w, far_pick = lax.optimization_barrier((near_x, mid_x, near_w, mid_w, far_pick))
+    outer_x = lax.ppermute(mid_x, "dp", outward)
+    inner_x = lax.ppermute(near_x, "dp", middle)
+    outer_w = lax.ppermute(mid_w, "dp", outward)
+    inner_w = lax.ppermute(near_w, "dp", middle)
+    first = place(ops[:2], intensities, near_x, own_w, near_w, own_pick)
+    far_send = far_pack(far_pick, outer_x, outer_w, inner_x, inner_w, first)
     far_got = spread(far_send)
-    second = place(ops[2:], table, far_send)
+    second = place(ops[2:], intensities, near_x, own_w, near_w, far_send)
     stats = plane_sums(own_got, far_got, first, second)
-    mine = plane_pearson(stats, blk, 0)
-    other = plane_pearson(stats, blk, 1)
+    stats = stats.reshape(2, PLANE, 2, SUB, NOPS * blk)
+    mine, other = stats[:, :, 0], stats[:, :, 1]
 
     from_near = lax.ppermute(other, "dp", near)
     pair = jnp.stack([mine, from_near], 1)
     pair = jnp.where(odd, pair[:, ::-1], pair)
     pair = jnp.where(upper, pair[::-1], pair)
-    corr = jnp.transpose(pair.reshape(groups, SUB, NOPS, blk), (2, 3, 0, 1)).reshape(NOPS, blk, groups * SUB)
-
-    both = jnp.stack([mine, other], 2)
-    both = jnp.where(upper, both[::-1], both)
-    back = jnp.repeat(both, 2, 0).reshape(groups, 2, SUB, NOPS, blk)
+    corr = pair.reshape(groups * SUB, NOPS * blk).T.reshape(NOPS, blk, groups * SUB)
+
+    both = jnp.where(upper, stats[::-1], stats).reshape(2, 1, PLANE, 2 * SUB, NOPS * blk)
+    back = jnp.broadcast_to(both, (2, 2, PLANE, 2 * SUB, NOPS * blk)).reshape(groups, 2 * SUB, NOPS * blk)
     back = lax.all_to_all(back, "dp", split_axis=0, concat_axis=0, tiled=True)
     back = back.reshape(2, 2, PLANE, 2, SUB, NOPS, blk)
     back = jnp.where(odd, back[:, 1, :, ::-1], back[:, 0])

time: 305 us -> 205 us (0.67)
  waiting for transfers between devices: 141 us -> 61.6 us
  Pallas kernels: 120 us -> 104 us
  local copies, waits for them, and re-layouts: 13 us -> 6.14 us
  starting transfers between devices: 24.9 us -> 28.3 us
    ppermute x1, waiting for transfers between devices: 87.7 us -> 32.2 us  [shards_by_plane(): far_pick = lax.ppermute(own_pick, 'dp', far)]
    ppermute x1, waiting for transfers between devices: 23.8 us -> 0.01 us  [shards_by_plane(): near_w = lax.ppermute(own_w, 'dp', near)]
    ppermute x1, waiting for transfers between devices: 22.2 us -> 0.01 us  [shards_by_plane(): near_x = lax.ppermute(intensities, 'dp', near)]
    pallas_call x3 -> x2, Pallas kernels: 23.8 us -> 9.31 us  [pack_call(): pl.pallas_call(kernel, out_shape=jax.ShapeDtypeStruct((PLANE, 2, SLAB, wi...]
    all_to_all x2, waiting for transfers between devices: 0.01 us -> 11.6 us  [spread(): lax.all_to_all(send, 'dp', split_axis=0, concat_axis=0, axis_index_groups...]
    ppermute x2 -> x6, waiting for transfers between devices: 0.01 us -> 10.4 us  [the longest x1 10.4 us: shards_by_plane(): outer_w = lax.ppermute(mid_w, 'dp', outward)]
    pallas_call x1, Pallas kernels: 28.2 us -> 21.5 us  [plane_sums(): pl.pallas_call(plane_sums_kernel, grid=(width // depth,), out_shape=jax.S...]
    pallas_call x2, Pallas kernels: 67.7 us -> 73.5 us  [place(): pl.pallas_call(place_kernel, grid=(count, width // depth), out_shape=jax....]
  transfers between devices with their start and end apart: 9 -> 13, of which waited for: 4 -> 4; matrix products, arithmetic and copies ran while one was open for 1% -> 2% of each run, Pallas kernels for 29% -> 40%
where the time goes in v3:
time: 205 us
  Pallas kernels  104 us (51%)
  waiting for transfers between devices  61.6 us (30%)
  starting transfers between devices  28.3 us (14%)
  local copies, waits for them, and re-layouts  6.14 us (3%)
  other arithmetic  3.29 us (2%)
    pallas_call x2, Pallas kernels, place(): pl.pallas_call(place_kernel, grid=(count, width // depth), out_shape=jax....  73.5 us
    ppermute x1, waiting for transfers between devices, shards_by_plane(): far_pick = lax.ppermute(own_pick, 'dp', far)  32.2 us
    pallas_call x1, Pallas kernels, plane_sums(): pl.pallas_call(plane_sums_kernel, grid=(width // depth,), out_shape=jax.S...  21.5 us
    all_to_all x2, waiting for transfers between devices, spread(): lax.all_to_all(send, 'dp', split_axis=0, concat_axis=0, axis_index_groups...  11.6 us
    ppermute x1, waiting for transfers between devices, shards_by_plane(): outer_w = lax.ppermute(mid_w, 'dp', outward)  10.4 us
    all_to_all x2, starting transfers between devices, spread(): lax.all_to_all(send, 'dp', split_axis=0, concat_axis=0, axis_index_groups...  9.34 us
    pallas_call x2, Pallas kernels, pack_call(): pl.pallas_call(kernel, out_shape=jax.ShapeDtypeStruct((PLANE, 2, SLAB, wi...  9.31 us
    all_to_all x1, waiting for transfers between devices, shards_by_plane(): back = lax.all_to_all(back, 'dp', split_axis=0, concat_axis=0, tiled=True)  7.42 us
  transfers between devices with their start and end apart: 13, of which 4 were waited for; matrix products, arithmetic and copies ran while one was open for 2% of the time, Pallas kernels for 40%

profile of v3, /device:TPU:0, one launch (start us, length us, event | category | flops | bytes accessed | tf_op | source)
XLA Modules:
  0.0 204.7 jit_solution(17195427027009730243)
XLA Ops:
  0.6 0.0 copy-start.1
  0.6 2.2 %multiply_convert_fusion.w_ref = bf16[32,16384]{1,0:T(8,128)(2,1)S(1)} fusion(bf16[32,16384]{1,0:T(8,128)(2,1)} %param.7, s32[32,16384]{1,0:T(8,128)} %param.6), kind=kLoop, calls=%fused_computation | loop fusion | flops 2097152 | bytes 4194304 | tf_op jit(solution)/shard_map/convert_element_type | solution.py:474
  2.9 0.0 copy-start
  2.9 3.1 %collective-permute-start.2 = (bf16[32,16384]{1,0:T(8,128)(2,1)S(1)}, bf16[32,16384]{1,0:T(8,128)(2,1)S(1)}, u32[]{:S(2)}, u32[]{:S(2)}) collective-permute-start(bf16[32,16384]{1,0:T(8,128)(2,1)S(1)} %multiply_convert_fusion.w_ref), channel_id=1, source_target_pairs={{0,8},{1,9},{2,10},{3,11},{4,12},{5,13},{6,14},{7,15},{8,0},{9,1},... | collective-permute-start | bytes 3145736 | tf_op jit(solution)/shard_map/ppermute | solution.py:475
  6.0 1.7 collective-permute-start.3
  7.7 0.0 copy-done.1
  7.7 3.4 %collective-permute-start = (bf16[32,16384]{1,0:T(8,128)(2,1)S(1)}, bf16[32,16384]{1,0:T(8,128)(2,1)}, u32[]{:S(2)}, u32[]{:S(2)}) collective-permute-start(bf16[32,16384]{1,0:T(8,128)(2,1)S(1)} %copy-done.1), channel_id=1, source_target_pairs={{0,8},{1,9},{2,10},{3,11},{4,12},{5,13},{6,14},{7,15},{8,0},{9,1},... | collective-permute-start | bytes 3145736 | tf_op jit(solution)/shard_map/ppermute | solution.py:471
  11.1 1.6 collective-permute-start.1
  12.7 0.0 copy-done
  12.7 4.3 %own_pack.1 = bf16[8,2,8,16384]{3,2,1,0:T(8,128)(2,1)} custom-call(s32[32]{0:T(128)} %bitcast.31, bf16[32,16384]{1,0:T(8,128)(2,1)} %x_ref.5, bf16[32,16384]{1,0:T(8,128)(2,1)} %copy-done), custom_call_target="tpu_custom_call" | custom-call | flops 2097152 | bytes 6291456 | tf_op jit(solution)/shard_map/own_pack/pallas_call | solution.py:254
  17.1 0.0 copy-start.8
  17.1 0.0 copy-start.7
  17.1 4.7 %all-to-all-start = ((bf16[8,2,8,16384]{3,2,1,0:T(8,128)(2,1)}), bf16[8,2,8,16384]{3,2,1,0:T(8,128)(2,1)}, u32[]{:S(2)}, u32[]{:S(2)}) async-start(bf16[8,2,8,16384]{3,2,1,0:T(8,128)(2,1)} %own_pack.1), calls=%async_computation | async-start | bytes 8388608 | tf_op jit(solution)/shard_map/all_to_all | solution.py:467
  21.8 0.0 copy-done.8
  21.8 1.8 collective-permute-start.4
  23.6 32.2 %collective-permute-done.4.pick_ref = s32[32]{0:T(128)S(1)} collective-permute-done((s32[32]{0:T(128)S(1)}, s32[32]{0:T(128)S(1)}, u32[]{:S(2)}, u32[]{:S(2)}) %collective-permute-start.4) | collective-permute-done | bytes 160 | tf_op jit(solution)/shard_map/ppermute | solution.py:473
  55.8 0.0 copy-start.9
  55.8 0.0 collective-permute-done.2.w1_ref
  55.8 0.0 copy-start.2
  55.8 0.0 collective-permute-done.3
  55.8 0.0 collective-permute-done.x1_ref
  55.8 0.0 collective-permute-done.1
  55.8 0.7 collective-permute-start.7
  56.6 0.7 collective-permute-start.8
  57.3 1.3 collective-permute-start.5
  58.6 1.3 collective-permute-start.6
  59.9 0.0 copy-done.7
  59.9 0.1 fusion.1
  60.0 0.7 broadcast_in_dim.13.ops_ref
  60.8 0.0 copy-done.2
  60.8 36.8 %place.2.after_ref.first_ref = bf16[16384,256]{1,0:T(8,128)(2,1)} custom-call(s32[2,1,16384]{2,1,0:T(1,128)} %broadcast_in_dim.13.ops_ref, bf16[32,16384]{1,0:T(8,128)(2,1)} %x_ref.5, bf16[32,16384]{1,0:T(8,128)(2,1)} %collective-permute-done.x1_ref, bf16[32,16384]{1,0:T(8,128)(2,1)} %copy-done, bf16[32,16384]{1,0:T(8,128)(2,1)} %copy-done.2, s32[32]{0:T(128)} %bitcast.32), custom_call_target="tpu_custom_call" | custom-call | bytes 268435456 | tf_op jit(solution)/shard_map/place/pallas_call | solution.py:331
  97.6 0.0 copy-done.9
  97.6 0.0 collective-permute-done.7.xi
  97.6 0.0 copy-start.3
  97.6 0.0 collective-permute-done.8.wi
  97.6 0.0 copy-start.4
  97.6 0.0 collective-permute-done.5.xo
  97.6 0.0 copy-start.5
  97.6 10.4 %collective-permute-done.6.wo = bf16[32,16384]{1,0:T(8,128)(2,1)S(1)} collective-permute-done((bf16[32,16384]{1,0:T(8,128)(2,1)}, bf16[32,16384]{1,0:T(8,128)(2,1)S(1)}, u32[]{:S(2)}, u32[]{:S(2)}) %collective-permute-start.6) | collective-permute-done | bytes 1048608 | tf_op jit(solution)/shard_map/ppermute | solution.py:481
  108.0 0.0 copy-done.3
  108.0 0.0 copy-done.4
  108.0 0.0 copy-done.5
  108.0 0.0 copy-start.6
  108.0 1.0 copy-done.6
  109.1 5.0 %far_pack.1.after_ref = bf16[8,2,8,16384]{3,2,1,0:T(8,128)(2,1)} custom-call(s32[32]{0:T(128)} %copy-done.9, bf16[32,16384]{1,0:T(8,128)(2,1)} %copy-done.5, bf16[32,16384]{1,0:T(8,128)(2,1)} %copy-done.6, bf16[32,16384]{1,0:T(8,128)(2,1)} %copy-done.3, bf16[32,16384]{1,0:T(8,128)(2,1)} %copy-done.4, bf16[16384,256]{1,0:T(8,128)(2,1)} %place.2.after_ref.first_ref), custom_call_target="tpu_custom_call" | custom-call | flops 2097152 | bytes 6291456 | tf_op jit(solution)/shard_map/far_pack/pallas_call | solution.py:254
  114.1 0.0 all-to-all-done
  114.1 4.6 %all-to-all-start.1 = ((bf16[8,2,8,16384]{3,2,1,0:T(8,128)(2,1)}), bf16[8,2,8,16384]{3,2,1,0:T(8,128)(2,1)}, u32[]{:S(2)}, u32[]{:S(2)}) async-start(bf16[8,2,8,16384]{3,2,1,0:T(8,128)(2,1)} %far_pack.1.after_ref), calls=%async_computation.1 | async-start | bytes 8388608 | tf_op jit(solution)/shard_map/all_to_all | solution.py:467
  118.8 0.7 broadcast_in_dim.14.ops_ref
  119.5 36.7 %place.3.second_ref = bf16[16384,256]{1,0:T(8,128)(2,1)} custom-call(s32[2,1,16384]{2,1,0:T(1,128)} %broadcast_in_dim.14.ops_ref, bf16[32,16384]{1,0:T(8,128)(2,1)} %x_ref.5, bf16[32,16384]{1,0:T(8,128)(2,1)} %collective-permute-done.x1_ref, bf16[32,16384]{1,0:T(8,128)(2,1)} %copy-done, bf16[32,16384]{1,0:T(8,128)(2,1)} %copy-done.2, ...), custom_call_target="tpu_custom_call" | custom-call | bytes 268435456 | tf_op jit(solution)/shard_map/place/pallas_call | solution.py:331
  156.2 11.6 %all-to-all-done.1 = bf16[8,2,8,16384]{3,2,1,0:T(8,128)(2,1)} async-done(((bf16[8,2,8,16384]{3,2,1,0:T(8,128)(2,1)}), bf16[8,2,8,16384]{3,2,1,0:T(8,128)(2,1)}, u32[]{:S(2)}, u32[]{:S(2)}) %all-to-all-start.1) | async-done | bytes 4194336 | tf_op jit(solution)/shard_map/all_to_all | solution.py:467
  167.8 21.5 %plane_sums.1 = f32[128,128]{1,0:T(8,128)} custom-call(bf16[128,16384]{1,0:T(8,128)(2,1)} %bitcast.1.own_ref, bf16[128,16384]{1,0:T(8,128)(2,1)} %bitcast.2.far_ref, bf16[16384,256]{1,0:T(8,128)(2,1)} %place.2.after_ref.first_ref, bf16[16384,256]{1,0:T(8,128)(2,1)} %place.3.second_ref), custom_call_target="tpu_custom_call" | custom-call | flops 9663676416 | bytes 25165824 | tf_op jit(solution)/shard_map/plane_sums/pallas_call | solution.py:438
  189.4 0.8 slice_bitcast_fusion.1
  190.2 0.0 collective-permute-start.9
  190.2 0.9 reverse_select_fusion
  191.1 0.7 broadcast_in_dim.16
  191.8 3.3 %all-to-all-start.2 = ((f32[32,8,128]{2,1,0:T(8,128)}), f32[32,8,128]{2,1,0:T(8,128)S(1)}, u32[]{:S(2)}, u32[]{:S(2)}) async-start(f32[32,8,128]{2,1,0:T(8,128)} %bitcast.11), calls=%async_computation.2 | async-start | bytes 262144 | tf_op jit(solution)/shard_map/all_to_all | solution.py:499
  195.0 0.0 collective-permute-done.9
  195.1 0.7 copy.13
  195.9 7.4 %all-to-all-done.2 = f32[32,8,128]{2,1,0:T(8,128)S(1)} async-done(((f32[32,8,128]{2,1,0:T(8,128)}), f32[32,8,128]{2,1,0:T(8,128)S(1)}, u32[]{:S(2)}, u32[]{:S(2)}) %all-to-all-start.2) | async-done | bytes 131104 | tf_op jit(solution)/shard_map/all_to_all | solution.py:499
  203.3 0.3 reshape.38
  203.6 0.1 fusion
  203.6 0.2 copy.14
  203.8 0.9 copy.15
  (4 shorter events, 0.1 us)
Async XLA Ops:
  0.6 7.0 %copy-start.1 = (bf16[32,16384]{1,0:T(8,128)(2,1)S(1)}, bf16[32,16384]{1,0:T(8,128)(2,1)}, u32[]{:S(2)}) copy-start(bf16[32,16384]{1,0:T(8,128)(2,1)} %x_ref.5) | copy-start | bytes 3145732
  2.9 9.9 %copy-start = (bf16[32,16384]{1,0:T(8,128)(2,1)}, bf16[32,16384]{1,0:T(8,128)(2,1)S(1)}, u32[]{:S(2)}) copy-start(bf16[32,16384]{1,0:T(8,128)(2,1)S(1)} %multiply_convert_fusion.w_ref) | copy-start | bytes 3145732
  2.9 52.9 %collective-permute-start.2 = (bf16[32,16384]{1,0:T(8,128)(2,1)S(1)}, bf16[32,16384]{1,0:T(8,128)(2,1)S(1)}, u32[]{:S(2)}, u32[]{:S(2)}) collective-permute-start(bf16[32,16384]{1,0:T(8,128)(2,1)S(1)} %multiply_convert_fusion.w_ref), channel_id=1, source_target_pairs={{0,8},{1,9},{2,10},{3,11},{4,12},{5,13},{6,14},{7,15},{8,0},{9,1},... | collective-permute-start | bytes 3145736 | tf_op jit(solution)/shard_map/ppermute | solution.py:475
  6.0 49.8 %collective-permute-start.3 = (bf16[32,16384]{1,0:T(8,128)(2,1)S(1)}, bf16[32,16384]{1,0:T(8,128)(2,1)}, u32[]{:S(2)}, u32[]{:S(2)}) collective-permute-start(bf16[32,16384]{1,0:T(8,128)(2,1)S(1)} %multiply_convert_fusion.w_ref), channel_id=1, source_target_pairs={{8,16},{9,17},{10,18},{11,19},{12,20},{13,21},{14,22},{15,23},{16,... | collective-permute-start | bytes 3145736 | tf_op jit(solution)/shard_map/ppermute | solution.py:476
  7.7 48.1 %collective-permute-start = (bf16[32,16384]{1,0:T(8,128)(2,1)S(1)}, bf16[32,16384]{1,0:T(8,128)(2,1)}, u32[]{:S(2)}, u32[]{:S(2)}) collective-permute-start(bf16[32,16384]{1,0:T(8,128)(2,1)S(1)} %copy-done.1), channel_id=1, source_target_pairs={{0,8},{1,9},{2,10},{3,11},{4,12},{5,13},{6,14},{7,15},{8,0},{9,1},... | collective-permute-start | bytes 3145736 | tf_op jit(solution)/shard_map/ppermute | solution.py:471
  11.1 44.7 %collective-permute-start.1 = (bf16[32,16384]{1,0:T(8,128)(2,1)S(1)}, bf16[32,16384]{1,0:T(8,128)(2,1)}, u32[]{:S(2)}, u32[]{:S(2)}) collective-permute-start(bf16[32,16384]{1,0:T(8,128)(2,1)S(1)} %copy-done.1), channel_id=1, source_target_pairs={{8,16},{9,17},{10,18},{11,19},{12,20},{13,21},{14,22},{15,23},{16,... | collective-permute-start | bytes 3145736 | tf_op jit(solution)/shard_map/ppermute | solution.py:472
  17.1 4.7 %copy-start.8 = (s32[32,1]{0,1:T(1,128)S(1)}, s32[32,1]{0,1:T(1,128)}, u32[]{:S(2)}) copy-start(s32[32,1]{0,1:T(1,128)} %param.9) | copy-start | bytes 388
  17.1 42.8 %copy-start.7 = (s32[4,16384]{1,0:T(4,128)S(1)}, s32[4,16384]{1,0:T(4,128)}, u32[]{:S(2)}) copy-start(s32[4,16384]{1,0:T(4,128)} %param.8) | copy-start | bytes 786436
  17.1 97.0 %all-to-all-start = ((bf16[8,2,8,16384]{3,2,1,0:T(8,128)(2,1)}), bf16[8,2,8,16384]{3,2,1,0:T(8,128)(2,1)}, u32[]{:S(2)}, u32[]{:S(2)}) async-start(bf16[8,2,8,16384]{3,2,1,0:T(8,128)(2,1)} %own_pack.1), calls=%async_computation | async-start | bytes 8388608 | tf_op jit(solution)/shard_map/all_to_all | solution.py:467
  21.8 34.0 %collective-permute-start.4 = (s32[32]{0:T(128)S(1)}, s32[32]{0:T(128)S(1)}, u32[]{:S(2)}, u32[]{:S(2)}) collective-permute-start(s32[32]{0:T(128)S(1)} %bitcast.33), channel_id=1, source_target_pairs={{0,16},{1,17},{2,18},{3,19},{4,20},{5,21},{6,22},{7,23},{8,24},{9,... | collective-permute-start | bytes 392 | tf_op jit(solution)/shard_map/ppermute | solution.py:473
  55.8 41.8 %copy-start.9 = (s32[32]{0:T(128)}, s32[32]{0:T(128)S(1)}, u32[]{:S(2)}) copy-start(s32[32]{0:T(128)S(1)} %collective-permute-done.4.pick_ref) | copy-start | bytes 388
  55.8 5.0 %copy-start.2 = (bf16[32,16384]{1,0:T(8,128)(2,1)}, bf16[32,16384]{1,0:T(8,128)(2,1)S(1)}, u32[]{:S(2)}) copy-start(bf16[32,16384]{1,0:T(8,128)(2,1)S(1)} %collective-permute-done.2.w1_ref) | copy-start | bytes 3145732
  55.8 41.8 %collective-permute-start.7 = (bf16[32,16384]{1,0:T(8,128)(2,1)}, bf16[32,16384]{1,0:T(8,128)(2,1)S(1)}, u32[]{:S(2)}, u32[]{:S(2)}) collective-permute-start(bf16[32,16384]{1,0:T(8,128)(2,1)} %collective-permute-done.x1_ref), channel_id=1, source_target_pairs={{8,16},{9,17},{10,18},{11,19},{12,20},{13,21},{14,22},{15,23},{16,... | collective-permute-start | bytes 3145736 | tf_op jit(solution)/shard_map/ppermute | solution.py:480
  56.6 41.0 %collective-permute-start.8 = (bf16[32,16384]{1,0:T(8,128)(2,1)S(1)}, bf16[32,16384]{1,0:T(8,128)(2,1)S(1)}, u32[]{:S(2)}, u32[]{:S(2)}) collective-permute-start(bf16[32,16384]{1,0:T(8,128)(2,1)S(1)} %collective-permute-done.2.w1_ref), channel_id=1, source_target_pairs={{8,16},{9,17},{10,18},{11,19},{12,20},{13,21},{14,22},{15,23},{16,... | collective-permute-start | bytes 3145736 | tf_op jit(solution)/shard_map/ppermute | solution.py:482
  57.3 40.3 %collective-permute-start.5 = (bf16[32,16384]{1,0:T(8,128)(2,1)}, bf16[32,16384]{1,0:T(8,128)(2,1)S(1)}, u32[]{:S(2)}, u32[]{:S(2)}) collective-permute-start(bf16[32,16384]{1,0:T(8,128)(2,1)} %collective-permute-done.1), channel_id=1, source_target_pairs={{8,0},{9,1},{10,2},{11,3},{12,4},{13,5},{14,6},{15,7},{16,24},{17,... | collective-permute-start | bytes 3145736 | tf_op jit(solution)/shard_map/ppermute | solution.py:479
  58.6 49.4 %collective-permute-start.6 = (bf16[32,16384]{1,0:T(8,128)(2,1)}, bf16[32,16384]{1,0:T(8,128)(2,1)S(1)}, u32[]{:S(2)}, u32[]{:S(2)}) collective-permute-start(bf16[32,16384]{1,0:T(8,128)(2,1)} %collective-permute-done.3), channel_id=1, source_target_pairs={{8,0},{9,1},{10,2},{11,3},{12,4},{13,5},{14,6},{15,7},{16,24},{17,... | collective-permute-start | bytes 3145736 | tf_op jit(solution)/shard_map/ppermute | solution.py:481
  97.6 10.4 %copy-start.3 = (bf16[32,16384]{1,0:T(8,128)(2,1)}, bf16[32,16384]{1,0:T(8,128)(2,1)S(1)}, u32[]{:S(2)}) copy-start(bf16[32,16384]{1,0:T(8,128)(2,1)S(1)} %collective-permute-done.7.xi) | copy-start | bytes 3145732
  97.6 10.4 %copy-start.4 = (bf16[32,16384]{1,0:T(8,128)(2,1)}, bf16[32,16384]{1,0:T(8,128)(2,1)S(1)}, u32[]{:S(2)}) copy-start(bf16[32,16384]{1,0:T(8,128)(2,1)S(1)} %collective-permute-done.8.wi) | copy-start | bytes 3145732
  97.6 10.4 %copy-start.5 = (bf16[32,16384]{1,0:T(8,128)(2,1)}, bf16[32,16384]{1,0:T(8,128)(2,1)S(1)}, u32[]{:S(2)}) copy-start(bf16[32,16384]{1,0:T(8,128)(2,1)S(1)} %collective-permute-done.5.xo) | copy-start | bytes 3145732
  108.0 1.0 copy-start.6
  114.1 53.8 %all-to-all-start.1 = ((bf16[8,2,8,16384]{3,2,1,0:T(8,128)(2,1)}), bf16[8,2,8,16384]{3,2,1,0:T(8,128)(2,1)}, u32[]{:S(2)}, u32[]{:S(2)}) async-start(bf16[8,2,8,16384]{3,2,1,0:T(8,128)(2,1)} %far_pack.1.after_ref), calls=%async_computation.1 | async-start | bytes 8388608 | tf_op jit(solution)/shard_map/all_to_all | solution.py:467
  190.2 4.9 %collective-permute-start.9 = (f32[2,8,4,128]{3,2,1,0:T(4,128)S(1)}, f32[2,8,4,128]{3,2,1,0:T(4,128)S(1)}, u32[]{:S(2)}, u32[]{:S(2)}) collective-permute-start(f32[2,8,4,128]{3,2,1,0:T(4,128)S(1)} %get-tuple-element.19), channel_id=1, source_target_pairs={{0,8},{1,9},{2,10},{3,11},{4,12},{5,13},{6,14},{7,15},{8,0},{9,1},... | collective-permute-start | bytes 98312 | tf_op jit(solution)/shard_map/ppermute | solution.py:491
  191.8 11.5 %all-to-all-start.2 = ((f32[32,8,128]{2,1,0:T(8,128)}), f32[32,8,128]{2,1,0:T(8,128)S(1)}, u32[]{:S(2)}, u32[]{:S(2)}) async-start(f32[32,8,128]{2,1,0:T(8,128)} %bitcast.11), calls=%async_computation.2 | async-start | bytes 262144 | tf_op jit(solution)/shard_map/all_to_all | solution.py:499

commit v4 on v3

--- a/solution.py
+++ b/solution.py
@@ -15,6 +15,7 @@
 PLANES = 4
 PLANE = 8
 UNROLL = 64
+HALVES = 2
 
 
 def params():
@@ -190,19 +191,44 @@
     return numer / jnp.sqrt(var_x * var_y)
 
 
-def fill_slabs(slabs, x_ref, w_ref):
-    blk, width = x_ref.shape
+def weigh_kernel(x_ref, obs_ref, qw_ref, out_ref):
+    blk = x_ref.shape[0]
+    weights = obs_ref[...].astype(jnp.float32) * qw_ref[...].astype(jnp.float32)
+    out_ref[:blk, :] = x_ref[...]
+    out_ref[blk:, :] = weights.astype(jnp.bfloat16)
+
+
+def weigh(x, observed, qweights, part):
+    blk, width = x.shape
+    depth = min(2048, width // HALVES)
+    count = width // HALVES // depth
+    spec = pl.BlockSpec((blk, depth), lambda i: (0, part * count + i))
+    return pl.pallas_call(
+        weigh_kernel,
+        grid=(count,),
+        out_shape=jax.ShapeDtypeStruct((2 * blk, width // HALVES), jnp.bfloat16),
+        in_specs=[spec] * 3,
+        out_specs=pl.BlockSpec((2 * blk, depth), lambda i: (0, i)),
+        compiler_params=params(),
+        cost_estimate=pl.CostEstimate(
+            flops=blk * width, bytes_accessed=blk * width * 12 // HALVES, transcendentals=0
+        ),
+        name="weigh",
+    )(x, observed, qweights)
+
+
+def fill_slabs(slabs, xw_ref, offset):
+    blk, width = xw_ref.shape[0] // 2, xw_ref.shape[1]
     step = min(512, width)
 
     @pl.loop(0, width // step)
     def _(i):
-        cols = pl.ds(pl.multiple_of(i * step, step), step)
-        wide_x = x_ref[:, cols].astype(jnp.float32)
-        wide_w = w_ref[:, cols].astype(jnp.float32)
+        start = pl.multiple_of(i * step, step)
+        wide = xw_ref[:, pl.ds(start, step)].astype(jnp.float32)
         for g in range(blk // SUB):
             rows = slice(g * SUB, (g + 1) * SUB)
-            slab = jnp.concatenate([wide_x[rows], wide_w[rows]], 0)
-            slabs[g, :, cols] = slab.astype(jnp.bfloat16)
+            slab = jnp.concatenate([wide[:blk][rows], wide[blk:][rows]], 0)
+            slabs[g, :, pl.ds(offset + start, step)] = slab.astype(jnp.bfloat16)
 
 
 def send_slabs(slabs, pick_ref, send_ref, sems):
@@ -219,34 +245,31 @@
         copy.wait()
 
 
-def own_pack_kernel(pick_ref, x_ref, w_ref, send_ref, slabs, sems):
-    fill_slabs(slabs, x_ref, w_ref)
+def own_pack_kernel(pick_ref, *refs):
+    halves, (send_ref, slabs, sems) = refs[:HALVES], refs[HALVES:]
+    for part, ref in enumerate(halves):
+        fill_slabs(slabs, ref, part * ref.shape[1])
     send_slabs(slabs, pick_ref, send_ref, sems)
 
 
-def far_pack_kernel(pick_ref, xo_ref, wo_ref, xi_ref, wi_ref, after_ref, send_ref, x_buf, w_buf, slabs, sems, in_sems):
+def far_pack_kernel(pick_ref, outer_ref, inner_ref, after_ref, send_ref, buf, in_sem, slabs, sems):
     plane = lax.div(lax.axis_index("dp"), PLANE)
     inner = (plane == 1) | (plane == 2)
 
-    def fetch(x_ref, w_ref):
-        copies = (
-            pltpu.make_async_copy(x_ref, x_buf, in_sems.at[0]),
-            pltpu.make_async_copy(w_ref, w_buf, in_sems.at[1]),
-        )
-        for copy in copies:
-            copy.start()
-        for copy in copies:
-            copy.wait()
+    def fetch(ref):
+        copy = pltpu.make_async_copy(ref, buf, in_sem)
+        copy.start()
+        copy.wait()
 
     @pl.when(inner)
     def _():
-        fetch(xi_ref, wi_ref)
+        fetch(inner_ref)
 
     @pl.when(jnp.logical_not(inner))
     def _():
-        fetch(xo_ref, wo_ref)
-
-    fill_slabs(slabs, x_buf, w_buf)
+        fetch(outer_ref)
+
+    fill_slabs(slabs, buf, 0)
     send_slabs(slabs, pick_ref, send_ref, sems)
 
 
@@ -266,43 +289,51 @@
     )(*operands)
 
 
-def own_pack(pick, x, w):
-    specs = [pl.BlockSpec(memory_space=pltpu.VMEM)] * 2
-    return pack_call(own_pack_kernel, "own_pack", specs, [], *x.shape, pick, x, w)
-
-
-def far_pack(pick, x_outer, w_outer, x_inner, w_inner, after):
-    blk, width = x_outer.shape
-    buf = pltpu.VMEM((blk, width), jnp.bfloat16)
-
-    def kernel(pick_ref, xo, wo, xi, wi, after_ref, send_ref, x_buf, w_buf, in_sems, slabs, sems):
-        far_pack_kernel(pick_ref, xo, wo, xi, wi, after_ref, send_ref, x_buf, w_buf, slabs, sems, in_sems)
-
-    return pack_call(
-        kernel, "far_pack", [pl.BlockSpec(memory_space=pl.ANY)] * 5,
-        [buf, buf, pltpu.SemaphoreType.DMA((2,))], blk, width,
-        pick, x_outer, w_outer, x_inner, w_inner, after,
-    )
-
-
-def place_kernel(ops_ref, x_ref, x1_ref, w_ref, w1_ref, after_ref, moved_ref, table, target):
-    depth = x_ref.shape[1]
+def own_pack(pick, halves):
+    rows, width = halves[0].shape
+    specs = [pl.BlockSpec(memory_space=pltpu.VMEM)] * HALVES
+    return pack_call(own_pack_kernel, "own_pack", specs, [], rows // 2, HALVES * width, pick, *halves)
+
+
+def far_pack(pick, outer, inner, after):
+    rows, width = outer.shape
+    scratch = [pltpu.VMEM((rows, width), jnp.bfloat16), pltpu.SemaphoreType.DMA]
+    specs = [pl.BlockSpec(memory_space=pl.ANY)] * 3
+    return pack_call(far_pack_kernel, "far_pack", specs, scratch, rows // 2, width, pick, outer, inner, after)
+
+
+def place_kernel(begun, ops_ref, mine_ref, near_ref, before_ref, after_ref, moved_ref, table, target):
+    rows, depth = mine_ref.shape
+    blk = rows // 2
     width = target.shape[0]
+    step = min(512, width)
     part = pl.multiple_of(pl.program_id(1) * depth, depth)
 
     @pl.when(pl.program_id(0) == 0)
     def _():
-        step = min(256, depth)
-        diagonal = lax.broadcasted_iota(jnp.int32, (step, step), 0) == lax.broadcasted_iota(
-            jnp.int32, (step, step), 1
+        size = min(256, depth)
+        diagonal = lax.broadcasted_iota(jnp.int32, (size, size), 0) == lax.broadcasted_iota(
+            jnp.int32, (size, size), 1
         )
         identity = jnp.where(diagonal, 1.0, 0.0).astype(jnp.bfloat16)
-        for i in range(depth // step):
-            cols = slice(i * step, (i + 1) * step)
-            rows = jnp.concatenate([x_ref[:, cols], x1_ref[:, cols], w_ref[:, cols], w1_ref[:, cols]], 0)
-            table[pl.ds(part + i * step, step), :] = lax.dot_general(
-                identity, rows, (((1,), (1,)), ((), ())), preferred_element_type=jnp.float32
+        for i in range(depth // size):
+            cols = slice(i * size, (i + 1) * size)
+            both = [mine_ref[:blk, cols], near_ref[:blk, cols], mine_ref[blk:, cols], near_ref[blk:, cols]]
+            table[pl.ds(part + i * size, size), :] = lax.dot_general(
+                identity,
+                jnp.concatenate(both, 0),
+                (((1,), (1,)), ((), ())),
+                preferred_element_type=jnp.float32,
             )
+
+    if begun:
+
+        @pl.when(pl.program_id(1) == 0)
+        def _():
+            @pl.loop(0, width // step)
+            def _(i):
+                here = pl.ds(pl.multiple_of(i * step, step), step)
+                target[here, :] = before_ref[here, :].astype(jnp.float32)
 
     @pl.loop(0, depth // UNROLL)
     def _(i):
@@ -314,40 +345,39 @@
 
     @pl.when(pl.program_id(1) == pl.num_programs(1) - 1)
     def _():
-        step = min(512, width)
-
         @pl.loop(0, width // step)
         def _(i):
-            rows = pl.ds(pl.multiple_of(i * step, step), step)
-            moved_ref[rows, :] = target[rows, :].astype(jnp.bfloat16)
-
-
-def place(ops, x, x1, w, w1, after):
-    count = ops.shape[0]
-    blk, width = x.shape
-    depth = min(2048, width)
-    last = width // depth - 1
-    part = pl.BlockSpec((blk, depth), lambda k, i: (0, jnp.where(k == 0, i, last)))
+            here = pl.ds(pl.multiple_of(i * step, step), step)
+            moved_ref[here, :] = target[here, :].astype(jnp.bfloat16)
+
+
+def place(ops, first, count, part, mine, near, before, after):
+    width = ops.shape[2]
+    rows, span = mine.shape
+    depth = min(2048, span)
+    chunks = span // depth
+    some = pl.BlockSpec((rows, depth), lambda k, i: (0, jnp.where(k == 0, i, chunks - 1)))
+    anywhere = pl.BlockSpec(memory_space=pl.ANY)
+    begun = before is not None
     return pl.pallas_call(
-        place_kernel,
-        grid=(count, width // depth),
+        functools.partial(place_kernel, begun),
+        grid=(count, chunks),
         out_shape=jax.ShapeDtypeStruct((width, count * LANES), jnp.bfloat16),
         in_specs=[
-            pl.BlockSpec((1, 1, depth), lambda k, i: (k, 0, i), memory_space=pltpu.SMEM),
-            part,
-            part,
-            part,
-            part,
-            pl.BlockSpec(memory_space=pl.ANY),
+            pl.BlockSpec((1, 1, depth), lambda k, i: (first + k, 0, part * chunks + i), memory_space=pltpu.SMEM),
+            some,
+            some,
+            pl.BlockSpec((width, LANES), lambda k, i: (0, first + k)) if begun else anywhere,
+            anywhere,
         ],
         out_specs=pl.BlockSpec((width, LANES), lambda k, i: (0, k)),
-        scratch_shapes=[pltpu.VMEM((width, LANES), jnp.float32)] * 2,
+        scratch_shapes=[pltpu.VMEM((span, LANES), jnp.float32), pltpu.VMEM((width, LANES), jnp.float32)],
         compiler_params=params(),
         cost_estimate=pl.CostEstimate(
-            flops=0, bytes_accessed=count * width * LANES * 64, transcendentals=0
+            flops=0, bytes_accessed=count * span * LANES * 64, transcendentals=0
         ),
         name="place",
-    )(ops[:, None, :], x, x1, w, w1, after)
+    )(ops, mine, near, before if begun else after, after)
 
 
 def ratio(total_w, sum_x, sum_xx, sum_y, sum_xy, sum_yy):
@@ -357,16 +387,21 @@
     return numer / jnp.sqrt(var_x * var_y)
 
 
-def plane_sums_kernel(own_ref, far_ref, first_ref, second_ref, out_ref, acc):
+def plane_sums_kernel(begun, ended, own_ref, far_ref, first_ref, second_ref, before_ref, out_ref, *scratch):
     rows, depth = own_ref.shape
     step = min(1024, depth)
     half = LANES // 2
     slabs = rows // SLAB
     blk = half // 2
 
+    acc = scratch[0] if ended else out_ref
+
     @pl.when(pl.program_id(0) == 0)
     def _():
-        acc[...] = jnp.zeros_like(acc)
+        if begun:
+            acc[...] = before_ref[...]
+        else:
+            acc[...] = jnp.zeros_like(acc)
 
     @pl.loop(0, depth // step)
     def _(i):
@@ -401,6 +436,9 @@
         right = jnp.concatenate(linear + square, 1)
         acc[...] += jnp.dot(left, right, preferred_element_type=jnp.float32)
 
+    if not ended:
+        return
+
     @pl.when(pl.program_id(0) == pl.num_programs(0) - 1)
     def _():
         tiles = slabs
@@ -429,19 +467,28 @@
         out_ref[...] = result
 
 
-def plane_sums(own, far, first, second):
-    rows, width = own.shape
+def plane_sums(part, own, far, first, second, before):
+    rows, width = far.shape
     depth = min(2048, width)
+    chunks = width // depth
     lanes = (NOPS + NOPS // 2) * LANES
-    part = pl.BlockSpec((rows, depth), lambda i: (0, i))
-    moved = pl.BlockSpec((depth, 2 * LANES), lambda i: (i, 0))
+    moved = pl.BlockSpec((depth, 2 * LANES), lambda i: (part * chunks + i, 0))
+    begun, ended = before is not None, part == HALVES - 1
+    total = (3 * rows, lanes)
+    shape = (rows, LANES) if ended else total
     return pl.pallas_call(
-        plane_sums_kernel,
-        grid=(width // depth,),
-        out_shape=jax.ShapeDtypeStruct((rows, LANES), jnp.float32),
-        in_specs=[part, part, moved, moved],
-        out_specs=pl.BlockSpec((rows, LANES), lambda i: (0, 0)),
-        scratch_shapes=[pltpu.VMEM((3 * rows, lanes), jnp.float32)],
+        functools.partial(plane_sums_kernel, begun, ended),
+        grid=(chunks,),
+        out_shape=jax.ShapeDtypeStruct(shape, jnp.float32),
+        in_specs=[
+            pl.BlockSpec((rows, depth), lambda i: (0, part * chunks + i)),
+            pl.BlockSpec((rows, depth), lambda i: (0, i)),
+            moved,
+            moved,
+            pl.BlockSpec(total, lambda i: (0, 0)) if begun else pl.BlockSpec(memory_space=pl.ANY),
+        ],
+        out_specs=pl.BlockSpec(shape, lambda i: (0, 0)),
+        scratch_shapes=[pltpu.VMEM(total, jnp.float32)] if ended else [],
         compiler_params=params(),
         cost_estimate=pl.CostEstimate(
             flops=6 * rows * width * lanes,
@@ -449,11 +496,11 @@
             transcendentals=0,
         ),
         name="plane_sums",
-    )(own, far, first, second)
+    )(own, far, first, second, before if begun else far)
 
 
 def shards_by_plane(intensities, observed, qweights, ops, pick):
-    blk, width = intensities.shape
+    blk = intensities.shape[0]
     groups = PLANES * PLANE
     near = [(i, i ^ PLANE) for i in range(groups)]
     far = [(i, i ^ (2 * PLANE)) for i in range(groups)]
@@ -465,26 +512,33 @@
 
     def spread(send):
         got = lax.all_to_all(send, "dp", split_axis=0, concat_axis=0, axis_index_groups=rings, tiled=True)
-        return got.reshape(PLANE * 2 * SLAB, width)
+        return got.reshape(PLANE * 2 * SLAB, send.shape[-1])
 
     own_pick = pick[:, 0]
-    near_x = lax.ppermute(intensities, "dp", near)
-    mid_x = lax.ppermute(intensities, "dp", middle)
+    ops = ops[:, None, :]
+    mine_0 = weigh(intensities, observed, qweights, 0)
+    near_0 = lax.ppermute(mine_0, "dp", near)
+    mid_0 = lax.ppermute(mine_0, "dp", middle)
     far_pick = lax.ppermute(own_pick, "dp", far)
-    own_w = (observed.astype(jnp.float32) * qweights.astype(jnp.float32)).astype(jnp.bfloat16)
-    near_w = lax.ppermute(own_w, "dp", near)
-    mid_w = lax.ppermute(own_w, "dp", middle)
-    own_got = spread(own_pack(own_pick, intensities, own_w))
-    near_x, mid_x, near_w, mid_w, far_pick = lax.optimization_barrier((near_x, mid_x, near_w, mid_w, far_pick))
-    outer_x = lax.ppermute(mid_x, "dp", outward)
-    inner_x = lax.ppermute(near_x, "dp", middle)
-    outer_w = lax.ppermute(mid_w, "dp", outward)
-    inner_w = lax.ppermute(near_w, "dp", middle)
-    first = place(ops[:2], intensities, near_x, own_w, near_w, own_pick)
-    far_send = far_pack(far_pick, outer_x, outer_w, inner_x, inner_w, first)
-    far_got = spread(far_send)
-    second = place(ops[2:], intensities, near_x, own_w, near_w, far_send)
-    stats = plane_sums(own_got, far_got, first, second)
+    mine_1 = weigh(intensities, observed, qweights, 1)
+    own_got = spread(own_pack(own_pick, (mine_0, mine_1)))
+    near_0, mid_0, far_pick, later_1 = lax.optimization_barrier((near_0, mid_0, far_pick, mine_1))
+    near_1 = lax.ppermute(later_1, "dp", near)
+    mid_1 = lax.ppermute(later_1, "dp", middle)
+    outer_0 = lax.ppermute(mid_0, "dp", outward)
+    inner_0 = lax.ppermute(near_0, "dp", middle)
+    moved_0 = place(ops, 0, NOPS, 0, mine_0, near_0, None, own_pick)
+    near_1, mid_1, outer_0, inner_0 = lax.optimization_barrier((near_1, mid_1, outer_0, inner_0))
+    outer_1 = lax.ppermute(mid_1, "dp", outward)
+    inner_1 = lax.ppermute(near_1, "dp", middle)
+    far_send_0 = far_pack(far_pick, outer_0, inner_0, moved_0)
+    far_got_0 = spread(far_send_0)
+    first = place(ops, 0, NOPS // 2, 1, mine_1, near_1, moved_0, far_send_0)
+    far_send_1 = far_pack(far_pick, outer_1, inner_1, first)
+    far_got_1 = spread(far_send_1)
+    second = place(ops, NOPS // 2, NOPS // 2, 1, mine_1, near_1, moved_0, far_send_1)
+    sums_0 = plane_sums(0, own_got, far_got_0, first, second, None)
+    stats = plane_sums(1, own_got, far_got_1, first, second, sums_0)
     stats = stats.reshape(2, PLANE, 2, SUB, NOPS * blk)
     mine, other = stats[:, :, 0], stats[:, :, 1]
 

time: 205 us -> 212 us (1.034)
  Pallas kernels: 104 us -> 128 us
  waiting for transfers between devices: 61.6 us -> 43.4 us
  starting transfers between devices: 28.3 us -> 31.2 us
  other arithmetic: 3.29 us -> 1.05 us
    pallas_call x3 -> x7, Pallas kernels: 95.1 us -> 116 us  [the longest x3 83.8 us: place(): pl.pallas_call(functools.partial(place_kernel, begun), grid=(count, chunk...]
    all_to_all x2 -> x3, waiting for transfers between devices: 11.6 us -> 0.01 us  [spread(): lax.all_to_all(send, 'dp', split_axis=0, concat_axis=0, axis_index_groups...]
    ppermute x1, waiting for transfers between devices: 32.2 us -> 23.2 us  [shards_by_plane(): far_pick = lax.ppermute(own_pick, 'dp', far)]
    ppermute x8, starting transfers between devices: 13.9 us -> 8.53 us  [the longest x1 2.49 us: shards_by_plane(): near_0 = lax.ppermute(mine_0, 'dp', near)]
    all_to_all x2 -> x3, starting transfers between devices: 9.34 us -> 13.8 us  [spread(): lax.all_to_all(send, 'dp', split_axis=0, concat_axis=0, axis_index_groups...]
    pallas_call x2 -> x3, Pallas kernels: 9.31 us -> 11.7 us  [pack_call(): pl.pallas_call(kernel, out_shape=jax.ShapeDtypeStruct((PLANE, 2, SLAB, wi...]
    ppermute x8, waiting for transfers between devices: 10.4 us -> 12.7 us  [the longest x1 7.41 us: shards_by_plane(): outer_1 = lax.ppermute(mid_1, 'dp', outward)]
    convert_element_type x1 -> x0, other arithmetic: 2.23 us -> none  [shards_by_plane(): (observed.astype(jnp.float32) * qweights.astype(jnp.float32)).astype(jnp....]
  transfers between devices with their start and end apart: 13 -> 14, of which waited for: 4 -> 4; matrix products, arithmetic and copies ran while one was open for 2% -> 2% of each run, Pallas kernels for 40% -> 49%
where the time goes in v4:
time: 212 us; the launch traced here: 211 us
  Pallas kernels  128 us (60%)
  waiting for transfers between devices  43.4 us (20%)
  starting transfers between devices  31.2 us (15%)
  local copies, waits for them, and re-layouts  6.5 us (3%)
    pallas_call x3, Pallas kernels, place(): pl.pallas_call(functools.partial(place_kernel, begun), grid=(count, chunk...  83.8 us
    pallas_call x2, Pallas kernels, plane_sums(): pl.pallas_call(functools.partial(plane_sums_kernel, begun, ended), grid=(...  25 us
    ppermute x1, waiting for transfers between devices, shards_by_plane(): far_pick = lax.ppermute(own_pick, 'dp', far)  23.2 us
    all_to_all x3, starting transfers between devices, spread(): lax.all_to_all(send, 'dp', split_axis=0, concat_axis=0, axis_index_groups...  13.8 us
    pallas_call x3, Pallas kernels, pack_call(): pl.pallas_call(kernel, out_shape=jax.ShapeDtypeStruct((PLANE, 2, SLAB, wi...  11.7 us
    all_to_all x1, waiting for transfers between devices, shards_by_plane(): back = lax.all_to_all(back, 'dp', split_axis=0, concat_axis=0, tiled=True)  7.42 us
    ppermute x1, waiting for transfers between devices, shards_by_plane(): outer_1 = lax.ppermute(mid_1, 'dp', outward)  7.41 us
    pallas_call x2, Pallas kernels, weigh(): pl.pallas_call(weigh_kernel, grid=(count,), out_shape=jax.ShapeDtypeStruc...  7.19 us
  transfers between devices with their start and end apart: 14, of which 4 were waited for; matrix products, arithmetic and copies ran while one was open for 2% of the time, Pallas kernels for 49%

profile of v4, /device:TPU:0, one launch (start us, length us, event | category | flops | bytes accessed | tf_op | source)
XLA Modules:
  0.0 210.7 jit_solution(14680726034793947892)
XLA Ops:
  0.6 3.6 %weigh.2.refs_0_.mine_ref = bf16[64,8192]{1,0:T(8,128)(2,1)} custom-call(bf16[32,16384]{1,0:T(8,128)(2,1)} %x_ref.3, s32[32,16384]{1,0:T(8,128)} %obs_ref.3, bf16[32,16384]{1,0:T(8,128)(2,1)} %qw_ref.3), custom_call_target="tpu_custom_call" | custom-call | flops 524288 | bytes 3145728 | tf_op jit(solution)/shard_map/weigh/pallas_call | solution.py:206
  4.2 3.6 %weigh.3.refs_1_.mine_ref = bf16[64,8192]{1,0:T(8,128)(2,1)} custom-call(bf16[32,16384]{1,0:T(8,128)(2,1)} %x_ref.3, s32[32,16384]{1,0:T(8,128)} %obs_ref.3, bf16[32,16384]{1,0:T(8,128)(2,1)} %qw_ref.3), custom_call_target="tpu_custom_call" | custom-call | flops 524288 | bytes 3145728 | tf_op jit(solution)/shard_map/weigh/pallas_call | solution.py:206
  7.8 4.3 %own_pack.1 = bf16[8,2,8,16384]{3,2,1,0:T(8,128)(2,1)} custom-call(s32[32]{0:T(128)} %bitcast.34, bf16[64,8192]{1,0:T(8,128)(2,1)} %weigh.2.refs_0_.mine_ref, bf16[64,8192]{1,0:T(8,128)(2,1)} %weigh.3.refs_1_.mine_ref), custom_call_target="tpu_custom_call" | custom-call | flops 2097152 | bytes 6291456 | tf_op jit(solution)/shard_map/own_pack/pallas_call | solution.py:277
  12.1 0.0 copy-start.2
  12.1 0.0 copy-start.10
  12.1 0.0 copy-start.1
  12.1 0.0 copy-start.9
  12.2 5.3 %all-to-all-start = ((bf16[8,2,8,16384]{3,2,1,0:T(8,128)(2,1)}), bf16[8,2,8,16384]{3,2,1,0:T(8,128)(2,1)}, u32[]{:S(2)}, u32[]{:S(2)}) async-start(bf16[8,2,8,16384]{3,2,1,0:T(8,128)(2,1)} %own_pack.1), calls=%async_computation | async-start | bytes 8388608 | tf_op jit(solution)/shard_map/all_to_all | solution.py:514
  17.5 0.0 copy-done.2
  17.5 2.5 %collective-permute-start = (bf16[64,8192]{1,0:T(8,128)(2,1)S(1)}, bf16[64,8192]{1,0:T(8,128)(2,1)S(1)}, u32[]{:S(2)}, u32[]{:S(2)}) collective-permute-start(bf16[64,8192]{1,0:T(8,128)(2,1)S(1)} %copy-done.2), channel_id=1, source_target_pairs={{0,8},{1,9},{2,10},{3,11},{4,12},{5,13},{6,14},{7,15},{8,0},{9,1},... | collective-permute-start | bytes 3145736 | tf_op jit(solution)/shard_map/ppermute | solution.py:520
  20.0 0.7 collective-permute-start.1
  20.7 0.0 copy-done.10
  20.7 3.8 %collective-permute-start.2 = (s32[32]{0:T(128)S(1)}, s32[32]{0:T(128)S(1)}, u32[]{:S(2)}, u32[]{:S(2)}) collective-permute-start(s32[32]{0:T(128)S(1)} %bitcast.37), channel_id=1, source_target_pairs={{0,16},{1,17},{2,18},{3,19},{4,20},{5,21},{6,22},{7,23},{8,24},{9,... | collective-permute-start | bytes 392 | tf_op jit(solution)/shard_map/ppermute | solution.py:522
  24.6 23.2 %collective-permute-done.2.pick_ref = s32[32]{0:T(128)S(1)} collective-permute-done((s32[32]{0:T(128)S(1)}, s32[32]{0:T(128)S(1)}, u32[]{:S(2)}, u32[]{:S(2)}) %collective-permute-start.2) | collective-permute-done | bytes 160 | tf_op jit(solution)/shard_map/ppermute | solution.py:522
  47.8 0.0 collective-permute-done.near_ref
  47.8 0.0 collective-permute-done.1
  47.8 0.0 copy-done.1
  47.8 0.6 collective-permute-start.3
  48.4 0.7 collective-permute-start.4
  49.1 0.7 collective-permute-start.6
  49.8 1.3 collective-permute-start.5
  51.1 0.0 copy-done.9
  51.1 0.9 broadcast_in_dim.10.ops_ref
  52.0 0.0 copy-done.4
  52.0 37.2 %place.3.after_ref.before_ref = bf16[16384,512]{1,0:T(8,128)(2,1)} custom-call(s32[4,1,16384]{2,1,0:T(1,128)} %broadcast_in_dim.10.ops_ref, bf16[64,8192]{1,0:T(8,128)(2,1)} %weigh.2.refs_0_.mine_ref, bf16[64,8192]{1,0:T(8,128)(2,1)} %copy-done.4, s32[32]{0:T(128)} %bitcast.35, s32[32]{0:T(128)} %bitcast.36), custom_call_target="tpu_custom_call" | custom-call | bytes 268435456 | tf_op jit(solution)/shard_map/place/pallas_call | solution.py:362
  89.2 0.0 copy-done.11
  89.2 0.0 collective-permute-done.3.near_ref
  89.3 0.0 copy-start.3
  89.3 0.0 collective-permute-done.4
  89.3 0.0 copy-start.12
  89.3 0.0 collective-permute-done.6.inner_ref
  89.3 0.0 copy-start.5
  89.3 5.3 %collective-permute-done.5.outer_ref = bf16[64,8192]{1,0:T(8,128)(2,1)S(1)} collective-permute-done((bf16[64,8192]{1,0:T(8,128)(2,1)S(1)}, bf16[64,8192]{1,0:T(8,128)(2,1)S(1)}, u32[]{:S(2)}, u32[]{:S(2)}) %collective-permute-start.5) | collective-permute-done | bytes 1048608 | tf_op jit(solution)/shard_map/ppermute | solution.py:528
  94.6 0.0 copy-done.12
  94.6 0.0 copy-done.5
  94.6 1.0 copy-done.6
  95.6 3.7 %far_pack.2.after_ref = bf16[8,2,8,8192]{3,2,1,0:T(8,128)(2,1)} custom-call(s32[32]{0:T(128)} %copy-done.11, bf16[64,8192]{1,0:T(8,128)(2,1)} %copy-done.6, bf16[64,8192]{1,0:T(8,128)(2,1)} %copy-done.5, bf16[16384,512]{1,0:T(8,128)(2,1)} %place.3.after_ref.before_ref), custom_call_target="tpu_custom_call" | custom-call | flops 1048576 | bytes 3145728 | tf_op jit(solution)/shard_map/far_pack/pallas_call | solution.py:277
  99.4 0.0 all-to-all-done
  99.4 4.1 %all-to-all-start.2 = ((bf16[8,2,8,8192]{3,2,1,0:T(8,128)(2,1)}), bf16[8,2,8,8192]{3,2,1,0:T(8,128)(2,1)S(1)}, u32[]{:S(2)}, u32[]{:S(2)}) async-start(bf16[8,2,8,8192]{3,2,1,0:T(8,128)(2,1)} %far_pack.2.after_ref), calls=%async_computation.2 | async-start | bytes 4194304 | tf_op jit(solution)/shard_map/all_to_all | solution.py:514
  103.5 0.7 collective-permute-start.8
  104.2 1.3 collective-permute-start.7
  105.5 23.5 %place.4.after_ref.first_ref = bf16[16384,256]{1,0:T(8,128)(2,1)} custom-call(s32[4,1,16384]{2,1,0:T(1,128)} %broadcast_in_dim.10.ops_ref, bf16[64,8192]{1,0:T(8,128)(2,1)} %weigh.3.refs_1_.mine_ref, bf16[64,8192]{1,0:T(8,128)(2,1)} %copy-done.3, bf16[16384,512]{1,0:T(8,128)(2,1)} %place.3.after_ref.before_ref, bf16[8,2,8,8192]{3,2,1,0:T(8,128)(2,1)} %far_pack.2.after_ref), custom_call_target="tpu_custom_call" | custom-call | bytes 134217728 | tf_op jit(solution)/shard_map/place/pallas_call | solution.py:362
  129.1 0.0 collective-permute-done.8.inner_ref
  129.1 7.4 %collective-permute-done.7.outer_ref = bf16[64,8192]{1,0:T(8,128)(2,1)S(1)} collective-permute-done((bf16[64,8192]{1,0:T(8,128)(2,1)}, bf16[64,8192]{1,0:T(8,128)(2,1)S(1)}, u32[]{:S(2)}, u32[]{:S(2)}) %collective-permute-start.7) | collective-permute-done | bytes 1048608 | tf_op jit(solution)/shard_map/ppermute | solution.py:532
  136.5 1.1 copy-done.8
  137.5 3.6 %far_pack.3.after_ref = bf16[8,2,8,8192]{3,2,1,0:T(8,128)(2,1)} custom-call(s32[32]{0:T(128)} %copy-done.11, bf16[64,8192]{1,0:T(8,128)(2,1)} %copy-done.8, bf16[64,8192]{1,0:T(8,128)(2,1)} %copy-done.7, bf16[16384,256]{1,0:T(8,128)(2,1)} %place.4.after_ref.first_ref), custom_call_target="tpu_custom_call" | custom-call | flops 1048576 | bytes 3145728 | tf_op jit(solution)/shard_map/far_pack/pallas_call | solution.py:277
  141.2 0.0 all-to-all-done.2
  141.2 4.4 %all-to-all-start.1 = ((bf16[8,2,8,8192]{3,2,1,0:T(8,128)(2,1)}), bf16[8,2,8,8192]{3,2,1,0:T(8,128)(2,1)}, u32[]{:S(2)}, u32[]{:S(2)}) async-start(bf16[8,2,8,8192]{3,2,1,0:T(8,128)(2,1)} %far_pack.3.after_ref), calls=%async_computation.1 | async-start | bytes 4194304 | tf_op jit(solution)/shard_map/all_to_all | solution.py:514
  145.6 23.1 %place.5.second_ref = bf16[16384,256]{1,0:T(8,128)(2,1)} custom-call(s32[4,1,16384]{2,1,0:T(1,128)} %broadcast_in_dim.10.ops_ref, bf16[64,8192]{1,0:T(8,128)(2,1)} %weigh.3.refs_1_.mine_ref, bf16[64,8192]{1,0:T(8,128)(2,1)} %copy-done.3, bf16[16384,512]{1,0:T(8,128)(2,1)} %place.3.after_ref.before_ref, bf16[8,2,8,8192]{3,2,1,0:T(8,128)(2,1)} %far_pack.3.after_ref), custom_call_target="tpu_custom_call" | custom-call | bytes 134217728 | tf_op jit(solution)/shard_map/place/pallas_call | solution.py:362
  168.7 12.0 %plane_sums.2.before_ref = f32[384,768]{1,0:T(8,128)} custom-call(bf16[128,16384]{1,0:T(8,128)(2,1)} %bitcast.1.own_ref, bf16[128,8192]{1,0:T(8,128)(2,1)} %bitcast.25, bf16[16384,256]{1,0:T(8,128)(2,1)} %place.4.after_ref.first_ref, bf16[16384,256]{1,0:T(8,128)(2,1)} %place.5.second_ref, bf16[128,8192]{1,0:T(8,128)(2,1)} %bitcast.26), custom_call_target="tpu_custom_call" | custom-call | flops 4831838208 | bytes 12582912 | tf_op jit(solution)/shard_map/plane_sums/pallas_call | solution.py:479
  180.7 0.0 all-to-all-done.1
  180.7 13.0 %plane_sums.3 = f32[128,128]{1,0:T(8,128)} custom-call(bf16[128,16384]{1,0:T(8,128)(2,1)} %bitcast.1.own_ref, bf16[128,8192]{1,0:T(8,128)(2,1)} %bitcast.2.far_ref, bf16[16384,256]{1,0:T(8,128)(2,1)} %place.4.after_ref.first_ref, bf16[16384,256]{1,0:T(8,128)(2,1)} %place.5.second_ref, f32[384,768]{1,0:T(8,128)} %plane_sums.2.before_ref), custom_call_target="tpu_custom_call" | custom-call | flops 4831838208 | bytes 12582912 | tf_op jit(solution)/shard_map/plane_sums/pallas_call | solution.py:479
  193.7 0.8 slice_bitcast_fusion.1
  194.5 0.8 collective-permute-start.9
  195.3 0.9 reverse_select_fusion
  196.2 0.7 broadcast_in_dim.12
  196.9 4.2 %all-to-all-start.3 = ((f32[32,8,128]{2,1,0:T(8,128)}), f32[32,8,128]{2,1,0:T(8,128)S(1)}, u32[]{:S(2)}, u32[]{:S(2)}) async-start(f32[32,8,128]{2,1,0:T(8,128)} %bitcast.12), calls=%async_computation.3 | async-start | bytes 262144 | tf_op jit(solution)/shard_map/all_to_all | solution.py:553
  201.1 0.0 collective-permute-done.9
  201.2 0.7 copy.13
  201.9 7.4 %all-to-all-done.3 = f32[32,8,128]{2,1,0:T(8,128)S(1)} async-done(((f32[32,8,128]{2,1,0:T(8,128)}), f32[32,8,128]{2,1,0:T(8,128)S(1)}, u32[]{:S(2)}, u32[]{:S(2)}) %all-to-all-start.3) | async-done | bytes 131104 | tf_op jit(solution)/shard_map/all_to_all | solution.py:553
  209.3 0.3 reshape.42
  209.6 0.1 fusion
  209.7 0.2 copy.14
  209.9 0.9 copy.15
  (13 shorter events, 0.1 us)
Async XLA Ops:
  12.1 5.4 %copy-start.2 = (bf16[64,8192]{1,0:T(8,128)(2,1)S(1)}, bf16[64,8192]{1,0:T(8,128)(2,1)}, u32[]{:S(2)}) copy-start(bf16[64,8192]{1,0:T(8,128)(2,1)} %weigh.2.refs_0_.mine_ref) | copy-start | bytes 3145732
  12.1 8.6 %copy-start.10 = (s32[32,1]{0,1:T(1,128)S(1)}, s32[32,1]{0,1:T(1,128)}, u32[]{:S(2)}) copy-start(s32[32,1]{0,1:T(1,128)} %param.9) | copy-start | bytes 388
  12.1 35.7 %copy-start.1 = (bf16[64,8192]{1,0:T(8,128)(2,1)S(1)}, bf16[64,8192]{1,0:T(8,128)(2,1)}, u32[]{:S(2)}) copy-start(bf16[64,8192]{1,0:T(8,128)(2,1)} %weigh.3.refs_1_.mine_ref) | copy-start | bytes 3145732
  12.1 39.0 %copy-start.9 = (s32[4,16384]{1,0:T(4,128)S(1)}, s32[4,16384]{1,0:T(4,128)}, u32[]{:S(2)}) copy-start(s32[4,16384]{1,0:T(4,128)} %param.8) | copy-start | bytes 786436
  12.2 87.2 %all-to-all-start = ((bf16[8,2,8,16384]{3,2,1,0:T(8,128)(2,1)}), bf16[8,2,8,16384]{3,2,1,0:T(8,128)(2,1)}, u32[]{:S(2)}, u32[]{:S(2)}) async-start(bf16[8,2,8,16384]{3,2,1,0:T(8,128)(2,1)} %own_pack.1), calls=%async_computation | async-start | bytes 8388608 | tf_op jit(solution)/shard_map/all_to_all | solution.py:514
  17.5 30.3 %collective-permute-start = (bf16[64,8192]{1,0:T(8,128)(2,1)S(1)}, bf16[64,8192]{1,0:T(8,128)(2,1)S(1)}, u32[]{:S(2)}, u32[]{:S(2)}) collective-permute-start(bf16[64,8192]{1,0:T(8,128)(2,1)S(1)} %copy-done.2), channel_id=1, source_target_pairs={{0,8},{1,9},{2,10},{3,11},{4,12},{5,13},{6,14},{7,15},{8,0},{9,1},... | collective-permute-start | bytes 3145736 | tf_op jit(solution)/shard_map/ppermute | solution.py:520
  20.0 27.8 %collective-permute-start.1 = (bf16[64,8192]{1,0:T(8,128)(2,1)S(1)}, bf16[64,8192]{1,0:T(8,128)(2,1)S(1)}, u32[]{:S(2)}, u32[]{:S(2)}) collective-permute-start(bf16[64,8192]{1,0:T(8,128)(2,1)S(1)} %copy-done.2), channel_id=1, source_target_pairs={{8,16},{9,17},{10,18},{11,19},{12,20},{13,21},{14,22},{15,23},{16,... | collective-permute-start | bytes 3145736 | tf_op jit(solution)/shard_map/ppermute | solution.py:521
  20.7 27.1 %collective-permute-start.2 = (s32[32]{0:T(128)S(1)}, s32[32]{0:T(128)S(1)}, u32[]{:S(2)}, u32[]{:S(2)}) collective-permute-start(s32[32]{0:T(128)S(1)} %bitcast.37), channel_id=1, source_target_pairs={{0,16},{1,17},{2,18},{3,19},{4,20},{5,21},{6,22},{7,23},{8,24},{9,... | collective-permute-start | bytes 392 | tf_op jit(solution)/shard_map/ppermute | solution.py:522
  47.8 41.5 %copy-start.11 = (s32[32]{0:T(128)}, s32[32]{0:T(128)S(1)}, u32[]{:S(2)}) copy-start(s32[32]{0:T(128)S(1)} %collective-permute-done.2.pick_ref) | copy-start | bytes 388
  47.8 4.2 %copy-start.4 = (bf16[64,8192]{1,0:T(8,128)(2,1)}, bf16[64,8192]{1,0:T(8,128)(2,1)S(1)}, u32[]{:S(2)}) copy-start(bf16[64,8192]{1,0:T(8,128)(2,1)S(1)} %collective-permute-done.near_ref) | copy-start | bytes 3145732
  47.8 41.4 %collective-permute-start.3 = (bf16[64,8192]{1,0:T(8,128)(2,1)S(1)}, bf16[64,8192]{1,0:T(8,128)(2,1)S(1)}, u32[]{:S(2)}, u32[]{:S(2)}) collective-permute-start(bf16[64,8192]{1,0:T(8,128)(2,1)S(1)} %copy-done.1), channel_id=1, source_target_pairs={{0,8},{1,9},{2,10},{3,11},{4,12},{5,13},{6,14},{7,15},{8,0},{9,1},... | collective-permute-start | bytes 3145736 | tf_op jit(solution)/shard_map/ppermute | solution.py:526
  48.4 40.9 %collective-permute-start.4 = (bf16[64,8192]{1,0:T(8,128)(2,1)S(1)}, bf16[64,8192]{1,0:T(8,128)(2,1)S(1)}, u32[]{:S(2)}, u32[]{:S(2)}) collective-permute-start(bf16[64,8192]{1,0:T(8,128)(2,1)S(1)} %copy-done.1), channel_id=1, source_target_pairs={{8,16},{9,17},{10,18},{11,19},{12,20},{13,21},{14,22},{15,23},{16,... | collective-permute-start | bytes 3145736 | tf_op jit(solution)/shard_map/ppermute | solution.py:527
  49.1 40.2 %collective-permute-start.6 = (bf16[64,8192]{1,0:T(8,128)(2,1)S(1)}, bf16[64,8192]{1,0:T(8,128)(2,1)S(1)}, u32[]{:S(2)}, u32[]{:S(2)}) collective-permute-start(bf16[64,8192]{1,0:T(8,128)(2,1)S(1)} %collective-permute-done.near_ref), channel_id=1, source_target_pairs={{8,16},{9,17},{10,18},{11,19},{12,20},{13,21},{14,22},{15,23},{16,... | collective-permute-start | bytes 3145736 | tf_op jit(solution)/shard_map/ppermute | solution.py:529
  49.8 44.8 %collective-permute-start.5 = (bf16[64,8192]{1,0:T(8,128)(2,1)S(1)}, bf16[64,8192]{1,0:T(8,128)(2,1)S(1)}, u32[]{:S(2)}, u32[]{:S(2)}) collective-permute-start(bf16[64,8192]{1,0:T(8,128)(2,1)S(1)} %collective-permute-done.1), channel_id=1, source_target_pairs={{8,0},{9,1},{10,2},{11,3},{12,4},{13,5},{14,6},{15,7},{16,24},{17,... | collective-permute-start | bytes 3145736 | tf_op jit(solution)/shard_map/ppermute | solution.py:528
  89.3 14.2 %copy-start.3 = (bf16[64,8192]{1,0:T(8,128)(2,1)}, bf16[64,8192]{1,0:T(8,128)(2,1)S(1)}, u32[]{:S(2)}) copy-start(bf16[64,8192]{1,0:T(8,128)(2,1)S(1)} %collective-permute-done.3.near_ref) | copy-start | bytes 3145732
  89.3 5.3 %copy-start.12 = (bf16[64,8192]{1,0:T(8,128)(2,1)}, bf16[64,8192]{1,0:T(8,128)(2,1)S(1)}, u32[]{:S(2)}) copy-start(bf16[64,8192]{1,0:T(8,128)(2,1)S(1)} %collective-permute-done.4) | copy-start | bytes 3145732
  89.3 5.3 %copy-start.5 = (bf16[64,8192]{1,0:T(8,128)(2,1)}, bf16[64,8192]{1,0:T(8,128)(2,1)S(1)}, u32[]{:S(2)}) copy-start(bf16[64,8192]{1,0:T(8,128)(2,1)S(1)} %collective-permute-done.6.inner_ref) | copy-start | bytes 3145732
  94.6 1.0 copy-start.6
  99.4 41.8 %all-to-all-start.2 = ((bf16[8,2,8,8192]{3,2,1,0:T(8,128)(2,1)}), bf16[8,2,8,8192]{3,2,1,0:T(8,128)(2,1)S(1)}, u32[]{:S(2)}, u32[]{:S(2)}) async-start(bf16[8,2,8,8192]{3,2,1,0:T(8,128)(2,1)} %far_pack.2.after_ref), calls=%async_computation.2 | async-start | bytes 4194304 | tf_op jit(solution)/shard_map/all_to_all | solution.py:514
  103.5 25.5 %collective-permute-start.8 = (bf16[64,8192]{1,0:T(8,128)(2,1)S(1)}, bf16[64,8192]{1,0:T(8,128)(2,1)S(1)}, u32[]{:S(2)}, u32[]{:S(2)}) collective-permute-start(bf16[64,8192]{1,0:T(8,128)(2,1)S(1)} %collective-permute-done.3.near_ref), channel_id=1, source_target_pairs={{8,16},{9,17},{10,18},{11,19},{12,20},{13,21},{14,22},{15,23},{16,... | collective-permute-start | bytes 3145736 | tf_op jit(solution)/shard_map/ppermute | solution.py:533
  104.2 32.2 %collective-permute-start.7 = (bf16[64,8192]{1,0:T(8,128)(2,1)}, bf16[64,8192]{1,0:T(8,128)(2,1)S(1)}, u32[]{:S(2)}, u32[]{:S(2)}) collective-permute-start(bf16[64,8192]{1,0:T(8,128)(2,1)} %copy-done.12), channel_id=1, source_target_pairs={{8,0},{9,1},{10,2},{11,3},{12,4},{13,5},{14,6},{15,7},{16,24},{17,... | collective-permute-start | bytes 3145736 | tf_op jit(solution)/shard_map/ppermute | solution.py:532
  129.1 7.4 %copy-start.7 = (bf16[64,8192]{1,0:T(8,128)(2,1)}, bf16[64,8192]{1,0:T(8,128)(2,1)S(1)}, u32[]{:S(2)}) copy-start(bf16[64,8192]{1,0:T(8,128)(2,1)S(1)} %collective-permute-done.8.inner_ref) | copy-start | bytes 3145732
  136.5 1.1 copy-start.8
  141.2 4.4 %copy-start = (bf16[8,2,8,8192]{3,2,1,0:T(8,128)(2,1)}, bf16[8,2,8,8192]{3,2,1,0:T(8,128)(2,1)S(1)}, u32[]{:S(2)}) copy-start(bf16[8,2,8,8192]{3,2,1,0:T(8,128)(2,1)S(1)} %all-to-all-done.2) | copy-start | bytes 6291460
  141.2 39.5 %all-to-all-start.1 = ((bf16[8,2,8,8192]{3,2,1,0:T(8,128)(2,1)}), bf16[8,2,8,8192]{3,2,1,0:T(8,128)(2,1)}, u32[]{:S(2)}, u32[]{:S(2)}) async-start(bf16[8,2,8,8192]{3,2,1,0:T(8,128)(2,1)} %far_pack.3.after_ref), calls=%async_computation.1 | async-start | bytes 4194304 | tf_op jit(solution)/shard_map/all_to_all | solution.py:514
  194.5 6.6 %collective-permute-start.9 = (f32[2,8,4,128]{3,2,1,0:T(4,128)S(1)}, f32[2,8,4,128]{3,2,1,0:T(4,128)S(1)}, u32[]{:S(2)}, u32[]{:S(2)}) collective-permute-start(f32[2,8,4,128]{3,2,1,0:T(4,128)S(1)} %get-tuple-element.23), channel_id=1, source_target_pairs={{0,8},{1,9},{2,10},{3,11},{4,12},{5,13},{6,14},{7,15},{8,0},{9,1},... | collective-permute-start | bytes 98312 | tf_op jit(solution)/shard_map/ppermute | solution.py:545
  196.9 12.4 %all-to-all-start.3 = ((f32[32,8,128]{2,1,0:T(8,128)}), f32[32,8,128]{2,1,0:T(8,128)S(1)}, u32[]{:S(2)}, u32[]{:S(2)}) async-start(f32[32,8,128]{2,1,0:T(8,128)} %bitcast.12), calls=%async_computation.3 | async-start | bytes 262144 | tf_op jit(solution)/shard_map/all_to_all | solution.py:553

commit v5 on v4

--- a/solution.py
+++ b/solution.py
@@ -252,35 +252,28 @@
     send_slabs(slabs, pick_ref, send_ref, sems)
 
 
-def far_pack_kernel(pick_ref, outer_ref, inner_ref, after_ref, send_ref, buf, in_sem, slabs, sems):
+def far_pack_kernel(pick_ref, outer_ref, inner_ref, after_ref, send_ref, slabs, sems):
     plane = lax.div(lax.axis_index("dp"), PLANE)
     inner = (plane == 1) | (plane == 2)
 
-    def fetch(ref):
-        copy = pltpu.make_async_copy(ref, buf, in_sem)
-        copy.start()
-        copy.wait()
-
     @pl.when(inner)
     def _():
-        fetch(inner_ref)
+        fill_slabs(slabs, inner_ref, 0)
 
     @pl.when(jnp.logical_not(inner))
     def _():
-        fetch(outer_ref)
-
-    fill_slabs(slabs, buf, 0)
+        fill_slabs(slabs, outer_ref, 0)
+
     send_slabs(slabs, pick_ref, send_ref, sems)
 
 
-def pack_call(kernel, name, specs, scratch, blk, width, *operands):
+def pack_call(kernel, name, specs, blk, width, *operands):
     return pl.pallas_call(
         kernel,
         out_shape=jax.ShapeDtypeStruct((PLANE, 2, SLAB, width), jnp.bfloat16),
         in_specs=[pl.BlockSpec(memory_space=pltpu.SMEM)] + specs,
         out_specs=pl.BlockSpec(memory_space=pl.ANY),
-        scratch_shapes=scratch
-        + [pltpu.VMEM((blk // SUB, SLAB, width), jnp.bfloat16), pltpu.SemaphoreType.DMA((PLANE, 2))],
+        scratch_shapes=[pltpu.VMEM((blk // SUB, SLAB, width), jnp.bfloat16), pltpu.SemaphoreType.DMA((PLANE, 2))],
         compiler_params=params(),
         cost_estimate=pl.CostEstimate(
             flops=blk * width * 4, bytes_accessed=(PLANE * 2 * SLAB * 2 + blk * 4) * width, transcendentals=0
@@ -292,14 +285,13 @@
 def own_pack(pick, halves):
     rows, width = halves[0].shape
     specs = [pl.BlockSpec(memory_space=pltpu.VMEM)] * HALVES
-    return pack_call(own_pack_kernel, "own_pack", specs, [], rows // 2, HALVES * width, pick, *halves)
+    return pack_call(own_pack_kernel, "own_pack", specs, rows // 2, HALVES * width, pick, *halves)
 
 
 def far_pack(pick, outer, inner, after):
     rows, width = outer.shape
-    scratch = [pltpu.VMEM((rows, width), jnp.bfloat16), pltpu.SemaphoreType.DMA]
-    specs = [pl.BlockSpec(memory_space=pl.ANY)] * 3
-    return pack_call(far_pack_kernel, "far_pack", specs, scratch, rows // 2, width, pick, outer, inner, after)
+    specs = [pl.BlockSpec(memory_space=pltpu.VMEM)] * 2 + [pl.BlockSpec(memory_space=pl.ANY)]
+    return pack_call(far_pack_kernel, "far_pack", specs, rows // 2, width, pick, outer, inner, after)
 
 
 def place_kernel(begun, ops_ref, mine_ref, near_ref, before_ref, after_ref, moved_ref, table, target):
@@ -308,6 +300,8 @@
     width = target.shape[0]
     step = min(512, width)
     part = pl.multiple_of(pl.program_id(1) * depth, depth)
+    table_rows = table.reshape(table.shape[0], 1, LANES)
+    target_rows = target.reshape(width, 1, LANES)
 
     @pl.when(pl.program_id(0) == 0)
     def _():
@@ -340,8 +334,7 @@
         base = pl.multiple_of(i * UNROLL, UNROLL)
         row = pl.multiple_of(part + base, UNROLL)
         for j in range(UNROLL):
-            to = ops_ref[0, 0, base + j]
-            target[pl.ds(to, 1), :] = table[pl.ds(row + j, 1), :]
+            target_rows[ops_ref[0, 0, base + j]] = table_rows[row + j]
 
     @pl.when(pl.program_id(1) == pl.num_programs(1) - 1)
     def _():
@@ -403,9 +396,8 @@
         else:
             acc[...] = jnp.zeros_like(acc)
 
-    @pl.loop(0, depth // step)
-    def _(i):
-        cols = pl.ds(pl.multiple_of(i * step, step), step)
+    for i in range(depth // step):
+        cols = slice(i * step, (i + 1) * step)
         is_x = lax.broadcasted_iota(jnp.int32, (slabs, SLAB, step), 1) < SUB
         weights, products = [], []
         for ref in (own_ref, far_ref):
@@ -469,7 +461,7 @@
 
 def plane_sums(part, own, far, first, second, before):
     rows, width = far.shape
-    depth = min(2048, width)
+    depth = min(4096, width)
     chunks = width // depth
     lanes = (NOPS + NOPS // 2) * LANES
     moved = pl.BlockSpec((depth, 2 * LANES), lambda i: (part * chunks + i, 0))
@@ -521,8 +513,9 @@
     mid_0 = lax.ppermute(mine_0, "dp", middle)
     far_pick = lax.ppermute(own_pick, "dp", far)
     mine_1 = weigh(intensities, observed, qweights, 1)
-    own_got = spread(own_pack(own_pick, (mine_0, mine_1)))
-    near_0, mid_0, far_pick, later_1 = lax.optimization_barrier((near_0, mid_0, far_pick, mine_1))
+    own_send = own_pack(own_pick, (mine_0, mine_1))
+    near_0, mid_0, far_pick, later_1, own_send = lax.optimization_barrier((near_0, mid_0, far_pick, mine_1, own_send))
+    own_got = spread(own_send)
     near_1 = lax.ppermute(later_1, "dp", near)
     mid_1 = lax.ppermute(later_1, "dp", middle)
     outer_0 = lax.ppermute(mid_0, "dp", outward)

time: 212 us -> 244 us (1.15)
  blocking collectives: 0 us -> 30.9 us
    all_to_all x0 -> x1, blocking collectives: none -> 30.9 us  [spread(): lax.all_to_all(send, 'dp', split_axis=0, concat_axis=0, axis_index_groups...]
    all_to_all x3 -> x2, waiting for transfers between devices: 0.01 us -> 12 us  [spread(): lax.all_to_all(send, 'dp', split_axis=0, concat_axis=0, axis_index_groups...]
    ppermute x1, waiting for transfers between devices: 23.2 us -> 14.9 us  [shards_by_plane(): far_pick = lax.ppermute(own_pick, 'dp', far)]
    all_to_all x3 -> x2, starting transfers between devices: 13.8 us -> 8.34 us  [spread(): lax.all_to_all(send, 'dp', split_axis=0, concat_axis=0, axis_index_groups...]
    ppermute x1, starting transfers between devices: 0.82 us -> 4.63 us  [shards_by_plane(): from_near = lax.ppermute(other, 'dp', near)]
  transfers between devices with their start and end apart: 14 -> 13, of which waited for: 4 -> 5; matrix products, arithmetic and copies ran while one was open for 2% -> 1% of each run, Pallas kernels for 49% -> 44%
where the time goes in v5:
time: 244 us
  Pallas kernels  126 us (52%)
  waiting for transfers between devices  45.8 us (19%)
  blocking collectives  30.9 us (13%)
  starting transfers between devices  30.6 us (13%)
  local copies, waits for them, and re-layouts  8.16 us (3%)
    pallas_call x3, Pallas kernels, place(): pl.pallas_call(functools.partial(place_kernel, begun), grid=(count, chunk...  84.1 us
    all_to_all x1, blocking collectives, spread(): lax.all_to_all(send, 'dp', split_axis=0, concat_axis=0, axis_index_groups...  30.9 us
    pallas_call x2, Pallas kernels, plane_sums(): pl.pallas_call(functools.partial(plane_sums_kernel, begun, ended), grid=(...  23.4 us
    ppermute x1, waiting for transfers between devices, shards_by_plane(): far_pick = lax.ppermute(own_pick, 'dp', far)  14.9 us
    all_to_all x2, waiting for transfers between devices, spread(): lax.all_to_all(send, 'dp', split_axis=0, concat_axis=0, axis_index_groups...  12 us
    pallas_call x3, Pallas kernels, pack_call(): pl.pallas_call(kernel, out_shape=jax.ShapeDtypeStruct((PLANE, 2, SLAB, wi...  11.1 us
    all_to_all x2, starting transfers between devices, spread(): lax.all_to_all(send, 'dp', split_axis=0, concat_axis=0, axis_index_groups...  8.34 us
    all_to_all x1, waiting for transfers between devices, shards_by_plane(): back = lax.all_to_all(back, 'dp', split_axis=0, concat_axis=0, tiled=True)  7.42 us
  transfers between devices with their start and end apart: 13, of which 5 were waited for; matrix products, arithmetic and copies ran while one was open for 1% of the time, Pallas kernels for 44%

profile of v5, /device:TPU:0, one launch (start us, length us, event | category | flops | bytes accessed | tf_op | source)
XLA Modules:
  0.0 243.5 jit_solution(16292226639775598594)
XLA Ops:
  0.6 0.0 copy-start.9
  0.6 3.7 %weigh.2.refs_0_.mine_ref = bf16[64,8192]{1,0:T(8,128)(2,1)} custom-call(bf16[32,16384]{1,0:T(8,128)(2,1)} %x_ref.3, s32[32,16384]{1,0:T(8,128)} %obs_ref.3, bf16[32,16384]{1,0:T(8,128)(2,1)} %qw_ref.3), custom_call_target="tpu_custom_call" | custom-call | flops 524288 | bytes 3145728 | tf_op jit(solution)/shard_map/weigh/pallas_call | solution.py:206
  4.3 3.0 %collective-permute-start = (bf16[64,8192]{1,0:T(8,128)(2,1)}, bf16[64,8192]{1,0:T(8,128)(2,1)S(1)}, u32[]{:S(2)}, u32[]{:S(2)}) collective-permute-start(bf16[64,8192]{1,0:T(8,128)(2,1)} %weigh.2.refs_0_.mine_ref), channel_id=1, source_target_pairs={{0,8},{1,9},{2,10},{3,11},{4,12},{5,13},{6,14},{7,15},{8,0},{9,1},... | collective-permute-start | bytes 3145736 | tf_op jit(solution)/shard_map/ppermute | solution.py:512
  7.3 0.7 collective-permute-start.1
  8.1 0.0 copy-done.9
  8.1 3.8 %collective-permute-start.2 = (s32[32]{0:T(128)S(1)}, s32[32]{0:T(128)S(1)}, u32[]{:S(2)}, u32[]{:S(2)}) collective-permute-start(s32[32]{0:T(128)S(1)} %bitcast.38), channel_id=1, source_target_pairs={{0,16},{1,17},{2,18},{3,19},{4,20},{5,21},{6,22},{7,23},{8,24},{9,... | collective-permute-start | bytes 392 | tf_op jit(solution)/shard_map/ppermute | solution.py:514
  11.9 3.6 %weigh.3.refs_1_.mine_ref = bf16[64,8192]{1,0:T(8,128)(2,1)} custom-call(bf16[32,16384]{1,0:T(8,128)(2,1)} %x_ref.3, s32[32,16384]{1,0:T(8,128)} %obs_ref.3, bf16[32,16384]{1,0:T(8,128)(2,1)} %qw_ref.3), custom_call_target="tpu_custom_call" | custom-call | flops 524288 | bytes 3145728 | tf_op jit(solution)/shard_map/weigh/pallas_call | solution.py:206
  15.6 0.0 copy-start
  15.6 0.0 copy-start.8
  15.6 4.4 %own_pack.1 = bf16[8,2,8,16384]{3,2,1,0:T(8,128)(2,1)} custom-call(s32[32]{0:T(128)} %bitcast.35, bf16[64,8192]{1,0:T(8,128)(2,1)} %weigh.2.refs_0_.mine_ref, bf16[64,8192]{1,0:T(8,128)(2,1)} %weigh.3.refs_1_.mine_ref), custom_call_target="tpu_custom_call" | custom-call | flops 2097152 | bytes 6291456 | tf_op jit(solution)/shard_map/own_pack/pallas_call | solution.py:271
  20.0 14.9 %collective-permute-done.2.pick_ref = s32[32]{0:T(128)S(1)} collective-permute-done((s32[32]{0:T(128)S(1)}, s32[32]{0:T(128)S(1)}, u32[]{:S(2)}, u32[]{:S(2)}) %collective-permute-start.2) | collective-permute-done | bytes 160 | tf_op jit(solution)/shard_map/ppermute | solution.py:514
  34.9 0.0 collective-permute-done.near_ref
  34.9 0.0 collective-permute-done.1
  34.9 0.0 copy-done
  34.9 0.0 copy-start.11
  34.9 0.6 collective-permute-start.3
  35.5 0.4 copy-done.11
  35.9 0.7 collective-permute-start.4
  36.7 0.7 collective-permute-start.6
  37.4 1.3 collective-permute-start.5
  38.7 0.0 copy-done.8
  38.7 0.9 broadcast_in_dim.10.ops_ref
  39.6 0.0 copy-done.3
  39.6 37.2 %place.3.after_ref.before_ref = bf16[16384,512]{1,0:T(8,128)(2,1)} custom-call(s32[4,1,16384]{2,1,0:T(1,128)} %broadcast_in_dim.10.ops_ref, bf16[64,8192]{1,0:T(8,128)(2,1)} %weigh.2.refs_0_.mine_ref, bf16[64,8192]{1,0:T(8,128)(2,1)} %copy-done.3, s32[32]{0:T(128)} %bitcast.36, s32[32]{0:T(128)} %bitcast.37), custom_call_target="tpu_custom_call" | custom-call | bytes 268435456 | tf_op jit(solution)/shard_map/place/pallas_call | solution.py:355
  76.8 0.0 copy-done.10
  76.8 0.0 collective-permute-done.3.near_ref
  76.8 0.0 copy-start.2
  76.8 0.0 collective-permute-done.4
  76.8 0.0 collective-permute-done.6.inner_ref
  76.8 0.0 copy-start.4
  76.9 4.4 %collective-permute-done.5.outer_ref = bf16[64,8192]{1,0:T(8,128)(2,1)S(1)} collective-permute-done((bf16[64,8192]{1,0:T(8,128)(2,1)}, bf16[64,8192]{1,0:T(8,128)(2,1)S(1)}, u32[]{:S(2)}, u32[]{:S(2)}) %collective-permute-start.5) | collective-permute-done | bytes 1048608 | tf_op jit(solution)/shard_map/ppermute | solution.py:521
  81.2 0.0 copy-done.4
  81.2 1.0 copy-done.5
  82.2 3.3 %far_pack.2.after_ref = bf16[8,2,8,8192]{3,2,1,0:T(8,128)(2,1)} custom-call(s32[32]{0:T(128)} %copy-done.10, bf16[64,8192]{1,0:T(8,128)(2,1)} %copy-done.5, bf16[64,8192]{1,0:T(8,128)(2,1)} %copy-done.4, bf16[16384,512]{1,0:T(8,128)(2,1)} %place.3.after_ref.before_ref), custom_call_target="tpu_custom_call" | custom-call | flops 1048576 | bytes 3145728 | tf_op jit(solution)/shard_map/far_pack/pallas_call | solution.py:271
  85.5 30.9 %all_to_all.20 = bf16[8,2,8,8192]{3,2,1,0:T(8,128)(2,1)} all-to-all(bf16[8,2,8,8192]{3,2,1,0:T(8,128)(2,1)} %far_pack.2.after_ref), channel_id=1, replica_groups={{0,1,2,3,4,5,6,7},{8,9,10,11,12,13,14,15},{16,17,18,19,20,21,22,23},{24..., dimensions={0} | all-to-all | bytes 4194304 | tf_op jit(solution)/shard_map/all_to_all | solution.py:506
  116.4 4.6 %all-to-all-start = ((bf16[8,2,8,16384]{3,2,1,0:T(8,128)(2,1)}), bf16[8,2,8,16384]{3,2,1,0:T(8,128)(2,1)}, u32[]{:S(2)}, u32[]{:S(2)}) async-start(bf16[8,2,8,16384]{3,2,1,0:T(8,128)(2,1)} %own_pack.1), calls=%async_computation | async-start | bytes 8388608 | tf_op jit(solution)/shard_map/all_to_all | solution.py:506
  121.0 0.0 copy-done.2
  121.0 0.7 collective-permute-start.8
  121.7 1.3 collective-permute-start.7
  123.0 23.5 %place.4.after_ref.first_ref = bf16[16384,256]{1,0:T(8,128)(2,1)} custom-call(s32[4,1,16384]{2,1,0:T(1,128)} %broadcast_in_dim.10.ops_ref, bf16[64,8192]{1,0:T(8,128)(2,1)} %weigh.3.refs_1_.mine_ref, bf16[64,8192]{1,0:T(8,128)(2,1)} %copy-done.2, bf16[16384,512]{1,0:T(8,128)(2,1)} %place.3.after_ref.before_ref, bf16[8,2,8,8192]{3,2,1,0:T(8,128)(2,1)} %far_pack.2.after_ref), custom_call_target="tpu_custom_call" | custom-call | bytes 134217728 | tf_op jit(solution)/shard_map/place/pallas_call | solution.py:355
  146.5 0.0 collective-permute-done.8.inner_ref
  146.6 7.1 %collective-permute-done.7.outer_ref = bf16[64,8192]{1,0:T(8,128)(2,1)S(1)} collective-permute-done((bf16[64,8192]{1,0:T(8,128)(2,1)S(1)}, bf16[64,8192]{1,0:T(8,128)(2,1)S(1)}, u32[]{:S(2)}, u32[]{:S(2)}) %collective-permute-start.7) | collective-permute-done | bytes 1048608 | tf_op jit(solution)/shard_map/ppermute | solution.py:525
  153.6 0.0 copy-done.6
  153.7 1.0 copy-done.7
  154.7 3.4 %far_pack.3.after_ref = bf16[8,2,8,8192]{3,2,1,0:T(8,128)(2,1)} custom-call(s32[32]{0:T(128)} %copy-done.10, bf16[64,8192]{1,0:T(8,128)(2,1)} %copy-done.7, bf16[64,8192]{1,0:T(8,128)(2,1)} %copy-done.6, bf16[16384,256]{1,0:T(8,128)(2,1)} %place.4.after_ref.first_ref), custom_call_target="tpu_custom_call" | custom-call | flops 1048576 | bytes 3145728 | tf_op jit(solution)/shard_map/far_pack/pallas_call | solution.py:271
  158.1 12.0 %all-to-all-done = bf16[8,2,8,16384]{3,2,1,0:T(8,128)(2,1)} async-done(((bf16[8,2,8,16384]{3,2,1,0:T(8,128)(2,1)}), bf16[8,2,8,16384]{3,2,1,0:T(8,128)(2,1)}, u32[]{:S(2)}, u32[]{:S(2)}) %all-to-all-start) | async-done | bytes 4194336 | tf_op jit(solution)/shard_map/all_to_all | solution.py:506
  170.1 3.8 %all-to-all-start.1 = ((bf16[8,2,8,8192]{3,2,1,0:T(8,128)(2,1)}), bf16[8,2,8,8192]{3,2,1,0:T(8,128)(2,1)S(1)}, u32[]{:S(2)}, u32[]{:S(2)}) async-start(bf16[8,2,8,8192]{3,2,1,0:T(8,128)(2,1)} %far_pack.3.after_ref), calls=%async_computation.1 | async-start | bytes 4194304 | tf_op jit(solution)/shard_map/all_to_all | solution.py:506
  173.9 23.4 %place.5.second_ref = bf16[16384,256]{1,0:T(8,128)(2,1)} custom-call(s32[4,1,16384]{2,1,0:T(1,128)} %broadcast_in_dim.10.ops_ref, bf16[64,8192]{1,0:T(8,128)(2,1)} %weigh.3.refs_1_.mine_ref, bf16[64,8192]{1,0:T(8,128)(2,1)} %copy-done.2, bf16[16384,512]{1,0:T(8,128)(2,1)} %place.3.after_ref.before_ref, bf16[8,2,8,8192]{3,2,1,0:T(8,128)(2,1)} %far_pack.3.after_ref), custom_call_target="tpu_custom_call" | custom-call | bytes 134217728 | tf_op jit(solution)/shard_map/place/pallas_call | solution.py:355
  197.3 11.2 %plane_sums.2.before_ref = f32[384,768]{1,0:T(8,128)} custom-call(bf16[128,16384]{1,0:T(8,128)(2,1)} %bitcast.1.own_ref, bf16[128,8192]{1,0:T(8,128)(2,1)} %bitcast.25, bf16[16384,256]{1,0:T(8,128)(2,1)} %place.4.after_ref.first_ref, bf16[16384,256]{1,0:T(8,128)(2,1)} %place.5.second_ref, bf16[128,8192]{1,0:T(8,128)(2,1)} %bitcast.26), custom_call_target="tpu_custom_call" | custom-call | flops 4831838208 | bytes 12582912 | tf_op jit(solution)/shard_map/plane_sums/pallas_call | solution.py:471
  208.6 0.0 all-to-all-done.1
  208.6 1.3 copy-done.1
  209.9 12.2 %plane_sums.3 = f32[128,128]{1,0:T(8,128)} custom-call(bf16[128,16384]{1,0:T(8,128)(2,1)} %bitcast.1.own_ref, bf16[128,8192]{1,0:T(8,128)(2,1)} %bitcast.27, bf16[16384,256]{1,0:T(8,128)(2,1)} %place.4.after_ref.first_ref, bf16[16384,256]{1,0:T(8,128)(2,1)} %place.5.second_ref, f32[384,768]{1,0:T(8,128)} %plane_sums.2.before_ref), custom_call_target="tpu_custom_call" | custom-call | flops 4831838208 | bytes 12582912 | tf_op jit(solution)/shard_map/plane_sums/pallas_call | solution.py:471
  222.1 0.8 slice_bitcast_fusion.1
  222.9 4.6 %collective-permute-start.9 = (f32[2,8,4,128]{3,2,1,0:T(4,128)S(1)}, f32[2,8,4,128]{3,2,1,0:T(4,128)S(1)}, u32[]{:S(2)}, u32[]{:S(2)}) collective-permute-start(f32[2,8,4,128]{3,2,1,0:T(4,128)S(1)} %get-tuple-element.25), channel_id=1, source_target_pairs={{0,8},{1,9},{2,10},{3,11},{4,12},{5,13},{6,14},{7,15},{8,0},{9,1},... | collective-permute-start | bytes 98312 | tf_op jit(solution)/shard_map/ppermute | solution.py:538
  227.5 0.9 reverse_select_fusion
  228.5 0.7 broadcast_in_dim.12
  229.1 4.7 %all-to-all-start.3 = ((f32[32,8,128]{2,1,0:T(8,128)}), f32[32,8,128]{2,1,0:T(8,128)S(1)}, u32[]{:S(2)}, u32[]{:S(2)}) async-start(f32[32,8,128]{2,1,0:T(8,128)} %bitcast.12), calls=%async_computation.3 | async-start | bytes 262144 | tf_op jit(solution)/shard_map/all_to_all | solution.py:546
  233.9 0.0 collective-permute-done.9
  234.0 0.7 copy.13
  234.7 7.4 %all-to-all-done.3 = f32[32,8,128]{2,1,0:T(8,128)S(1)} async-done(((f32[32,8,128]{2,1,0:T(8,128)}), f32[32,8,128]{2,1,0:T(8,128)S(1)}, u32[]{:S(2)}, u32[]{:S(2)}) %all-to-all-start.3) | async-done | bytes 131104 | tf_op jit(solution)/shard_map/all_to_all | solution.py:546
  242.1 0.3 reshape.42
  242.4 0.1 fusion
  242.5 0.2 copy.14
  242.7 0.9 copy.15
  (10 shorter events, 0.1 us)
Async XLA Ops:
  0.6 7.4 %copy-start.9 = (s32[32,1]{0,1:T(1,128)S(1)}, s32[32,1]{0,1:T(1,128)}, u32[]{:S(2)}) copy-start(s32[32,1]{0,1:T(1,128)} %param.9) | copy-start | bytes 388
  4.3 30.6 %collective-permute-start = (bf16[64,8192]{1,0:T(8,128)(2,1)}, bf16[64,8192]{1,0:T(8,128)(2,1)S(1)}, u32[]{:S(2)}, u32[]{:S(2)}) collective-permute-start(bf16[64,8192]{1,0:T(8,128)(2,1)} %weigh.2.refs_0_.mine_ref), channel_id=1, source_target_pairs={{0,8},{1,9},{2,10},{3,11},{4,12},{5,13},{6,14},{7,15},{8,0},{9,1},... | collective-permute-start | bytes 3145736 | tf_op jit(solution)/shard_map/ppermute | solution.py:512
  7.3 27.6 %collective-permute-start.1 = (bf16[64,8192]{1,0:T(8,128)(2,1)}, bf16[64,8192]{1,0:T(8,128)(2,1)S(1)}, u32[]{:S(2)}, u32[]{:S(2)}) collective-permute-start(bf16[64,8192]{1,0:T(8,128)(2,1)} %weigh.2.refs_0_.mine_ref), channel_id=1, source_target_pairs={{8,16},{9,17},{10,18},{11,19},{12,20},{13,21},{14,22},{15,23},{16,... | collective-permute-start | bytes 3145736 | tf_op jit(solution)/shard_map/ppermute | solution.py:513
  8.1 26.8 %collective-permute-start.2 = (s32[32]{0:T(128)S(1)}, s32[32]{0:T(128)S(1)}, u32[]{:S(2)}, u32[]{:S(2)}) collective-permute-start(s32[32]{0:T(128)S(1)} %bitcast.38), channel_id=1, source_target_pairs={{0,16},{1,17},{2,18},{3,19},{4,20},{5,21},{6,22},{7,23},{8,24},{9,... | collective-permute-start | bytes 392 | tf_op jit(solution)/shard_map/ppermute | solution.py:514
  15.6 19.4 %copy-start = (bf16[64,8192]{1,0:T(8,128)(2,1)S(1)}, bf16[64,8192]{1,0:T(8,128)(2,1)}, u32[]{:S(2)}) copy-start(bf16[64,8192]{1,0:T(8,128)(2,1)} %weigh.3.refs_1_.mine_ref) | copy-start | bytes 3145732
  15.6 23.1 %copy-start.8 = (s32[4,16384]{1,0:T(4,128)S(1)}, s32[4,16384]{1,0:T(4,128)}, u32[]{:S(2)}) copy-start(s32[4,16384]{1,0:T(4,128)} %param.8) | copy-start | bytes 786436
  34.9 41.9 %copy-start.10 = (s32[32]{0:T(128)}, s32[32]{0:T(128)S(1)}, u32[]{:S(2)}) copy-start(s32[32]{0:T(128)S(1)} %collective-permute-done.2.pick_ref) | copy-start | bytes 388
  34.9 4.7 %copy-start.3 = (bf16[64,8192]{1,0:T(8,128)(2,1)}, bf16[64,8192]{1,0:T(8,128)(2,1)S(1)}, u32[]{:S(2)}) copy-start(bf16[64,8192]{1,0:T(8,128)(2,1)S(1)} %collective-permute-done.near_ref) | copy-start | bytes 3145732
  34.9 1.0 copy-start.11
  34.9 41.9 %collective-permute-start.3 = (bf16[64,8192]{1,0:T(8,128)(2,1)S(1)}, bf16[64,8192]{1,0:T(8,128)(2,1)S(1)}, u32[]{:S(2)}, u32[]{:S(2)}) collective-permute-start(bf16[64,8192]{1,0:T(8,128)(2,1)S(1)} %copy-done), channel_id=1, source_target_pairs={{0,8},{1,9},{2,10},{3,11},{4,12},{5,13},{6,14},{7,15},{8,0},{9,1},... | collective-permute-start | bytes 3145736 | tf_op jit(solution)/shard_map/ppermute | solution.py:519
  35.9 40.9 %collective-permute-start.4 = (bf16[64,8192]{1,0:T(8,128)(2,1)S(1)}, bf16[64,8192]{1,0:T(8,128)(2,1)S(1)}, u32[]{:S(2)}, u32[]{:S(2)}) collective-permute-start(bf16[64,8192]{1,0:T(8,128)(2,1)S(1)} %copy-done), channel_id=1, source_target_pairs={{8,16},{9,17},{10,18},{11,19},{12,20},{13,21},{14,22},{15,23},{16,... | collective-permute-start | bytes 3145736 | tf_op jit(solution)/shard_map/ppermute | solution.py:520
  36.7 40.2 %collective-permute-start.6 = (bf16[64,8192]{1,0:T(8,128)(2,1)S(1)}, bf16[64,8192]{1,0:T(8,128)(2,1)S(1)}, u32[]{:S(2)}, u32[]{:S(2)}) collective-permute-start(bf16[64,8192]{1,0:T(8,128)(2,1)S(1)} %collective-permute-done.near_ref), channel_id=1, source_target_pairs={{8,16},{9,17},{10,18},{11,19},{12,20},{13,21},{14,22},{15,23},{16,... | collective-permute-start | bytes 3145736 | tf_op jit(solution)/shard_map/ppermute | solution.py:522
  37.4 43.8 %collective-permute-start.5 = (bf16[64,8192]{1,0:T(8,128)(2,1)}, bf16[64,8192]{1,0:T(8,128)(2,1)S(1)}, u32[]{:S(2)}, u32[]{:S(2)}) collective-permute-start(bf16[64,8192]{1,0:T(8,128)(2,1)} %copy-done.11), channel_id=1, source_target_pairs={{8,0},{9,1},{10,2},{11,3},{12,4},{13,5},{14,6},{15,7},{16,24},{17,... | collective-permute-start | bytes 3145736 | tf_op jit(solution)/shard_map/ppermute | solution.py:521
  76.8 44.2 %copy-start.2 = (bf16[64,8192]{1,0:T(8,128)(2,1)}, bf16[64,8192]{1,0:T(8,128)(2,1)S(1)}, u32[]{:S(2)}) copy-start(bf16[64,8192]{1,0:T(8,128)(2,1)S(1)} %collective-permute-done.3.near_ref) | copy-start | bytes 3145732
  76.8 4.4 %copy-start.4 = (bf16[64,8192]{1,0:T(8,128)(2,1)}, bf16[64,8192]{1,0:T(8,128)(2,1)S(1)}, u32[]{:S(2)}) copy-start(bf16[64,8192]{1,0:T(8,128)(2,1)S(1)} %collective-permute-done.6.inner_ref) | copy-start | bytes 3145732
  81.2 1.0 copy-start.5
  116.4 53.7 %all-to-all-start = ((bf16[8,2,8,16384]{3,2,1,0:T(8,128)(2,1)}), bf16[8,2,8,16384]{3,2,1,0:T(8,128)(2,1)}, u32[]{:S(2)}, u32[]{:S(2)}) async-start(bf16[8,2,8,16384]{3,2,1,0:T(8,128)(2,1)} %own_pack.1), calls=%async_computation | async-start | bytes 8388608 | tf_op jit(solution)/shard_map/all_to_all | solution.py:506
  121.0 25.5 %collective-permute-start.8 = (bf16[64,8192]{1,0:T(8,128)(2,1)S(1)}, bf16[64,8192]{1,0:T(8,128)(2,1)S(1)}, u32[]{:S(2)}, u32[]{:S(2)}) collective-permute-start(bf16[64,8192]{1,0:T(8,128)(2,1)S(1)} %collective-permute-done.3.near_ref), channel_id=1, source_target_pairs={{8,16},{9,17},{10,18},{11,19},{12,20},{13,21},{14,22},{15,23},{16,... | collective-permute-start | bytes 3145736 | tf_op jit(solution)/shard_map/ppermute | solution.py:526
  121.7 31.9 %collective-permute-start.7 = (bf16[64,8192]{1,0:T(8,128)(2,1)S(1)}, bf16[64,8192]{1,0:T(8,128)(2,1)S(1)}, u32[]{:S(2)}, u32[]{:S(2)}) collective-permute-start(bf16[64,8192]{1,0:T(8,128)(2,1)S(1)} %collective-permute-done.4), channel_id=1, source_target_pairs={{8,0},{9,1},{10,2},{11,3},{12,4},{13,5},{14,6},{15,7},{16,24},{17,... | collective-permute-start | bytes 3145736 | tf_op jit(solution)/shard_map/ppermute | solution.py:525
  146.6 7.1 %copy-start.6 = (bf16[64,8192]{1,0:T(8,128)(2,1)}, bf16[64,8192]{1,0:T(8,128)(2,1)S(1)}, u32[]{:S(2)}) copy-start(bf16[64,8192]{1,0:T(8,128)(2,1)S(1)} %collective-permute-done.8.inner_ref) | copy-start | bytes 3145732
  153.7 1.0 copy-start.7
  170.1 38.5 %all-to-all-start.1 = ((bf16[8,2,8,8192]{3,2,1,0:T(8,128)(2,1)}), bf16[8,2,8,8192]{3,2,1,0:T(8,128)(2,1)S(1)}, u32[]{:S(2)}, u32[]{:S(2)}) async-start(bf16[8,2,8,8192]{3,2,1,0:T(8,128)(2,1)} %far_pack.3.after_ref), calls=%async_computation.1 | async-start | bytes 4194304 | tf_op jit(solution)/shard_map/all_to_all | solution.py:506
  208.6 1.3 copy-start.1
  222.9 11.0 %collective-permute-start.9 = (f32[2,8,4,128]{3,2,1,0:T(4,128)S(1)}, f32[2,8,4,128]{3,2,1,0:T(4,128)S(1)}, u32[]{:S(2)}, u32[]{:S(2)}) collective-permute-start(f32[2,8,4,128]{3,2,1,0:T(4,128)S(1)} %get-tuple-element.25), channel_id=1, source_target_pairs={{0,8},{1,9},{2,10},{3,11},{4,12},{5,13},{6,14},{7,15},{8,0},{9,1},... | collective-permute-start | bytes 98312 | tf_op jit(solution)/shard_map/ppermute | solution.py:538
  229.1 13.0 %all-to-all-start.3 = ((f32[32,8,128]{2,1,0:T(8,128)}), f32[32,8,128]{2,1,0:T(8,128)S(1)}, u32[]{:S(2)}, u32[]{:S(2)}) async-start(f32[32,8,128]{2,1,0:T(8,128)} %bitcast.12), calls=%async_computation.3 | async-start | bytes 262144 | tf_op jit(solution)/shard_map/all_to_all | solution.py:546

commit v6 on v5

--- a/solution.py
+++ b/solution.py
@@ -294,18 +294,17 @@
     return pack_call(far_pack_kernel, "far_pack", specs, rows // 2, width, pick, outer, inner, after)
 
 
-def place_kernel(begun, ops_ref, mine_ref, near_ref, before_ref, after_ref, moved_ref, table, target):
-    rows, depth = mine_ref.shape
+def place_kernel(joined, ops_ref, *refs):
+    blocks, refs = refs[: 2 * HALVES], refs[2 * HALVES :]
+    other_ref, outs, (table, target) = refs[0], refs[2 if joined else 1 : -2], refs[-2:]
+    rows, depth = blocks[0].shape
     blk = rows // 2
     width = target.shape[0]
+    chunks = width // HALVES // depth
     step = min(512, width)
-    part = pl.multiple_of(pl.program_id(1) * depth, depth)
-    table_rows = table.reshape(table.shape[0], 1, LANES)
-    target_rows = target.reshape(width, 1, LANES)
-
-    @pl.when(pl.program_id(0) == 0)
-    def _():
-        size = min(256, depth)
+    size = min(256, depth)
+
+    def fill(mine_ref, near_ref):
         diagonal = lax.broadcasted_iota(jnp.int32, (size, size), 0) == lax.broadcasted_iota(
             jnp.int32, (size, size), 1
         )
@@ -313,64 +312,75 @@
         for i in range(depth // size):
             cols = slice(i * size, (i + 1) * size)
             both = [mine_ref[:blk, cols], near_ref[:blk, cols], mine_ref[blk:, cols], near_ref[blk:, cols]]
-            table[pl.ds(part + i * size, size), :] = lax.dot_general(
+            table[cols, :] = lax.dot_general(
                 identity,
                 jnp.concatenate(both, 0),
                 (((1,), (1,)), ((), ())),
                 preferred_element_type=jnp.float32,
             )
 
-    if begun:
-
-        @pl.when(pl.program_id(1) == 0)
+    for part in range(HALVES):
+
+        @pl.when(lax.div(pl.program_id(0), chunks) == part)
         def _():
-            @pl.loop(0, width // step)
-            def _(i):
-                here = pl.ds(pl.multiple_of(i * step, step), step)
-                target[here, :] = before_ref[here, :].astype(jnp.float32)
+            fill(blocks[part], blocks[HALVES + part])
 
     @pl.loop(0, depth // UNROLL)
     def _(i):
         base = pl.multiple_of(i * UNROLL, UNROLL)
-        row = pl.multiple_of(part + base, UNROLL)
         for j in range(UNROLL):
-            target_rows[ops_ref[0, 0, base + j]] = table_rows[row + j]
-
-    @pl.when(pl.program_id(1) == pl.num_programs(1) - 1)
+            target[pl.ds(ops_ref[0, 0, base + j], 1), :] = table[pl.ds(base + j, 1), :]
+
+    @pl.when(pl.program_id(0) == pl.num_programs(0) - 1)
     def _():
+        lane = lax.broadcasted_iota(jnp.int32, (step, LANES), 1)
+        first = lax.rem(lane, 2 * blk) < blk
+
         @pl.loop(0, width // step)
         def _(i):
             here = pl.ds(pl.multiple_of(i * step, step), step)
-            moved_ref[here, :] = target[here, :].astype(jnp.bfloat16)
-
-
-def place(ops, first, count, part, mine, near, before, after):
+            values = target[here, :]
+            if joined:
+                earlier = other_ref[here, :].astype(jnp.float32)
+                keep = jnp.where(first, earlier, pltpu.roll(values, blk, 1))
+                give = jnp.where(first, pltpu.roll(earlier, LANES - blk, 1), values)
+                outs[0][here, :] = keep.astype(jnp.bfloat16)
+                outs[1][here, :] = give.astype(jnp.bfloat16)
+            else:
+                outs[0][here, :] = values.astype(jnp.bfloat16)
+
+
+def place(ops, which, mine, near, earlier, after, weight):
     width = ops.shape[2]
-    rows, span = mine.shape
+    rows, span = mine[0].shape
     depth = min(2048, span)
     chunks = span // depth
-    some = pl.BlockSpec((rows, depth), lambda k, i: (0, jnp.where(k == 0, i, chunks - 1)))
+    some = [
+        pl.BlockSpec((rows, depth), lambda i, part=part: (0, jnp.clip(i - part * chunks, 0, chunks - 1)))
+        for part in range(HALVES)
+    ]
     anywhere = pl.BlockSpec(memory_space=pl.ANY)
-    begun = before is not None
-    return pl.pallas_call(
-        functools.partial(place_kernel, begun),
-        grid=(count, chunks),
-        out_shape=jax.ShapeDtypeStruct((width, count * LANES), jnp.bfloat16),
+    whole = pl.BlockSpec((width, LANES), lambda i: (0, 0))
+    joined = earlier is not None
+    count = 2 if joined else 1
+    outs = pl.pallas_call(
+        functools.partial(place_kernel, joined),
+        grid=(HALVES * chunks,),
+        out_shape=(jax.ShapeDtypeStruct((width, LANES), jnp.bfloat16),) * count,
         in_specs=[
-            pl.BlockSpec((1, 1, depth), lambda k, i: (first + k, 0, part * chunks + i), memory_space=pltpu.SMEM),
-            some,
-            some,
-            pl.BlockSpec((width, LANES), lambda k, i: (0, first + k)) if begun else anywhere,
-            anywhere,
+            pl.BlockSpec((1, 1, depth), lambda i: (which, 0, i), memory_space=pltpu.SMEM),
+            *some,
+            *some,
+            whole if joined else anywhere,
+            *([anywhere] if joined else []),
         ],
-        out_specs=pl.BlockSpec((width, LANES), lambda k, i: (0, k)),
-        scratch_shapes=[pltpu.VMEM((span, LANES), jnp.float32), pltpu.VMEM((width, LANES), jnp.float32)],
+        out_specs=(whole,) * count,
+        scratch_shapes=[pltpu.VMEM((depth, LANES), jnp.float32), pltpu.VMEM((width, LANES), jnp.float32)],
         compiler_params=params(),
-        cost_estimate=pl.CostEstimate(
-            flops=0, bytes_accessed=count * span * LANES * 64, transcendentals=0
-        ),
+        cost_estimate=pl.CostEstimate(flops=0, bytes_accessed=weight * width * LANES, transcendentals=0),
         name="place",
-    )(ops, mine, near, before if begun else after, after)
+    )(ops, *mine, *near, *((earlier, after) if joined else (after,)))
+    return outs if joined else outs[0]
 
 
 def ratio(total_w, sum_x, sum_xx, sum_y, sum_xy, sum_yy):
@@ -380,14 +390,13 @@
     return numer / jnp.sqrt(var_x * var_y)
 
 
-def plane_sums_kernel(begun, ended, own_ref, far_ref, first_ref, second_ref, before_ref, out_ref, *scratch):
+def plane_sums_kernel(begun, ended, own_ref, far_ref, *refs):
+    moved_refs, (before_ref, *outs) = refs[:4], refs[4:]
+    acc = outs[-1]
     rows, depth = own_ref.shape
     step = min(1024, depth)
     half = LANES // 2
-    slabs = rows // SLAB
-    blk = half // 2
-
-    acc = scratch[0] if ended else out_ref
+    slabs = rows // SLAB // 2
 
     @pl.when(pl.program_id(0) == 0)
     def _():
@@ -399,103 +408,117 @@
     for i in range(depth // step):
         cols = slice(i * step, (i + 1) * step)
         is_x = lax.broadcasted_iota(jnp.int32, (slabs, SLAB, step), 1) < SUB
-        weights, products = [], []
+        weights, products = ([], []), ([], [])
         for ref in (own_ref, far_ref):
-            wide = ref[:, cols].astype(jnp.float32).reshape(slabs, SLAB, step)
-            rolled = pltpu.roll(wide, SUB, 1)
-            product = wide * rolled
-            both = jnp.where(is_x, product * wide, product)
-            products.append(both.reshape(rows, step).astype(jnp.bfloat16))
-            mine = rolled.reshape(slabs // 2, 2, SLAB, step)[:, 0]
-            partner = wide.reshape(slabs // 2, 2, SLAB, step)[:, 1]
-            pair = jnp.where(is_x[: slabs // 2], mine, partner)
-            weights.append(pair.reshape(rows // 2, step).astype(jnp.bfloat16))
+            full = ref[:, cols].astype(jnp.float32).reshape(slabs, 2, SLAB, step)
+            for t in range(2):
+                wide = full[:, t]
+                rolled = pltpu.roll(wide, SUB, 1)
+                product = wide * rolled
+                both = jnp.where(is_x, product * wide, product)
+                products[t].append(both.reshape(slabs * SLAB, step))
+                even = rolled.reshape(slabs // 2, 2, SLAB, step)[:, 0]
+                odd = wide.reshape(slabs // 2, 2, SLAB, step)[:, 1]
+                pair = jnp.where(is_x[: slabs // 2], even, odd)
+                weights[t].append(pair.reshape(slabs // 2 * SLAB, step))
         low = lax.broadcasted_iota(jnp.int32, (step, LANES), 1) < half
-        linear, square = [], []
-        for ref in (first_ref, second_ref):
-            even, odd = None, None
-            for k in range(2):
-                values = ref[cols, k * LANES : (k + 1) * LANES].astype(jnp.float32)
+        for t in range(2):
+            linear, square = [], []
+            for a in range(2):
+                values = moved_refs[2 * t + a][cols, :].astype(jnp.float32)
                 swapped = pltpu.roll(values, half, 1)
                 product = values * swapped
                 linear.append(jnp.where(low, product, values).astype(jnp.bfloat16))
-                if k == 0:
-                    even = product * values
-                else:
-                    odd = product * swapped
-            square.append(jnp.where(low, even, odd).astype(jnp.bfloat16))
-        left = jnp.concatenate(weights + products, 0)
-        right = jnp.concatenate(linear + square, 1)
-        acc[...] += jnp.dot(left, right, preferred_element_type=jnp.float32)
+                square.append(product * (values if a == 0 else swapped))
+            right = jnp.concatenate(linear + [jnp.where(low, *square).astype(jnp.bfloat16)], 1)
+            left = jnp.concatenate(weights[t] + products[t], 0).astype(jnp.bfloat16)
+            acc[t] += jnp.dot(left, right, preferred_element_type=jnp.float32)
 
     if not ended:
         return
 
     @pl.when(pl.program_id(0) == pl.num_programs(0) - 1)
     def _():
-        tiles = slabs
+        near_ref, back_ref = outs[0], outs[1]
+        count = 2 * slabs * SUB
+        tiles = count // SLAB
         top = lax.broadcasted_iota(jnp.int32, (tiles, SLAB, LANES), 1) < SUB
-        lane = lax.broadcasted_iota(jnp.int32, (tiles * SLAB, LANES), 1)
-        result = jnp.zeros((tiles * SLAB, LANES), jnp.float32)
-        for k in range(NOPS):
-            lanes = slice(k * LANES, (k + 1) * LANES)
-            squares = slice((NOPS + k // 2) * LANES, (NOPS + k // 2 + 1) * LANES)
-            with_w = acc[:rows, lanes]
-            with_y = acc[rows:, lanes].reshape(tiles, 2, SLAB, LANES)
-            mine, partner = with_y[:, 0], with_y[:, 1]
-            y = jnp.where(top, pltpu.roll(mine, SUB, 1), partner).reshape(tiles * SLAB, LANES)
-            yy = jnp.where(top, mine, pltpu.roll(partner, SUB, 1)).reshape(tiles * SLAB, LANES)
-            sum_xx = acc[:rows, squares]
-            if k % 2 == 1:
-                sum_xx = pltpu.roll(sum_xx, half, 1)
-            both = ratio(
-                pltpu.roll(with_w, half, 1), with_w, sum_xx, pltpu.roll(y, half, 1), y, pltpu.roll(yy, half, 1)
-            )
-            both = jnp.where(
-                top.reshape(tiles * SLAB, LANES), both, pltpu.roll(both, LANES - blk, 1)
-            )
-            moved = both if k == 0 else pltpu.roll(both, k * blk, 1)
-            result = jnp.where((lane >= k * blk) & (lane < (k + 1) * blk), moved, result)
-        out_ref[...] = result
-
-
-def plane_sums(part, own, far, first, second, before):
+        low = lax.broadcasted_iota(jnp.int32, (count, LANES), 1) < half
+        me = lax.axis_index("dp")
+        results = []
+        for t in range(2):
+            ratios = []
+            for a in range(2):
+                lanes = slice(a * LANES, (a + 1) * LANES)
+                with_w = acc[t, :count, lanes]
+                with_y = acc[t, count:, lanes].reshape(tiles, 2, SLAB, LANES)
+                even, odd = with_y[:, 0], with_y[:, 1]
+                y = jnp.where(top, pltpu.roll(even, SUB, 1), odd).reshape(count, LANES)
+                yy = jnp.where(top, even, pltpu.roll(odd, SUB, 1)).reshape(count, LANES)
+                sum_xx = acc[t, :count, 2 * LANES :]
+                if a == 1:
+                    sum_xx = pltpu.roll(sum_xx, half, 1)
+                ratios.append(
+                    ratio(
+                        pltpu.roll(with_w, half, 1), with_w, sum_xx, pltpu.roll(y, half, 1), y, pltpu.roll(yy, half, 1)
+                    )
+                )
+            kept, got = ratios
+            straight = jnp.where(low, kept, pltpu.roll(got, half, 1))
+            crossed = jnp.where(low, got, pltpu.roll(kept, half, 1))
+            results.append(jnp.where(lax.rem(me, 2) == 0, straight, crossed))
+        mine, near = results
+        near_ref[...] = near
+        back_ref[0] = mine
+        back_ref[1] = near
+
+
+def plane_sums(part, own, far, moved, before):
     rows, width = far.shape
-    depth = min(4096, width)
+    depth = min(2048, width)
     chunks = width // depth
-    lanes = (NOPS + NOPS // 2) * LANES
-    moved = pl.BlockSpec((depth, 2 * LANES), lambda i: (part * chunks + i, 0))
     begun, ended = before is not None, part == HALVES - 1
-    total = (3 * rows, lanes)
-    shape = (rows, LANES) if ended else total
-    return pl.pallas_call(
+    total = (2, 2 * rows * 3 // 4, 3 * LANES)
+    count = rows // 2
+    placed = pl.BlockSpec((depth, LANES), lambda i: (part * chunks + i, 0))
+    entire = pl.BlockSpec(total, lambda i: (0, 0, 0))
+    if ended:
+        shapes = ((count, LANES), (2, count, LANES))
+        out_specs = (pl.BlockSpec(shapes[0], lambda i: (0, 0)), pl.BlockSpec(shapes[1], lambda i: (0, 0, 0)))
+    else:
+        shapes, out_specs = (total,), (entire,)
+    outs = pl.pallas_call(
         functools.partial(plane_sums_kernel, begun, ended),
         grid=(chunks,),
-        out_shape=jax.ShapeDtypeStruct(shape, jnp.float32),
+        out_shape=tuple(jax.ShapeDtypeStruct(shape, jnp.float32) for shape in shapes),
         in_specs=[
             pl.BlockSpec((rows, depth), lambda i: (0, part * chunks + i)),
             pl.BlockSpec((rows, depth), lambda i: (0, i)),
-            moved,
-            moved,
-            pl.BlockSpec(total, lambda i: (0, 0)) if begun else pl.BlockSpec(memory_space=pl.ANY),
+            placed,
+            placed,
+            placed,
+            placed,
+            entire if begun else pl.BlockSpec(memory_space=pl.ANY),
         ],
-        out_specs=pl.BlockSpec(shape, lambda i: (0, 0)),
+        out_specs=out_specs,
         scratch_shapes=[pltpu.VMEM(total, jnp.float32)] if ended else [],
         compiler_params=params(),
         cost_estimate=pl.CostEstimate(
-            flops=6 * rows * width * lanes,
+            flops=18 * rows * width * LANES,
             bytes_accessed=width * (4 * rows + 8 * LANES),
             transcendentals=0,
         ),
         name="plane_sums",
-    )(own, far, first, second, before if begun else far)
+    )(own, far, *moved, before if begun else far)
+    return outs if ended else outs[0]
 
 
 def shards_by_plane(intensities, observed, qweights, ops, pick):
     blk = intensities.shape[0]
     groups = PLANES * PLANE
-    near = [(i, i ^ PLANE) for i in range(groups)]
-    far = [(i, i ^ (2 * PLANE)) for i in range(groups)]
+    swap = [(i, i ^ 1) for i in range(groups)]
+    beside = [(i, i ^ PLANE) for i in range(groups)]
+    across = [(i, i ^ (2 * PLANE)) for i in range(groups)]
     middle = [(i, 3 * PLANE + 2 * (i % PLANE) - i) for i in range(PLANE, 3 * PLANE)]
     outward = [(i, i - PLANE if i < 2 * PLANE else i + PLANE) for i in range(PLANE, 3 * PLANE)]
     rings = [[z * PLANE + c for c in range(PLANE)] for z in range(PLANES)]
@@ -507,41 +530,48 @@
         return got.reshape(PLANE * 2 * SLAB, send.shape[-1])
 
     own_pick = pick[:, 0]
-    ops = ops[:, None, :]
-    mine_0 = weigh(intensities, observed, qweights, 0)
-    near_0 = lax.ppermute(mine_0, "dp", near)
-    mid_0 = lax.ppermute(mine_0, "dp", middle)
-    far_pick = lax.ppermute(own_pick, "dp", far)
-    mine_1 = weigh(intensities, observed, qweights, 1)
-    own_send = own_pack(own_pick, (mine_0, mine_1))
-    near_0, mid_0, far_pick, later_1, own_send = lax.optimization_barrier((near_0, mid_0, far_pick, mine_1, own_send))
+    core = lax.axis_index("dp") % 2
+    ops = lax.dynamic_slice_in_dim(ops, core * (NOPS // 2), NOPS // 2, 0)[:, None, :]
+    mine = [weigh(intensities, observed, qweights, part) for part in range(HALVES)]
+    near = [lax.ppermute(rows, "dp", beside) for rows in mine]
+    mid = [lax.ppermute(rows, "dp", middle) for rows in mine]
+    other = [lax.ppermute(rows, "dp", swap) for rows in mine]
+    far_pick = lax.ppermute(own_pick, "dp", across)
+
+    own_send = own_pack(own_pick, mine)
+    own_send, other = lax.optimization_barrier((own_send, other))
     own_got = spread(own_send)
-    near_1 = lax.ppermute(later_1, "dp", near)
-    mid_1 = lax.ppermute(later_1, "dp", middle)
-    outer_0 = lax.ppermute(mid_0, "dp", outward)
-    inner_0 = lax.ppermute(near_0, "dp", middle)
-    moved_0 = place(ops, 0, NOPS, 0, mine_0, near_0, None, own_pick)
-    near_1, mid_1, outer_0, inner_0 = lax.optimization_barrier((near_1, mid_1, outer_0, inner_0))
+    placed = place(ops, 0, mine, other, None, own_pick, 4)
+    keep, give = place(ops, 1, mine, other, placed, own_pick, 4)
+    own_moved = [keep, lax.ppermute(give, "dp", swap)]
+
+    near, mid, far_pick, keep = lax.optimization_barrier((near, mid, far_pick, keep))
+    own_moved[0] = keep
+    near_other = [lax.ppermute(rows, "dp", swap) for rows in near]
+    outer_0 = lax.ppermute(mid[0], "dp", outward)
+    inner_0 = lax.ppermute(near[0], "dp", middle)
+    placed = place(ops, 0, near, near_other, None, own_got, 32)
+    outer_0, inner_0, mid_1, near_1 = lax.optimization_barrier((outer_0, inner_0, mid[1], near[1]))
     outer_1 = lax.ppermute(mid_1, "dp", outward)
     inner_1 = lax.ppermute(near_1, "dp", middle)
-    far_send_0 = far_pack(far_pick, outer_0, inner_0, moved_0)
+    far_send_0 = far_pack(far_pick, outer_0, inner_0, placed)
     far_got_0 = spread(far_send_0)
-    first = place(ops, 0, NOPS // 2, 1, mine_1, near_1, moved_0, far_send_0)
-    far_send_1 = far_pack(far_pick, outer_1, inner_1, first)
+    keep, give = place(ops, 1, near, near_other, placed, far_send_0, 32)
+    far_send_1 = far_pack(far_pick, outer_1, inner_1, keep)
+    moved = own_moved + [keep, lax.ppermute(give, "dp", swap)]
     far_got_1 = spread(far_send_1)
-    second = place(ops, NOPS // 2, NOPS // 2, 1, mine_1, near_1, moved_0, far_send_1)
-    sums_0 = plane_sums(0, own_got, far_got_0, first, second, None)
-    stats = plane_sums(1, own_got, far_got_1, first, second, sums_0)
-    stats = stats.reshape(2, PLANE, 2, SUB, NOPS * blk)
-    mine, other = stats[:, :, 0], stats[:, :, 1]
-
-    from_near = lax.ppermute(other, "dp", near)
-    pair = jnp.stack([mine, from_near], 1)
+    sums = plane_sums(0, own_got, far_got_0, moved, None)
+    theirs, both = plane_sums(1, own_got, far_got_1, moved, sums)
+    both = both.reshape(2, 2, PLANE, SUB, NOPS * blk)
+
+    from_near = lax.ppermute(theirs, "dp", beside).reshape(2, PLANE, SUB, NOPS * blk)
+    pair = jnp.stack([both[0], from_near], 1)
     pair = jnp.where(odd, pair[:, ::-1], pair)
     pair = jnp.where(upper, pair[::-1], pair)
     corr = pair.reshape(groups * SUB, NOPS * blk).T.reshape(NOPS, blk, groups * SUB)
 
-    both = jnp.where(upper, stats[::-1], stats).reshape(2, 1, PLANE, 2 * SUB, NOPS * blk)
+    both = jnp.transpose(both, (1, 2, 0, 3, 4))
+    both = jnp.where(upper, both[::-1], both).reshape(2, 1, PLANE, 2 * SUB, NOPS * blk)
     back = jnp.broadcast_to(both, (2, 2, PLANE, 2 * SUB, NOPS * blk)).reshape(groups, 2 * SUB, NOPS * blk)
     back = lax.all_to_all(back, "dp", split_axis=0, concat_axis=0, tiled=True)
     back = back.reshape(2, 2, PLANE, 2, SUB, NOPS, blk)

time: 244 us -> 260 us (1.066)
  blocking collectives: 30.9 us -> 0 us
  waiting for transfers between devices: 45.8 us -> 76.4 us
  Pallas kernels: 126 us -> 139 us
  starting transfers between devices: 30.6 us -> 33.9 us
    all_to_all x1 -> x0, blocking collectives: 30.9 us -> none  [spread(): lax.all_to_all(send, 'dp', split_axis=0, concat_axis=0, axis_index_groups...]
    ppermute x1, waiting for transfers between devices: 7.09 us -> 29 us  [shards_by_plane(): outer_1 = lax.ppermute(mid_1, 'dp', outward)]
    pallas_call x3 -> x4, Pallas kernels: 84.1 us -> 100 us  [place(): pl.pallas_call(functools.partial(place_kernel, joined), grid=(HALVES * ch...]
    all_to_all x2 -> x3, starting transfers between devices: 8.34 us -> 13.8 us  [spread(): lax.all_to_all(send, 'dp', split_axis=0, concat_axis=0, axis_index_groups...]
    all_to_all x2 -> x3, waiting for transfers between devices: 12 us -> 16.6 us  [spread(): lax.all_to_all(send, 'dp', split_axis=0, concat_axis=0, axis_index_groups...]
    ppermute x8 -> x14, waiting for transfers between devices: 19.3 us -> 23.4 us  [the longest x1 23.4 us: shards_by_plane(): outer_0 = lax.ppermute(mid[0], 'dp', outward)]
    pallas_call x2, Pallas kernels: 23.4 us -> 20.7 us  [plane_sums(): pl.pallas_call(functools.partial(plane_sums_kernel, begun, ended), grid=(...]
    ppermute x8 -> x14, starting transfers between devices: 15.5 us -> 15.2 us  [the longest x1 5.58 us: shards_by_plane(): far_pick = lax.ppermute(own_pick, 'dp', across)]
  transfers between devices with their start and end apart: 13 -> 20, of which waited for: 5 -> 4; matrix products, arithmetic and copies ran while one was open for 1% -> 1% of each run, Pallas kernels for 44% -> 48%
where the time goes in v6:
time: 260 us; the launch traced here: 259 us
  Pallas kernels  139 us (53%)
  waiting for transfers between devices  76.4 us (29%)
  starting transfers between devices  33.9 us (13%)
  local copies, waits for them, and re-layouts  8.47 us (3%)
    pallas_call x4, Pallas kernels, place(): pl.pallas_call(functools.partial(place_kernel, joined), grid=(HALVES * ch...  100 us
    ppermute x1, waiting for transfers between devices, shards_by_plane(): outer_1 = lax.ppermute(mid_1, 'dp', outward)  29 us
    ppermute x1, waiting for transfers between devices, shards_by_plane(): outer_0 = lax.ppermute(mid[0], 'dp', outward)  23.4 us
    pallas_call x2, Pallas kernels, plane_sums(): pl.pallas_call(functools.partial(plane_sums_kernel, begun, ended), grid=(...  20.7 us
    all_to_all x3, waiting for transfers between devices, spread(): lax.all_to_all(send, 'dp', split_axis=0, concat_axis=0, axis_index_groups...  16.6 us
    all_to_all x3, starting transfers between devices, spread(): lax.all_to_all(send, 'dp', split_axis=0, concat_axis=0, axis_index_groups...  13.8 us
    pallas_call x3, Pallas kernels, pack_call(): pl.pallas_call(kernel, out_shape=jax.ShapeDtypeStruct((PLANE, 2, SLAB, wi...  11 us
    all_to_all x1, waiting for transfers between devices, shards_by_plane(): back = lax.all_to_all(back, 'dp', split_axis=0, concat_axis=0, tiled=True)  7.42 us
  transfers between devices with their start and end apart: 20, of which 4 were waited for; matrix products, arithmetic and copies ran while one was open for 1% of the time, Pallas kernels for 48%

profile of v6, /device:TPU:0, one launch (start us, length us, event | category | flops | bytes accessed | tf_op | source)
XLA Modules:
  0.0 259.4 jit_solution(15336143494526257385)
XLA Ops:
  0.6 0.0 copy-start
  0.6 3.7 %weigh.2.refs_0_ = bf16[64,8192]{1,0:T(8,128)(2,1)} custom-call(bf16[32,16384]{1,0:T(8,128)(2,1)} %x_ref.3, s32[32,16384]{1,0:T(8,128)} %obs_ref.3, bf16[32,16384]{1,0:T(8,128)(2,1)} %qw_ref.3), custom_call_target="tpu_custom_call" | custom-call | flops 524288 | bytes 3145728 | tf_op jit(solution)/shard_map/weigh/pallas_call | solution.py:206
  4.3 0.5 collective-permute-start
  4.8 3.6 %weigh.3.refs_1_ = bf16[64,8192]{1,0:T(8,128)(2,1)} custom-call(bf16[32,16384]{1,0:T(8,128)(2,1)} %x_ref.3, s32[32,16384]{1,0:T(8,128)} %obs_ref.3, bf16[32,16384]{1,0:T(8,128)(2,1)} %qw_ref.3), custom_call_target="tpu_custom_call" | custom-call | flops 524288 | bytes 3145728 | tf_op jit(solution)/shard_map/weigh/pallas_call | solution.py:206
  8.4 0.1 collective-permute-start.1
  8.5 4.3 %own_pack.1 = bf16[8,2,8,16384]{3,2,1,0:T(8,128)(2,1)} custom-call(s32[32]{0:T(128)} %bitcast.35, bf16[64,8192]{1,0:T(8,128)(2,1)} %weigh.2.refs_0_, bf16[64,8192]{1,0:T(8,128)(2,1)} %weigh.3.refs_1_), custom_call_target="tpu_custom_call" | custom-call | flops 2097152 | bytes 6291456 | tf_op jit(solution)/shard_map/own_pack/pallas_call | solution.py:271
  12.8 0.0 copy-start.12
  12.8 0.0 collective-permute-done.refs_2_
  12.8 0.0 collective-permute-done.1.refs_3_
  12.9 5.4 %all-to-all-start = ((bf16[8,2,8,16384]{3,2,1,0:T(8,128)(2,1)}), bf16[8,2,8,16384]{3,2,1,0:T(8,128)(2,1)}, u32[]{:S(2)}, u32[]{:S(2)}) async-start(bf16[8,2,8,16384]{3,2,1,0:T(8,128)(2,1)} %own_pack.1), calls=%async_computation | async-start | bytes 8388608 | tf_op jit(solution)/shard_map/all_to_all | solution.py:529
  18.3 2.5 collective-permute-start.2
  20.8 0.1 collective-permute-start.3
  20.9 1.7 collective-permute-start.4
  22.5 1.6 collective-permute-start.5
  24.2 5.6 %collective-permute-start.6 = (s32[32]{0:T(128)S(1)}, s32[32]{0:T(128)S(1)}, u32[]{:S(2)}, u32[]{:S(2)}) collective-permute-start(s32[32]{0:T(128)S(1)} %bitcast.38), channel_id=1, source_target_pairs={{0,16},{1,17},{2,18},{3,19},{4,20},{5,21},{6,22},{7,23},{8,24},{9,... | collective-permute-start | bytes 392 | tf_op jit(solution)/shard_map/ppermute | solution.py:539
  29.8 0.1 constant_dynamic-slice_fusion
  29.8 0.7 broadcast_in_dim.10.ops_ref
  30.6 21.8 %place.4.refs_4_ = bf16[16384,128]{1,0:T(8,128)(2,1)} custom-call(s32[2,1,16384]{2,1,0:T(1,128)} %broadcast_in_dim.10.ops_ref, bf16[64,8192]{1,0:T(8,128)(2,1)} %weigh.2.refs_0_, bf16[64,8192]{1,0:T(8,128)(2,1)} %weigh.3.refs_1_, bf16[64,8192]{1,0:T(8,128)(2,1)} %copy-done.5, bf16[64,8192]{1,0:T(8,128)(2,1)} %collective-permute-done.1.refs_3_, s32[32]{0:T(128)} %bitcast.36), custom_call_target="tpu_custom_call" | custom-call | bytes 8388608 | tf_op jit(solution)/shard_map/place/pallas_call | solution.py:366
  52.4 28.4 %place.5 = (bf16[16384,128]{1,0:T(8,128)(2,1)}, bf16[16384,128]{1,0:T(8,128)(2,1)}) custom-call(s32[2,1,16384]{2,1,0:T(1,128)} %broadcast_in_dim.10.ops_ref, bf16[64,8192]{1,0:T(8,128)(2,1)} %weigh.2.refs_0_, bf16[64,8192]{1,0:T(8,128)(2,1)} %weigh.3.refs_1_, bf16[64,8192]{1,0:T(8,128)(2,1)} %copy-done.5, bf16[64,8192]{1,0:T(8,128)(2,1)} %collective-permute-done.1.refs_3_, ...), custom_call_target="tpu_custom_call" | custom-call | bytes 8388608 | tf_op jit(solution)/shard_map/place/pallas_call | solution.py:366
  80.8 0.0 collective-permute-done.6.pick_ref
  80.8 0.0 copy-start.13
  80.8 0.0 collective-permute-done.2.refs_0_
  80.8 0.0 collective-permute-done.3.refs_1_
  80.8 0.0 collective-permute-done.4
  80.8 1.3 collective-permute-start.7
  82.1 0.7 collective-permute-start.8
  82.9 0.1 collective-permute-start.11
  82.9 0.5 collective-permute-start.12
  83.4 0.1 collective-permute-start.13
  83.5 23.4 %collective-permute-done.7.outer_ref = bf16[64,8192]{1,0:T(8,128)(2,1)S(1)} collective-permute-done((bf16[64,8192]{1,0:T(8,128)(2,1)}, bf16[64,8192]{1,0:T(8,128)(2,1)S(1)}, u32[]{:S(2)}, u32[]{:S(2)}) %collective-permute-start.7) | collective-permute-done | bytes 1048608 | tf_op jit(solution)/shard_map/ppermute | solution.py:551
  106.9 0.0 collective-permute-done.11.refs_2_
  106.9 1.0 copy-done.9
  107.9 0.0 all-to-all-done
  107.9 1.0 copy-done.6
  108.9 0.3 copy-done.7
  109.2 21.8 %place.6.after_ref.refs_4_ = bf16[16384,128]{1,0:T(8,128)(2,1)} custom-call(s32[2,1,16384]{2,1,0:T(1,128)} %broadcast_in_dim.10.ops_ref, bf16[64,8192]{1,0:T(8,128)(2,1)} %collective-permute-done.2.refs_0_, bf16[64,8192]{1,0:T(8,128)(2,1)} %collective-permute-done.3.refs_1_, bf16[64,8192]{1,0:T(8,128)(2,1)} %copy-done.6, bf16[64,8192]{1,0:T(8,128)(2,1)} %copy-done.7, ...), custom_call_target="tpu_custom_call" | custom-call | bytes 67108864 | tf_op jit(solution)/shard_map/place/pallas_call | solution.py:366
  131.1 3.3 %far_pack.2.refs_5_ = bf16[8,2,8,8192]{3,2,1,0:T(8,128)(2,1)} custom-call(s32[32]{0:T(128)} %copy-done.13, bf16[64,8192]{1,0:T(8,128)(2,1)} %copy-done.8, bf16[64,8192]{1,0:T(8,128)(2,1)} %copy-done.9, bf16[16384,128]{1,0:T(8,128)(2,1)} %place.6.after_ref.refs_4_), custom_call_target="tpu_custom_call" | custom-call | flops 1048576 | bytes 3145728 | tf_op jit(solution)/shard_map/far_pack/pallas_call | solution.py:271
  134.4 28.4 %place.7 = (bf16[16384,128]{1,0:T(8,128)(2,1)}, bf16[16384,128]{1,0:T(8,128)(2,1)}) custom-call(s32[2,1,16384]{2,1,0:T(1,128)} %broadcast_in_dim.10.ops_ref, bf16[64,8192]{1,0:T(8,128)(2,1)} %collective-permute-done.2.refs_0_, bf16[64,8192]{1,0:T(8,128)(2,1)} %collective-permute-done.3.refs_1_, bf16[64,8192]{1,0:T(8,128)(2,1)} %copy-done.6, ...), custom_call_target="tpu_custom_call" | custom-call | bytes 67108864 | tf_op jit(solution)/shard_map/place/pallas_call | solution.py:366
  162.8 0.0 collective-permute-start.14
  162.8 4.0 %all-to-all-start.2 = ((bf16[8,2,8,8192]{3,2,1,0:T(8,128)(2,1)}), bf16[8,2,8,8192]{3,2,1,0:T(8,128)(2,1)S(1)}, u32[]{:S(2)}, u32[]{:S(2)}) async-start(bf16[8,2,8,8192]{3,2,1,0:T(8,128)(2,1)} %far_pack.2.refs_5_), calls=%async_computation.2 | async-start | bytes 4194304 | tf_op jit(solution)/shard_map/all_to_all | solution.py:529
  166.8 0.7 collective-permute-start.10
  167.5 1.3 collective-permute-start.9
  168.8 0.0 collective-permute-done.10.inner_ref
  168.9 29.0 %collective-permute-done.9.outer_ref = bf16[64,8192]{1,0:T(8,128)(2,1)S(1)} collective-permute-done((bf16[64,8192]{1,0:T(8,128)(2,1)}, bf16[64,8192]{1,0:T(8,128)(2,1)S(1)}, u32[]{:S(2)}, u32[]{:S(2)}) %collective-permute-start.9) | collective-permute-done | bytes 1048608 | tf_op jit(solution)/shard_map/ppermute | solution.py:555
  197.9 1.0 copy-done.11
  198.9 3.3 %far_pack.3 = bf16[8,2,8,8192]{3,2,1,0:T(8,128)(2,1)} custom-call(s32[32]{0:T(128)} %copy-done.13, bf16[64,8192]{1,0:T(8,128)(2,1)} %copy-done.11, bf16[64,8192]{1,0:T(8,128)(2,1)} %copy-done.10, bf16[16384,128]{1,0:T(8,128)(2,1)} %get-tuple-element.34.after_ref.refs_2_), custom_call_target="tpu_custom_call" | custom-call | flops 1048576 | bytes 3145728 | tf_op jit(solution)/shard_map/far_pack/pallas_call | solution.py:271
  202.2 0.0 all-to-all-done.2
  202.2 4.4 %all-to-all-start.1 = ((bf16[8,2,8,8192]{3,2,1,0:T(8,128)(2,1)}), bf16[8,2,8,8192]{3,2,1,0:T(8,128)(2,1)}, u32[]{:S(2)}, u32[]{:S(2)}) async-start(bf16[8,2,8,8192]{3,2,1,0:T(8,128)(2,1)} %far_pack.3), calls=%async_computation.1 | async-start | bytes 4194304 | tf_op jit(solution)/shard_map/all_to_all | solution.py:529
  206.6 0.0 collective-permute-done.14.refs_3_
  206.7 10.0 %plane_sums.2.refs_4_ = f32[2,192,384]{2,1,0:T(8,128)} custom-call(bf16[128,16384]{1,0:T(8,128)(2,1)} %bitcast.1.refs_4_.own_ref, bf16[128,8192]{1,0:T(8,128)(2,1)} %bitcast.25, bf16[16384,128]{1,0:T(8,128)(2,1)} %get-tuple-element.35.refs_0_, bf16[16384,128]{1,0:T(8,128)(2,1)} %collective-permute-done.13.refs_1_, ...), custom_call_target="tpu_custom_call" | custom-call | flops 2415919104 | bytes 12582912 | tf_op jit(solution)/shard_map/plane_sums/pallas_call | solution.py:490
  216.7 16.6 %all-to-all-done.1 = bf16[8,2,8,8192]{3,2,1,0:T(8,128)(2,1)} async-done(((bf16[8,2,8,8192]{3,2,1,0:T(8,128)(2,1)}), bf16[8,2,8,8192]{3,2,1,0:T(8,128)(2,1)}, u32[]{:S(2)}, u32[]{:S(2)}) %all-to-all-start.1) | async-done | bytes 2097184 | tf_op jit(solution)/shard_map/all_to_all | solution.py:529
  233.3 10.7 %plane_sums.3 = (f32[64,128]{1,0:T(8,128)}, f32[2,64,128]{2,1,0:T(8,128)}) custom-call(bf16[128,16384]{1,0:T(8,128)(2,1)} %bitcast.1.refs_4_.own_ref, bf16[128,8192]{1,0:T(8,128)(2,1)} %bitcast.2.far_ref, bf16[16384,128]{1,0:T(8,128)(2,1)} %get-tuple-element.35.refs_0_, bf16[16384,128]{1,0:T(8,128)(2,1)} %collective-permute-done.13.refs_1_, ...), custom_call_target="tpu_custom_call" | custom-call | flops 2415919104 | bytes 12582912 | tf_op jit(solution)/shard_map/plane_sums/pallas_call | solution.py:490
  244.0 0.8 copy.20
  244.8 0.6 collective-permute-start.15
  245.5 0.8 slice.10
  246.2 0.7 broadcast_in_dim.12
  246.9 2.8 %all-to-all-start.3 = ((f32[32,8,128]{2,1,0:T(8,128)}), f32[32,8,128]{2,1,0:T(8,128)S(1)}, u32[]{:S(2)}, u32[]{:S(2)}) async-start(f32[32,8,128]{2,1,0:T(8,128)} %bitcast.14), calls=%async_computation.3 | async-start | bytes 262144 | tf_op jit(solution)/shard_map/all_to_all | solution.py:576
  249.7 0.0 collective-permute-done.15
  249.8 0.7 copy.14
  250.5 7.4 %all-to-all-done.3 = f32[32,8,128]{2,1,0:T(8,128)S(1)} async-done(((f32[32,8,128]{2,1,0:T(8,128)}), f32[32,8,128]{2,1,0:T(8,128)S(1)}, u32[]{:S(2)}, u32[]{:S(2)}) %all-to-all-start.3) | async-done | bytes 131104 | tf_op jit(solution)/shard_map/all_to_all | solution.py:576
  258.0 0.3 reshape.44
  258.2 0.1 fusion
  258.3 0.2 copy.17
  258.5 0.9 copy.18
  (31 shorter events, 0.1 us)
Async XLA Ops:
  0.6 29.1 %copy-start = (s32[4,16384]{1,0:T(4,128)S(1)}, s32[4,16384]{1,0:T(4,128)}, u32[]{:S(2)}) copy-start(s32[4,16384]{1,0:T(4,128)} %param.8) | copy-start | bytes 786436
  4.3 8.5 %collective-permute-start = (bf16[64,8192]{1,0:T(8,128)(2,1)}, bf16[64,8192]{1,0:T(8,128)(2,1)S(1)}, u32[]{:S(2)}, u32[]{:S(2)}) collective-permute-start(bf16[64,8192]{1,0:T(8,128)(2,1)} %weigh.2.refs_0_), channel_id=1, source_target_pairs={{0,1},{1,0},{2,3},{3,2},{4,5},{5,4},{6,7},{7,6},{8,9},{9,8},{10,11... | collective-permute-start | bytes 3145736 | tf_op jit(solution)/shard_map/ppermute | solution.py:538
  8.4 4.4 %collective-permute-start.1 = (bf16[64,8192]{1,0:T(8,128)(2,1)}, bf16[64,8192]{1,0:T(8,128)(2,1)}, u32[]{:S(2)}, u32[]{:S(2)}) collective-permute-start(bf16[64,8192]{1,0:T(8,128)(2,1)} %weigh.3.refs_1_), channel_id=1, source_target_pairs={{0,1},{1,0},{2,3},{3,2},{4,5},{5,4},{6,7},{7,6},{8,9},{9,8},{10,11... | collective-permute-start | bytes 3145736 | tf_op jit(solution)/shard_map/ppermute | solution.py:538
  12.8 5.5 %copy-start.3 = (bf16[64,8192]{1,0:T(8,128)(2,1)S(1)}, bf16[64,8192]{1,0:T(8,128)(2,1)}, u32[]{:S(2)}) copy-start(bf16[64,8192]{1,0:T(8,128)(2,1)} %weigh.2.refs_0_) | copy-start | bytes 3145732
  12.8 8.0 %copy-start.4 = (bf16[64,8192]{1,0:T(8,128)(2,1)S(1)}, bf16[64,8192]{1,0:T(8,128)(2,1)}, u32[]{:S(2)}) copy-start(bf16[64,8192]{1,0:T(8,128)(2,1)} %weigh.3.refs_1_) | copy-start | bytes 3145732
  12.8 11.4 %copy-start.12 = (s32[32,1]{0,1:T(1,128)S(1)}, s32[32,1]{0,1:T(1,128)}, u32[]{:S(2)}) copy-start(s32[32,1]{0,1:T(1,128)} %param.9) | copy-start | bytes 388
  12.8 16.9 %copy-start.5 = (bf16[64,8192]{1,0:T(8,128)(2,1)}, bf16[64,8192]{1,0:T(8,128)(2,1)S(1)}, u32[]{:S(2)}) copy-start(bf16[64,8192]{1,0:T(8,128)(2,1)S(1)} %collective-permute-done.refs_2_) | copy-start | bytes 3145732
  12.9 95.1 %all-to-all-start = ((bf16[8,2,8,16384]{3,2,1,0:T(8,128)(2,1)}), bf16[8,2,8,16384]{3,2,1,0:T(8,128)(2,1)}, u32[]{:S(2)}, u32[]{:S(2)}) async-start(bf16[8,2,8,16384]{3,2,1,0:T(8,128)(2,1)} %own_pack.1), calls=%async_computation | async-start | bytes 8388608 | tf_op jit(solution)/shard_map/all_to_all | solution.py:529
  18.3 62.5 %collective-permute-start.2 = (bf16[64,8192]{1,0:T(8,128)(2,1)S(1)}, bf16[64,8192]{1,0:T(8,128)(2,1)}, u32[]{:S(2)}, u32[]{:S(2)}) collective-permute-start(bf16[64,8192]{1,0:T(8,128)(2,1)S(1)} %copy-done.3), channel_id=1, source_target_pairs={{0,8},{1,9},{2,10},{3,11},{4,12},{5,13},{6,14},{7,15},{8,0},{9,1},... | collective-permute-start | bytes 3145736 | tf_op jit(solution)/shard_map/ppermute | solution.py:536
  20.8 60.0 %collective-permute-start.3 = (bf16[64,8192]{1,0:T(8,128)(2,1)S(1)}, bf16[64,8192]{1,0:T(8,128)(2,1)}, u32[]{:S(2)}, u32[]{:S(2)}) collective-permute-start(bf16[64,8192]{1,0:T(8,128)(2,1)S(1)} %copy-done.4), channel_id=1, source_target_pairs={{0,8},{1,9},{2,10},{3,11},{4,12},{5,13},{6,14},{7,15},{8,0},{9,1},... | collective-permute-start | bytes 3145736 | tf_op jit(solution)/shard_map/ppermute | solution.py:536
  20.9 59.9 %collective-permute-start.4 = (bf16[64,8192]{1,0:T(8,128)(2,1)S(1)}, bf16[64,8192]{1,0:T(8,128)(2,1)}, u32[]{:S(2)}, u32[]{:S(2)}) collective-permute-start(bf16[64,8192]{1,0:T(8,128)(2,1)S(1)} %copy-done.3), channel_id=1, source_target_pairs={{8,16},{9,17},{10,18},{11,19},{12,20},{13,21},{14,22},{15,23},{16,... | collective-permute-start | bytes 3145736 | tf_op jit(solution)/shard_map/ppermute | solution.py:537
  22.5 58.3 %collective-permute-start.5 = (bf16[64,8192]{1,0:T(8,128)(2,1)S(1)}, bf16[64,8192]{1,0:T(8,128)(2,1)}, u32[]{:S(2)}, u32[]{:S(2)}) collective-permute-start(bf16[64,8192]{1,0:T(8,128)(2,1)S(1)} %copy-done.4), channel_id=1, source_target_pairs={{8,16},{9,17},{10,18},{11,19},{12,20},{13,21},{14,22},{15,23},{16,... | collective-permute-start | bytes 3145736 | tf_op jit(solution)/shard_map/ppermute | solution.py:537
  24.2 56.6 %collective-permute-start.6 = (s32[32]{0:T(128)S(1)}, s32[32]{0:T(128)S(1)}, u32[]{:S(2)}, u32[]{:S(2)}) collective-permute-start(s32[32]{0:T(128)S(1)} %bitcast.38), channel_id=1, source_target_pairs={{0,16},{1,17},{2,18},{3,19},{4,20},{5,21},{6,22},{7,23},{8,24},{9,... | collective-permute-start | bytes 392 | tf_op jit(solution)/shard_map/ppermute | solution.py:539
  80.8 50.3 %copy-start.13 = (s32[32]{0:T(128)}, s32[32]{0:T(128)S(1)}, u32[]{:S(2)}) copy-start(s32[32]{0:T(128)S(1)} %collective-permute-done.6.pick_ref) | copy-start | bytes 388
  80.8 26.1 %collective-permute-start.7 = (bf16[64,8192]{1,0:T(8,128)(2,1)}, bf16[64,8192]{1,0:T(8,128)(2,1)S(1)}, u32[]{:S(2)}, u32[]{:S(2)}) collective-permute-start(bf16[64,8192]{1,0:T(8,128)(2,1)} %collective-permute-done.4), channel_id=1, source_target_pairs={{8,0},{9,1},{10,2},{11,3},{12,4},{13,5},{14,6},{15,7},{16,24},{17,... | collective-permute-start | bytes 3145736 | tf_op jit(solution)/shard_map/ppermute | solution.py:551
  82.1 24.8 %collective-permute-start.8 = (bf16[64,8192]{1,0:T(8,128)(2,1)}, bf16[64,8192]{1,0:T(8,128)(2,1)S(1)}, u32[]{:S(2)}, u32[]{:S(2)}) collective-permute-start(bf16[64,8192]{1,0:T(8,128)(2,1)} %collective-permute-done.2.refs_0_), channel_id=1, source_target_pairs={{8,16},{9,17},{10,18},{11,19},{12,20},{13,21},{14,22},{15,23},{16,... | collective-permute-start | bytes 3145736 | tf_op jit(solution)/shard_map/ppermute | solution.py:552
  82.9 24.0 %collective-permute-start.11 = (bf16[64,8192]{1,0:T(8,128)(2,1)}, bf16[64,8192]{1,0:T(8,128)(2,1)S(1)}, u32[]{:S(2)}, u32[]{:S(2)}) collective-permute-start(bf16[64,8192]{1,0:T(8,128)(2,1)} %collective-permute-done.2.refs_0_), channel_id=1, source_target_pairs={{0,1},{1,0},{2,3},{3,2},{4,5},{5,4},{6,7},{7,6},{8,9},{9,8},{10,11... | collective-permute-start | bytes 3145736 | tf_op jit(solution)/shard_map/ppermute | solution.py:550
  82.9 25.0 %collective-permute-start.12 = (bf16[64,8192]{1,0:T(8,128)(2,1)}, bf16[64,8192]{1,0:T(8,128)(2,1)S(1)}, u32[]{:S(2)}, u32[]{:S(2)}) collective-permute-start(bf16[64,8192]{1,0:T(8,128)(2,1)} %collective-permute-done.3.refs_1_), channel_id=1, source_target_pairs={{0,1},{1,0},{2,3},{3,2},{4,5},{5,4},{6,7},{7,6},{8,9},{9,8},{10,11... | collective-permute-start | bytes 3145736 | tf_op jit(solution)/shard_map/ppermute | solution.py:550
  83.4 123.2 %collective-permute-start.13 = (bf16[16384,128]{1,0:T(8,128)(2,1)}, bf16[16384,128]{1,0:T(8,128)(2,1)}, u32[]{:S(2)}, u32[]{:S(2)}) collective-permute-start(bf16[16384,128]{1,0:T(8,128)(2,1)} %get-tuple-element.36), channel_id=1, source_target_pairs={{0,1},{1,0},{2,3},{3,2},{4,5},{5,4},{6,7},{7,6},{8,9},{9,8},{10,11... | collective-permute-start | bytes 12582920 | tf_op jit(solution)/shard_map/ppermute | solution.py:546
  106.9 24.2 %copy-start.8 = (bf16[64,8192]{1,0:T(8,128)(2,1)}, bf16[64,8192]{1,0:T(8,128)(2,1)S(1)}, u32[]{:S(2)}) copy-start(bf16[64,8192]{1,0:T(8,128)(2,1)S(1)} %collective-permute-done.7.outer_ref) | copy-start | bytes 3145732
  106.9 1.0 copy-start.9
  107.9 1.0 copy-start.6
  107.9 1.3 copy-start.7
  162.8 43.8 %collective-permute-start.14 = (bf16[16384,128]{1,0:T(8,128)(2,1)}, bf16[16384,128]{1,0:T(8,128)(2,1)}, u32[]{:S(2)}, u32[]{:S(2)}) collective-permute-start(bf16[16384,128]{1,0:T(8,128)(2,1)} %get-tuple-element.37), channel_id=1, source_target_pairs={{0,1},{1,0},{2,3},{3,2},{4,5},{5,4},{6,7},{7,6},{8,9},{9,8},{10,11... | collective-permute-start | bytes 12582920 | tf_op jit(solution)/shard_map/ppermute | solution.py:561
  162.8 39.4 %all-to-all-start.2 = ((bf16[8,2,8,8192]{3,2,1,0:T(8,128)(2,1)}), bf16[8,2,8,8192]{3,2,1,0:T(8,128)(2,1)S(1)}, u32[]{:S(2)}, u32[]{:S(2)}) async-start(bf16[8,2,8,8192]{3,2,1,0:T(8,128)(2,1)} %far_pack.2.refs_5_), calls=%async_computation.2 | async-start | bytes 4194304 | tf_op jit(solution)/shard_map/all_to_all | solution.py:529
  166.8 2.0 collective-permute-start.10
  167.5 30.3 %collective-permute-start.9 = (bf16[64,8192]{1,0:T(8,128)(2,1)}, bf16[64,8192]{1,0:T(8,128)(2,1)S(1)}, u32[]{:S(2)}, u32[]{:S(2)}) collective-permute-start(bf16[64,8192]{1,0:T(8,128)(2,1)} %collective-permute-done.5), channel_id=1, source_target_pairs={{8,0},{9,1},{10,2},{11,3},{12,4},{13,5},{14,6},{15,7},{16,24},{17,... | collective-permute-start | bytes 3145736 | tf_op jit(solution)/shard_map/ppermute | solution.py:555
  168.9 29.0 %copy-start.10 = (bf16[64,8192]{1,0:T(8,128)(2,1)}, bf16[64,8192]{1,0:T(8,128)(2,1)S(1)}, u32[]{:S(2)}) copy-start(bf16[64,8192]{1,0:T(8,128)(2,1)S(1)} %collective-permute-done.10.inner_ref) | copy-start | bytes 3145732
  197.9 1.0 copy-start.11
  202.2 4.4 %copy-start.2 = (bf16[8,2,8,8192]{3,2,1,0:T(8,128)(2,1)}, bf16[8,2,8,8192]{3,2,1,0:T(8,128)(2,1)S(1)}, u32[]{:S(2)}) copy-start(bf16[8,2,8,8192]{3,2,1,0:T(8,128)(2,1)S(1)} %all-to-all-done.2) | copy-start | bytes 6291460
  202.2 31.0 %all-to-all-start.1 = ((bf16[8,2,8,8192]{3,2,1,0:T(8,128)(2,1)}), bf16[8,2,8,8192]{3,2,1,0:T(8,128)(2,1)}, u32[]{:S(2)}, u32[]{:S(2)}) async-start(bf16[8,2,8,8192]{3,2,1,0:T(8,128)(2,1)} %far_pack.3), calls=%async_computation.1 | async-start | bytes 4194304 | tf_op jit(solution)/shard_map/all_to_all | solution.py:529
  233.3 26.1 %copy-start.1 = (s32[4,16384]{1,0:T(4,128)S(1)}, s32[4,16384]{1,0:T(4,128)}, u32[]{:S(2)}) copy-start(s32[4,16384]{1,0:T(4,128)} %param.8) | copy-start | bytes 786436
  244.8 4.9 %collective-permute-start.15 = (f32[64,128]{1,0:T(8,128)}, f32[64,128]{1,0:T(8,128)S(1)}, u32[]{:S(2)}, u32[]{:S(2)}) collective-permute-start(f32[64,128]{1,0:T(8,128)} %get-tuple-element.39), channel_id=1, source_target_pairs={{0,8},{1,9},{2,10},{3,11},{4,12},{5,13},{6,14},{7,15},{8,0},{9,1},... | collective-permute-start | bytes 98312 | tf_op jit(solution)/shard_map/ppermute | solution.py:567
  246.9 11.1 %all-to-all-start.3 = ((f32[32,8,128]{2,1,0:T(8,128)}), f32[32,8,128]{2,1,0:T(8,128)S(1)}, u32[]{:S(2)}, u32[]{:S(2)}) async-start(f32[32,8,128]{2,1,0:T(8,128)} %bitcast.14), calls=%async_computation.3 | async-start | bytes 262144 | tf_op jit(solution)/shard_map/all_to_all | solution.py:576

commit v7 on v6

--- a/solution.py
+++ b/solution.py
@@ -11,15 +11,15 @@
 NOPS = 4
 LANES = 128
 SLAB = 2 * SUB
-VMEM_LIMIT = 56 * 1024 * 1024
+MIB = 1024 * 1024
 PLANES = 4
 PLANE = 8
 UNROLL = 64
 HALVES = 2
 
 
-def params():
-    return pltpu.CompilerParams(vmem_limit_bytes=VMEM_LIMIT)
+def params(mib=56):
+    return pltpu.CompilerParams(vmem_limit_bytes=mib * MIB)
 
 
 def pack_kernel(pick_ref, x_ref, obs_ref, qw_ref, send_ref, w_ref, slabs, sems):
@@ -209,7 +209,7 @@
         out_shape=jax.ShapeDtypeStruct((2 * blk, width // HALVES), jnp.bfloat16),
         in_specs=[spec] * 3,
         out_specs=pl.BlockSpec((2 * blk, depth), lambda i: (0, i)),
-        compiler_params=params(),
+        compiler_params=params(16),
         cost_estimate=pl.CostEstimate(
             flops=blk * width, bytes_accessed=blk * width * 12 // HALVES, transcendentals=0
         ),
@@ -267,16 +267,16 @@
     send_slabs(slabs, pick_ref, send_ref, sems)
 
 
-def pack_call(kernel, name, specs, blk, width, *operands):
+def pack_call(kernel, name, specs, blk, width, weight, *operands):
     return pl.pallas_call(
         kernel,
         out_shape=jax.ShapeDtypeStruct((PLANE, 2, SLAB, width), jnp.bfloat16),
         in_specs=[pl.BlockSpec(memory_space=pltpu.SMEM)] + specs,
         out_specs=pl.BlockSpec(memory_space=pl.ANY),
         scratch_shapes=[pltpu.VMEM((blk // SUB, SLAB, width), jnp.bfloat16), pltpu.SemaphoreType.DMA((PLANE, 2))],
-        compiler_params=params(),
+        compiler_params=params(16),
         cost_estimate=pl.CostEstimate(
-            flops=blk * width * 4, bytes_accessed=(PLANE * 2 * SLAB * 2 + blk * 4) * width, transcendentals=0
+            flops=blk * width * 4, bytes_accessed=weight * (PLANE * 2 * SLAB * 2 + blk * 4) * width, transcendentals=0
         ),
         name=name,
     )(*operands)
@@ -285,39 +285,43 @@
 def own_pack(pick, halves):
     rows, width = halves[0].shape
     specs = [pl.BlockSpec(memory_space=pltpu.VMEM)] * HALVES
-    return pack_call(own_pack_kernel, "own_pack", specs, rows // 2, HALVES * width, pick, *halves)
+    return pack_call(own_pack_kernel, "own_pack", specs, rows // 2, HALVES * width, 1, pick, *halves)
 
 
 def far_pack(pick, outer, inner, after):
     rows, width = outer.shape
     specs = [pl.BlockSpec(memory_space=pltpu.VMEM)] * 2 + [pl.BlockSpec(memory_space=pl.ANY)]
-    return pack_call(far_pack_kernel, "far_pack", specs, rows // 2, width, pick, outer, inner, after)
-
-
-def place_kernel(joined, ops_ref, *refs):
+    return pack_call(far_pack_kernel, "far_pack", specs, rows // 2, width, 60, pick, outer, inner, after)
+
+
+def place_kernel(flips, joined, ops_ref, *refs):
+    count = len(flips)
     blocks, refs = refs[: 2 * HALVES], refs[2 * HALVES :]
-    other_ref, outs, (table, target) = refs[0], refs[2 if joined else 1 : -2], refs[-2:]
+    earlier_ref, refs = refs[0], refs[2 if joined else 1 :]
+    outs, tables, targets = refs[: -2 * count], refs[-2 * count : -count], refs[-count:]
     rows, depth = blocks[0].shape
     blk = rows // 2
-    width = target.shape[0]
+    width = targets[0].shape[0]
     chunks = width // HALVES // depth
     step = min(512, width)
     size = min(256, depth)
 
-    def fill(mine_ref, near_ref):
+    def fill(one_ref, two_ref):
         diagonal = lax.broadcasted_iota(jnp.int32, (size, size), 0) == lax.broadcasted_iota(
             jnp.int32, (size, size), 1
         )
         identity = jnp.where(diagonal, 1.0, 0.0).astype(jnp.bfloat16)
-        for i in range(depth // size):
-            cols = slice(i * size, (i + 1) * size)
-            both = [mine_ref[:blk, cols], near_ref[:blk, cols], mine_ref[blk:, cols], near_ref[blk:, cols]]
-            table[cols, :] = lax.dot_general(
-                identity,
-                jnp.concatenate(both, 0),
-                (((1,), (1,)), ((), ())),
-                preferred_element_type=jnp.float32,
-            )
+        for table, flip in zip(tables, flips):
+            pair = (two_ref, one_ref) if flip else (one_ref, two_ref)
+            for i in range(depth // size):
+                cols = slice(i * size, (i + 1) * size)
+                four = [ref[:blk, cols] for ref in pair] + [ref[blk:, cols] for ref in pair]
+                table[cols, :] = lax.dot_general(
+                    identity,
+                    jnp.concatenate(four, 0),
+                    (((1,), (1,)), ((), ())),
+                    preferred_element_type=jnp.float32,
+                )
 
     for part in range(HALVES):
 
@@ -329,7 +333,8 @@
     def _(i):
         base = pl.multiple_of(i * UNROLL, UNROLL)
         for j in range(UNROLL):
-            target[pl.ds(ops_ref[0, 0, base + j], 1), :] = table[pl.ds(base + j, 1), :]
+            for k, (table, target) in enumerate(zip(tables, targets)):
+                target[pl.ds(ops_ref[k, 0, base + j], 1), :] = table[pl.ds(base + j, 1), :]
 
     @pl.when(pl.program_id(0) == pl.num_programs(0) - 1)
     def _():
@@ -339,20 +344,19 @@
         @pl.loop(0, width // step)
         def _(i):
             here = pl.ds(pl.multiple_of(i * step, step), step)
-            values = target[here, :]
+            values = [target[here, :] for target in targets]
             if joined:
-                earlier = other_ref[here, :].astype(jnp.float32)
-                keep = jnp.where(first, earlier, pltpu.roll(values, blk, 1))
-                give = jnp.where(first, pltpu.roll(earlier, LANES - blk, 1), values)
-                outs[0][here, :] = keep.astype(jnp.bfloat16)
-                outs[1][here, :] = give.astype(jnp.bfloat16)
+                values.insert(0, earlier_ref[here, :].astype(jnp.float32))
+            if len(values) == 2:
+                outs[0][here, :] = jnp.where(first, *values).astype(jnp.bfloat16)
+                outs[1][here, :] = jnp.where(first, *values[::-1]).astype(jnp.bfloat16)
             else:
-                outs[0][here, :] = values.astype(jnp.bfloat16)
-
-
-def place(ops, which, mine, near, earlier, after, weight):
+                outs[0][here, :] = values[0].astype(jnp.bfloat16)
+
+
+def place(ops, first, count, one, two, earlier, after, weight):
     width = ops.shape[2]
-    rows, span = mine[0].shape
+    rows, span = one[0].shape
     depth = min(2048, span)
     chunks = span // depth
     some = [
@@ -362,25 +366,27 @@
     anywhere = pl.BlockSpec(memory_space=pl.ANY)
     whole = pl.BlockSpec((width, LANES), lambda i: (0, 0))
     joined = earlier is not None
-    count = 2 if joined else 1
+    outputs = 2 if joined or count == 2 else 1
+    flips = (True,) if joined else (False, True)[:count]
     outs = pl.pallas_call(
-        functools.partial(place_kernel, joined),
+        functools.partial(place_kernel, flips, joined),
         grid=(HALVES * chunks,),
-        out_shape=(jax.ShapeDtypeStruct((width, LANES), jnp.bfloat16),) * count,
+        out_shape=(jax.ShapeDtypeStruct((width, LANES), jnp.bfloat16),) * outputs,
         in_specs=[
-            pl.BlockSpec((1, 1, depth), lambda i: (which, 0, i), memory_space=pltpu.SMEM),
+            pl.BlockSpec((count, 1, depth), lambda i: (first, 0, i), memory_space=pltpu.SMEM),
             *some,
             *some,
-            whole if joined else anywhere,
-            *([anywhere] if joined else []),
+            *([whole] if joined else []),
+            anywhere,
         ],
-        out_specs=(whole,) * count,
-        scratch_shapes=[pltpu.VMEM((depth, LANES), jnp.float32), pltpu.VMEM((width, LANES), jnp.float32)],
-        compiler_params=params(),
+        out_specs=(whole,) * outputs,
+        scratch_shapes=[pltpu.VMEM((depth, LANES), jnp.float32)] * count
+        + [pltpu.VMEM((width, LANES), jnp.float32)] * count,
+        compiler_params=params(40),
         cost_estimate=pl.CostEstimate(flops=0, bytes_accessed=weight * width * LANES, transcendentals=0),
         name="place",
-    )(ops, *mine, *near, *((earlier, after) if joined else (after,)))
-    return outs if joined else outs[0]
+    )(ops, *one, *two, *((earlier,) if joined else ()), after)
+    return outs if outputs == 2 else outs[0]
 
 
 def ratio(total_w, sum_x, sum_xx, sum_y, sum_xy, sum_yy):
@@ -444,6 +450,7 @@
         tiles = count // SLAB
         top = lax.broadcasted_iota(jnp.int32, (tiles, SLAB, LANES), 1) < SUB
         low = lax.broadcasted_iota(jnp.int32, (count, LANES), 1) < half
+        early = lax.rem(lax.broadcasted_iota(jnp.int32, (count, LANES), 1), half) < half // 2
         me = lax.axis_index("dp")
         results = []
         for t in range(2):
@@ -464,6 +471,7 @@
                     )
                 )
             kept, got = ratios
+            got = jnp.where(early, pltpu.roll(got, LANES - half // 2, 1), pltpu.roll(got, half // 2, 1))
             straight = jnp.where(low, kept, pltpu.roll(got, half, 1))
             crossed = jnp.where(low, got, pltpu.roll(kept, half, 1))
             results.append(jnp.where(lax.rem(me, 2) == 0, straight, crossed))
@@ -502,7 +510,7 @@
         ],
         out_specs=out_specs,
         scratch_shapes=[pltpu.VMEM(total, jnp.float32)] if ended else [],
-        compiler_params=params(),
+        compiler_params=params(32),
         cost_estimate=pl.CostEstimate(
             flops=18 * rows * width * LANES,
             bytes_accessed=width * (4 * rows + 8 * LANES),
@@ -541,8 +549,7 @@
     own_send = own_pack(own_pick, mine)
     own_send, other = lax.optimization_barrier((own_send, other))
     own_got = spread(own_send)
-    placed = place(ops, 0, mine, other, None, own_pick, 4)
-    keep, give = place(ops, 1, mine, other, placed, own_pick, 4)
+    keep, give = place(ops, 0, 2, mine, other, None, own_pick, 4)
     own_moved = [keep, lax.ppermute(give, "dp", swap)]
 
     near, mid, far_pick, keep = lax.optimization_barrier((near, mid, far_pick, keep))
@@ -550,13 +557,13 @@
     near_other = [lax.ppermute(rows, "dp", swap) for rows in near]
     outer_0 = lax.ppermute(mid[0], "dp", outward)
     inner_0 = lax.ppermute(near[0], "dp", middle)
-    placed = place(ops, 0, near, near_other, None, own_got, 32)
+    placed = place(ops, 0, 1, near, near_other, None, own_got, 32)
     outer_0, inner_0, mid_1, near_1 = lax.optimization_barrier((outer_0, inner_0, mid[1], near[1]))
     outer_1 = lax.ppermute(mid_1, "dp", outward)
     inner_1 = lax.ppermute(near_1, "dp", middle)
     far_send_0 = far_pack(far_pick, outer_0, inner_0, placed)
     far_got_0 = spread(far_send_0)
-    keep, give = place(ops, 1, near, near_other, placed, far_send_0, 32)
+    keep, give = place(ops, 1, 1, near, near_other, placed, far_send_0, 32)
     far_send_1 = far_pack(far_pick, outer_1, inner_1, keep)
     moved = own_moved + [keep, lax.ppermute(give, "dp", swap)]
     far_got_1 = spread(far_send_1)

time: 260 us -> 267 us (1.027)
  local copies, waits for them, and re-layouts: 8.47 us -> 31.7 us
  Pallas kernels: 139 us -> 127 us
  waiting for transfers between devices: 76.4 us -> 72.4 us
    unnamed x29 -> x51, local copies, waits for them, and re-layouts: 4.22 us -> 29.7 us
    pallas_call x2, Pallas kernels: 7.33 us -> 0.91 us  [weigh(): pl.pallas_call(weigh_kernel, grid=(count,), out_shape=jax.ShapeDtypeStruc...]
    all_to_all x3, waiting for transfers between devices: 16.6 us -> 13.5 us  [spread(): lax.all_to_all(send, 'dp', split_axis=0, concat_axis=0, axis_index_groups...]
    pallas_call x2, Pallas kernels: 20.7 us -> 18.1 us  [plane_sums(): pl.pallas_call(functools.partial(plane_sums_kernel, begun, ended), grid=(...]
    pallas_call x4 -> x3, Pallas kernels: 100 us -> 99.3 us  [place(): pl.pallas_call(functools.partial(place_kernel, flips, joined), grid=(HALV...]
  transfers between devices with their start and end apart: 20 -> 20, of which waited for: 4 -> 4; matrix products, arithmetic and copies ran while one was open for 1% -> 1% of each run, Pallas kernels for 48% -> 44%
where the time goes in v7:
time: 267 us
  Pallas kernels  127 us (48%)
  waiting for transfers between devices  72.4 us (27%)
  starting transfers between devices  33.8 us (13%)
  local copies, waits for them, and re-layouts  31.7 us (12%)
    pallas_call x3, Pallas kernels, place(): pl.pallas_call(functools.partial(place_kernel, flips, joined), grid=(HALV...  99.3 us
    unnamed x51, local copies, waits for them, and re-layouts  29.7 us
    ppermute x1, waiting for transfers between devices, shards_by_plane(): outer_1 = lax.ppermute(mid_1, 'dp', outward)  28.1 us
    ppermute x1, waiting for transfers between devices, shards_by_plane(): outer_0 = lax.ppermute(mid[0], 'dp', outward)  23.4 us
    pallas_call x2, Pallas kernels, plane_sums(): pl.pallas_call(functools.partial(plane_sums_kernel, begun, ended), grid=(...  18.1 us
    all_to_all x3, starting transfers between devices, spread(): lax.all_to_all(send, 'dp', split_axis=0, concat_axis=0, axis_index_groups...  13.5 us
    all_to_all x3, waiting for transfers between devices, spread(): lax.all_to_all(send, 'dp', split_axis=0, concat_axis=0, axis_index_groups...  13.5 us
    pallas_call x3, Pallas kernels, pack_call(): pl.pallas_call(kernel, out_shape=jax.ShapeDtypeStruct((PLANE, 2, SLAB, wi...  9.16 us
  transfers between devices with their start and end apart: 20, of which 4 were waited for; matrix products, arithmetic and copies ran while one was open for 1% of the time, Pallas kernels for 44%

profile of v7, /device:TPU:0, one launch (start us, length us, event | category | flops | bytes accessed | tf_op | source)
XLA Modules:
  0.0 266.5 jit_solution(1198956609915789143)
XLA Ops:
  0.6 0.0 copy-start
  0.7 1.6 copy-done.12
  2.3 1.2 copy-done.14
  3.5 1.2 copy-done.15
  4.7 0.4 weigh.2.refs_0_
  5.2 0.5 collective-permute-start
  5.7 0.5 weigh.3.refs_1_
  6.2 0.1 collective-permute-start.1
  6.3 1.6 own_pack.1
  8.0 2.0 copy-done.11
  9.9 0.0 collective-permute-done.refs_2_
  9.9 1.0 copy-done.16
  10.9 0.0 collective-permute-done.1.refs_3_
  10.9 1.0 copy-done.18
  11.9 5.2 %all-to-all-start = ((bf16[8,2,8,16384]{3,2,1,0:T(8,128)(2,1)}), bf16[8,2,8,16384]{3,2,1,0:T(8,128)(2,1)}, u32[]{:S(2)}, u32[]{:S(2)}) async-start(bf16[8,2,8,16384]{3,2,1,0:T(8,128)(2,1)} %copy-done.11), calls=%async_computation | async-start | bytes 8388608 | tf_op jit(solution)/shard_map/all_to_all | solution.py:537
  17.1 2.5 collective-permute-start.2
  19.6 0.1 collective-permute-start.3
  19.6 1.7 collective-permute-start.4
  21.3 1.6 collective-permute-start.5
  22.9 5.6 %collective-permute-start.6 = (s32[32]{0:T(128)S(1)}, s32[32]{0:T(128)S(1)}, u32[]{:S(2)}, u32[]{:S(2)}) collective-permute-start(s32[32]{0:T(128)S(1)} %bitcast.29), channel_id=1, source_target_pairs={{0,16},{1,17},{2,18},{3,19},{4,20},{5,21},{6,22},{7,23},{8,24},{9,... | collective-permute-start | bytes 392 | tf_op jit(solution)/shard_map/ppermute | solution.py:547
  28.5 0.1 constant_dynamic-slice_fusion
  28.6 0.1 broadcast_in_dim.10.ops_ref
  28.7 1.2 copy-done.17
  29.9 1.2 copy-done.19
  31.1 54.5 %place.3 = (bf16[16384,128]{1,0:T(8,128)(2,1)S(1)}, bf16[16384,128]{1,0:T(8,128)(2,1)}) custom-call(s32[2,1,16384]{2,1,0:T(1,128)S(1)} %broadcast_in_dim.10.ops_ref, bf16[64,8192]{1,0:T(8,128)(2,1)S(1)} %weigh.2.refs_0_, bf16[64,8192]{1,0:T(8,128)(2,1)S(1)} %weigh.3.refs_1_, bf16[64,8192]{1,0:T(8,128)(2,1)S(1)} %copy-done.17, ...), custom_call_target="tpu_custom_call" | custom-call | bytes 8388608 | tf_op jit(solution)/shard_map/place/pallas_call | solution.py:371
  85.6 2.1 copy-done.8
  87.7 0.0 collective-permute-done.6.pick_ref
  87.7 0.0 collective-permute-done.2.refs_0_
  87.7 1.3 collective-permute-start.7
  89.0 0.7 collective-permute-start.8
  89.7 0.1 collective-permute-start.11
  89.8 0.5 collective-permute-start.12
  90.3 0.1 collective-permute-start.13
  90.4 23.4 %collective-permute-done.7.outer_ref = bf16[64,8192]{1,0:T(8,128)(2,1)S(1)} collective-permute-done((bf16[64,8192]{1,0:T(8,128)(2,1)}, bf16[64,8192]{1,0:T(8,128)(2,1)S(1)}, u32[]{:S(2)}, u32[]{:S(2)}) %collective-permute-start.7) | collective-permute-done | bytes 1048608 | tf_op jit(solution)/shard_map/ppermute | solution.py:558
  113.8 1.0 copy-done.20
  114.8 1.0 copy-done.22
  115.8 19.9 %place.4.after_ref.refs_4_ = bf16[16384,128]{1,0:T(8,128)(2,1)S(1)} custom-call(s32[2,1,16384]{2,1,0:T(1,128)S(1)} %broadcast_in_dim.10.ops_ref, bf16[64,8192]{1,0:T(8,128)(2,1)} %collective-permute-done.2.refs_0_, bf16[64,8192]{1,0:T(8,128)(2,1)S(1)} %collective-permute-done.3.refs_1_, bf16[64,8192]{1,0:T(8,128)(2,1)S(1)} %collective-permute-done.11.refs_2_, ...), custom_call_target="tpu_custom_call" | custom-call | bytes 67108864 | tf_op jit(solution)/shard_map/place/pallas_call | solution.py:371
  135.7 3.8 %far_pack.2.refs_5_ = bf16[8,2,8,8192]{3,2,1,0:T(8,128)(2,1)S(1)} custom-call(s32[32]{0:T(128)S(1)} %collective-permute-done.6.pick_ref, bf16[64,8192]{1,0:T(8,128)(2,1)S(1)} %copy-done.21, bf16[64,8192]{1,0:T(8,128)(2,1)S(1)} %copy-done.23, bf16[16384,128]{1,0:T(8,128)(2,1)S(1)} %place.4.after_ref.refs_4_), custom_call_target="tpu_custom_call" | custom-call | flops 1048576 | bytes 188743680 | tf_op jit(solution)/shard_map/far_pack/pallas_call | solution.py:271
  139.5 25.0 %place.5 = (bf16[16384,128]{1,0:T(8,128)(2,1)S(1)}, bf16[16384,128]{1,0:T(8,128)(2,1)}) custom-call(s32[2,1,16384]{2,1,0:T(1,128)S(1)} %broadcast_in_dim.10.ops_ref, bf16[64,8192]{1,0:T(8,128)(2,1)} %collective-permute-done.2.refs_0_, bf16[64,8192]{1,0:T(8,128)(2,1)S(1)} %collective-permute-done.3.refs_1_, ...), custom_call_target="tpu_custom_call" | custom-call | bytes 67108864 | tf_op jit(solution)/shard_map/place/pallas_call | solution.py:371
  164.5 2.1 copy-done.2
  166.5 4.0 %all-to-all-start.2 = ((bf16[8,2,8,8192]{3,2,1,0:T(8,128)(2,1)}), bf16[8,2,8,8192]{3,2,1,0:T(8,128)(2,1)S(1)}, u32[]{:S(2)}, u32[]{:S(2)}) async-start(bf16[8,2,8,8192]{3,2,1,0:T(8,128)(2,1)} %copy-done.7), calls=%async_computation.2 | async-start | bytes 4194304 | tf_op jit(solution)/shard_map/all_to_all | solution.py:537
  170.5 0.7 collective-permute-start.10
  171.3 1.3 collective-permute-start.9
  172.6 28.1 %collective-permute-done.9.outer_ref = bf16[64,8192]{1,0:T(8,128)(2,1)S(1)} collective-permute-done((bf16[64,8192]{1,0:T(8,128)(2,1)}, bf16[64,8192]{1,0:T(8,128)(2,1)S(1)}, u32[]{:S(2)}, u32[]{:S(2)}) %collective-permute-start.9) | collective-permute-done | bytes 1048608 | tf_op jit(solution)/shard_map/ppermute | solution.py:562
  200.6 2.2 copy-done.3
  202.8 3.8 %far_pack.3 = bf16[8,2,8,8192]{3,2,1,0:T(8,128)(2,1)S(1)} custom-call(s32[32]{0:T(128)S(1)} %collective-permute-done.6.pick_ref, bf16[64,8192]{1,0:T(8,128)(2,1)S(1)} %collective-permute-done.9.outer_ref, bf16[64,8192]{1,0:T(8,128)(2,1)S(1)} %collective-permute-done.10.inner_ref, bf16[16384,128]{1,0:T(8,128)(2,1)S(1)} %copy-done.3), custom_call_target="tpu_custom_call" | custom-call | flops 1048576 | bytes 188743680 | tf_op jit(solution)/shard_map/far_pack/pallas_call | solution.py:271
  206.6 1.3 copy-done.13
  207.9 4.4 %all-to-all-start.1 = ((bf16[8,2,8,8192]{3,2,1,0:T(8,128)(2,1)}), bf16[8,2,8,8192]{3,2,1,0:T(8,128)(2,1)}, u32[]{:S(2)}, u32[]{:S(2)}) async-start(bf16[8,2,8,8192]{3,2,1,0:T(8,128)(2,1)} %copy-done.13), calls=%async_computation.1 | async-start | bytes 4194304 | tf_op jit(solution)/shard_map/all_to_all | solution.py:537
  212.3 2.2 copy-done.4
  214.5 2.2 copy-done.9
  216.7 8.7 %plane_sums.2.refs_4_ = f32[2,192,384]{2,1,0:T(8,128)S(1)} custom-call(bf16[128,16384]{1,0:T(8,128)(2,1)} %bitcast.1.refs_4_.own_ref, bf16[128,8192]{1,0:T(8,128)(2,1)S(1)} %bitcast.25, bf16[16384,128]{1,0:T(8,128)(2,1)S(1)} %copy-done.9, bf16[16384,128]{1,0:T(8,128)(2,1)} %collective-permute-done.13.refs_1_, bf16[16384,128]{1,0:T(8,128)(2,1)S(1)} %copy-done.4, ...), custom_call_target="tpu_custom_call" | custom-call | flops 2415919104 | bytes 12582912 | tf_op jit(solution)/shard_map/plane_sums/pallas_call | solution.py:498
  225.5 13.5 %all-to-all-done.1 = bf16[8,2,8,8192]{3,2,1,0:T(8,128)(2,1)} async-done(((bf16[8,2,8,8192]{3,2,1,0:T(8,128)(2,1)}), bf16[8,2,8,8192]{3,2,1,0:T(8,128)(2,1)}, u32[]{:S(2)}, u32[]{:S(2)}) %all-to-all-start.1) | async-done | bytes 2097184 | tf_op jit(solution)/shard_map/all_to_all | solution.py:537
  238.9 2.2 copy-done.5
  241.1 2.2 copy-done.10
  243.3 9.3 %plane_sums.3 = (f32[64,128]{1,0:T(8,128)S(1)}, f32[2,64,128]{2,1,0:T(8,128)S(1)}) custom-call(bf16[128,16384]{1,0:T(8,128)(2,1)} %bitcast.1.refs_4_.own_ref, bf16[128,8192]{1,0:T(8,128)(2,1)} %bitcast.2.far_ref, bf16[16384,128]{1,0:T(8,128)(2,1)S(1)} %copy-done.10, bf16[16384,128]{1,0:T(8,128)(2,1)} %collective-permute-done.13.refs_1_, ...), custom_call_target="tpu_custom_call" | custom-call | flops 2415919104 | bytes 12582912 | tf_op jit(solution)/shard_map/plane_sums/pallas_call | solution.py:498
  252.7 0.1 collective-permute-start.15
  252.8 0.7 broadcast_in_dim.12
  253.5 3.4 %all-to-all-start.3 = ((f32[32,8,128]{2,1,0:T(8,128)}), f32[32,8,128]{2,1,0:T(8,128)S(1)}, u32[]{:S(2)}, u32[]{:S(2)}) async-start(f32[32,8,128]{2,1,0:T(8,128)} %bitcast.14), calls=%async_computation.3 | async-start | bytes 262144 | tf_op jit(solution)/shard_map/all_to_all | solution.py:583
  256.9 0.7 copy.14
  257.7 7.4 %all-to-all-done.3 = f32[32,8,128]{2,1,0:T(8,128)S(1)} async-done(((f32[32,8,128]{2,1,0:T(8,128)}), f32[32,8,128]{2,1,0:T(8,128)S(1)}, u32[]{:S(2)}, u32[]{:S(2)}) %all-to-all-start.3) | async-done | bytes 131104 | tf_op jit(solution)/shard_map/all_to_all | solution.py:583
  265.1 0.3 reshape.44
  265.4 0.1 fusion
  265.5 0.2 copy.17
  265.6 0.9 copy.18
  (52 shorter events, 0.2 us)
Async XLA Ops:
  0.6 27.9 %copy-start = (s32[4,16384]{1,0:T(4,128)S(1)}, s32[4,16384]{1,0:T(4,128)}, u32[]{:S(2)}) copy-start(s32[4,16384]{1,0:T(4,128)} %param.8) | copy-start | bytes 786436
  0.6 1.6 copy-start.12
  2.3 1.2 copy-start.14
  3.5 1.2 copy-start.15
  4.7 1.6 copy-start.24
  5.2 4.7 %collective-permute-start = (bf16[64,8192]{1,0:T(8,128)(2,1)S(1)}, bf16[64,8192]{1,0:T(8,128)(2,1)S(1)}, u32[]{:S(2)}, u32[]{:S(2)}) collective-permute-start(bf16[64,8192]{1,0:T(8,128)(2,1)S(1)} %weigh.2.refs_0_), channel_id=1, source_target_pairs={{0,1},{1,0},{2,3},{3,2},{4,5},{5,4},{6,7},{7,6},{8,9},{9,8},{10,11... | collective-permute-start | bytes 3145736 | tf_op jit(solution)/shard_map/ppermute | solution.py:546
  6.2 4.7 %collective-permute-start.1 = (bf16[64,8192]{1,0:T(8,128)(2,1)S(1)}, bf16[64,8192]{1,0:T(8,128)(2,1)S(1)}, u32[]{:S(2)}, u32[]{:S(2)}) collective-permute-start(bf16[64,8192]{1,0:T(8,128)(2,1)S(1)} %weigh.3.refs_1_), channel_id=1, source_target_pairs={{0,1},{1,0},{2,3},{3,2},{4,5},{5,4},{6,7},{7,6},{8,9},{9,8},{10,11... | collective-permute-start | bytes 3145736 | tf_op jit(solution)/shard_map/ppermute | solution.py:546
  8.0 2.0 copy-start.11
  9.9 1.0 copy-start.16
  10.9 1.0 copy-start.18
  11.9 103.9 %all-to-all-start = ((bf16[8,2,8,16384]{3,2,1,0:T(8,128)(2,1)}), bf16[8,2,8,16384]{3,2,1,0:T(8,128)(2,1)}, u32[]{:S(2)}, u32[]{:S(2)}) async-start(bf16[8,2,8,16384]{3,2,1,0:T(8,128)(2,1)} %copy-done.11), calls=%async_computation | async-start | bytes 8388608 | tf_op jit(solution)/shard_map/all_to_all | solution.py:537
  17.1 70.6 %collective-permute-start.2 = (bf16[64,8192]{1,0:T(8,128)(2,1)S(1)}, bf16[64,8192]{1,0:T(8,128)(2,1)}, u32[]{:S(2)}, u32[]{:S(2)}) collective-permute-start(bf16[64,8192]{1,0:T(8,128)(2,1)S(1)} %weigh.2.refs_0_), channel_id=1, source_target_pairs={{0,8},{1,9},{2,10},{3,11},{4,12},{5,13},{6,14},{7,15},{8,0},{9,1},... | collective-permute-start | bytes 3145736 | tf_op jit(solution)/shard_map/ppermute | solution.py:544
  19.6 68.1 %collective-permute-start.3 = (bf16[64,8192]{1,0:T(8,128)(2,1)S(1)}, bf16[64,8192]{1,0:T(8,128)(2,1)S(1)}, u32[]{:S(2)}, u32[]{:S(2)}) collective-permute-start(bf16[64,8192]{1,0:T(8,128)(2,1)S(1)} %weigh.3.refs_1_), channel_id=1, source_target_pairs={{0,8},{1,9},{2,10},{3,11},{4,12},{5,13},{6,14},{7,15},{8,0},{9,1},... | collective-permute-start | bytes 3145736 | tf_op jit(solution)/shard_map/ppermute | solution.py:544
  19.6 68.0 %collective-permute-start.4 = (bf16[64,8192]{1,0:T(8,128)(2,1)S(1)}, bf16[64,8192]{1,0:T(8,128)(2,1)}, u32[]{:S(2)}, u32[]{:S(2)}) collective-permute-start(bf16[64,8192]{1,0:T(8,128)(2,1)S(1)} %weigh.2.refs_0_), channel_id=1, source_target_pairs={{8,16},{9,17},{10,18},{11,19},{12,20},{13,21},{14,22},{15,23},{16,... | collective-permute-start | bytes 3145736 | tf_op jit(solution)/shard_map/ppermute | solution.py:545
  21.3 66.4 %collective-permute-start.5 = (bf16[64,8192]{1,0:T(8,128)(2,1)S(1)}, bf16[64,8192]{1,0:T(8,128)(2,1)}, u32[]{:S(2)}, u32[]{:S(2)}) collective-permute-start(bf16[64,8192]{1,0:T(8,128)(2,1)S(1)} %weigh.3.refs_1_), channel_id=1, source_target_pairs={{8,16},{9,17},{10,18},{11,19},{12,20},{13,21},{14,22},{15,23},{16,... | collective-permute-start | bytes 3145736 | tf_op jit(solution)/shard_map/ppermute | solution.py:545
  22.9 64.7 %collective-permute-start.6 = (s32[32]{0:T(128)S(1)}, s32[32]{0:T(128)S(1)}, u32[]{:S(2)}, u32[]{:S(2)}) collective-permute-start(s32[32]{0:T(128)S(1)} %bitcast.29), channel_id=1, source_target_pairs={{0,16},{1,17},{2,18},{3,19},{4,20},{5,21},{6,22},{7,23},{8,24},{9,... | collective-permute-start | bytes 392 | tf_op jit(solution)/shard_map/ppermute | solution.py:547
  28.7 1.2 copy-start.17
  29.9 1.2 copy-start.19
  85.6 2.1 copy-start.8
  87.7 26.1 %collective-permute-start.7 = (bf16[64,8192]{1,0:T(8,128)(2,1)}, bf16[64,8192]{1,0:T(8,128)(2,1)S(1)}, u32[]{:S(2)}, u32[]{:S(2)}) collective-permute-start(bf16[64,8192]{1,0:T(8,128)(2,1)} %collective-permute-done.4), channel_id=1, source_target_pairs={{8,0},{9,1},{10,2},{11,3},{12,4},{13,5},{14,6},{15,7},{16,24},{17,... | collective-permute-start | bytes 3145736 | tf_op jit(solution)/shard_map/ppermute | solution.py:558
  89.0 25.8 %collective-permute-start.8 = (bf16[64,8192]{1,0:T(8,128)(2,1)}, bf16[64,8192]{1,0:T(8,128)(2,1)S(1)}, u32[]{:S(2)}, u32[]{:S(2)}) collective-permute-start(bf16[64,8192]{1,0:T(8,128)(2,1)} %collective-permute-done.2.refs_0_), channel_id=1, source_target_pairs={{8,16},{9,17},{10,18},{11,19},{12,20},{13,21},{14,22},{15,23},{16,... | collective-permute-start | bytes 3145736 | tf_op jit(solution)/shard_map/ppermute | solution.py:559
  89.7 26.0 %collective-permute-start.11 = (bf16[64,8192]{1,0:T(8,128)(2,1)}, bf16[64,8192]{1,0:T(8,128)(2,1)S(1)}, u32[]{:S(2)}, u32[]{:S(2)}) collective-permute-start(bf16[64,8192]{1,0:T(8,128)(2,1)} %collective-permute-done.2.refs_0_), channel_id=1, source_target_pairs={{0,1},{1,0},{2,3},{3,2},{4,5},{5,4},{6,7},{7,6},{8,9},{9,8},{10,11... | collective-permute-start | bytes 3145736 | tf_op jit(solution)/shard_map/ppermute | solution.py:557
  89.8 26.0 %collective-permute-start.12 = (bf16[64,8192]{1,0:T(8,128)(2,1)S(1)}, bf16[64,8192]{1,0:T(8,128)(2,1)S(1)}, u32[]{:S(2)}, u32[]{:S(2)}) collective-permute-start(bf16[64,8192]{1,0:T(8,128)(2,1)S(1)} %collective-permute-done.3.refs_1_), channel_id=1, source_target_pairs={{0,1},{1,0},{2,3},{3,2},{4,5},{5,4},{6,7},{7,6},{8,9},{9,8},{10,11... | collective-permute-start | bytes 3145736 | tf_op jit(solution)/shard_map/ppermute | solution.py:557
  90.3 122.0 %collective-permute-start.13 = (bf16[16384,128]{1,0:T(8,128)(2,1)}, bf16[16384,128]{1,0:T(8,128)(2,1)}, u32[]{:S(2)}, u32[]{:S(2)}) collective-permute-start(bf16[16384,128]{1,0:T(8,128)(2,1)} %get-tuple-element.36), channel_id=1, source_target_pairs={{0,1},{1,0},{2,3},{3,2},{4,5},{5,4},{6,7},{7,6},{8,9},{9,8},{10,11... | collective-permute-start | bytes 12582920 | tf_op jit(solution)/shard_map/ppermute | solution.py:553
  113.8 1.0 copy-start.20
  114.8 1.0 copy-start.22
  115.8 19.9 %copy-start.21 = (bf16[64,8192]{1,0:T(8,128)(2,1)S(1)}, bf16[64,8192]{1,0:T(8,128)(2,1)}, u32[]{:S(2)}) copy-start(bf16[64,8192]{1,0:T(8,128)(2,1)} %copy-done.20) | copy-start | bytes 3145732
  115.8 19.9 %copy-start.23 = (bf16[64,8192]{1,0:T(8,128)(2,1)S(1)}, bf16[64,8192]{1,0:T(8,128)(2,1)}, u32[]{:S(2)}) copy-start(bf16[64,8192]{1,0:T(8,128)(2,1)} %copy-done.22) | copy-start | bytes 3145732
  135.7 3.8 %copy-start.6 = (bf16[16384,128]{1,0:T(8,128)(2,1)}, bf16[16384,128]{1,0:T(8,128)(2,1)S(1)}, u32[]{:S(2)}) copy-start(bf16[16384,128]{1,0:T(8,128)(2,1)S(1)} %place.4.after_ref.refs_4_) | copy-start | bytes 12582916
  139.5 25.0 %copy-start.7 = (bf16[8,2,8,8192]{3,2,1,0:T(8,128)(2,1)}, bf16[8,2,8,8192]{3,2,1,0:T(8,128)(2,1)S(1)}, u32[]{:S(2)}) copy-start(bf16[8,2,8,8192]{3,2,1,0:T(8,128)(2,1)S(1)} %far_pack.2.refs_5_) | copy-start | bytes 6291460
  164.5 2.1 copy-start.2
  166.5 45.8 %collective-permute-start.14 = (bf16[16384,128]{1,0:T(8,128)(2,1)}, bf16[16384,128]{1,0:T(8,128)(2,1)}, u32[]{:S(2)}, u32[]{:S(2)}) collective-permute-start(bf16[16384,128]{1,0:T(8,128)(2,1)} %get-tuple-element.37), channel_id=1, source_target_pairs={{0,1},{1,0},{2,3},{3,2},{4,5},{5,4},{6,7},{7,6},{8,9},{9,8},{10,11... | collective-permute-start | bytes 12582920 | tf_op jit(solution)/shard_map/ppermute | solution.py:568
  166.5 41.4 %all-to-all-start.2 = ((bf16[8,2,8,8192]{3,2,1,0:T(8,128)(2,1)}), bf16[8,2,8,8192]{3,2,1,0:T(8,128)(2,1)S(1)}, u32[]{:S(2)}, u32[]{:S(2)}) async-start(bf16[8,2,8,8192]{3,2,1,0:T(8,128)(2,1)} %copy-done.7), calls=%async_computation.2 | async-start | bytes 4194304 | tf_op jit(solution)/shard_map/all_to_all | solution.py:537
  170.5 2.0 collective-permute-start.10
  171.3 29.4 %collective-permute-start.9 = (bf16[64,8192]{1,0:T(8,128)(2,1)}, bf16[64,8192]{1,0:T(8,128)(2,1)S(1)}, u32[]{:S(2)}, u32[]{:S(2)}) collective-permute-start(bf16[64,8192]{1,0:T(8,128)(2,1)} %collective-permute-done.5), channel_id=1, source_target_pairs={{8,0},{9,1},{10,2},{11,3},{12,4},{13,5},{14,6},{15,7},{16,24},{17,... | collective-permute-start | bytes 3145736 | tf_op jit(solution)/shard_map/ppermute | solution.py:562
  200.6 2.2 copy-start.3
  206.6 1.3 copy-start.13
  207.9 31.0 %all-to-all-start.1 = ((bf16[8,2,8,8192]{3,2,1,0:T(8,128)(2,1)}), bf16[8,2,8,8192]{3,2,1,0:T(8,128)(2,1)}, u32[]{:S(2)}, u32[]{:S(2)}) async-start(bf16[8,2,8,8192]{3,2,1,0:T(8,128)(2,1)} %copy-done.13), calls=%async_computation.1 | async-start | bytes 4194304 | tf_op jit(solution)/shard_map/all_to_all | solution.py:537
  212.3 2.2 copy-start.4
  214.5 2.2 copy-start.9
  238.9 2.2 copy-start.5
  241.1 2.2 copy-start.10
  243.3 23.2 %copy-start.1 = (s32[4,16384]{1,0:T(4,128)S(1)}, s32[4,16384]{1,0:T(4,128)}, u32[]{:S(2)}) copy-start(s32[4,16384]{1,0:T(4,128)} %param.8) | copy-start | bytes 786436
  252.7 4.2 %collective-permute-start.15 = (f32[64,128]{1,0:T(8,128)S(1)}, f32[64,128]{1,0:T(8,128)S(1)}, u32[]{:S(2)}, u32[]{:S(2)}) collective-permute-start(f32[64,128]{1,0:T(8,128)S(1)} %get-tuple-element.39), channel_id=1, source_target_pairs={{0,8},{1,9},{2,10},{3,11},{4,12},{5,13},{6,14},{7,15},{8,0},{9,1},... | collective-permute-start | bytes 98312 | tf_op jit(solution)/shard_map/ppermute | solution.py:574
  253.5 11.6 %all-to-all-start.3 = ((f32[32,8,128]{2,1,0:T(8,128)}), f32[32,8,128]{2,1,0:T(8,128)S(1)}, u32[]{:S(2)}, u32[]{:S(2)}) async-start(f32[32,8,128]{2,1,0:T(8,128)} %bitcast.14), calls=%async_computation.3 | async-start | bytes 262144 | tf_op jit(solution)/shard_map/all_to_all | solution.py:583

commit v8 on v5

--- a/solution.py
+++ b/solution.py
@@ -15,6 +15,7 @@
 PLANES = 4
 PLANE = 8
 UNROLL = 64
+BATCH = 16
 HALVES = 2
 
 
@@ -217,63 +218,62 @@
     )(x, observed, qweights)
 
 
-def fill_slabs(slabs, xw_ref, offset):
+def fill_slabs(slabs, xw_ref):
     blk, width = xw_ref.shape[0] // 2, xw_ref.shape[1]
     step = min(512, width)
 
     @pl.loop(0, width // step)
     def _(i):
-        start = pl.multiple_of(i * step, step)
-        wide = xw_ref[:, pl.ds(start, step)].astype(jnp.float32)
+        cols = pl.ds(pl.multiple_of(i * step, step), step)
+        wide = xw_ref[:, cols].astype(jnp.float32)
         for g in range(blk // SUB):
             rows = slice(g * SUB, (g + 1) * SUB)
             slab = jnp.concatenate([wide[:blk][rows], wide[blk:][rows]], 0)
-            slabs[g, :, pl.ds(offset + start, step)] = slab.astype(jnp.bfloat16)
-
-
-def send_slabs(slabs, pick_ref, send_ref, sems):
+            slabs[g, :, cols] = slab.astype(jnp.bfloat16)
+
+
+def send_slabs(slabs, pick_ref, send_ref, source, sems):
     mine = lax.div(lax.axis_index("dp"), PLANE)
     partner = mine + 1 - 2 * lax.rem(mine, 2)
     copies = []
     for c in range(PLANE):
         for t, plane in enumerate((mine, partner)):
             group = pick_ref[plane * PLANE + c]
-            copies.append(pltpu.make_async_copy(slabs.at[group], send_ref.at[c, t], sems.at[c, t]))
+            copies.append(pltpu.make_async_copy(slabs.at[group], send_ref.at[c, source, t], sems.at[c, t]))
     for copy in copies:
         copy.start()
     for copy in copies:
         copy.wait()
 
 
-def own_pack_kernel(pick_ref, *refs):
-    halves, (send_ref, slabs, sems) = refs[:HALVES], refs[HALVES:]
-    for part, ref in enumerate(halves):
-        fill_slabs(slabs, ref, part * ref.shape[1])
-    send_slabs(slabs, pick_ref, send_ref, sems)
-
-
-def far_pack_kernel(pick_ref, outer_ref, inner_ref, after_ref, send_ref, slabs, sems):
+def own_pack_kernel(pick_ref, mine_ref, send_ref, slabs, sems):
+    fill_slabs(slabs, mine_ref)
+    send_slabs(slabs, pick_ref, send_ref, 0, sems)
+
+
+def far_pack_kernel(pick_ref, outer_ref, inner_ref, own_ref, after_ref, send_ref, slabs, sems):
     plane = lax.div(lax.axis_index("dp"), PLANE)
     inner = (plane == 1) | (plane == 2)
 
     @pl.when(inner)
     def _():
-        fill_slabs(slabs, inner_ref, 0)
+        fill_slabs(slabs, inner_ref)
 
     @pl.when(jnp.logical_not(inner))
     def _():
-        fill_slabs(slabs, outer_ref, 0)
-
-    send_slabs(slabs, pick_ref, send_ref, sems)
-
-
-def pack_call(kernel, name, specs, blk, width, *operands):
+        fill_slabs(slabs, outer_ref)
+
+    send_slabs(slabs, pick_ref, send_ref, 1, sems)
+
+
+def pack_call(kernel, name, specs, aliases, blk, width, *operands):
     return pl.pallas_call(
         kernel,
-        out_shape=jax.ShapeDtypeStruct((PLANE, 2, SLAB, width), jnp.bfloat16),
+        out_shape=jax.ShapeDtypeStruct((PLANE, 2, 2, SLAB, width), jnp.bfloat16),
         in_specs=[pl.BlockSpec(memory_space=pltpu.SMEM)] + specs,
         out_specs=pl.BlockSpec(memory_space=pl.ANY),
         scratch_shapes=[pltpu.VMEM((blk // SUB, SLAB, width), jnp.bfloat16), pltpu.SemaphoreType.DMA((PLANE, 2))],
+        input_output_aliases=aliases,
         compiler_params=params(),
         cost_estimate=pl.CostEstimate(
             flops=blk * width * 4, bytes_accessed=(PLANE * 2 * SLAB * 2 + blk * 4) * width, transcendentals=0
@@ -282,16 +282,15 @@
     )(*operands)
 
 
-def own_pack(pick, halves):
-    rows, width = halves[0].shape
-    specs = [pl.BlockSpec(memory_space=pltpu.VMEM)] * HALVES
-    return pack_call(own_pack_kernel, "own_pack", specs, rows // 2, HALVES * width, pick, *halves)
-
-
-def far_pack(pick, outer, inner, after):
+def own_pack(pick, mine):
+    rows, width = mine.shape
+    return pack_call(own_pack_kernel, "own_pack", [pl.BlockSpec(memory_space=pltpu.VMEM)], {}, rows // 2, width, pick, mine)
+
+
+def far_pack(pick, outer, inner, send, after):
     rows, width = outer.shape
-    specs = [pl.BlockSpec(memory_space=pltpu.VMEM)] * 2 + [pl.BlockSpec(memory_space=pl.ANY)]
-    return pack_call(far_pack_kernel, "far_pack", specs, rows // 2, width, pick, outer, inner, after)
+    specs = [pl.BlockSpec(memory_space=pltpu.VMEM)] * 2 + [pl.BlockSpec(memory_space=pl.ANY)] * 2
+    return pack_call(far_pack_kernel, "far_pack", specs, {3: 0}, rows // 2, width, pick, outer, inner, send, after)
 
 
 def place_kernel(begun, ops_ref, mine_ref, near_ref, before_ref, after_ref, moved_ref, table, target):
@@ -300,8 +299,6 @@
     width = target.shape[0]
     step = min(512, width)
     part = pl.multiple_of(pl.program_id(1) * depth, depth)
-    table_rows = table.reshape(table.shape[0], 1, LANES)
-    target_rows = target.reshape(width, 1, LANES)
 
     @pl.when(pl.program_id(0) == 0)
     def _():
@@ -333,8 +330,12 @@
     def _(i):
         base = pl.multiple_of(i * UNROLL, UNROLL)
         row = pl.multiple_of(part + base, UNROLL)
-        for j in range(UNROLL):
-            target_rows[ops_ref[0, 0, base + j]] = table_rows[row + j]
+        for start in range(0, UNROLL, BATCH):
+            span = range(start, start + BATCH)
+            places = [ops_ref[0, 0, base + j] for j in span]
+            values = [table[pl.ds(row + j, 1), :] for j in span]
+            for to, value in zip(places, values):
+                target[pl.ds(to, 1), :] = value
 
     @pl.when(pl.program_id(1) == pl.num_programs(1) - 1)
     def _():
@@ -380,8 +381,8 @@
     return numer / jnp.sqrt(var_x * var_y)
 
 
-def plane_sums_kernel(begun, ended, own_ref, far_ref, first_ref, second_ref, before_ref, out_ref, *scratch):
-    rows, depth = own_ref.shape
+def plane_sums_kernel(begun, ended, got_ref, first_ref, second_ref, before_ref, out_ref, *scratch):
+    rows, depth = got_ref.shape[0] // 2, got_ref.shape[1]
     step = min(1024, depth)
     half = LANES // 2
     slabs = rows // SLAB
@@ -398,18 +399,15 @@
 
     for i in range(depth // step):
         cols = slice(i * step, (i + 1) * step)
-        is_x = lax.broadcasted_iota(jnp.int32, (slabs, SLAB, step), 1) < SUB
-        weights, products = [], []
-        for ref in (own_ref, far_ref):
-            wide = ref[:, cols].astype(jnp.float32).reshape(slabs, SLAB, step)
-            rolled = pltpu.roll(wide, SUB, 1)
-            product = wide * rolled
-            both = jnp.where(is_x, product * wide, product)
-            products.append(both.reshape(rows, step).astype(jnp.bfloat16))
-            mine = rolled.reshape(slabs // 2, 2, SLAB, step)[:, 0]
-            partner = wide.reshape(slabs // 2, 2, SLAB, step)[:, 1]
-            pair = jnp.where(is_x[: slabs // 2], mine, partner)
-            weights.append(pair.reshape(rows // 2, step).astype(jnp.bfloat16))
+        is_x = lax.broadcasted_iota(jnp.int32, (2 * slabs, SLAB, step), 1) < SUB
+        wide = got_ref[:, cols].astype(jnp.float32).reshape(2 * slabs, SLAB, step)
+        rolled = pltpu.roll(wide, SUB, 1)
+        product = wide * rolled
+        both = jnp.where(is_x, product * wide, product)
+        products = both.reshape(2 * rows, step).astype(jnp.bfloat16)
+        mine = rolled.reshape(slabs, 2, SLAB, step)[:, 0]
+        partner = wide.reshape(slabs, 2, SLAB, step)[:, 1]
+        weights = jnp.where(is_x[:slabs], mine, partner).reshape(rows, step).astype(jnp.bfloat16)
         low = lax.broadcasted_iota(jnp.int32, (step, LANES), 1) < half
         linear, square = [], []
         for ref in (first_ref, second_ref):
@@ -424,7 +422,7 @@
                 else:
                     odd = product * swapped
             square.append(jnp.where(low, even, odd).astype(jnp.bfloat16))
-        left = jnp.concatenate(weights + products, 0)
+        left = jnp.concatenate([weights, products], 0)
         right = jnp.concatenate(linear + square, 1)
         acc[...] += jnp.dot(left, right, preferred_element_type=jnp.float32)
 
@@ -459,8 +457,8 @@
         out_ref[...] = result
 
 
-def plane_sums(part, own, far, first, second, before):
-    rows, width = far.shape
+def plane_sums(part, got, first, second, before):
+    rows, width = got.shape[0] // 2, got.shape[1]
     depth = min(4096, width)
     chunks = width // depth
     lanes = (NOPS + NOPS // 2) * LANES
@@ -473,8 +471,7 @@
         grid=(chunks,),
         out_shape=jax.ShapeDtypeStruct(shape, jnp.float32),
         in_specs=[
-            pl.BlockSpec((rows, depth), lambda i: (0, part * chunks + i)),
-            pl.BlockSpec((rows, depth), lambda i: (0, i)),
+            pl.BlockSpec((2 * rows, depth), lambda i: (0, i)),
             moved,
             moved,
             pl.BlockSpec(total, lambda i: (0, 0)) if begun else pl.BlockSpec(memory_space=pl.ANY),
@@ -488,7 +485,7 @@
             transcendentals=0,
         ),
         name="plane_sums",
-    )(own, far, first, second, before if begun else far)
+    )(got, first, second, before if begun else got)
 
 
 def shards_by_plane(intensities, observed, qweights, ops, pick):
@@ -504,7 +501,7 @@
 
     def spread(send):
         got = lax.all_to_all(send, "dp", split_axis=0, concat_axis=0, axis_index_groups=rings, tiled=True)
-        return got.reshape(PLANE * 2 * SLAB, send.shape[-1])
+        return got.reshape(4 * PLANE * SLAB, send.shape[-1])
 
     own_pick = pick[:, 0]
     ops = ops[:, None, :]
@@ -513,26 +510,26 @@
     mid_0 = lax.ppermute(mine_0, "dp", middle)
     far_pick = lax.ppermute(own_pick, "dp", far)
     mine_1 = weigh(intensities, observed, qweights, 1)
-    own_send = own_pack(own_pick, (mine_0, mine_1))
-    near_0, mid_0, far_pick, later_1, own_send = lax.optimization_barrier((near_0, mid_0, far_pick, mine_1, own_send))
-    own_got = spread(own_send)
+    own_send_0 = own_pack(own_pick, mine_0)
+    own_send_1 = own_pack(own_pick, mine_1)
+    near_0, mid_0, far_pick, later_1 = lax.optimization_barrier((near_0, mid_0, far_pick, mine_1))
     near_1 = lax.ppermute(later_1, "dp", near)
     mid_1 = lax.ppermute(later_1, "dp", middle)
     outer_0 = lax.ppermute(mid_0, "dp", outward)
     inner_0 = lax.ppermute(near_0, "dp", middle)
-    moved_0 = place(ops, 0, NOPS, 0, mine_0, near_0, None, own_pick)
+    moved_0 = place(ops, 0, NOPS, 0, mine_0, near_0, None, own_send_1)
     near_1, mid_1, outer_0, inner_0 = lax.optimization_barrier((near_1, mid_1, outer_0, inner_0))
     outer_1 = lax.ppermute(mid_1, "dp", outward)
     inner_1 = lax.ppermute(near_1, "dp", middle)
-    far_send_0 = far_pack(far_pick, outer_0, inner_0, moved_0)
-    far_got_0 = spread(far_send_0)
-    first = place(ops, 0, NOPS // 2, 1, mine_1, near_1, moved_0, far_send_0)
-    far_send_1 = far_pack(far_pick, outer_1, inner_1, first)
-    far_got_1 = spread(far_send_1)
-    second = place(ops, NOPS // 2, NOPS // 2, 1, mine_1, near_1, moved_0, far_send_1)
-    sums_0 = plane_sums(0, own_got, far_got_0, first, second, None)
-    stats = plane_sums(1, own_got, far_got_1, first, second, sums_0)
-    stats = stats.reshape(2, PLANE, 2, SUB, NOPS * blk)
+    send_0 = far_pack(far_pick, outer_0, inner_0, own_send_0, moved_0)
+    got_0 = spread(send_0)
+    first = place(ops, 0, NOPS // 2, 1, mine_1, near_1, moved_0, send_0)
+    send_1 = far_pack(far_pick, outer_1, inner_1, own_send_1, first)
+    got_1 = spread(send_1)
+    second = place(ops, NOPS // 2, NOPS // 2, 1, mine_1, near_1, moved_0, send_1)
+    sums_0 = plane_sums(0, got_0, first, second, None)
+    stats = plane_sums(1, got_1, first, second, sums_0)
+    stats = jnp.transpose(stats.reshape(PLANE, 2, 2, SUB, NOPS * blk), (1, 0, 2, 3, 4))
     mine, other = stats[:, :, 0], stats[:, :, 1]
 
     from_near = lax.ppermute(other, "dp", near)

time: 244 us -> 228 us (0.934)
  blocking collectives: 30.9 us -> 0 us
  waiting for transfers between devices: 45.8 us -> 58.7 us
    all_to_all x1 -> x0, blocking collectives: 30.9 us -> none  [spread(): lax.all_to_all(send, 'dp', split_axis=0, concat_axis=0, axis_index_groups...]
    all_to_all x2, waiting for transfers between devices: 12 us -> 25 us  [spread(): lax.all_to_all(send, 'dp', split_axis=0, concat_axis=0, axis_index_groups...]
    all_to_all x1, waiting for transfers between devices: 7.42 us -> 2.72 us  [shards_by_plane(): back = lax.all_to_all(back, 'dp', split_axis=0, concat_axis=0, tiled=True)]
    ppermute x1, waiting for transfers between devices: 14.9 us -> 19.4 us  [shards_by_plane(): far_pick = lax.ppermute(own_pick, 'dp', far)]
    ppermute x1, waiting for transfers between devices: 4.35 us -> 0.01 us  [shards_by_plane(): outer_0 = lax.ppermute(mid_0, 'dp', outward)]
    ppermute x1, waiting for transfers between devices: 0.01 us -> 2.91 us  [shards_by_plane(): from_near = lax.ppermute(other, 'dp', near)]
    ppermute x1, starting transfers between devices: 4.63 us -> 1.84 us  [shards_by_plane(): from_near = lax.ppermute(other, 'dp', near)]
    all_to_all x1, starting transfers between devices: 4.74 us -> 7.53 us  [shards_by_plane(): back = lax.all_to_all(back, 'dp', split_axis=0, concat_axis=0, tiled=True)]
  transfers between devices with their start and end apart: 13 -> 13, of which waited for: 5 -> 6; matrix products, arithmetic and copies ran while one was open for 1% -> 1% of each run, Pallas kernels for 44% -> 48%
where the time goes in v8:
time: 228 us
  Pallas kernels  128 us (56%)
  waiting for transfers between devices  58.7 us (26%)
  starting transfers between devices  31.6 us (14%)
  local copies, waits for them, and re-layouts  8.47 us (4%)
    pallas_call x3, Pallas kernels, place(): pl.pallas_call(functools.partial(place_kernel, begun), grid=(count, chunk...  83.9 us
    all_to_all x2, waiting for transfers between devices, spread(): lax.all_to_all(send, 'dp', split_axis=0, concat_axis=0, axis_index_groups...  25 us
    pallas_call x2, Pallas kernels, plane_sums(): pl.pallas_call(functools.partial(plane_sums_kernel, begun, ended), grid=(...  23.7 us
    ppermute x1, waiting for transfers between devices, shards_by_plane(): far_pick = lax.ppermute(own_pick, 'dp', far)  19.4 us
    pallas_call x4, Pallas kernels, pack_call(): pl.pallas_call(kernel, out_shape=jax.ShapeDtypeStruct((PLANE, 2, 2, SLAB,...  12.8 us
    all_to_all x2, starting transfers between devices, spread(): lax.all_to_all(send, 'dp', split_axis=0, concat_axis=0, axis_index_groups...  9.28 us
    ppermute x1, waiting for transfers between devices, shards_by_plane(): outer_1 = lax.ppermute(mid_1, 'dp', outward)  8.74 us
    all_to_all x1, starting transfers between devices, shards_by_plane(): back = lax.all_to_all(back, 'dp', split_axis=0, concat_axis=0, tiled=True)  7.53 us
  transfers between devices with their start and end apart: 13, of which 6 were waited for; matrix products, arithmetic and copies ran while one was open for 1% of the time, Pallas kernels for 48%

profile of v8, /device:TPU:0, one launch (start us, length us, event | category | flops | bytes accessed | tf_op | source)
XLA Modules:
  0.0 227.5 jit_solution(17801992118072798603)
XLA Ops:
  0.6 0.0 copy-start.8
  0.6 0.0 copy-start.6
  0.7 3.7 %weigh.2.mine_ref = bf16[64,8192]{1,0:T(8,128)(2,1)} custom-call(bf16[32,16384]{1,0:T(8,128)(2,1)} %x_ref.3, s32[32,16384]{1,0:T(8,128)} %obs_ref.3, bf16[32,16384]{1,0:T(8,128)(2,1)} %qw_ref.3), custom_call_target="tpu_custom_call" | custom-call | flops 524288 | bytes 3145728 | tf_op jit(solution)/shard_map/weigh/pallas_call | solution.py:207
  4.4 3.0 %collective-permute-start = (bf16[64,8192]{1,0:T(8,128)(2,1)}, bf16[64,8192]{1,0:T(8,128)(2,1)S(1)}, u32[]{:S(2)}, u32[]{:S(2)}) collective-permute-start(bf16[64,8192]{1,0:T(8,128)(2,1)} %weigh.2.mine_ref), channel_id=1, source_target_pairs={{0,8},{1,9},{2,10},{3,11},{4,12},{5,13},{6,14},{7,15},{8,0},{9,1},... | collective-permute-start | bytes 3145736 | tf_op jit(solution)/shard_map/ppermute | solution.py:509
  7.4 0.7 collective-permute-start.1
  8.1 0.0 copy-done.8
  8.1 3.8 %collective-permute-start.2 = (s32[32]{0:T(128)S(1)}, s32[32]{0:T(128)S(1)}, u32[]{:S(2)}, u32[]{:S(2)}) collective-permute-start(s32[32]{0:T(128)S(1)} %bitcast.38), channel_id=1, source_target_pairs={{0,16},{1,17},{2,18},{3,19},{4,20},{5,21},{6,22},{7,23},{8,24},{9,... | collective-permute-start | bytes 392 | tf_op jit(solution)/shard_map/ppermute | solution.py:511
  12.0 3.6 %weigh.3.mine_ref = bf16[64,8192]{1,0:T(8,128)(2,1)} custom-call(bf16[32,16384]{1,0:T(8,128)(2,1)} %x_ref.3, s32[32,16384]{1,0:T(8,128)} %obs_ref.3, bf16[32,16384]{1,0:T(8,128)(2,1)} %qw_ref.3), custom_call_target="tpu_custom_call" | custom-call | flops 524288 | bytes 3145728 | tf_op jit(solution)/shard_map/weigh/pallas_call | solution.py:207
  15.6 19.4 %collective-permute-done.2.pick_ref = s32[32]{0:T(128)S(1)} collective-permute-done((s32[32]{0:T(128)S(1)}, s32[32]{0:T(128)S(1)}, u32[]{:S(2)}, u32[]{:S(2)}) %collective-permute-start.2) | collective-permute-done | bytes 160 | tf_op jit(solution)/shard_map/ppermute | solution.py:511
  35.0 0.0 copy-start.7
  35.0 0.0 collective-permute-done.near_ref
  35.0 0.0 copy-start.3
  35.0 0.0 collective-permute-done.1
  35.0 0.6 collective-permute-start.3
  35.5 0.7 collective-permute-start.4
  36.3 0.7 collective-permute-start.6
  37.0 1.3 collective-permute-start.5
  38.3 0.0 copy-done.6
  38.3 0.9 broadcast_in_dim.10.ops_ref
  39.2 3.1 %own_pack.2.before_ref.after_ref.own_ref = bf16[8,2,2,8,8192]{4,3,2,1,0:T(8,128)(2,1)} custom-call(s32[32]{0:T(128)} %bitcast.36, bf16[64,8192]{1,0:T(8,128)(2,1)} %weigh.3.mine_ref), custom_call_target="tpu_custom_call" | custom-call | flops 1048576 | bytes 3145728 | tf_op jit(solution)/shard_map/own_pack/pallas_call | solution.py:270
  42.3 3.0 %own_pack.3.own_ref = bf16[8,2,2,8,8192]{4,3,2,1,0:T(8,128)(2,1)} custom-call(s32[32]{0:T(128)} %bitcast.37, bf16[64,8192]{1,0:T(8,128)(2,1)} %weigh.2.mine_ref), custom_call_target="tpu_custom_call" | custom-call | flops 1048576 | bytes 3145728 | tf_op jit(solution)/shard_map/own_pack/pallas_call | solution.py:270
  45.3 0.0 copy-done.7
  45.3 0.0 copy-done.3
  45.4 37.2 %place.3.after_ref.before_ref = bf16[16384,512]{1,0:T(8,128)(2,1)} custom-call(s32[4,1,16384]{2,1,0:T(1,128)} %broadcast_in_dim.10.ops_ref, bf16[64,8192]{1,0:T(8,128)(2,1)} %weigh.2.mine_ref, bf16[64,8192]{1,0:T(8,128)(2,1)} %copy-done.3, bf16[8,2,2,8,8192]{4,3,2,1,0:T(8,128)(2,1)} %own_pack.2.before_ref.after_ref.own_ref, ...), custom_call_target="tpu_custom_call" | custom-call | bytes 268435456 | tf_op jit(solution)/shard_map/place/pallas_call | solution.py:356
  82.6 0.0 collective-permute-done.3.near_ref
  82.6 0.0 copy-start
  82.6 0.0 collective-permute-done.4
  82.6 0.0 collective-permute-done.6.inner_ref
  82.6 0.0 copy-start.1
  82.6 0.0 collective-permute-done.5.outer_ref
  82.6 1.0 copy-done.1
  83.6 0.0 copy-start.2
  83.6 1.0 copy-done.2
  84.7 3.3 %far_pack.2.after_ref = bf16[8,2,2,8,8192]{4,3,2,1,0:T(8,128)(2,1)} custom-call(s32[32]{0:T(128)} %copy-done.7, bf16[64,8192]{1,0:T(8,128)(2,1)} %copy-done.2, bf16[64,8192]{1,0:T(8,128)(2,1)} %copy-done.1, bf16[8,2,2,8,8192]{4,3,2,1,0:T(8,128)(2,1)} %own_pack.3.own_ref, bf16[16384,512]{1,0:T(8,128)(2,1)} %place.3.after_ref.before_ref), custom_call_target="tpu_custom_call", output_to_operand_aliasing={{}: (3, {})} | custom-call | flops 1048576 | bytes 3145728 | tf_op jit(solution)/shard_map/far_pack/pallas_call | solution.py:270
  88.0 4.6 %all-to-all-start.1 = ((bf16[8,2,2,8,8192]{4,3,2,1,0:T(8,128)(2,1)}), bf16[8,2,2,8,8192]{4,3,2,1,0:T(8,128)(2,1)}, u32[]{:S(2)}, u32[]{:S(2)}) async-start(bf16[8,2,2,8,8192]{4,3,2,1,0:T(8,128)(2,1)} %far_pack.2.after_ref), calls=%async_computation.1 | async-start | bytes 8388608 | tf_op jit(solution)/shard_map/all_to_all | solution.py:503
  92.6 0.0 copy-done
  92.6 0.7 collective-permute-start.8
  93.3 1.3 collective-permute-start.7
  94.6 23.5 %place.4.after_ref.first_ref = bf16[16384,256]{1,0:T(8,128)(2,1)} custom-call(s32[4,1,16384]{2,1,0:T(1,128)} %broadcast_in_dim.10.ops_ref, bf16[64,8192]{1,0:T(8,128)(2,1)} %weigh.3.mine_ref, bf16[64,8192]{1,0:T(8,128)(2,1)} %copy-done, bf16[16384,512]{1,0:T(8,128)(2,1)} %place.3.after_ref.before_ref, bf16[8,2,2,8,8192]{4,3,2,1,0:T(8,128)(2,1)} %far_pack.2.after_ref), custom_call_target="tpu_custom_call" | custom-call | bytes 134217728 | tf_op jit(solution)/shard_map/place/pallas_call | solution.py:356
  118.1 0.0 collective-permute-done.8.inner_ref
  118.1 0.0 copy-start.4
  118.1 8.7 %collective-permute-done.7.outer_ref = bf16[64,8192]{1,0:T(8,128)(2,1)S(1)} collective-permute-done((bf16[64,8192]{1,0:T(8,128)(2,1)S(1)}, bf16[64,8192]{1,0:T(8,128)(2,1)S(1)}, u32[]{:S(2)}, u32[]{:S(2)}) %collective-permute-start.7) | collective-permute-done | bytes 1048608 | tf_op jit(solution)/shard_map/ppermute | solution.py:522
  126.9 0.0 copy-done.4
  126.9 0.0 copy-start.5
  126.9 1.0 copy-done.5
  127.9 3.4 %far_pack.3.after_ref = bf16[8,2,2,8,8192]{4,3,2,1,0:T(8,128)(2,1)} custom-call(s32[32]{0:T(128)} %copy-done.7, bf16[64,8192]{1,0:T(8,128)(2,1)} %copy-done.5, bf16[64,8192]{1,0:T(8,128)(2,1)} %copy-done.4, bf16[8,2,2,8,8192]{4,3,2,1,0:T(8,128)(2,1)} %own_pack.2.before_ref.after_ref.own_ref, ...), custom_call_target="tpu_custom_call", output_to_operand_aliasing={{}: (3, {})} | custom-call | flops 1048576 | bytes 3145728 | tf_op jit(solution)/shard_map/far_pack/pallas_call | solution.py:270
  131.3 10.4 %all-to-all-done.1 = bf16[8,2,2,8,8192]{4,3,2,1,0:T(8,128)(2,1)} async-done(((bf16[8,2,2,8,8192]{4,3,2,1,0:T(8,128)(2,1)}), bf16[8,2,2,8,8192]{4,3,2,1,0:T(8,128)(2,1)}, u32[]{:S(2)}, u32[]{:S(2)}) %all-to-all-start.1) | async-done | bytes 4194336 | tf_op jit(solution)/shard_map/all_to_all | solution.py:503
  141.7 4.7 %all-to-all-start = ((bf16[8,2,2,8,8192]{4,3,2,1,0:T(8,128)(2,1)}), bf16[8,2,2,8,8192]{4,3,2,1,0:T(8,128)(2,1)}, u32[]{:S(2)}, u32[]{:S(2)}) async-start(bf16[8,2,2,8,8192]{4,3,2,1,0:T(8,128)(2,1)} %far_pack.3.after_ref), calls=%async_computation | async-start | bytes 8388608 | tf_op jit(solution)/shard_map/all_to_all | solution.py:503
  146.5 23.1 %place.5.second_ref = bf16[16384,256]{1,0:T(8,128)(2,1)} custom-call(s32[4,1,16384]{2,1,0:T(1,128)} %broadcast_in_dim.10.ops_ref, bf16[64,8192]{1,0:T(8,128)(2,1)} %weigh.3.mine_ref, bf16[64,8192]{1,0:T(8,128)(2,1)} %copy-done, bf16[16384,512]{1,0:T(8,128)(2,1)} %place.3.after_ref.before_ref, bf16[8,2,2,8,8192]{4,3,2,1,0:T(8,128)(2,1)} %far_pack.3.after_ref), custom_call_target="tpu_custom_call" | custom-call | bytes 134217728 | tf_op jit(solution)/shard_map/place/pallas_call | solution.py:356
  169.6 11.2 %plane_sums.2.before_ref = f32[384,768]{1,0:T(8,128)} custom-call(bf16[256,8192]{1,0:T(8,128)(2,1)} %bitcast.2.got_ref.before_ref, bf16[16384,256]{1,0:T(8,128)(2,1)} %place.4.after_ref.first_ref, bf16[16384,256]{1,0:T(8,128)(2,1)} %place.5.second_ref, bf16[256,8192]{1,0:T(8,128)(2,1)} %bitcast.2.got_ref.before_ref), custom_call_target="tpu_custom_call" | custom-call | flops 4831838208 | bytes 12582912 | tf_op jit(solution)/shard_map/plane_sums/pallas_call | solution.py:469
  180.8 14.6 %all-to-all-done = bf16[8,2,2,8,8192]{4,3,2,1,0:T(8,128)(2,1)} async-done(((bf16[8,2,2,8,8192]{4,3,2,1,0:T(8,128)(2,1)}), bf16[8,2,2,8,8192]{4,3,2,1,0:T(8,128)(2,1)}, u32[]{:S(2)}, u32[]{:S(2)}) %all-to-all-start) | async-done | bytes 4194336 | tf_op jit(solution)/shard_map/all_to_all | solution.py:503
  195.4 12.5 %plane_sums.3 = f32[128,128]{1,0:T(8,128)} custom-call(bf16[256,8192]{1,0:T(8,128)(2,1)} %bitcast.1.got_ref, bf16[16384,256]{1,0:T(8,128)(2,1)} %place.4.after_ref.first_ref, bf16[16384,256]{1,0:T(8,128)(2,1)} %place.5.second_ref, f32[384,768]{1,0:T(8,128)} %plane_sums.2.before_ref), custom_call_target="tpu_custom_call" | custom-call | flops 4831838208 | bytes 12582912 | tf_op jit(solution)/shard_map/plane_sums/pallas_call | solution.py:469
  207.9 0.9 copy.25
  208.7 0.9 copy.24
  209.7 0.7 broadcast_in_dim.12
  210.3 7.5 %all-to-all-start.2 = ((f32[32,8,128]{2,1,0:T(8,128)}), f32[32,8,128]{2,1,0:T(8,128)S(1)}, u32[]{:S(2)}, u32[]{:S(2)}) async-start(f32[32,8,128]{2,1,0:T(8,128)} %bitcast.13), calls=%async_computation.2 | async-start | bytes 262144 | tf_op jit(solution)/shard_map/all_to_all | solution.py:543
  217.9 1.8 collective-permute-start.9
  219.7 2.9 %collective-permute-done.9 = f32[2,8,4,128]{3,1,2,0:T(8,128)S(1)} collective-permute-done((f32[2,8,4,128]{3,1,2,0:T(8,128)S(1)}, f32[2,8,4,128]{3,1,2,0:T(8,128)S(1)}, u32[]{:S(2)}, u32[]{:S(2)}) %collective-permute-start.9) | collective-permute-done | bytes 32800 | tf_op jit(solution)/shard_map/ppermute | solution.py:535
  222.7 0.7 copy.17
  223.4 2.7 %all-to-all-done.2 = f32[32,8,128]{2,1,0:T(8,128)S(1)} async-done(((f32[32,8,128]{2,1,0:T(8,128)}), f32[32,8,128]{2,1,0:T(8,128)S(1)}, u32[]{:S(2)}, u32[]{:S(2)}) %all-to-all-start.2) | async-done | bytes 131104 | tf_op jit(solution)/shard_map/all_to_all | solution.py:543
  226.1 0.3 reshape.38
  226.4 0.1 fusion
  226.5 0.2 copy.19
  226.7 0.9 copy.20
  (9 shorter events, 0.1 us)
Async XLA Ops:
  0.6 7.5 %copy-start.8 = (s32[32,1]{0,1:T(1,128)S(1)}, s32[32,1]{0,1:T(1,128)}, u32[]{:S(2)}) copy-start(s32[32,1]{0,1:T(1,128)} %param.9) | copy-start | bytes 388
  0.6 37.7 %copy-start.6 = (s32[4,16384]{1,0:T(4,128)S(1)}, s32[4,16384]{1,0:T(4,128)}, u32[]{:S(2)}) copy-start(s32[4,16384]{1,0:T(4,128)} %param.8) | copy-start | bytes 786436
  4.4 30.6 %collective-permute-start = (bf16[64,8192]{1,0:T(8,128)(2,1)}, bf16[64,8192]{1,0:T(8,128)(2,1)S(1)}, u32[]{:S(2)}, u32[]{:S(2)}) collective-permute-start(bf16[64,8192]{1,0:T(8,128)(2,1)} %weigh.2.mine_ref), channel_id=1, source_target_pairs={{0,8},{1,9},{2,10},{3,11},{4,12},{5,13},{6,14},{7,15},{8,0},{9,1},... | collective-permute-start | bytes 3145736 | tf_op jit(solution)/shard_map/ppermute | solution.py:509
  7.4 27.6 %collective-permute-start.1 = (bf16[64,8192]{1,0:T(8,128)(2,1)}, bf16[64,8192]{1,0:T(8,128)(2,1)S(1)}, u32[]{:S(2)}, u32[]{:S(2)}) collective-permute-start(bf16[64,8192]{1,0:T(8,128)(2,1)} %weigh.2.mine_ref), channel_id=1, source_target_pairs={{8,16},{9,17},{10,18},{11,19},{12,20},{13,21},{14,22},{15,23},{16,... | collective-permute-start | bytes 3145736 | tf_op jit(solution)/shard_map/ppermute | solution.py:510
  8.1 26.8 %collective-permute-start.2 = (s32[32]{0:T(128)S(1)}, s32[32]{0:T(128)S(1)}, u32[]{:S(2)}, u32[]{:S(2)}) collective-permute-start(s32[32]{0:T(128)S(1)} %bitcast.38), channel_id=1, source_target_pairs={{0,16},{1,17},{2,18},{3,19},{4,20},{5,21},{6,22},{7,23},{8,24},{9,... | collective-permute-start | bytes 392 | tf_op jit(solution)/shard_map/ppermute | solution.py:511
  35.0 10.4 %copy-start.7 = (s32[32]{0:T(128)}, s32[32]{0:T(128)S(1)}, u32[]{:S(2)}) copy-start(s32[32]{0:T(128)S(1)} %collective-permute-done.2.pick_ref) | copy-start | bytes 388
  35.0 10.4 %copy-start.3 = (bf16[64,8192]{1,0:T(8,128)(2,1)}, bf16[64,8192]{1,0:T(8,128)(2,1)S(1)}, u32[]{:S(2)}) copy-start(bf16[64,8192]{1,0:T(8,128)(2,1)S(1)} %collective-permute-done.near_ref) | copy-start | bytes 3145732
  35.0 47.6 %collective-permute-start.3 = (bf16[64,8192]{1,0:T(8,128)(2,1)}, bf16[64,8192]{1,0:T(8,128)(2,1)S(1)}, u32[]{:S(2)}, u32[]{:S(2)}) collective-permute-start(bf16[64,8192]{1,0:T(8,128)(2,1)} %weigh.3.mine_ref), channel_id=1, source_target_pairs={{0,8},{1,9},{2,10},{3,11},{4,12},{5,13},{6,14},{7,15},{8,0},{9,1},... | collective-permute-start | bytes 3145736 | tf_op jit(solution)/shard_map/ppermute | solution.py:516
  35.5 47.1 %collective-permute-start.4 = (bf16[64,8192]{1,0:T(8,128)(2,1)}, bf16[64,8192]{1,0:T(8,128)(2,1)S(1)}, u32[]{:S(2)}, u32[]{:S(2)}) collective-permute-start(bf16[64,8192]{1,0:T(8,128)(2,1)} %weigh.3.mine_ref), channel_id=1, source_target_pairs={{8,16},{9,17},{10,18},{11,19},{12,20},{13,21},{14,22},{15,23},{16,... | collective-permute-start | bytes 3145736 | tf_op jit(solution)/shard_map/ppermute | solution.py:517
  36.3 46.4 %collective-permute-start.6 = (bf16[64,8192]{1,0:T(8,128)(2,1)S(1)}, bf16[64,8192]{1,0:T(8,128)(2,1)S(1)}, u32[]{:S(2)}, u32[]{:S(2)}) collective-permute-start(bf16[64,8192]{1,0:T(8,128)(2,1)S(1)} %collective-permute-done.near_ref), channel_id=1, source_target_pairs={{8,16},{9,17},{10,18},{11,19},{12,20},{13,21},{14,22},{15,23},{16,... | collective-permute-start | bytes 3145736 | tf_op jit(solution)/shard_map/ppermute | solution.py:519
  37.0 45.6 %collective-permute-start.5 = (bf16[64,8192]{1,0:T(8,128)(2,1)S(1)}, bf16[64,8192]{1,0:T(8,128)(2,1)S(1)}, u32[]{:S(2)}, u32[]{:S(2)}) collective-permute-start(bf16[64,8192]{1,0:T(8,128)(2,1)S(1)} %collective-permute-done.1), channel_id=1, source_target_pairs={{8,0},{9,1},{10,2},{11,3},{12,4},{13,5},{14,6},{15,7},{16,24},{17,... | collective-permute-start | bytes 3145736 | tf_op jit(solution)/shard_map/ppermute | solution.py:518
  82.6 10.0 %copy-start = (bf16[64,8192]{1,0:T(8,128)(2,1)}, bf16[64,8192]{1,0:T(8,128)(2,1)S(1)}, u32[]{:S(2)}) copy-start(bf16[64,8192]{1,0:T(8,128)(2,1)S(1)} %collective-permute-done.3.near_ref) | copy-start | bytes 3145732
  82.6 1.0 copy-start.1
  83.6 1.0 copy-start.2
  88.0 53.7 %all-to-all-start.1 = ((bf16[8,2,2,8,8192]{4,3,2,1,0:T(8,128)(2,1)}), bf16[8,2,2,8,8192]{4,3,2,1,0:T(8,128)(2,1)}, u32[]{:S(2)}, u32[]{:S(2)}) async-start(bf16[8,2,2,8,8192]{4,3,2,1,0:T(8,128)(2,1)} %far_pack.2.after_ref), calls=%async_computation.1 | async-start | bytes 8388608 | tf_op jit(solution)/shard_map/all_to_all | solution.py:503
  92.6 25.5 %collective-permute-start.8 = (bf16[64,8192]{1,0:T(8,128)(2,1)S(1)}, bf16[64,8192]{1,0:T(8,128)(2,1)S(1)}, u32[]{:S(2)}, u32[]{:S(2)}) collective-permute-start(bf16[64,8192]{1,0:T(8,128)(2,1)S(1)} %collective-permute-done.3.near_ref), channel_id=1, source_target_pairs={{8,16},{9,17},{10,18},{11,19},{12,20},{13,21},{14,22},{15,23},{16,... | collective-permute-start | bytes 3145736 | tf_op jit(solution)/shard_map/ppermute | solution.py:523
  93.3 33.6 %collective-permute-start.7 = (bf16[64,8192]{1,0:T(8,128)(2,1)S(1)}, bf16[64,8192]{1,0:T(8,128)(2,1)S(1)}, u32[]{:S(2)}, u32[]{:S(2)}) collective-permute-start(bf16[64,8192]{1,0:T(8,128)(2,1)S(1)} %collective-permute-done.4), channel_id=1, source_target_pairs={{8,0},{9,1},{10,2},{11,3},{12,4},{13,5},{14,6},{15,7},{16,24},{17,... | collective-permute-start | bytes 3145736 | tf_op jit(solution)/shard_map/ppermute | solution.py:522
  118.1 8.7 %copy-start.4 = (bf16[64,8192]{1,0:T(8,128)(2,1)}, bf16[64,8192]{1,0:T(8,128)(2,1)S(1)}, u32[]{:S(2)}) copy-start(bf16[64,8192]{1,0:T(8,128)(2,1)S(1)} %collective-permute-done.8.inner_ref) | copy-start | bytes 3145732
  126.9 1.0 copy-start.5
  141.7 53.7 %all-to-all-start = ((bf16[8,2,2,8,8192]{4,3,2,1,0:T(8,128)(2,1)}), bf16[8,2,2,8,8192]{4,3,2,1,0:T(8,128)(2,1)}, u32[]{:S(2)}, u32[]{:S(2)}) async-start(bf16[8,2,2,8,8192]{4,3,2,1,0:T(8,128)(2,1)} %far_pack.3.after_ref), calls=%async_computation | async-start | bytes 8388608 | tf_op jit(solution)/shard_map/all_to_all | solution.py:503
  210.3 15.8 %all-to-all-start.2 = ((f32[32,8,128]{2,1,0:T(8,128)}), f32[32,8,128]{2,1,0:T(8,128)S(1)}, u32[]{:S(2)}, u32[]{:S(2)}) async-start(f32[32,8,128]{2,1,0:T(8,128)} %bitcast.13), calls=%async_computation.2 | async-start | bytes 262144 | tf_op jit(solution)/shard_map/all_to_all | solution.py:543
  217.9 4.8 %collective-permute-start.9 = (f32[2,8,4,128]{3,1,2,0:T(8,128)S(1)}, f32[2,8,4,128]{3,1,2,0:T(8,128)S(1)}, u32[]{:S(2)}, u32[]{:S(2)}) collective-permute-start(f32[2,8,4,128]{3,1,2,0:T(8,128)S(1)} %slice_bitcast_fusion), channel_id=1, source_target_pairs={{0,8},{1,9},{2,10},{3,11},{4,12},{5,13},{6,14},{7,15},{8,0},{9,1},... | collective-permute-start | bytes 98312 | tf_op jit(solution)/shard_map/ppermute | solution.py:535

commit v9 on v3

--- a/solution.py
+++ b/solution.py
@@ -357,33 +357,61 @@
     return numer / jnp.sqrt(var_x * var_y)
 
 
-def plane_sums_kernel(own_ref, far_ref, first_ref, second_ref, out_ref, acc):
-    rows, depth = own_ref.shape
+def add_sums(acc, got_ref, cols, right):
+    rows = got_ref.shape[0]
+    slabs = rows // SLAB
+    wide = got_ref[:, cols].astype(jnp.float32).reshape(slabs, SLAB, -1)
+    is_x = lax.broadcasted_iota(jnp.int32, wide.shape, 1) < SUB
+    rolled = pltpu.roll(wide, SUB, 1)
+    product = wide * rolled
+    products = jnp.where(is_x, product * wide, product).reshape(rows, -1)
+    mine = rolled.reshape(slabs // 2, 2, SLAB, -1)[:, 0]
+    partner = wide.reshape(slabs // 2, 2, SLAB, -1)[:, 1]
+    weights = jnp.where(is_x[: slabs // 2], mine, partner).reshape(rows // 2, -1)
+    left = jnp.concatenate([weights, products], 0).astype(jnp.bfloat16)
+    acc[...] += jnp.dot(left, right, preferred_element_type=jnp.float32)
+
+
+def correlations(acc):
+    rows = acc.shape[0] // 3
+    half = LANES // 2
+    blk = half // 2
+    tiles = rows // SLAB
+    top = lax.broadcasted_iota(jnp.int32, (tiles, SLAB, LANES), 1) < SUB
+    lane = lax.broadcasted_iota(jnp.int32, (rows, LANES), 1)
+    result = jnp.zeros((rows, LANES), jnp.float32)
+    for k in range(NOPS):
+        lanes = slice(k * LANES, (k + 1) * LANES)
+        squares = slice((NOPS + k // 2) * LANES, (NOPS + k // 2 + 1) * LANES)
+        with_w = acc[:rows, lanes]
+        with_y = acc[rows:, lanes].reshape(tiles, 2, SLAB, LANES)
+        mine, partner = with_y[:, 0], with_y[:, 1]
+        y = jnp.where(top, pltpu.roll(mine, SUB, 1), partner).reshape(rows, LANES)
+        yy = jnp.where(top, mine, pltpu.roll(partner, SUB, 1)).reshape(rows, LANES)
+        sum_xx = acc[:rows, squares]
+        if k % 2 == 1:
+            sum_xx = pltpu.roll(sum_xx, half, 1)
+        both = ratio(
+            pltpu.roll(with_w, half, 1), with_w, sum_xx, pltpu.roll(y, half, 1), y, pltpu.roll(yy, half, 1)
+        )
+        both = jnp.where(top.reshape(rows, LANES), both, pltpu.roll(both, LANES - blk, 1))
+        moved = both if k == 0 else pltpu.roll(both, k * blk, 1)
+        result = jnp.where((lane >= k * blk) & (lane < (k + 1) * blk), moved, result)
+    return result
+
+
+def own_sums_kernel(got_ref, first_ref, second_ref, out_ref, right_ref, acc):
+    depth = got_ref.shape[1]
     step = min(1024, depth)
     half = LANES // 2
-    slabs = rows // SLAB
-    blk = half // 2
 
     @pl.when(pl.program_id(0) == 0)
     def _():
         acc[...] = jnp.zeros_like(acc)
 
-    @pl.loop(0, depth // step)
-    def _(i):
-        cols = pl.ds(pl.multiple_of(i * step, step), step)
-        is_x = lax.broadcasted_iota(jnp.int32, (slabs, SLAB, step), 1) < SUB
-        weights, products = [], []
-        for ref in (own_ref, far_ref):
-            wide = ref[:, cols].astype(jnp.float32).reshape(slabs, SLAB, step)
-            rolled = pltpu.roll(wide, SUB, 1)
-            product = wide * rolled
-            both = jnp.where(is_x, product * wide, product)
-            products.append(both.reshape(rows, step).astype(jnp.bfloat16))
-            mine = rolled.reshape(slabs // 2, 2, SLAB, step)[:, 0]
-            partner = wide.reshape(slabs // 2, 2, SLAB, step)[:, 1]
-            pair = jnp.where(is_x[: slabs // 2], mine, partner)
-            weights.append(pair.reshape(rows // 2, step).astype(jnp.bfloat16))
-        low = lax.broadcasted_iota(jnp.int32, (step, LANES), 1) < half
+    low = lax.broadcasted_iota(jnp.int32, (step, LANES), 1) < half
+    for i in range(depth // step):
+        cols = slice(i * step, (i + 1) * step)
         linear, square = [], []
         for ref in (first_ref, second_ref):
             even, odd = None, None
@@ -397,59 +425,94 @@
                 else:
                     odd = product * swapped
             square.append(jnp.where(low, even, odd).astype(jnp.bfloat16))
-        left = jnp.concatenate(weights + products, 0)
         right = jnp.concatenate(linear + square, 1)
-        acc[...] += jnp.dot(left, right, preferred_element_type=jnp.float32)
+        right_ref[cols, :] = right
+        add_sums(acc, got_ref, cols, right)
 
     @pl.when(pl.program_id(0) == pl.num_programs(0) - 1)
     def _():
-        tiles = slabs
-        top = lax.broadcasted_iota(jnp.int32, (tiles, SLAB, LANES), 1) < SUB
-        lane = lax.broadcasted_iota(jnp.int32, (tiles * SLAB, LANES), 1)
-        result = jnp.zeros((tiles * SLAB, LANES), jnp.float32)
-        for k in range(NOPS):
-            lanes = slice(k * LANES, (k + 1) * LANES)
-            squares = slice((NOPS + k // 2) * LANES, (NOPS + k // 2 + 1) * LANES)
-            with_w = acc[:rows, lanes]
-            with_y = acc[rows:, lanes].reshape(tiles, 2, SLAB, LANES)
-            mine, partner = with_y[:, 0], with_y[:, 1]
-            y = jnp.where(top, pltpu.roll(mine, SUB, 1), partner).reshape(tiles * SLAB, LANES)
-            yy = jnp.where(top, mine, pltpu.roll(partner, SUB, 1)).reshape(tiles * SLAB, LANES)
-            sum_xx = acc[:rows, squares]
-            if k % 2 == 1:
-                sum_xx = pltpu.roll(sum_xx, half, 1)
-            both = ratio(
-                pltpu.roll(with_w, half, 1), with_w, sum_xx, pltpu.roll(y, half, 1), y, pltpu.roll(yy, half, 1)
-            )
-            both = jnp.where(
-                top.reshape(tiles * SLAB, LANES), both, pltpu.roll(both, LANES - blk, 1)
-            )
-            moved = both if k == 0 else pltpu.roll(both, k * blk, 1)
-            result = jnp.where((lane >= k * blk) & (lane < (k + 1) * blk), moved, result)
-        out_ref[...] = result
-
-
-def plane_sums(own, far, first, second):
-    rows, width = own.shape
+        out_ref[...] = correlations(acc)
+
+
+def far_sums_kernel(got_ref, right_ref, own_ref, mine_ref, other_ref, back_ref, acc):
+    depth = got_ref.shape[1]
+    step = min(1024, depth)
+
+    @pl.when(pl.program_id(0) == 0)
+    def _():
+        acc[...] = jnp.zeros_like(acc)
+
+    for i in range(depth // step):
+        cols = slice(i * step, (i + 1) * step)
+        add_sums(acc, got_ref, cols, right_ref[cols, :])
+
+    @pl.when(pl.program_id(0) == pl.num_programs(0) - 1)
+    def _():
+        upper = lax.div(lax.axis_index("dp"), 2 * PLANE)
+        count = own_ref.shape[0] // 2
+        for part, result in enumerate((own_ref[...], correlations(acc))):
+            tiles = result.reshape(PLANE, SLAB, LANES)
+            slot = part + upper - 2 * part * upper
+            for twin in range(2):
+                back_ref[slot, twin] = tiles
+            pairs = result.reshape(PLANE // 2, 2, SLAB, LANES)
+            even, odd = pairs[:, 0], pairs[:, 1]
+            top = lax.broadcasted_iota(jnp.int32, even.shape, 1) < SUB
+            here = slice(part * count, (part + 1) * count)
+            mine_ref[here, :] = jnp.where(top, even, pltpu.roll(odd, SUB, 1)).reshape(count, LANES)
+            other_ref[here, :] = jnp.where(top, pltpu.roll(even, SUB, 1), odd).reshape(count, LANES)
+
+
+def own_sums(got, first, second):
+    rows, width = got.shape
     depth = min(2048, width)
     lanes = (NOPS + NOPS // 2) * LANES
-    part = pl.BlockSpec((rows, depth), lambda i: (0, i))
     moved = pl.BlockSpec((depth, 2 * LANES), lambda i: (i, 0))
     return pl.pallas_call(
-        plane_sums_kernel,
+        own_sums_kernel,
         grid=(width // depth,),
-        out_shape=jax.ShapeDtypeStruct((rows, LANES), jnp.float32),
-        in_specs=[part, part, moved, moved],
-        out_specs=pl.BlockSpec((rows, LANES), lambda i: (0, 0)),
-        scratch_shapes=[pltpu.VMEM((3 * rows, lanes), jnp.float32)],
+        out_shape=(
+            jax.ShapeDtypeStruct((rows // 2, LANES), jnp.float32),
+            jax.ShapeDtypeStruct((width, lanes), jnp.bfloat16),
+        ),
+        in_specs=[pl.BlockSpec((rows, depth), lambda i: (0, i)), moved, moved],
+        out_specs=(
+            pl.BlockSpec((rows // 2, LANES), lambda i: (0, 0)),
+            pl.BlockSpec((depth, lanes), lambda i: (i, 0)),
+        ),
+        scratch_shapes=[pltpu.VMEM((rows * 3 // 2, lanes), jnp.float32)],
         compiler_params=params(),
         cost_estimate=pl.CostEstimate(
-            flops=6 * rows * width * lanes,
-            bytes_accessed=width * (4 * rows + 8 * LANES),
+            flops=3 * rows * width * lanes,
+            bytes_accessed=2 * width * (rows + 4 * LANES + lanes),
             transcendentals=0,
         ),
-        name="plane_sums",
-    )(own, far, first, second)
+        name="own_sums",
+    )(got, first, second)
+
+
+def far_sums(got, right, own):
+    rows, width = got.shape
+    depth = min(2048, width)
+    lanes = right.shape[1]
+    shapes = (own.shape, own.shape, (2, 2, PLANE, SLAB, LANES))
+    return pl.pallas_call(
+        far_sums_kernel,
+        grid=(width // depth,),
+        out_shape=tuple(jax.ShapeDtypeStruct(shape, jnp.float32) for shape in shapes),
+        in_specs=[
+            pl.BlockSpec((rows, depth), lambda i: (0, i)),
+            pl.BlockSpec((depth, lanes), lambda i: (i, 0)),
+            pl.BlockSpec(own.shape, lambda i: (0, 0)),
+        ],
+        out_specs=tuple(pl.BlockSpec(shape, lambda i, shape=shape: (0,) * len(shape)) for shape in shapes),
+        scratch_shapes=[pltpu.VMEM((rows * 3 // 2, lanes), jnp.float32)],
+        compiler_params=params(),
+        cost_estimate=pl.CostEstimate(
+            flops=3 * rows * width * lanes, bytes_accessed=2 * width * (rows + lanes), transcendentals=0
+        ),
+        name="far_sums",
+    )(got, right, own)
 
 
 def shards_by_plane(intensities, observed, qweights, ops, pick):
@@ -484,18 +547,17 @@
     far_send = far_pack(far_pick, outer_x, outer_w, inner_x, inner_w, first)
     far_got = spread(far_send)
     second = place(ops[2:], intensities, near_x, own_w, near_w, far_send)
-    stats = plane_sums(own_got, far_got, first, second)
-    stats = stats.reshape(2, PLANE, 2, SUB, NOPS * blk)
-    mine, other = stats[:, :, 0], stats[:, :, 1]
+    own_corr, right = own_sums(own_got, first, second)
+    mine, other, back = far_sums(far_got, right, own_corr)
 
     from_near = lax.ppermute(other, "dp", near)
-    pair = jnp.stack([mine, from_near], 1)
+    pair = [each.reshape(2, PLANE, SUB, NOPS * blk) for each in (mine, from_near)]
+    pair = jnp.stack(pair, 1)
     pair = jnp.where(odd, pair[:, ::-1], pair)
     pair = jnp.where(upper, pair[::-1], pair)
     corr = pair.reshape(groups * SUB, NOPS * blk).T.reshape(NOPS, blk, groups * SUB)
 
-    both = jnp.where(upper, stats[::-1], stats).reshape(2, 1, PLANE, 2 * SUB, NOPS * blk)
-    back = jnp.broadcast_to(both, (2, 2, PLANE, 2 * SUB, NOPS * blk)).reshape(groups, 2 * SUB, NOPS * blk)
+    back = back.reshape(groups, 2 * SUB, NOPS * blk)
     back = lax.all_to_all(back, "dp", split_axis=0, concat_axis=0, tiled=True)
     back = back.reshape(2, 2, PLANE, 2, SUB, NOPS, blk)
     back = jnp.where(odd, back[:, 1, :, ::-1], back[:, 0])

time: 205 us -> 208 us (1.015)
  Pallas kernels: 104 us -> 119 us
  waiting for transfers between devices: 61.6 us -> 49.2 us
  local copies, waits for them, and re-layouts: 6.14 us -> 3.72 us
  starting transfers between devices: 28.3 us -> 30.5 us
    pallas_call x1 -> x2, Pallas kernels: 21.5 us -> 36.5 us  [the longest x1 22.2 us: own_sums(): pl.pallas_call(own_sums_kernel, grid=(width // depth,), out_shape=(jax.Sh...]
    all_to_all x2, waiting for transfers between devices: 11.6 us -> 0.01 us  [spread(): lax.all_to_all(send, 'dp', split_axis=0, concat_axis=0, axis_index_groups...]
    all_to_all x1, starting transfers between devices: 3.26 us -> 5.5 us  [shards_by_plane(): back = lax.all_to_all(back, 'dp', split_axis=0, concat_axis=0, tiled=True)]
  transfers between devices with their start and end apart: 13 -> 13, of which waited for: 4 -> 3; matrix products, arithmetic and copies ran while one was open for 2% -> 2% of each run, Pallas kernels for 40% -> 51%
where the time goes in v9:
time: 208 us; the launch traced here: 207 us
  Pallas kernels  119 us (57%)
  waiting for transfers between devices  49.2 us (24%)
  starting transfers between devices  30.5 us (15%)
  other arithmetic  3.84 us (2%)
  local copies, waits for them, and re-layouts  3.72 us (2%)
    pallas_call x2, Pallas kernels, place(): pl.pallas_call(place_kernel, grid=(count, width // depth), out_shape=jax....  73.5 us
    ppermute x1, waiting for transfers between devices, shards_by_plane(): far_pick = lax.ppermute(own_pick, 'dp', far)  32.1 us
    pallas_call x1, Pallas kernels, own_sums(): pl.pallas_call(own_sums_kernel, grid=(width // depth,), out_shape=(jax.Sh...  22.2 us
    pallas_call x1, Pallas kernels, far_sums(): pl.pallas_call(far_sums_kernel, grid=(width // depth,), out_shape=tuple((...  14.3 us
    ppermute x1, waiting for transfers between devices, shards_by_plane(): outer_w = lax.ppermute(mid_w, 'dp', outward)  10.4 us
    pallas_call x2, Pallas kernels, pack_call(): pl.pallas_call(kernel, out_shape=jax.ShapeDtypeStruct((PLANE, 2, SLAB, wi...  9.33 us
    all_to_all x2, starting transfers between devices, spread(): lax.all_to_all(send, 'dp', split_axis=0, concat_axis=0, axis_index_groups...  9.25 us
    all_to_all x1, waiting for transfers between devices, shards_by_plane(): back = lax.all_to_all(back, 'dp', split_axis=0, concat_axis=0, tiled=True)  6.66 us
  transfers between devices with their start and end apart: 13, of which 3 were waited for; matrix products, arithmetic and copies ran while one was open for 2% of the time, Pallas kernels for 51%

profile of v9, /device:TPU:0, one launch (start us, length us, event | category | flops | bytes accessed | tf_op | source)
XLA Modules:
  0.0 207.4 jit_solution(9182959274743185952)
XLA Ops:
  0.6 0.0 copy-start.1
  0.6 2.2 %multiply_convert_fusion.w_ref = bf16[32,16384]{1,0:T(8,128)(2,1)S(1)} fusion(bf16[32,16384]{1,0:T(8,128)(2,1)} %param.7, s32[32,16384]{1,0:T(8,128)} %param.6), kind=kLoop, calls=%fused_computation | loop fusion | flops 2097152 | bytes 4194304 | tf_op jit(solution)/shard_map/convert_element_type | solution.py:537
  2.9 0.0 copy-start
  2.9 3.1 %collective-permute-start.2 = (bf16[32,16384]{1,0:T(8,128)(2,1)S(1)}, bf16[32,16384]{1,0:T(8,128)(2,1)S(1)}, u32[]{:S(2)}, u32[]{:S(2)}) collective-permute-start(bf16[32,16384]{1,0:T(8,128)(2,1)S(1)} %multiply_convert_fusion.w_ref), channel_id=1, source_target_pairs={{0,8},{1,9},{2,10},{3,11},{4,12},{5,13},{6,14},{7,15},{8,0},{9,1},... | collective-permute-start | bytes 3145736 | tf_op jit(solution)/shard_map/ppermute | solution.py:538
  6.0 1.7 collective-permute-start.3
  7.6 0.0 copy-done.1
  7.6 3.5 %collective-permute-start = (bf16[32,16384]{1,0:T(8,128)(2,1)S(1)}, bf16[32,16384]{1,0:T(8,128)(2,1)}, u32[]{:S(2)}, u32[]{:S(2)}) collective-permute-start(bf16[32,16384]{1,0:T(8,128)(2,1)S(1)} %copy-done.1), channel_id=1, source_target_pairs={{0,8},{1,9},{2,10},{3,11},{4,12},{5,13},{6,14},{7,15},{8,0},{9,1},... | collective-permute-start | bytes 3145736 | tf_op jit(solution)/shard_map/ppermute | solution.py:534
  11.1 1.6 collective-permute-start.1
  12.7 0.0 copy-done
  12.7 4.4 %own_pack.1 = bf16[8,2,8,16384]{3,2,1,0:T(8,128)(2,1)} custom-call(s32[32]{0:T(128)} %bitcast.25, bf16[32,16384]{1,0:T(8,128)(2,1)} %x_ref.5, bf16[32,16384]{1,0:T(8,128)(2,1)} %copy-done), custom_call_target="tpu_custom_call" | custom-call | flops 2097152 | bytes 6291456 | tf_op jit(solution)/shard_map/own_pack/pallas_call | solution.py:254
  17.1 0.0 copy-start.8
  17.1 0.0 copy-start.7
  17.2 4.7 %all-to-all-start.1 = ((bf16[8,2,8,16384]{3,2,1,0:T(8,128)(2,1)}), bf16[8,2,8,16384]{3,2,1,0:T(8,128)(2,1)}, u32[]{:S(2)}, u32[]{:S(2)}) async-start(bf16[8,2,8,16384]{3,2,1,0:T(8,128)(2,1)} %own_pack.1), calls=%async_computation.1 | async-start | bytes 8388608 | tf_op jit(solution)/shard_map/all_to_all | solution.py:530
  21.9 0.0 copy-done.8
  21.9 1.8 collective-permute-start.4
  23.7 32.1 %collective-permute-done.4.pick_ref = s32[32]{0:T(128)S(1)} collective-permute-done((s32[32]{0:T(128)S(1)}, s32[32]{0:T(128)S(1)}, u32[]{:S(2)}, u32[]{:S(2)}) %collective-permute-start.4) | collective-permute-done | bytes 160 | tf_op jit(solution)/shard_map/ppermute | solution.py:536
  55.8 0.0 copy-start.9
  55.8 0.0 collective-permute-done.2.w1_ref
  55.8 0.0 copy-start.2
  55.8 0.0 collective-permute-done.3
  55.8 0.0 collective-permute-done.x1_ref
  55.8 0.0 collective-permute-done.1
  55.8 0.7 collective-permute-start.7
  56.6 0.7 collective-permute-start.8
  57.3 1.3 collective-permute-start.5
  58.6 1.3 collective-permute-start.6
  59.9 0.0 copy-done.7
  59.9 0.1 fusion.1
  60.0 0.7 broadcast_in_dim.6.ops_ref
  60.8 0.0 copy-done.2
  60.8 36.8 %place.2.after_ref.first_ref = bf16[16384,256]{1,0:T(8,128)(2,1)} custom-call(s32[2,1,16384]{2,1,0:T(1,128)} %broadcast_in_dim.6.ops_ref, bf16[32,16384]{1,0:T(8,128)(2,1)} %x_ref.5, bf16[32,16384]{1,0:T(8,128)(2,1)} %collective-permute-done.x1_ref, bf16[32,16384]{1,0:T(8,128)(2,1)} %copy-done, bf16[32,16384]{1,0:T(8,128)(2,1)} %copy-done.2, s32[32]{0:T(128)} %bitcast.26), custom_call_target="tpu_custom_call" | custom-call | bytes 268435456 | tf_op jit(solution)/shard_map/place/pallas_call | solution.py:331
  97.6 0.0 copy-done.9
  97.6 0.0 collective-permute-done.7.xi
  97.6 0.0 copy-start.3
  97.6 0.0 collective-permute-done.8.wi
  97.6 0.0 copy-start.4
  97.6 0.0 collective-permute-done.5.xo
  97.6 0.0 copy-start.5
  97.6 10.4 %collective-permute-done.6.wo = bf16[32,16384]{1,0:T(8,128)(2,1)S(1)} collective-permute-done((bf16[32,16384]{1,0:T(8,128)(2,1)}, bf16[32,16384]{1,0:T(8,128)(2,1)S(1)}, u32[]{:S(2)}, u32[]{:S(2)}) %collective-permute-start.6) | collective-permute-done | bytes 1048608 | tf_op jit(solution)/shard_map/ppermute | solution.py:544
  108.0 0.0 copy-done.3
  108.0 0.0 copy-done.4
  108.0 0.0 copy-done.5
  108.0 0.0 copy-start.6
  108.0 1.0 copy-done.6
  109.0 4.9 %far_pack.1.after_ref = bf16[8,2,8,16384]{3,2,1,0:T(8,128)(2,1)} custom-call(s32[32]{0:T(128)} %copy-done.9, bf16[32,16384]{1,0:T(8,128)(2,1)} %copy-done.5, bf16[32,16384]{1,0:T(8,128)(2,1)} %copy-done.6, bf16[32,16384]{1,0:T(8,128)(2,1)} %copy-done.3, bf16[32,16384]{1,0:T(8,128)(2,1)} %copy-done.4, bf16[16384,256]{1,0:T(8,128)(2,1)} %place.2.after_ref.first_ref), custom_call_target="tpu_custom_call" | custom-call | flops 2097152 | bytes 6291456 | tf_op jit(solution)/shard_map/far_pack/pallas_call | solution.py:254
  114.0 0.0 all-to-all-done.1
  114.0 4.6 %all-to-all-start = ((bf16[8,2,8,16384]{3,2,1,0:T(8,128)(2,1)}), bf16[8,2,8,16384]{3,2,1,0:T(8,128)(2,1)}, u32[]{:S(2)}, u32[]{:S(2)}) async-start(bf16[8,2,8,16384]{3,2,1,0:T(8,128)(2,1)} %far_pack.1.after_ref), calls=%async_computation | async-start | bytes 8388608 | tf_op jit(solution)/shard_map/all_to_all | solution.py:530
  118.6 0.7 broadcast_in_dim.7.ops_ref
  119.3 36.7 %place.3.second_ref = bf16[16384,256]{1,0:T(8,128)(2,1)} custom-call(s32[2,1,16384]{2,1,0:T(1,128)} %broadcast_in_dim.7.ops_ref, bf16[32,16384]{1,0:T(8,128)(2,1)} %x_ref.5, bf16[32,16384]{1,0:T(8,128)(2,1)} %collective-permute-done.x1_ref, bf16[32,16384]{1,0:T(8,128)(2,1)} %copy-done, bf16[32,16384]{1,0:T(8,128)(2,1)} %copy-done.2, ...), custom_call_target="tpu_custom_call" | custom-call | bytes 268435456 | tf_op jit(solution)/shard_map/place/pallas_call | solution.py:331
  156.0 22.2 %own_sums.1 = (f32[64,128]{1,0:T(8,128)}, bf16[16384,768]{1,0:T(8,128)(2,1)}) custom-call(bf16[128,16384]{1,0:T(8,128)(2,1)} %bitcast.2.got_ref, bf16[16384,256]{1,0:T(8,128)(2,1)} %place.2.after_ref.first_ref, bf16[16384,256]{1,0:T(8,128)(2,1)} %place.3.second_ref), custom_call_target="tpu_custom_call" | custom-call | flops 4831838208 | bytes 46137344 | tf_op jit(solution)/shard_map/own_sums/pallas_call | solution.py:471
  178.2 0.0 all-to-all-done
  178.2 14.3 %far_sums.1 = (f32[64,128]{1,0:T(8,128)}, f32[64,128]{1,0:T(8,128)}, f32[2,2,8,8,128]{4,3,2,1,0:T(8,128)}) custom-call(bf16[128,16384]{1,0:T(8,128)(2,1)} %bitcast.1.got_ref, bf16[16384,768]{1,0:T(8,128)(2,1)} %get-tuple-element.17.right_ref, f32[64,128]{1,0:T(8,128)} %get-tuple-element.18.own_ref), custom_call_target="tpu_custom_call" | custom-call | flops 4831838208 | bytes 29360128 | tf_op jit(solution)/shard_map/far_sums/pallas_call | solution.py:499
  192.5 0.0 collective-permute-start.9
  192.5 5.5 %all-to-all-start.2 = ((f32[32,8,128]{2,1,0:T(8,128)}), f32[32,8,128]{2,1,0:T(8,128)S(1)}, u32[]{:S(2)}, u32[]{:S(2)}) async-start(f32[32,8,128]{2,1,0:T(8,128)} %bitcast.21), calls=%async_computation.2 | async-start | bytes 262144 | tf_op jit(solution)/shard_map/all_to_all | solution.py:561
  198.0 0.0 collective-permute-done.9
  198.0 0.8 pad_maximum_fusion
  198.9 0.7 copy.16
  199.6 6.7 %all-to-all-done.2 = f32[32,8,128]{2,1,0:T(8,128)S(1)} async-done(((f32[32,8,128]{2,1,0:T(8,128)}), f32[32,8,128]{2,1,0:T(8,128)S(1)}, u32[]{:S(2)}, u32[]{:S(2)}) %all-to-all-start.2) | async-done | bytes 131104 | tf_op jit(solution)/shard_map/all_to_all | solution.py:561
  206.3 0.3 reshape.32
  206.6 0.1 copy.19
  206.6 0.8 copy_select_fusion
  (3 shorter events, 0.1 us)
Async XLA Ops:
  0.6 7.0 %copy-start.1 = (bf16[32,16384]{1,0:T(8,128)(2,1)S(1)}, bf16[32,16384]{1,0:T(8,128)(2,1)}, u32[]{:S(2)}) copy-start(bf16[32,16384]{1,0:T(8,128)(2,1)} %x_ref.5) | copy-start | bytes 3145732
  2.9 9.9 %copy-start = (bf16[32,16384]{1,0:T(8,128)(2,1)}, bf16[32,16384]{1,0:T(8,128)(2,1)S(1)}, u32[]{:S(2)}) copy-start(bf16[32,16384]{1,0:T(8,128)(2,1)S(1)} %multiply_convert_fusion.w_ref) | copy-start | bytes 3145732
  2.9 52.9 %collective-permute-start.2 = (bf16[32,16384]{1,0:T(8,128)(2,1)S(1)}, bf16[32,16384]{1,0:T(8,128)(2,1)S(1)}, u32[]{:S(2)}, u32[]{:S(2)}) collective-permute-start(bf16[32,16384]{1,0:T(8,128)(2,1)S(1)} %multiply_convert_fusion.w_ref), channel_id=1, source_target_pairs={{0,8},{1,9},{2,10},{3,11},{4,12},{5,13},{6,14},{7,15},{8,0},{9,1},... | collective-permute-start | bytes 3145736 | tf_op jit(solution)/shard_map/ppermute | solution.py:538
  6.0 49.8 %collective-permute-start.3 = (bf16[32,16384]{1,0:T(8,128)(2,1)S(1)}, bf16[32,16384]{1,0:T(8,128)(2,1)}, u32[]{:S(2)}, u32[]{:S(2)}) collective-permute-start(bf16[32,16384]{1,0:T(8,128)(2,1)S(1)} %multiply_convert_fusion.w_ref), channel_id=1, source_target_pairs={{8,16},{9,17},{10,18},{11,19},{12,20},{13,21},{14,22},{15,23},{16,... | collective-permute-start | bytes 3145736 | tf_op jit(solution)/shard_map/ppermute | solution.py:539
  7.6 48.2 %collective-permute-start = (bf16[32,16384]{1,0:T(8,128)(2,1)S(1)}, bf16[32,16384]{1,0:T(8,128)(2,1)}, u32[]{:S(2)}, u32[]{:S(2)}) collective-permute-start(bf16[32,16384]{1,0:T(8,128)(2,1)S(1)} %copy-done.1), channel_id=1, source_target_pairs={{0,8},{1,9},{2,10},{3,11},{4,12},{5,13},{6,14},{7,15},{8,0},{9,1},... | collective-permute-start | bytes 3145736 | tf_op jit(solution)/shard_map/ppermute | solution.py:534
  11.1 44.7 %collective-permute-start.1 = (bf16[32,16384]{1,0:T(8,128)(2,1)S(1)}, bf16[32,16384]{1,0:T(8,128)(2,1)}, u32[]{:S(2)}, u32[]{:S(2)}) collective-permute-start(bf16[32,16384]{1,0:T(8,128)(2,1)S(1)} %copy-done.1), channel_id=1, source_target_pairs={{8,16},{9,17},{10,18},{11,19},{12,20},{13,21},{14,22},{15,23},{16,... | collective-permute-start | bytes 3145736 | tf_op jit(solution)/shard_map/ppermute | solution.py:535
  17.1 4.7 %copy-start.8 = (s32[32,1]{0,1:T(1,128)S(1)}, s32[32,1]{0,1:T(1,128)}, u32[]{:S(2)}) copy-start(s32[32,1]{0,1:T(1,128)} %param.9) | copy-start | bytes 388
  17.1 42.8 %copy-start.7 = (s32[4,16384]{1,0:T(4,128)S(1)}, s32[4,16384]{1,0:T(4,128)}, u32[]{:S(2)}) copy-start(s32[4,16384]{1,0:T(4,128)} %param.8) | copy-start | bytes 786436
  17.2 96.8 %all-to-all-start.1 = ((bf16[8,2,8,16384]{3,2,1,0:T(8,128)(2,1)}), bf16[8,2,8,16384]{3,2,1,0:T(8,128)(2,1)}, u32[]{:S(2)}, u32[]{:S(2)}) async-start(bf16[8,2,8,16384]{3,2,1,0:T(8,128)(2,1)} %own_pack.1), calls=%async_computation.1 | async-start | bytes 8388608 | tf_op jit(solution)/shard_map/all_to_all | solution.py:530
  21.9 33.9 %collective-permute-start.4 = (s32[32]{0:T(128)S(1)}, s32[32]{0:T(128)S(1)}, u32[]{:S(2)}, u32[]{:S(2)}) collective-permute-start(s32[32]{0:T(128)S(1)} %bitcast.27), channel_id=1, source_target_pairs={{0,16},{1,17},{2,18},{3,19},{4,20},{5,21},{6,22},{7,23},{8,24},{9,... | collective-permute-start | bytes 392 | tf_op jit(solution)/shard_map/ppermute | solution.py:536
  55.8 41.8 %copy-start.9 = (s32[32]{0:T(128)}, s32[32]{0:T(128)S(1)}, u32[]{:S(2)}) copy-start(s32[32]{0:T(128)S(1)} %collective-permute-done.4.pick_ref) | copy-start | bytes 388
  55.8 5.0 %copy-start.2 = (bf16[32,16384]{1,0:T(8,128)(2,1)}, bf16[32,16384]{1,0:T(8,128)(2,1)S(1)}, u32[]{:S(2)}) copy-start(bf16[32,16384]{1,0:T(8,128)(2,1)S(1)} %collective-permute-done.2.w1_ref) | copy-start | bytes 3145732
  55.8 41.7 %collective-permute-start.7 = (bf16[32,16384]{1,0:T(8,128)(2,1)}, bf16[32,16384]{1,0:T(8,128)(2,1)S(1)}, u32[]{:S(2)}, u32[]{:S(2)}) collective-permute-start(bf16[32,16384]{1,0:T(8,128)(2,1)} %collective-permute-done.x1_ref), channel_id=1, source_target_pairs={{8,16},{9,17},{10,18},{11,19},{12,20},{13,21},{14,22},{15,23},{16,... | collective-permute-start | bytes 3145736 | tf_op jit(solution)/shard_map/ppermute | solution.py:543
  56.6 41.0 %collective-permute-start.8 = (bf16[32,16384]{1,0:T(8,128)(2,1)S(1)}, bf16[32,16384]{1,0:T(8,128)(2,1)S(1)}, u32[]{:S(2)}, u32[]{:S(2)}) collective-permute-start(bf16[32,16384]{1,0:T(8,128)(2,1)S(1)} %collective-permute-done.2.w1_ref), channel_id=1, source_target_pairs={{8,16},{9,17},{10,18},{11,19},{12,20},{13,21},{14,22},{15,23},{16,... | collective-permute-start | bytes 3145736 | tf_op jit(solution)/shard_map/ppermute | solution.py:545
  57.3 40.3 %collective-permute-start.5 = (bf16[32,16384]{1,0:T(8,128)(2,1)}, bf16[32,16384]{1,0:T(8,128)(2,1)S(1)}, u32[]{:S(2)}, u32[]{:S(2)}) collective-permute-start(bf16[32,16384]{1,0:T(8,128)(2,1)} %collective-permute-done.1), channel_id=1, source_target_pairs={{8,0},{9,1},{10,2},{11,3},{12,4},{13,5},{14,6},{15,7},{16,24},{17,... | collective-permute-start | bytes 3145736 | tf_op jit(solution)/shard_map/ppermute | solution.py:542
  58.6 49.4 %collective-permute-start.6 = (bf16[32,16384]{1,0:T(8,128)(2,1)}, bf16[32,16384]{1,0:T(8,128)(2,1)S(1)}, u32[]{:S(2)}, u32[]{:S(2)}) collective-permute-start(bf16[32,16384]{1,0:T(8,128)(2,1)} %collective-permute-done.3), channel_id=1, source_target_pairs={{8,0},{9,1},{10,2},{11,3},{12,4},{13,5},{14,6},{15,7},{16,24},{17,... | collective-permute-start | bytes 3145736 | tf_op jit(solution)/shard_map/ppermute | solution.py:544
  97.6 10.4 %copy-start.3 = (bf16[32,16384]{1,0:T(8,128)(2,1)}, bf16[32,16384]{1,0:T(8,128)(2,1)S(1)}, u32[]{:S(2)}) copy-start(bf16[32,16384]{1,0:T(8,128)(2,1)S(1)} %collective-permute-done.7.xi) | copy-start | bytes 3145732
  97.6 10.4 %copy-start.4 = (bf16[32,16384]{1,0:T(8,128)(2,1)}, bf16[32,16384]{1,0:T(8,128)(2,1)S(1)}, u32[]{:S(2)}) copy-start(bf16[32,16384]{1,0:T(8,128)(2,1)S(1)} %collective-permute-done.8.wi) | copy-start | bytes 3145732
  97.6 10.4 %copy-start.5 = (bf16[32,16384]{1,0:T(8,128)(2,1)}, bf16[32,16384]{1,0:T(8,128)(2,1)S(1)}, u32[]{:S(2)}) copy-start(bf16[32,16384]{1,0:T(8,128)(2,1)S(1)} %collective-permute-done.5.xo) | copy-start | bytes 3145732
  108.0 1.0 copy-start.6
  114.0 64.2 %all-to-all-start = ((bf16[8,2,8,16384]{3,2,1,0:T(8,128)(2,1)}), bf16[8,2,8,16384]{3,2,1,0:T(8,128)(2,1)}, u32[]{:S(2)}, u32[]{:S(2)}) async-start(bf16[8,2,8,16384]{3,2,1,0:T(8,128)(2,1)} %far_pack.1.after_ref), calls=%async_computation | async-start | bytes 8388608 | tf_op jit(solution)/shard_map/all_to_all | solution.py:530
  192.5 5.5 %collective-permute-start.9 = (f32[64,128]{1,0:T(8,128)}, f32[64,128]{1,0:T(8,128)S(1)}, u32[]{:S(2)}, u32[]{:S(2)}) collective-permute-start(f32[64,128]{1,0:T(8,128)} %get-tuple-element.20), channel_id=1, source_target_pairs={{0,8},{1,9},{2,10},{3,11},{4,12},{5,13},{6,14},{7,15},{8,0},{9,1},... | collective-permute-start | bytes 98312 | tf_op jit(solution)/shard_map/ppermute | solution.py:553
  192.5 13.7 %all-to-all-start.2 = ((f32[32,8,128]{2,1,0:T(8,128)}), f32[32,8,128]{2,1,0:T(8,128)S(1)}, u32[]{:S(2)}, u32[]{:S(2)}) async-start(f32[32,8,128]{2,1,0:T(8,128)} %bitcast.21), calls=%async_computation.2 | async-start | bytes 262144 | tf_op jit(solution)/shard_map/all_to_all | solution.py:561

commit v10 on v6

--- a/solution.py
+++ b/solution.py
@@ -11,7 +11,7 @@
 NOPS = 4
 LANES = 128
 SLAB = 2 * SUB
-VMEM_LIMIT = 56 * 1024 * 1024
+MIB = 1024 * 1024
 PLANES = 4
 PLANE = 8
 UNROLL = 64
@@ -19,7 +19,7 @@
 
 
 def params():
-    return pltpu.CompilerParams(vmem_limit_bytes=VMEM_LIMIT)
+    return pltpu.CompilerParams(vmem_limit_bytes=56 * MIB)
 
 
 def pack_kernel(pick_ref, x_ref, obs_ref, qw_ref, send_ref, w_ref, slabs, sems):
@@ -252,22 +252,26 @@
     send_slabs(slabs, pick_ref, send_ref, sems)
 
 
-def far_pack_kernel(pick_ref, outer_ref, inner_ref, after_ref, send_ref, slabs, sems):
+def far_pack_kernel(pick_ref, *refs):
+    outer, inner = refs[:HALVES], refs[HALVES : 2 * HALVES]
+    send_ref, slabs, sems = refs[2 * HALVES + 1 :]
     plane = lax.div(lax.axis_index("dp"), PLANE)
-    inner = (plane == 1) | (plane == 2)
-
-    @pl.when(inner)
+    is_inner = (plane == 1) | (plane == 2)
+
+    @pl.when(is_inner)
     def _():
-        fill_slabs(slabs, inner_ref, 0)
-
-    @pl.when(jnp.logical_not(inner))
+        for part, ref in enumerate(inner):
+            fill_slabs(slabs, ref, part * ref.shape[1])
+
+    @pl.when(jnp.logical_not(is_inner))
     def _():
-        fill_slabs(slabs, outer_ref, 0)
+        for part, ref in enumerate(outer):
+            fill_slabs(slabs, ref, part * ref.shape[1])
 
     send_slabs(slabs, pick_ref, send_ref, sems)
 
 
-def pack_call(kernel, name, specs, blk, width, *operands):
+def pack_call(kernel, name, specs, blk, width, weight, *operands):
     return pl.pallas_call(
         kernel,
         out_shape=jax.ShapeDtypeStruct((PLANE, 2, SLAB, width), jnp.bfloat16),
@@ -276,7 +280,7 @@
         scratch_shapes=[pltpu.VMEM((blk // SUB, SLAB, width), jnp.bfloat16), pltpu.SemaphoreType.DMA((PLANE, 2))],
         compiler_params=params(),
         cost_estimate=pl.CostEstimate(
-            flops=blk * width * 4, bytes_accessed=(PLANE * 2 * SLAB * 2 + blk * 4) * width, transcendentals=0
+            flops=blk * width * 4, bytes_accessed=weight * (PLANE * 2 * SLAB * 2 + blk * 4) * width, transcendentals=0
         ),
         name=name,
     )(*operands)
@@ -285,53 +289,59 @@
 def own_pack(pick, halves):
     rows, width = halves[0].shape
     specs = [pl.BlockSpec(memory_space=pltpu.VMEM)] * HALVES
-    return pack_call(own_pack_kernel, "own_pack", specs, rows // 2, HALVES * width, pick, *halves)
+    return pack_call(own_pack_kernel, "own_pack", specs, rows // 2, HALVES * width, 1, pick, *halves)
 
 
 def far_pack(pick, outer, inner, after):
-    rows, width = outer.shape
-    specs = [pl.BlockSpec(memory_space=pltpu.VMEM)] * 2 + [pl.BlockSpec(memory_space=pl.ANY)]
-    return pack_call(far_pack_kernel, "far_pack", specs, rows // 2, width, pick, outer, inner, after)
-
-
-def place_kernel(joined, ops_ref, *refs):
-    blocks, refs = refs[: 2 * HALVES], refs[2 * HALVES :]
-    other_ref, outs, (table, target) = refs[0], refs[2 if joined else 1 : -2], refs[-2:]
+    rows, width = outer[0].shape
+    specs = [pl.BlockSpec(memory_space=pltpu.VMEM)] * (2 * HALVES) + [pl.BlockSpec(memory_space=pl.ANY)]
+    return pack_call(
+        far_pack_kernel, "far_pack", specs, rows // 2, HALVES * width, 1, pick, *outer, *inner, after
+    )
+
+
+def place_kernel(ops_ref, *refs):
+    blocks, (after_ref, keep_ref, give_ref, table, *targets) = refs[: 2 * HALVES], refs[2 * HALVES :]
     rows, depth = blocks[0].shape
     blk = rows // 2
-    width = target.shape[0]
+    width = targets[0].shape[0]
     chunks = width // HALVES // depth
     step = min(512, width)
     size = min(256, depth)
-
-    def fill(mine_ref, near_ref):
+    now = pl.program_id(1)
+
+    def fill(one_ref, two_ref):
         diagonal = lax.broadcasted_iota(jnp.int32, (size, size), 0) == lax.broadcasted_iota(
             jnp.int32, (size, size), 1
         )
         identity = jnp.where(diagonal, 1.0, 0.0).astype(jnp.bfloat16)
         for i in range(depth // size):
             cols = slice(i * size, (i + 1) * size)
-            both = [mine_ref[:blk, cols], near_ref[:blk, cols], mine_ref[blk:, cols], near_ref[blk:, cols]]
+            four = [one_ref[:blk, cols], two_ref[:blk, cols], one_ref[blk:, cols], two_ref[blk:, cols]]
             table[cols, :] = lax.dot_general(
                 identity,
-                jnp.concatenate(both, 0),
+                jnp.concatenate(four, 0),
                 (((1,), (1,)), ((), ())),
                 preferred_element_type=jnp.float32,
             )
 
-    for part in range(HALVES):
-
-        @pl.when(lax.div(pl.program_id(0), chunks) == part)
+    for k, target in enumerate(targets):
+        for part in range(HALVES):
+            pair = (blocks[part], blocks[HALVES + part])
+
+            @pl.when((pl.program_id(0) == k) & (lax.div(now, chunks) == part))
+            def _():
+                fill(*(pair if k == 0 else pair[::-1]))
+
+        @pl.when(pl.program_id(0) == k)
         def _():
-            fill(blocks[part], blocks[HALVES + part])
-
-    @pl.loop(0, depth // UNROLL)
-    def _(i):
-        base = pl.multiple_of(i * UNROLL, UNROLL)
-        for j in range(UNROLL):
-            target[pl.ds(ops_ref[0, 0, base + j], 1), :] = table[pl.ds(base + j, 1), :]
-
-    @pl.when(pl.program_id(0) == pl.num_programs(0) - 1)
+            @pl.loop(0, depth // UNROLL)
+            def _(i):
+                base = pl.multiple_of(i * UNROLL, UNROLL)
+                for j in range(UNROLL):
+                    target[pl.ds(ops_ref[0, 0, base + j], 1), :] = table[pl.ds(base + j, 1), :]
+
+    @pl.when((pl.program_id(0) == pl.num_programs(0) - 1) & (now == pl.num_programs(1) - 1))
     def _():
         lane = lax.broadcasted_iota(jnp.int32, (step, LANES), 1)
         first = lax.rem(lane, 2 * blk) < blk
@@ -339,48 +349,37 @@
         @pl.loop(0, width // step)
         def _(i):
             here = pl.ds(pl.multiple_of(i * step, step), step)
-            values = target[here, :]
-            if joined:
-                earlier = other_ref[here, :].astype(jnp.float32)
-                keep = jnp.where(first, earlier, pltpu.roll(values, blk, 1))
-                give = jnp.where(first, pltpu.roll(earlier, LANES - blk, 1), values)
-                outs[0][here, :] = keep.astype(jnp.bfloat16)
-                outs[1][here, :] = give.astype(jnp.bfloat16)
-            else:
-                outs[0][here, :] = values.astype(jnp.bfloat16)
-
-
-def place(ops, which, mine, near, earlier, after, weight):
-    width = ops.shape[2]
-    rows, span = mine[0].shape
+            values = [target[here, :] for target in targets]
+            keep_ref[here, :] = jnp.where(first, *values).astype(jnp.bfloat16)
+            give_ref[here, :] = jnp.where(first, *values[::-1]).astype(jnp.bfloat16)
+
+
+def place(ops, one, two, after, weight):
+    count, _, width = ops.shape
+    rows, span = one[0].shape
     depth = min(2048, span)
     chunks = span // depth
     some = [
-        pl.BlockSpec((rows, depth), lambda i, part=part: (0, jnp.clip(i - part * chunks, 0, chunks - 1)))
+        pl.BlockSpec((rows, depth), lambda k, i, part=part: (0, jnp.clip(i - part * chunks, 0, chunks - 1)))
         for part in range(HALVES)
     ]
-    anywhere = pl.BlockSpec(memory_space=pl.ANY)
-    whole = pl.BlockSpec((width, LANES), lambda i: (0, 0))
-    joined = earlier is not None
-    count = 2 if joined else 1
-    outs = pl.pallas_call(
-        functools.partial(place_kernel, joined),
-        grid=(HALVES * chunks,),
-        out_shape=(jax.ShapeDtypeStruct((width, LANES), jnp.bfloat16),) * count,
+    whole = pl.BlockSpec((width, LANES), lambda k, i: (0, 0))
+    return pl.pallas_call(
+        place_kernel,
+        grid=(count, HALVES * chunks),
+        out_shape=(jax.ShapeDtypeStruct((width, LANES), jnp.bfloat16),) * 2,
         in_specs=[
-            pl.BlockSpec((1, 1, depth), lambda i: (which, 0, i), memory_space=pltpu.SMEM),
+            pl.BlockSpec((1, 1, depth), lambda k, i: (k, 0, i), memory_space=pltpu.SMEM),
             *some,
             *some,
-            whole if joined else anywhere,
-            *([anywhere] if joined else []),
+            pl.BlockSpec(memory_space=pl.ANY),
         ],
-        out_specs=(whole,) * count,
-        scratch_shapes=[pltpu.VMEM((depth, LANES), jnp.float32), pltpu.VMEM((width, LANES), jnp.float32)],
+        out_specs=(whole, whole),
+        scratch_shapes=[pltpu.VMEM((depth, LANES), jnp.float32)] + [pltpu.VMEM((width, LANES), jnp.float32)] * count,
         compiler_params=params(),
         cost_estimate=pl.CostEstimate(flops=0, bytes_accessed=weight * width * LANES, transcendentals=0),
         name="place",
-    )(ops, *mine, *near, *((earlier, after) if joined else (after,)))
-    return outs if joined else outs[0]
+    )(ops, *one, *two, after)
 
 
 def ratio(total_w, sum_x, sum_xx, sum_y, sum_xy, sum_yy):
@@ -390,39 +389,30 @@
     return numer / jnp.sqrt(var_x * var_y)
 
 
-def plane_sums_kernel(begun, ended, own_ref, far_ref, *refs):
-    moved_refs, (before_ref, *outs) = refs[:4], refs[4:]
-    acc = outs[-1]
-    rows, depth = own_ref.shape
+def plane_sums_kernel(ended, got_ref, *refs):
+    moved_refs, before, outs, acc = refs[:4], refs[4 : 4 + ended], refs[4 + ended : -1], refs[-1]
+    rows, depth = got_ref.shape
     step = min(1024, depth)
     half = LANES // 2
     slabs = rows // SLAB // 2
 
     @pl.when(pl.program_id(0) == 0)
     def _():
-        if begun:
-            acc[...] = before_ref[...]
-        else:
-            acc[...] = jnp.zeros_like(acc)
+        acc[...] = jnp.zeros_like(acc)
 
     for i in range(depth // step):
         cols = slice(i * step, (i + 1) * step)
         is_x = lax.broadcasted_iota(jnp.int32, (slabs, SLAB, step), 1) < SUB
-        weights, products = ([], []), ([], [])
-        for ref in (own_ref, far_ref):
-            full = ref[:, cols].astype(jnp.float32).reshape(slabs, 2, SLAB, step)
-            for t in range(2):
-                wide = full[:, t]
-                rolled = pltpu.roll(wide, SUB, 1)
-                product = wide * rolled
-                both = jnp.where(is_x, product * wide, product)
-                products[t].append(both.reshape(slabs * SLAB, step))
-                even = rolled.reshape(slabs // 2, 2, SLAB, step)[:, 0]
-                odd = wide.reshape(slabs // 2, 2, SLAB, step)[:, 1]
-                pair = jnp.where(is_x[: slabs // 2], even, odd)
-                weights[t].append(pair.reshape(slabs // 2 * SLAB, step))
         low = lax.broadcasted_iota(jnp.int32, (step, LANES), 1) < half
+        full = got_ref[:, cols].astype(jnp.float32).reshape(slabs, 2, SLAB, step)
         for t in range(2):
+            wide = full[:, t]
+            rolled = pltpu.roll(wide, SUB, 1)
+            product = wide * rolled
+            both = jnp.where(is_x, product * wide, product).reshape(slabs * SLAB, step)
+            even = rolled.reshape(slabs // 2, 2, SLAB, step)[:, 0]
+            odd = wide.reshape(slabs // 2, 2, SLAB, step)[:, 1]
+            weights = jnp.where(is_x[: slabs // 2], even, odd).reshape(slabs // 2 * SLAB, step)
             linear, square = [], []
             for a in range(2):
                 values = moved_refs[2 * t + a][cols, :].astype(jnp.float32)
@@ -431,19 +421,16 @@
                 linear.append(jnp.where(low, product, values).astype(jnp.bfloat16))
                 square.append(product * (values if a == 0 else swapped))
             right = jnp.concatenate(linear + [jnp.where(low, *square).astype(jnp.bfloat16)], 1)
-            left = jnp.concatenate(weights[t] + products[t], 0).astype(jnp.bfloat16)
+            left = jnp.concatenate([weights, both], 0).astype(jnp.bfloat16)
             acc[t] += jnp.dot(left, right, preferred_element_type=jnp.float32)
-
-    if not ended:
-        return
 
     @pl.when(pl.program_id(0) == pl.num_programs(0) - 1)
     def _():
-        near_ref, back_ref = outs[0], outs[1]
-        count = 2 * slabs * SUB
+        count = slabs * SUB
         tiles = count // SLAB
         top = lax.broadcasted_iota(jnp.int32, (tiles, SLAB, LANES), 1) < SUB
         low = lax.broadcasted_iota(jnp.int32, (count, LANES), 1) < half
+        early = lax.rem(lax.broadcasted_iota(jnp.int32, (count, LANES), 1), half) < half // 2
         me = lax.axis_index("dp")
         results = []
         for t in range(2):
@@ -464,52 +451,52 @@
                     )
                 )
             kept, got = ratios
+            got = jnp.where(early, pltpu.roll(got, LANES - half // 2, 1), pltpu.roll(got, half // 2, 1))
             straight = jnp.where(low, kept, pltpu.roll(got, half, 1))
             crossed = jnp.where(low, got, pltpu.roll(kept, half, 1))
             results.append(jnp.where(lax.rem(me, 2) == 0, straight, crossed))
-        mine, near = results
-        near_ref[...] = near
-        back_ref[0] = mine
-        back_ref[1] = near
-
-
-def plane_sums(part, own, far, moved, before):
-    rows, width = far.shape
+        if not ended:
+            for t in range(2):
+                outs[0][t] = results[t]
+            return
+        mine_ref, near_ref, back_ref = outs
+        upper = lax.div(me, 2 * PLANE)
+        for part, (mine, near) in enumerate(((before[0][0], before[0][1]), results)):
+            mine_ref[part] = mine
+            near_ref[part] = near
+            mine, near = mine.reshape(tiles, SLAB, LANES), near.reshape(tiles, SLAB, LANES)
+            slot = part + upper - 2 * part * upper
+            even = jnp.where(top, mine, pltpu.roll(near, SUB, 1))
+            odd = jnp.where(top, pltpu.roll(mine, SUB, 1), near)
+            for i in range(tiles):
+                for twin in range(2):
+                    back_ref[slot, twin, 2 * i] = even[i]
+                    back_ref[slot, twin, 2 * i + 1] = odd[i]
+
+
+def plane_sums(got, moved, before):
+    rows, width = got.shape
     depth = min(2048, width)
-    chunks = width // depth
-    begun, ended = before is not None, part == HALVES - 1
-    total = (2, 2 * rows * 3 // 4, 3 * LANES)
-    count = rows // 2
-    placed = pl.BlockSpec((depth, LANES), lambda i: (part * chunks + i, 0))
-    entire = pl.BlockSpec(total, lambda i: (0, 0, 0))
-    if ended:
-        shapes = ((count, LANES), (2, count, LANES))
-        out_specs = (pl.BlockSpec(shapes[0], lambda i: (0, 0)), pl.BlockSpec(shapes[1], lambda i: (0, 0, 0)))
-    else:
-        shapes, out_specs = (total,), (entire,)
+    ended = before is not None
+    count = rows // 4
+    placed = pl.BlockSpec((depth, LANES), lambda i: (i, 0))
+    result = (2, count, LANES)
+    shapes = (result, result, (2, 2, PLANE, SLAB, LANES)) if ended else (result,)
+    entire = [pl.BlockSpec(shape, lambda i, shape=shape: (0,) * len(shape)) for shape in shapes]
     outs = pl.pallas_call(
-        functools.partial(plane_sums_kernel, begun, ended),
-        grid=(chunks,),
+        functools.partial(plane_sums_kernel, ended),
+        grid=(width // depth,),
         out_shape=tuple(jax.ShapeDtypeStruct(shape, jnp.float32) for shape in shapes),
-        in_specs=[
-            pl.BlockSpec((rows, depth), lambda i: (0, part * chunks + i)),
-            pl.BlockSpec((rows, depth), lambda i: (0, i)),
-            placed,
-            placed,
-            placed,
-            placed,
-            entire if begun else pl.BlockSpec(memory_space=pl.ANY),
-        ],
-        out_specs=out_specs,
-        scratch_shapes=[pltpu.VMEM(total, jnp.float32)] if ended else [],
+        in_specs=[pl.BlockSpec((rows, depth), lambda i: (0, i)), placed, placed, placed, placed]
+        + ([entire[0]] if ended else []),
+        out_specs=tuple(entire),
+        scratch_shapes=[pltpu.VMEM((2, 3 * count, 3 * LANES), jnp.float32)],
         compiler_params=params(),
         cost_estimate=pl.CostEstimate(
-            flops=18 * rows * width * LANES,
-            bytes_accessed=width * (4 * rows + 8 * LANES),
-            transcendentals=0,
+            flops=9 * rows * width * LANES, bytes_accessed=width * (2 * rows + 8 * LANES), transcendentals=0
         ),
         name="plane_sums",
-    )(own, far, *moved, before if begun else far)
+    )(got, *moved, *((before,) if ended else ()))
     return outs if ended else outs[0]
 
 
@@ -538,41 +525,31 @@
     other = [lax.ppermute(rows, "dp", swap) for rows in mine]
     far_pick = lax.ppermute(own_pick, "dp", across)
 
-    own_send = own_pack(own_pick, mine)
-    own_send, other = lax.optimization_barrier((own_send, other))
-    own_got = spread(own_send)
-    placed = place(ops, 0, mine, other, None, own_pick, 4)
-    keep, give = place(ops, 1, mine, other, placed, own_pick, 4)
+    own_got = spread(own_pack(own_pick, mine))
+    keep, give = place(ops, mine, other, own_pick, 4)
     own_moved = [keep, lax.ppermute(give, "dp", swap)]
 
     near, mid, far_pick, keep = lax.optimization_barrier((near, mid, far_pick, keep))
     own_moved[0] = keep
+    outer = [lax.ppermute(rows, "dp", outward) for rows in mid]
+    inner = [lax.ppermute(rows, "dp", middle) for rows in near]
     near_other = [lax.ppermute(rows, "dp", swap) for rows in near]
-    outer_0 = lax.ppermute(mid[0], "dp", outward)
-    inner_0 = lax.ppermute(near[0], "dp", middle)
-    placed = place(ops, 0, near, near_other, None, own_got, 32)
-    outer_0, inner_0, mid_1, near_1 = lax.optimization_barrier((outer_0, inner_0, mid[1], near[1]))
-    outer_1 = lax.ppermute(mid_1, "dp", outward)
-    inner_1 = lax.ppermute(near_1, "dp", middle)
-    far_send_0 = far_pack(far_pick, outer_0, inner_0, placed)
-    far_got_0 = spread(far_send_0)
-    keep, give = place(ops, 1, near, near_other, placed, far_send_0, 32)
-    far_send_1 = far_pack(far_pick, outer_1, inner_1, keep)
+    keep, give = place(ops, near, near_other, own_pick, 256)
+    far_send = far_pack(far_pick, outer, inner, keep)
+    far_send, give = lax.optimization_barrier((far_send, give))
+    far_got = spread(far_send)
     moved = own_moved + [keep, lax.ppermute(give, "dp", swap)]
-    far_got_1 = spread(far_send_1)
-    sums = plane_sums(0, own_got, far_got_0, moved, None)
-    theirs, both = plane_sums(1, own_got, far_got_1, moved, sums)
-    both = both.reshape(2, 2, PLANE, SUB, NOPS * blk)
-
-    from_near = lax.ppermute(theirs, "dp", beside).reshape(2, PLANE, SUB, NOPS * blk)
-    pair = jnp.stack([both[0], from_near], 1)
+    own_corr = plane_sums(own_got, moved, None)
+    ours, theirs, back = plane_sums(far_got, moved, own_corr)
+
+    from_near = lax.ppermute(theirs, "dp", beside)
+    pair = [each.reshape(2, PLANE, SUB, NOPS * blk) for each in (ours, from_near)]
+    pair = jnp.stack(pair, 1)
     pair = jnp.where(odd, pair[:, ::-1], pair)
     pair = jnp.where(upper, pair[::-1], pair)
     corr = pair.reshape(groups * SUB, NOPS * blk).T.reshape(NOPS, blk, groups * SUB)
 
-    both = jnp.transpose(both, (1, 2, 0, 3, 4))
-    both = jnp.where(upper, both[::-1], both).reshape(2, 1, PLANE, 2 * SUB, NOPS * blk)
-    back = jnp.broadcast_to(both, (2, 2, PLANE, 2 * SUB, NOPS * blk)).reshape(groups, 2 * SUB, NOPS * blk)
+    back = back.reshape(groups, 2 * SUB, NOPS * blk)
     back = lax.all_to_all(back, "dp", split_axis=0, concat_axis=0, tiled=True)
     back = back.reshape(2, 2, PLANE, 2, SUB, NOPS, blk)
     back = jnp.where(odd, back[:, 1, :, ::-1], back[:, 0])

time: 260 us -> 217 us (0.83)
  waiting for transfers between devices: 76.4 us -> 46.7 us
  Pallas kernels: 139 us -> 132 us
  local copies, waits for them, and re-layouts: 8.47 us -> 4.49 us
  starting transfers between devices: 33.9 us -> 30.8 us
    ppermute x5, waiting for transfers between devices: 52.4 us -> 3.48 us  [the longest x2 3.47 us: shards_by_plane(): outer = [lax.ppermute(rows, 'dp', outward) for rows in mid]]
    all_to_all x3 -> x2, waiting for transfers between devices: 16.6 us -> 30.9 us  [spread(): lax.all_to_all(send, 'dp', split_axis=0, concat_axis=0, axis_index_groups...]
    pallas_call x6 -> x4, Pallas kernels: 121 us -> 115 us  [the longest x2 84.2 us: place(): pl.pallas_call(place_kernel, grid=(count, HALVES * chunks), out_shape=(ja...]
    all_to_all x3 -> x2, starting transfers between devices: 13.8 us -> 9.3 us  [spread(): lax.all_to_all(send, 'dp', split_axis=0, concat_axis=0, axis_index_groups...]
    ppermute x1, starting transfers between devices: 5.58 us -> 1.73 us  [shards_by_plane(): far_pick = lax.ppermute(own_pick, 'dp', across)]
    ppermute x2, starting transfers between devices: 2.57 us -> 6.03 us  [shards_by_plane(): near = [lax.ppermute(rows, 'dp', beside) for rows in mine]]
    ppermute x1, waiting for transfers between devices: 0.01 us -> 2.85 us  [shards_by_plane(): moved = own_moved + [keep, lax.ppermute(give, 'dp', swap)]]
    ppermute x2, waiting for transfers between devices: 0.01 us -> 2.76 us  [shards_by_plane(): other = [lax.ppermute(rows, 'dp', swap) for rows in mine]]
  transfers between devices with their start and end apart: 20 -> 19, of which waited for: 4 -> 5; matrix products, arithmetic and copies ran while one was open for 1% -> 1% of each run, Pallas kernels for 48% -> 52%
where the time goes in v10:
time: 217 us; the launch traced here: 216 us
  Pallas kernels  132 us (61%)
  waiting for transfers between devices  46.7 us (22%)
  starting transfers between devices  30.8 us (14%)
  local copies, waits for them, and re-layouts  4.49 us (2%)
    pallas_call x2, Pallas kernels, place(): pl.pallas_call(place_kernel, grid=(count, HALVES * chunks), out_shape=(ja...  84.2 us
    pallas_call x2, Pallas kernels, plane_sums(): pl.pallas_call(functools.partial(plane_sums_kernel, ended), grid=(width /...  30.9 us
    all_to_all x2, waiting for transfers between devices, spread(): lax.all_to_all(send, 'dp', split_axis=0, concat_axis=0, axis_index_groups...  30.9 us
    pallas_call x2, Pallas kernels, pack_call(): pl.pallas_call(kernel, out_shape=jax.ShapeDtypeStruct((PLANE, 2, SLAB, wi...  9.33 us
    all_to_all x2, starting transfers between devices, spread(): lax.all_to_all(send, 'dp', split_axis=0, concat_axis=0, axis_index_groups...  9.3 us
    pallas_call x2, Pallas kernels, weigh(): pl.pallas_call(weigh_kernel, grid=(count,), out_shape=jax.ShapeDtypeStruc...  7.31 us
    all_to_all x1, waiting for transfers between devices, shards_by_plane(): back = lax.all_to_all(back, 'dp', split_axis=0, concat_axis=0, tiled=True)  6.66 us
    ppermute x2, starting transfers between devices, shards_by_plane(): near = [lax.ppermute(rows, 'dp', beside) for rows in mine]  6.03 us
  transfers between devices with their start and end apart: 19, of which 5 were waited for; matrix products, arithmetic and copies ran while one was open for 1% of the time, Pallas kernels for 52%

profile of v10, /device:TPU:0, one launch (start us, length us, event | category | flops | bytes accessed | tf_op | source)
XLA Modules:
  0.0 216.3 jit_solution(7610957272927422388)
XLA Ops:
  0.6 0.0 copy-start
  0.6 3.7 %weigh.2.refs_0_ = bf16[64,8192]{1,0:T(8,128)(2,1)} custom-call(bf16[32,16384]{1,0:T(8,128)(2,1)} %x_ref.3, s32[32,16384]{1,0:T(8,128)} %obs_ref.3, bf16[32,16384]{1,0:T(8,128)(2,1)} %qw_ref.3), custom_call_target="tpu_custom_call" | custom-call | flops 524288 | bytes 3145728 | tf_op jit(solution)/shard_map/weigh/pallas_call | solution.py:206
  4.3 0.5 collective-permute-start.5
  4.8 2.6 %collective-permute-start = (bf16[64,8192]{1,0:T(8,128)(2,1)}, bf16[64,8192]{1,0:T(8,128)(2,1)S(1)}, u32[]{:S(2)}, u32[]{:S(2)}) collective-permute-start(bf16[64,8192]{1,0:T(8,128)(2,1)} %weigh.2.refs_0_), channel_id=1, source_target_pairs={{0,8},{1,9},{2,10},{3,11},{4,12},{5,13},{6,14},{7,15},{8,0},{9,1},... | collective-permute-start | bytes 3145736 | tf_op jit(solution)/shard_map/ppermute | solution.py:523
  7.3 1.6 collective-permute-start.2
  9.0 3.7 %weigh.3.refs_1_ = bf16[64,8192]{1,0:T(8,128)(2,1)} custom-call(bf16[32,16384]{1,0:T(8,128)(2,1)} %x_ref.3, s32[32,16384]{1,0:T(8,128)} %obs_ref.3, bf16[32,16384]{1,0:T(8,128)(2,1)} %qw_ref.3), custom_call_target="tpu_custom_call" | custom-call | flops 524288 | bytes 3145728 | tf_op jit(solution)/shard_map/weigh/pallas_call | solution.py:206
  12.6 3.5 %collective-permute-start.1 = (bf16[64,8192]{1,0:T(8,128)(2,1)}, bf16[64,8192]{1,0:T(8,128)(2,1)S(1)}, u32[]{:S(2)}, u32[]{:S(2)}) collective-permute-start(bf16[64,8192]{1,0:T(8,128)(2,1)} %weigh.3.refs_1_), channel_id=1, source_target_pairs={{0,8},{1,9},{2,10},{3,11},{4,12},{5,13},{6,14},{7,15},{8,0},{9,1},... | collective-permute-start | bytes 3145736 | tf_op jit(solution)/shard_map/ppermute | solution.py:523
  16.1 1.6 collective-permute-start.3
  17.7 4.3 %own_pack.1 = bf16[8,2,8,16384]{3,2,1,0:T(8,128)(2,1)} custom-call(s32[32]{0:T(128)} %bitcast.25, bf16[64,8192]{1,0:T(8,128)(2,1)} %weigh.2.refs_0_, bf16[64,8192]{1,0:T(8,128)(2,1)} %weigh.3.refs_1_), custom_call_target="tpu_custom_call" | custom-call | flops 2097152 | bytes 6291456 | tf_op jit(solution)/shard_map/own_pack/pallas_call | solution.py:275
  22.0 0.0 copy-start.11
  22.1 4.7 %all-to-all-start.1 = ((bf16[8,2,8,16384]{3,2,1,0:T(8,128)(2,1)}), bf16[8,2,8,16384]{3,2,1,0:T(8,128)(2,1)}, u32[]{:S(2)}, u32[]{:S(2)}) async-start(bf16[8,2,8,16384]{3,2,1,0:T(8,128)(2,1)} %own_pack.1), calls=%async_computation.1 | async-start | bytes 8388608 | tf_op jit(solution)/shard_map/all_to_all | solution.py:516
  26.8 0.0 collective-permute-done.5.refs_2_
  26.8 0.4 collective-permute-start.6
  27.2 0.0 copy-done
  27.2 0.1 constant_dynamic-slice_fusion
  27.3 2.8 %collective-permute-done.6.refs_3_ = bf16[64,8192]{1,0:T(8,128)(2,1)S(1)} collective-permute-done((bf16[64,8192]{1,0:T(8,128)(2,1)S(1)}, bf16[64,8192]{1,0:T(8,128)(2,1)S(1)}, u32[]{:S(2)}, u32[]{:S(2)}) %collective-permute-start.6) | collective-permute-done | bytes 1048608 | tf_op jit(solution)/shard_map/ppermute | solution.py:525
  30.0 1.7 collective-permute-start.4
  31.8 0.7 broadcast_in_dim.3.ops_ref
  32.5 42.1 %place.2 = (bf16[16384,128]{1,0:T(8,128)(2,1)}, bf16[16384,128]{1,0:T(8,128)(2,1)}) custom-call(s32[2,1,16384]{2,1,0:T(1,128)} %broadcast_in_dim.3.ops_ref, bf16[64,8192]{1,0:T(8,128)(2,1)} %weigh.2.refs_0_, bf16[64,8192]{1,0:T(8,128)(2,1)} %weigh.3.refs_1_, bf16[64,8192]{1,0:T(8,128)(2,1)} %collective-permute-done.5.refs_2_, bf16[64,8192]{1,0:T(8,128)(2,1)} %copy-done.10, ...), custom_call_target="tpu_custom_call" | custom-call | bytes 8388608 | tf_op jit(solution)/shard_map/place/pallas_call | solution.py:367
  74.6 0.0 collective-permute-done.4.pick_ref
  74.6 0.0 collective-permute-done.refs_0_
  74.6 0.0 collective-permute-done.1.refs_1_
  74.6 0.0 copy-start.3
  74.6 0.0 collective-permute-done.2
  74.6 0.0 collective-permute-done.3
  74.6 0.1 collective-permute-start.11
  74.7 0.5 collective-permute-start.12
  75.2 0.7 collective-permute-start.9
  75.9 1.3 collective-permute-start.7
  77.2 1.3 collective-permute-start.8
  78.5 0.0 collective-permute-done.11.refs_2_
  78.6 0.0 copy-start.7
  78.6 0.7 collective-permute-start.10
  79.3 0.0 collective-permute-done.12.refs_3_
  79.3 1.0 copy-done.9
  80.3 0.1 collective-permute-start.13
  80.4 0.0 copy-done.2
  80.4 0.0 copy-done.7
  80.4 42.1 %place.3 = (bf16[16384,128]{1,0:T(8,128)(2,1)}, bf16[16384,128]{1,0:T(8,128)(2,1)}) custom-call(s32[2,1,16384]{2,1,0:T(1,128)} %broadcast_in_dim.3.ops_ref, bf16[64,8192]{1,0:T(8,128)(2,1)} %copy-done.2, bf16[64,8192]{1,0:T(8,128)(2,1)} %copy-done.3, bf16[64,8192]{1,0:T(8,128)(2,1)} %copy-done.7, bf16[64,8192]{1,0:T(8,128)(2,1)} %copy-done.9, s32[32]{0:T(128)} %bitcast.27), custom_call_target="tpu_custom_call" | custom-call | bytes 536870912 | tf_op jit(solution)/shard_map/place/pallas_call | solution.py:367
  122.5 0.0 collective-permute-done.7.refs_0_
  122.5 3.5 %collective-permute-done.8.refs_1_ = bf16[64,8192]{1,0:T(8,128)(2,1)S(1)} collective-permute-done((bf16[64,8192]{1,0:T(8,128)(2,1)}, bf16[64,8192]{1,0:T(8,128)(2,1)S(1)}, u32[]{:S(2)}, u32[]{:S(2)}) %collective-permute-start.8) | collective-permute-done | bytes 1048608 | tf_op jit(solution)/shard_map/ppermute | solution.py:534
  126.0 0.0 collective-permute-done.9.refs_2_
  126.0 0.0 collective-permute-done.10.refs_3_
  126.0 0.9 copy-done.6
  127.0 0.3 copy-done.4
  127.3 0.3 copy-done.8
  127.6 5.0 %far_pack.1 = bf16[8,2,8,16384]{3,2,1,0:T(8,128)(2,1)} custom-call(s32[32]{0:T(128)} %copy-done.12, bf16[64,8192]{1,0:T(8,128)(2,1)} %copy-done.5, bf16[64,8192]{1,0:T(8,128)(2,1)} %copy-done.6, bf16[64,8192]{1,0:T(8,128)(2,1)} %copy-done.4, bf16[64,8192]{1,0:T(8,128)(2,1)} %copy-done.8, bf16[16384,128]{1,0:T(8,128)(2,1)} %get-tuple-element.23.refs_4_.refs_2_), custom_call_target="tpu_custom_call" | custom-call | flops 2097152 | bytes 6291456 | tf_op jit(solution)/shard_map/far_pack/pallas_call | solution.py:275
  132.6 0.1 collective-permute-start.14
  132.7 0.0 all-to-all-done.1
  132.7 4.6 %all-to-all-start = ((bf16[8,2,8,16384]{3,2,1,0:T(8,128)(2,1)}), bf16[8,2,8,16384]{3,2,1,0:T(8,128)(2,1)}, u32[]{:S(2)}, u32[]{:S(2)}) async-start(bf16[8,2,8,16384]{3,2,1,0:T(8,128)(2,1)} %far_pack.1), calls=%async_computation | async-start | bytes 8388608 | tf_op jit(solution)/shard_map/all_to_all | solution.py:516
  137.3 0.0 collective-permute-done.13.refs_1_
  137.3 2.9 %collective-permute-done.14.refs_3_ = bf16[16384,128]{1,0:T(8,128)(2,1)} collective-permute-done((bf16[16384,128]{1,0:T(8,128)(2,1)}, bf16[16384,128]{1,0:T(8,128)(2,1)}, u32[]{:S(2)}, u32[]{:S(2)}) %collective-permute-start.14) | collective-permute-done | bytes 4194336 | tf_op jit(solution)/shard_map/ppermute | solution.py:541
  140.2 15.3 %plane_sums.2.refs_4_ = f32[2,32,128]{2,1,0:T(8,128)} custom-call(bf16[128,16384]{1,0:T(8,128)(2,1)} %bitcast.2.got_ref, bf16[16384,128]{1,0:T(8,128)(2,1)} %get-tuple-element.26.refs_0_, bf16[16384,128]{1,0:T(8,128)(2,1)} %collective-permute-done.13.refs_1_, bf16[16384,128]{1,0:T(8,128)(2,1)} %get-tuple-element.23.refs_4_.refs_2_, ...), custom_call_target="tpu_custom_call" | custom-call | flops 2415919104 | bytes 20971520 | tf_op jit(solution)/shard_map/plane_sums/pallas_call | solution.py:486
  155.5 30.9 %all-to-all-done = bf16[8,2,8,16384]{3,2,1,0:T(8,128)(2,1)} async-done(((bf16[8,2,8,16384]{3,2,1,0:T(8,128)(2,1)}), bf16[8,2,8,16384]{3,2,1,0:T(8,128)(2,1)}, u32[]{:S(2)}, u32[]{:S(2)}) %all-to-all-start) | async-done | bytes 4194336 | tf_op jit(solution)/shard_map/all_to_all | solution.py:516
  186.4 15.6 %plane_sums.3 = (f32[2,32,128]{2,1,0:T(8,128)}, f32[2,32,128]{2,1,0:T(8,128)}, f32[2,2,8,8,128]{4,3,2,1,0:T(8,128)}) custom-call(bf16[128,16384]{1,0:T(8,128)(2,1)} %bitcast.1.got_ref, bf16[16384,128]{1,0:T(8,128)(2,1)} %get-tuple-element.26.refs_0_, bf16[16384,128]{1,0:T(8,128)(2,1)} %collective-permute-done.13.refs_1_, ...), custom_call_target="tpu_custom_call" | custom-call | flops 2415919104 | bytes 20971520 | tf_op jit(solution)/shard_map/plane_sums/pallas_call | solution.py:486
  202.1 1.5 collective-permute-start.15
  203.6 3.3 %all-to-all-start.2 = ((f32[32,8,128]{2,1,0:T(8,128)}), f32[32,8,128]{2,1,0:T(8,128)S(1)}, u32[]{:S(2)}, u32[]{:S(2)}) async-start(f32[32,8,128]{2,1,0:T(8,128)} %bitcast.21), calls=%async_computation.2 | async-start | bytes 262144 | tf_op jit(solution)/shard_map/all_to_all | solution.py:553
  206.9 0.0 collective-permute-done.15
  206.9 0.8 pad_maximum_fusion
  207.7 0.7 copy.16
  208.5 6.7 %all-to-all-done.2 = f32[32,8,128]{2,1,0:T(8,128)S(1)} async-done(((f32[32,8,128]{2,1,0:T(8,128)}), f32[32,8,128]{2,1,0:T(8,128)S(1)}, u32[]{:S(2)}, u32[]{:S(2)}) %all-to-all-start.2) | async-done | bytes 131104 | tf_op jit(solution)/shard_map/all_to_all | solution.py:553
  215.1 0.3 reshape.32
  215.4 0.1 copy.19
  215.5 0.8 copy_select_fusion
  (18 shorter events, 0.1 us)
Async XLA Ops:
  0.6 26.6 %copy-start = (s32[4,16384]{1,0:T(4,128)S(1)}, s32[4,16384]{1,0:T(4,128)}, u32[]{:S(2)}) copy-start(s32[4,16384]{1,0:T(4,128)} %param.8) | copy-start | bytes 786436
  4.3 22.5 %collective-permute-start.5 = (bf16[64,8192]{1,0:T(8,128)(2,1)}, bf16[64,8192]{1,0:T(8,128)(2,1)}, u32[]{:S(2)}, u32[]{:S(2)}) collective-permute-start(bf16[64,8192]{1,0:T(8,128)(2,1)} %weigh.2.refs_0_), channel_id=1, source_target_pairs={{0,1},{1,0},{2,3},{3,2},{4,5},{5,4},{6,7},{7,6},{8,9},{9,8},{10,11... | collective-permute-start | bytes 3145736 | tf_op jit(solution)/shard_map/ppermute | solution.py:525
  4.8 69.8 %collective-permute-start = (bf16[64,8192]{1,0:T(8,128)(2,1)}, bf16[64,8192]{1,0:T(8,128)(2,1)S(1)}, u32[]{:S(2)}, u32[]{:S(2)}) collective-permute-start(bf16[64,8192]{1,0:T(8,128)(2,1)} %weigh.2.refs_0_), channel_id=1, source_target_pairs={{0,8},{1,9},{2,10},{3,11},{4,12},{5,13},{6,14},{7,15},{8,0},{9,1},... | collective-permute-start | bytes 3145736 | tf_op jit(solution)/shard_map/ppermute | solution.py:523
  7.3 67.3 %collective-permute-start.2 = (bf16[64,8192]{1,0:T(8,128)(2,1)}, bf16[64,8192]{1,0:T(8,128)(2,1)}, u32[]{:S(2)}, u32[]{:S(2)}) collective-permute-start(bf16[64,8192]{1,0:T(8,128)(2,1)} %weigh.2.refs_0_), channel_id=1, source_target_pairs={{8,16},{9,17},{10,18},{11,19},{12,20},{13,21},{14,22},{15,23},{16,... | collective-permute-start | bytes 3145736 | tf_op jit(solution)/shard_map/ppermute | solution.py:524
  12.6 62.0 %collective-permute-start.1 = (bf16[64,8192]{1,0:T(8,128)(2,1)}, bf16[64,8192]{1,0:T(8,128)(2,1)S(1)}, u32[]{:S(2)}, u32[]{:S(2)}) collective-permute-start(bf16[64,8192]{1,0:T(8,128)(2,1)} %weigh.3.refs_1_), channel_id=1, source_target_pairs={{0,8},{1,9},{2,10},{3,11},{4,12},{5,13},{6,14},{7,15},{8,0},{9,1},... | collective-permute-start | bytes 3145736 | tf_op jit(solution)/shard_map/ppermute | solution.py:523
  16.1 58.6 %collective-permute-start.3 = (bf16[64,8192]{1,0:T(8,128)(2,1)}, bf16[64,8192]{1,0:T(8,128)(2,1)}, u32[]{:S(2)}, u32[]{:S(2)}) collective-permute-start(bf16[64,8192]{1,0:T(8,128)(2,1)} %weigh.3.refs_1_), channel_id=1, source_target_pairs={{8,16},{9,17},{10,18},{11,19},{12,20},{13,21},{14,22},{15,23},{16,... | collective-permute-start | bytes 3145736 | tf_op jit(solution)/shard_map/ppermute | solution.py:524
  22.0 4.8 %copy-start.1 = (bf16[64,8192]{1,0:T(8,128)(2,1)S(1)}, bf16[64,8192]{1,0:T(8,128)(2,1)}, u32[]{:S(2)}) copy-start(bf16[64,8192]{1,0:T(8,128)(2,1)} %weigh.3.refs_1_) | copy-start | bytes 3145732
  22.0 8.0 %copy-start.11 = (s32[32,1]{0,1:T(1,128)S(1)}, s32[32,1]{0,1:T(1,128)}, u32[]{:S(2)}) copy-start(s32[32,1]{0,1:T(1,128)} %param.9) | copy-start | bytes 388
  22.1 110.6 %all-to-all-start.1 = ((bf16[8,2,8,16384]{3,2,1,0:T(8,128)(2,1)}), bf16[8,2,8,16384]{3,2,1,0:T(8,128)(2,1)}, u32[]{:S(2)}, u32[]{:S(2)}) async-start(bf16[8,2,8,16384]{3,2,1,0:T(8,128)(2,1)} %own_pack.1), calls=%async_computation.1 | async-start | bytes 8388608 | tf_op jit(solution)/shard_map/all_to_all | solution.py:516
  26.8 3.2 %collective-permute-start.6 = (bf16[64,8192]{1,0:T(8,128)(2,1)S(1)}, bf16[64,8192]{1,0:T(8,128)(2,1)S(1)}, u32[]{:S(2)}, u32[]{:S(2)}) collective-permute-start(bf16[64,8192]{1,0:T(8,128)(2,1)S(1)} %copy-done.1), channel_id=1, source_target_pairs={{0,1},{1,0},{2,3},{3,2},{4,5},{5,4},{6,7},{7,6},{8,9},{9,8},{10,11... | collective-permute-start | bytes 3145736 | tf_op jit(solution)/shard_map/ppermute | solution.py:525
  30.0 2.5 %copy-start.10 = (bf16[64,8192]{1,0:T(8,128)(2,1)}, bf16[64,8192]{1,0:T(8,128)(2,1)S(1)}, u32[]{:S(2)}) copy-start(bf16[64,8192]{1,0:T(8,128)(2,1)S(1)} %collective-permute-done.6.refs_3_) | copy-start | bytes 3145732
  30.0 44.5 %collective-permute-start.4 = (s32[32]{0:T(128)S(1)}, s32[32]{0:T(128)S(1)}, u32[]{:S(2)}, u32[]{:S(2)}) collective-permute-start(s32[32]{0:T(128)S(1)} %bitcast.28), channel_id=1, source_target_pairs={{0,16},{1,17},{2,18},{3,19},{4,20},{5,21},{6,22},{7,23},{8,24},{9,... | collective-permute-start | bytes 392 | tf_op jit(solution)/shard_map/ppermute | solution.py:526
  74.6 51.4 %copy-start.12 = (s32[32]{0:T(128)}, s32[32]{0:T(128)S(1)}, u32[]{:S(2)}) copy-start(s32[32]{0:T(128)S(1)} %collective-permute-done.4.pick_ref) | copy-start | bytes 388
  74.6 5.8 %copy-start.2 = (bf16[64,8192]{1,0:T(8,128)(2,1)}, bf16[64,8192]{1,0:T(8,128)(2,1)S(1)}, u32[]{:S(2)}) copy-start(bf16[64,8192]{1,0:T(8,128)(2,1)S(1)} %collective-permute-done.refs_0_) | copy-start | bytes 3145732
  74.6 5.7 %copy-start.3 = (bf16[64,8192]{1,0:T(8,128)(2,1)}, bf16[64,8192]{1,0:T(8,128)(2,1)S(1)}, u32[]{:S(2)}) copy-start(bf16[64,8192]{1,0:T(8,128)(2,1)S(1)} %collective-permute-done.1.refs_1_) | copy-start | bytes 3145732
  74.6 3.9 %collective-permute-start.11 = (bf16[64,8192]{1,0:T(8,128)(2,1)S(1)}, bf16[64,8192]{1,0:T(8,128)(2,1)S(1)}, u32[]{:S(2)}, u32[]{:S(2)}) collective-permute-start(bf16[64,8192]{1,0:T(8,128)(2,1)S(1)} %collective-permute-done.refs_0_), channel_id=1, source_target_pairs={{0,1},{1,0},{2,3},{3,2},{4,5},{5,4},{6,7},{7,6},{8,9},{9,8},{10,11... | collective-permute-start | bytes 3145736 | tf_op jit(solution)/shard_map/ppermute | solution.py:536
  74.7 4.6 %collective-permute-start.12 = (bf16[64,8192]{1,0:T(8,128)(2,1)S(1)}, bf16[64,8192]{1,0:T(8,128)(2,1)S(1)}, u32[]{:S(2)}, u32[]{:S(2)}) collective-permute-start(bf16[64,8192]{1,0:T(8,128)(2,1)S(1)} %collective-permute-done.1.refs_1_), channel_id=1, source_target_pairs={{0,1},{1,0},{2,3},{3,2},{4,5},{5,4},{6,7},{7,6},{8,9},{9,8},{10,11... | collective-permute-start | bytes 3145736 | tf_op jit(solution)/shard_map/ppermute | solution.py:536
  75.2 50.8 %collective-permute-start.9 = (bf16[64,8192]{1,0:T(8,128)(2,1)S(1)}, bf16[64,8192]{1,0:T(8,128)(2,1)S(1)}, u32[]{:S(2)}, u32[]{:S(2)}) collective-permute-start(bf16[64,8192]{1,0:T(8,128)(2,1)S(1)} %collective-permute-done.refs_0_), channel_id=1, source_target_pairs={{8,16},{9,17},{10,18},{11,19},{12,20},{13,21},{14,22},{15,23},{16,... | collective-permute-start | bytes 3145736 | tf_op jit(solution)/shard_map/ppermute | solution.py:535
  75.9 46.5 %collective-permute-start.7 = (bf16[64,8192]{1,0:T(8,128)(2,1)}, bf16[64,8192]{1,0:T(8,128)(2,1)S(1)}, u32[]{:S(2)}, u32[]{:S(2)}) collective-permute-start(bf16[64,8192]{1,0:T(8,128)(2,1)} %collective-permute-done.2), channel_id=1, source_target_pairs={{8,0},{9,1},{10,2},{11,3},{12,4},{13,5},{14,6},{15,7},{16,24},{17,... | collective-permute-start | bytes 3145736 | tf_op jit(solution)/shard_map/ppermute | solution.py:534
  77.2 48.7 %collective-permute-start.8 = (bf16[64,8192]{1,0:T(8,128)(2,1)}, bf16[64,8192]{1,0:T(8,128)(2,1)S(1)}, u32[]{:S(2)}, u32[]{:S(2)}) collective-permute-start(bf16[64,8192]{1,0:T(8,128)(2,1)} %collective-permute-done.3), channel_id=1, source_target_pairs={{8,0},{9,1},{10,2},{11,3},{12,4},{13,5},{14,6},{15,7},{16,24},{17,... | collective-permute-start | bytes 3145736 | tf_op jit(solution)/shard_map/ppermute | solution.py:534
  78.6 1.8 copy-start.7
  78.6 47.4 %collective-permute-start.10 = (bf16[64,8192]{1,0:T(8,128)(2,1)S(1)}, bf16[64,8192]{1,0:T(8,128)(2,1)S(1)}, u32[]{:S(2)}, u32[]{:S(2)}) collective-permute-start(bf16[64,8192]{1,0:T(8,128)(2,1)S(1)} %collective-permute-done.1.refs_1_), channel_id=1, source_target_pairs={{8,16},{9,17},{10,18},{11,19},{12,20},{13,21},{14,22},{15,23},{16,... | collective-permute-start | bytes 3145736 | tf_op jit(solution)/shard_map/ppermute | solution.py:535
  79.3 1.0 copy-start.9
  80.3 57.1 %collective-permute-start.13 = (bf16[16384,128]{1,0:T(8,128)(2,1)}, bf16[16384,128]{1,0:T(8,128)(2,1)}, u32[]{:S(2)}, u32[]{:S(2)}) collective-permute-start(bf16[16384,128]{1,0:T(8,128)(2,1)} %get-tuple-element.27), channel_id=1, source_target_pairs={{0,1},{1,0},{2,3},{3,2},{4,5},{5,4},{6,7},{7,6},{8,9},{9,8},{10,11... | collective-permute-start | bytes 12582920 | tf_op jit(solution)/shard_map/ppermute | solution.py:530
  122.5 3.5 %copy-start.5 = (bf16[64,8192]{1,0:T(8,128)(2,1)}, bf16[64,8192]{1,0:T(8,128)(2,1)S(1)}, u32[]{:S(2)}) copy-start(bf16[64,8192]{1,0:T(8,128)(2,1)S(1)} %collective-permute-done.7.refs_0_) | copy-start | bytes 3145732
  126.0 1.0 copy-start.6
  126.0 1.3 copy-start.4
  126.0 1.6 copy-start.8
  132.6 7.6 %collective-permute-start.14 = (bf16[16384,128]{1,0:T(8,128)(2,1)}, bf16[16384,128]{1,0:T(8,128)(2,1)}, u32[]{:S(2)}, u32[]{:S(2)}) collective-permute-start(bf16[16384,128]{1,0:T(8,128)(2,1)} %get-tuple-element.28), channel_id=1, source_target_pairs={{0,1},{1,0},{2,3},{3,2},{4,5},{5,4},{6,7},{7,6},{8,9},{9,8},{10,11... | collective-permute-start | bytes 12582920 | tf_op jit(solution)/shard_map/ppermute | solution.py:541
  132.7 53.7 %all-to-all-start = ((bf16[8,2,8,16384]{3,2,1,0:T(8,128)(2,1)}), bf16[8,2,8,16384]{3,2,1,0:T(8,128)(2,1)}, u32[]{:S(2)}, u32[]{:S(2)}) async-start(bf16[8,2,8,16384]{3,2,1,0:T(8,128)(2,1)} %far_pack.1), calls=%async_computation | async-start | bytes 8388608 | tf_op jit(solution)/shard_map/all_to_all | solution.py:516
  202.1 4.8 %collective-permute-start.15 = (f32[2,32,128]{2,1,0:T(8,128)}, f32[2,32,128]{2,1,0:T(8,128)S(1)}, u32[]{:S(2)}, u32[]{:S(2)}) collective-permute-start(f32[2,32,128]{2,1,0:T(8,128)} %get-tuple-element.30), channel_id=1, source_target_pairs={{0,8},{1,9},{2,10},{3,11},{4,12},{5,13},{6,14},{7,15},{8,0},{9,1},... | collective-permute-start | bytes 98312 | tf_op jit(solution)/shard_map/ppermute | solution.py:545
  203.6 11.5 %all-to-all-start.2 = ((f32[32,8,128]{2,1,0:T(8,128)}), f32[32,8,128]{2,1,0:T(8,128)S(1)}, u32[]{:S(2)}, u32[]{:S(2)}) async-start(f32[32,8,128]{2,1,0:T(8,128)} %bitcast.21), calls=%async_computation.2 | async-start | bytes 262144 | tf_op jit(solution)/shard_map/all_to_all | solution.py:553

commit v11 on v3

--- a/solution.py
+++ b/solution.py
@@ -205,26 +205,29 @@
             slabs[g, :, cols] = slab.astype(jnp.bfloat16)
 
 
-def send_slabs(slabs, pick_ref, send_ref, sems):
-    mine = lax.div(lax.axis_index("dp"), PLANE)
+def send_slabs(slabs, pick_ref, send_refs, sems):
+    me = lax.axis_index("dp")
+    mine, here = lax.div(me, PLANE), lax.rem(me, PLANE)
     partner = mine + 1 - 2 * lax.rem(mine, 2)
     copies = []
-    for c in range(PLANE):
+    for r, send_ref in enumerate(send_refs):
         for t, plane in enumerate((mine, partner)):
-            group = pick_ref[plane * PLANE + c]
-            copies.append(pltpu.make_async_copy(slabs.at[group], send_ref.at[c, t], sems.at[c, t]))
+            group = pick_ref[plane * PLANE + lax.bitwise_xor(here, r)]
+            copies.append(pltpu.make_async_copy(slabs.at[group], send_ref.at[t], sems.at[r, t]))
     for copy in copies:
         copy.start()
     for copy in copies:
         copy.wait()
 
 
-def own_pack_kernel(pick_ref, x_ref, w_ref, send_ref, slabs, sems):
+def own_pack_kernel(pick_ref, x_ref, w_ref, *refs):
+    send_refs, (slabs, sems) = refs[:PLANE], refs[PLANE:]
     fill_slabs(slabs, x_ref, w_ref)
-    send_slabs(slabs, pick_ref, send_ref, sems)
-
-
-def far_pack_kernel(pick_ref, xo_ref, wo_ref, xi_ref, wi_ref, after_ref, send_ref, x_buf, w_buf, slabs, sems, in_sems):
+    send_slabs(slabs, pick_ref, send_refs, sems)
+
+
+def far_pack_kernel(pick_ref, xo_ref, wo_ref, xi_ref, wi_ref, after_ref, *refs):
+    send_refs, (x_buf, w_buf, in_sems, slabs, sems) = refs[:PLANE], refs[PLANE:]
     plane = lax.div(lax.axis_index("dp"), PLANE)
     inner = (plane == 1) | (plane == 2)
 
@@ -247,15 +250,15 @@
         fetch(xo_ref, wo_ref)
 
     fill_slabs(slabs, x_buf, w_buf)
-    send_slabs(slabs, pick_ref, send_ref, sems)
+    send_slabs(slabs, pick_ref, send_refs, sems)
 
 
 def pack_call(kernel, name, specs, scratch, blk, width, *operands):
     return pl.pallas_call(
         kernel,
-        out_shape=jax.ShapeDtypeStruct((PLANE, 2, SLAB, width), jnp.bfloat16),
+        out_shape=(jax.ShapeDtypeStruct((2, SLAB, width), jnp.bfloat16),) * PLANE,
         in_specs=[pl.BlockSpec(memory_space=pltpu.SMEM)] + specs,
-        out_specs=pl.BlockSpec(memory_space=pl.ANY),
+        out_specs=(pl.BlockSpec(memory_space=pl.ANY),) * PLANE,
         scratch_shapes=scratch
         + [pltpu.VMEM((blk // SUB, SLAB, width), jnp.bfloat16), pltpu.SemaphoreType.DMA((PLANE, 2))],
         compiler_params=params(),
@@ -275,11 +278,8 @@
     blk, width = x_outer.shape
     buf = pltpu.VMEM((blk, width), jnp.bfloat16)
 
-    def kernel(pick_ref, xo, wo, xi, wi, after_ref, send_ref, x_buf, w_buf, in_sems, slabs, sems):
-        far_pack_kernel(pick_ref, xo, wo, xi, wi, after_ref, send_ref, x_buf, w_buf, slabs, sems, in_sems)
-
     return pack_call(
-        kernel, "far_pack", [pl.BlockSpec(memory_space=pl.ANY)] * 5,
+        far_pack_kernel, "far_pack", [pl.BlockSpec(memory_space=pl.ANY)] * 5,
         [buf, buf, pltpu.SemaphoreType.DMA((2,))], blk, width,
         pick, x_outer, w_outer, x_inner, w_inner, after,
     )
@@ -357,8 +357,11 @@
     return numer / jnp.sqrt(var_x * var_y)
 
 
-def plane_sums_kernel(own_ref, far_ref, first_ref, second_ref, out_ref, acc):
-    rows, depth = own_ref.shape
+def plane_sums_kernel(*refs):
+    own_refs, far_refs = refs[:PLANE], refs[PLANE : 2 * PLANE]
+    first_ref, second_ref, out_ref, acc = refs[2 * PLANE :]
+    depth = first_ref.shape[0]
+    rows = 2 * SLAB * PLANE
     step = min(1024, depth)
     half = LANES // 2
     slabs = rows // SLAB
@@ -373,8 +376,8 @@
         cols = pl.ds(pl.multiple_of(i * step, step), step)
         is_x = lax.broadcasted_iota(jnp.int32, (slabs, SLAB, step), 1) < SUB
         weights, products = [], []
-        for ref in (own_ref, far_ref):
-            wide = ref[:, cols].astype(jnp.float32).reshape(slabs, SLAB, step)
+        for group in (own_refs, far_refs):
+            wide = jnp.concatenate([ref[:, :, cols].astype(jnp.float32) for ref in group], 0)
             rolled = pltpu.roll(wide, SUB, 1)
             product = wide * rolled
             both = jnp.where(is_x, product * wide, product)
@@ -426,21 +429,25 @@
             )
             moved = both if k == 0 else pltpu.roll(both, k * blk, 1)
             result = jnp.where((lane >= k * blk) & (lane < (k + 1) * blk), moved, result)
-        out_ref[...] = result
+        here = lax.rem(lax.axis_index("dp"), PLANE)
+        for tile in range(tiles):
+            part, r = tile // PLANE, tile % PLANE
+            out_ref[part * PLANE + lax.bitwise_xor(here, r)] = result[tile * SLAB : (tile + 1) * SLAB]
 
 
 def plane_sums(own, far, first, second):
-    rows, width = own.shape
+    _, slab, width = own[0].shape
+    rows = 2 * slab * PLANE
     depth = min(2048, width)
     lanes = (NOPS + NOPS // 2) * LANES
-    part = pl.BlockSpec((rows, depth), lambda i: (0, i))
+    part = pl.BlockSpec((2, slab, depth), lambda i: (0, 0, i))
     moved = pl.BlockSpec((depth, 2 * LANES), lambda i: (i, 0))
     return pl.pallas_call(
         plane_sums_kernel,
         grid=(width // depth,),
-        out_shape=jax.ShapeDtypeStruct((rows, LANES), jnp.float32),
-        in_specs=[part, part, moved, moved],
-        out_specs=pl.BlockSpec((rows, LANES), lambda i: (0, 0)),
+        out_shape=jax.ShapeDtypeStruct((2 * PLANE, slab, LANES), jnp.float32),
+        in_specs=[part] * (2 * PLANE) + [moved, moved],
+        out_specs=pl.BlockSpec((2 * PLANE, slab, LANES), lambda i: (0, 0, 0)),
         scratch_shapes=[pltpu.VMEM((3 * rows, lanes), jnp.float32)],
         compiler_params=params(),
         cost_estimate=pl.CostEstimate(
@@ -449,7 +456,7 @@
             transcendentals=0,
         ),
         name="plane_sums",
-    )(own, far, first, second)
+    )(*own, *far, first, second)
 
 
 def shards_by_plane(intensities, observed, qweights, ops, pick):
@@ -459,13 +466,15 @@
     far = [(i, i ^ (2 * PLANE)) for i in range(groups)]
     middle = [(i, 3 * PLANE + 2 * (i % PLANE) - i) for i in range(PLANE, 3 * PLANE)]
     outward = [(i, i - PLANE if i < 2 * PLANE else i + PLANE) for i in range(PLANE, 3 * PLANE)]
-    rings = [[z * PLANE + c for c in range(PLANE)] for z in range(PLANES)]
+    couples = [[z * PLANE + c for z in (odd, odd + 2) for c in range(PLANE)] for odd in range(2)]
     plane = lax.axis_index("dp") // PLANE
     odd, upper = plane % 2 == 1, plane >= 2
 
     def spread(send):
-        got = lax.all_to_all(send, "dp", split_axis=0, concat_axis=0, axis_index_groups=rings, tiled=True)
-        return got.reshape(PLANE * 2 * SLAB, width)
+        got = [send[0]]
+        for r in range(1, PLANE):
+            got.append(lax.ppermute(send[r], "dp", [(i, i ^ r) for i in range(groups)]))
+        return got
 
     own_pick = pick[:, 0]
     near_x = lax.ppermute(intensities, "dp", near)
@@ -483,7 +492,7 @@
     first = place(ops[:2], intensities, near_x, own_w, near_w, own_pick)
     far_send = far_pack(far_pick, outer_x, outer_w, inner_x, inner_w, first)
     far_got = spread(far_send)
-    second = place(ops[2:], intensities, near_x, own_w, near_w, far_send)
+    second = place(ops[2:], intensities, near_x, own_w, near_w, far_send[0])
     stats = plane_sums(own_got, far_got, first, second)
     stats = stats.reshape(2, PLANE, 2, SUB, NOPS * blk)
     mine, other = stats[:, :, 0], stats[:, :, 1]
@@ -494,11 +503,10 @@
     pair = jnp.where(upper, pair[::-1], pair)
     corr = pair.reshape(groups * SUB, NOPS * blk).T.reshape(NOPS, blk, groups * SUB)
 
-    both = jnp.where(upper, stats[::-1], stats).reshape(2, 1, PLANE, 2 * SUB, NOPS * blk)
-    back = jnp.broadcast_to(both, (2, 2, PLANE, 2 * SUB, NOPS * blk)).reshape(groups, 2 * SUB, NOPS * blk)
-    back = lax.all_to_all(back, "dp", split_axis=0, concat_axis=0, tiled=True)
-    back = back.reshape(2, 2, PLANE, 2, SUB, NOPS, blk)
-    back = jnp.where(odd, back[:, 1, :, ::-1], back[:, 0])
+    back = jnp.where(upper, stats[::-1], stats).reshape(2 * PLANE, 2 * SUB, NOPS * blk)
+    back = lax.all_to_all(back, "dp", split_axis=0, concat_axis=0, axis_index_groups=couples, tiled=True)
+    back = back.reshape(2, PLANE, 2, SUB, NOPS, blk)
+    back = jnp.where(odd, back[:, :, ::-1], back)
     returned = jnp.transpose(back, (4, 0, 2, 1, 3, 5)).reshape(NOPS, 1, groups, SUB, blk)
     return (corr, returned)
 

time: 205 us -> 268 us (1.31)
  waiting for transfers between devices: 61.6 us -> 103 us
  starting transfers between devices: 28.3 us -> 49.1 us
    ppermute x0 -> x14, waiting for transfers between devices: none -> 32.7 us  [spread(): got.append(lax.ppermute(send[r], 'dp', [(i, i ^ r) for i in range(groups)]))]
    ppermute x1, waiting for transfers between devices: 0.01 us -> 20.1 us  [shards_by_plane(): outer_x = lax.ppermute(mid_x, 'dp', outward)]
    ppermute x1, starting transfers between devices: 0.01 us -> 17.1 us  [shards_by_plane(): from_near = lax.ppermute(other, 'dp', near)]
    all_to_all x3 -> x1, waiting for transfers between devices: 19 us -> 6.38 us  [shards_by_plane(): lax.all_to_all(back, 'dp', split_axis=0, concat_axis=0, axis_index_groups...]
    ppermute x0 -> x14, starting transfers between devices: none -> 12.4 us  [spread(): got.append(lax.ppermute(send[r], 'dp', [(i, i ^ r) for i in range(groups)]))]
    all_to_all x3 -> x1, starting transfers between devices: 12.6 us -> 3.5 us  [shards_by_plane(): lax.all_to_all(back, 'dp', split_axis=0, concat_axis=0, axis_index_groups...]
    ppermute x1, waiting for transfers between devices: 32.2 us -> 39.7 us  [shards_by_plane(): far_pick = lax.ppermute(own_pick, 'dp', far)]
    ppermute x1, waiting for transfers between devices: 10.4 us -> 3.96 us  [shards_by_plane(): outer_w = lax.ppermute(mid_w, 'dp', outward)]
  transfers between devices with their start and end apart: 13 -> 25, of which waited for: 4 -> 8; matrix products, arithmetic and copies ran while one was open for 2% -> 2% of each run, Pallas kernels for 40% -> 31%
where the time goes in v11:
time: 268 us; the launch traced here: 267 us
  Pallas kernels  105 us (39%)
  waiting for transfers between devices  103 us (38%)
  starting transfers between devices  49.1 us (18%)
  local copies, waits for them, and re-layouts  5.48 us (2%)
  other arithmetic  3.89 us (1%)
    pallas_call x2, Pallas kernels, place(): pl.pallas_call(place_kernel, grid=(count, width // depth), out_shape=jax....  73.6 us
    ppermute x1, waiting for transfers between devices, shards_by_plane(): far_pick = lax.ppermute(own_pick, 'dp', far)  39.7 us
    ppermute x14, waiting for transfers between devices, spread(): got.append(lax.ppermute(send[r], 'dp', [(i, i ^ r) for i in range(groups)]))  32.7 us
    pallas_call x1, Pallas kernels, plane_sums(): pl.pallas_call(plane_sums_kernel, grid=(width // depth,), out_shape=jax.S...  22 us
    ppermute x1, waiting for transfers between devices, shards_by_plane(): outer_x = lax.ppermute(mid_x, 'dp', outward)  20.1 us
    ppermute x1, starting transfers between devices, shards_by_plane(): from_near = lax.ppermute(other, 'dp', near)  17.1 us
    ppermute x14, starting transfers between devices, spread(): got.append(lax.ppermute(send[r], 'dp', [(i, i ^ r) for i in range(groups)]))  12.4 us
    pallas_call x2, Pallas kernels, pack_call(): pl.pallas_call(kernel, out_shape=(jax.ShapeDtypeStruct((2, SLAB, width),...  9.28 us
  transfers between devices with their start and end apart: 25, of which 8 were waited for; matrix products, arithmetic and copies ran while one was open for 2% of the time, Pallas kernels for 31%

profile of v11, /device:TPU:0, one launch (start us, length us, event | category | flops | bytes accessed | tf_op | source)
XLA Modules:
  0.0 267.3 jit_solution(10432456649865863927)
XLA Ops:
  0.6 0.0 copy-start.1
  0.6 0.0 copy-start.9
  0.7 2.2 multiply_convert_fusion.w_ref
  2.9 0.0 copy-start.8
  2.9 0.9 collective-permute-start.10
  3.8 5.8 %collective-permute-start.9 = (bf16[32,16384]{1,0:T(8,128)(2,1)S(1)}, bf16[32,16384]{1,0:T(8,128)(2,1)S(1)}, u32[]{:S(2)}, u32[]{:S(2)}) collective-permute-start(bf16[32,16384]{1,0:T(8,128)(2,1)S(1)} %multiply_convert_fusion.w_ref), channel_id=1, source_target_pairs={{0,8},{1,9},{2,10},{3,11},{4,12},{5,13},{6,14},{7,15},{8,0},{9,1},... | collective-permute-start | bytes 3145736 | tf_op jit(solution)/shard_map/ppermute | solution.py:484
  9.6 0.1 collective-permute-start.7
  9.7 1.7 collective-permute-start.8
  11.4 3.7 %collective-permute-start.11 = (s32[32]{0:T(128)S(1)}, s32[32]{0:T(128)S(1)}, u32[]{:S(2)}, u32[]{:S(2)}) collective-permute-start(s32[32]{0:T(128)S(1)} %bitcast.27), channel_id=1, source_target_pairs={{0,16},{1,17},{2,18},{3,19},{4,20},{5,21},{6,22},{7,23},{8,24},{9,... | collective-permute-start | bytes 392 | tf_op jit(solution)/shard_map/ppermute | solution.py:482
  15.1 39.7 %collective-permute-done.11.pick_ref = s32[32]{0:T(128)S(1)} collective-permute-done((s32[32]{0:T(128)S(1)}, s32[32]{0:T(128)S(1)}, u32[]{:S(2)}, u32[]{:S(2)}) %collective-permute-start.11) | collective-permute-done | bytes 160 | tf_op jit(solution)/shard_map/ppermute | solution.py:482
  54.8 0.0 collective-permute-done.10
  54.8 0.0 collective-permute-done.9.w1_ref
  54.8 0.2 collective-permute-done.7.x1_ref
  55.0 0.7 collective-permute-start.14
  55.7 0.7 collective-permute-start.15
  56.5 1.3 collective-permute-start.12
  57.8 4.3 %own_pack.1 = (bf16[2,8,16384]{2,1,0:T(8,128)(2,1)}, bf16[2,8,16384]{2,1,0:T(8,128)(2,1)}, bf16[2,8,16384]{2,1,0:T(8,128)(2,1)}, bf16[2,8,16384]{2,1,0:T(8,128)(...) custom-call(s32[32]{0:T(128)} %bitcast.25, ...), custom_call_target="tpu_custom_call" | custom-call | flops 2097152 | bytes 6291456 | tf_op jit(solution)/shard_map/own_pack/pallas_call | solution.py:257
  62.0 0.1 collective-permute-start
  62.1 1.6 collective-permute-start.1
  63.7 0.0 collective-permute-done.14.xi_ref
  63.7 0.3 collective-permute-start.2
  64.0 0.0 collective-permute-done.15.wi_ref
  64.0 1.5 collective-permute-start.3
  65.5 20.1 %collective-permute-done.12.xo_ref = bf16[32,16384]{1,0:T(8,128)(2,1)S(1)} collective-permute-done((bf16[32,16384]{1,0:T(8,128)(2,1)}, bf16[32,16384]{1,0:T(8,128)(2,1)S(1)}, u32[]{:S(2)}, u32[]{:S(2)}) %collective-permute-start.12) | collective-permute-done | bytes 1048608 | tf_op jit(solution)/shard_map/ppermute | solution.py:488
  85.6 1.3 collective-permute-start.13
  86.9 0.1 fusion.1
  87.0 0.7 broadcast_in_dim.6.ops_ref
  87.7 36.8 %place.2.after_ref.refs_16_ = bf16[16384,256]{1,0:T(8,128)(2,1)} custom-call(s32[2,1,16384]{2,1,0:T(1,128)} %broadcast_in_dim.6.ops_ref, bf16[32,16384]{1,0:T(8,128)(2,1)} %x_ref.5, bf16[32,16384]{1,0:T(8,128)(2,1)} %copy-done.3, bf16[32,16384]{1,0:T(8,128)(2,1)} %copy-done, bf16[32,16384]{1,0:T(8,128)(2,1)} %copy-done.2, s32[32]{0:T(128)} %bitcast.26), custom_call_target="tpu_custom_call" | custom-call | bytes 268435456 | tf_op jit(solution)/shard_map/place/pallas_call | solution.py:331
  124.6 4.0 %collective-permute-done.13.wo_ref = bf16[32,16384]{1,0:T(8,128)(2,1)S(1)} collective-permute-done((bf16[32,16384]{1,0:T(8,128)(2,1)S(1)}, bf16[32,16384]{1,0:T(8,128)(2,1)S(1)}, u32[]{:S(2)}, u32[]{:S(2)}) %collective-permute-start.13) | collective-permute-done | bytes 1048608 | tf_op jit(solution)/shard_map/ppermute | solution.py:490
  128.6 0.0 collective-permute-start.4
  128.6 1.0 copy-done.7
  129.6 5.0 %far_pack.1 = (bf16[2,8,16384]{2,1,0:T(8,128)(2,1)}, bf16[2,8,16384]{2,1,0:T(8,128)(2,1)}, bf16[2,8,16384]{2,1,0:T(8,128)(2,1)}, bf16[2,8,16384]{2,1,0:T(8,128)(...) custom-call(s32[32]{0:T(128)} %copy-done.10, ...), custom_call_target="tpu_custom_call" | custom-call | flops 2097152 | bytes 6291456 | tf_op jit(solution)/shard_map/far_pack/pallas_call | solution.py:257
  134.6 0.0 collective-permute-done.refs_1_
  134.6 1.5 collective-permute-start.5
  136.1 0.0 collective-permute-done.1.refs_2_
  136.1 0.4 collective-permute-start.6
  136.5 0.0 collective-permute-done.2.refs_3_
  136.5 1.2 collective-permute-start.16
  137.7 0.0 collective-permute-done.3.refs_4_
  137.7 1.5 collective-permute-start.17
  139.2 25.3 %collective-permute-done.4.refs_5_ = bf16[2,8,16384]{2,1,0:T(8,128)(2,1)S(1)} collective-permute-done((bf16[2,8,16384]{2,1,0:T(8,128)(2,1)}, bf16[2,8,16384]{2,1,0:T(8,128)(2,1)S(1)}, u32[]{:S(2)}, u32[]{:S(2)}) %collective-permute-start.4) | collective-permute-done | bytes 524320 | tf_op jit(solution)/shard_map/ppermute | solution.py:476
  164.5 0.3 collective-permute-start.18
  164.8 0.0 collective-permute-done.5.refs_6_
  164.8 2.4 collective-permute-start.19
  167.2 0.0 collective-permute-done.6.refs_7_
  167.2 0.3 collective-permute-start.20
  167.5 0.0 collective-permute-done.16.refs_9_
  167.5 1.3 collective-permute-start.21
  168.8 3.0 %collective-permute-done.17.refs_10_ = bf16[2,8,16384]{2,1,0:T(8,128)(2,1)S(1)} collective-permute-done((bf16[2,8,16384]{2,1,0:T(8,128)(2,1)}, bf16[2,8,16384]{2,1,0:T(8,128)(2,1)S(1)}, u32[]{:S(2)}, u32[]{:S(2)}) %collective-permute-start.17) | collective-permute-done | bytes 524320 | tf_op jit(solution)/shard_map/ppermute | solution.py:476
  171.9 0.8 broadcast_in_dim.7.ops_ref
  172.7 36.8 %place.3.refs_17_ = bf16[16384,256]{1,0:T(8,128)(2,1)} custom-call(s32[2,1,16384]{2,1,0:T(1,128)} %broadcast_in_dim.7.ops_ref, bf16[32,16384]{1,0:T(8,128)(2,1)} %x_ref.5, bf16[32,16384]{1,0:T(8,128)(2,1)} %copy-done.3, bf16[32,16384]{1,0:T(8,128)(2,1)} %copy-done, bf16[32,16384]{1,0:T(8,128)(2,1)} %copy-done.2, ...), custom_call_target="tpu_custom_call" | custom-call | bytes 268435456 | tf_op jit(solution)/shard_map/place/pallas_call | solution.py:331
  209.5 0.0 collective-permute-done.18.refs_11_
  209.5 0.0 collective-permute-done.19.refs_12_
  209.6 4.4 %collective-permute-done.20.refs_13_ = bf16[2,8,16384]{2,1,0:T(8,128)(2,1)} collective-permute-done((bf16[2,8,16384]{2,1,0:T(8,128)(2,1)}, bf16[2,8,16384]{2,1,0:T(8,128)(2,1)}, u32[]{:S(2)}, u32[]{:S(2)}) %collective-permute-start.20) | collective-permute-done | bytes 524320 | tf_op jit(solution)/shard_map/ppermute | solution.py:476
  214.0 22.0 %plane_sums.1 = f32[16,8,128]{2,1,0:T(8,128)} custom-call(bf16[2,8,16384]{2,1,0:T(8,128)(2,1)} %get-tuple-element.23.refs_0_, bf16[2,8,16384]{2,1,0:T(8,128)(2,1)} %collective-permute-done.refs_1_, bf16[2,8,16384]{2,1,0:T(8,128)(2,1)} %collective-permute-done.1.refs_2_, bf16[2,8,16384]{2,1,0:T(8,128)(2,1)} %collective-permute-done.2.refs_3_, ...), custom_call_target="tpu_custom_call" | custom-call | flops 9663676416 | bytes 25165824 | tf_op jit(solution)/shard_map/plane_sums/pallas_call | solution.py:445
  236.0 0.8 slice_bitcast_fusion.1
  236.8 17.1 %collective-permute-start.23 = (f32[2,8,4,128]{3,2,1,0:T(4,128)S(1)}, f32[2,8,4,128]{3,2,1,0:T(4,128)S(1)}, u32[]{:S(2)}, u32[]{:S(2)}) collective-permute-start(f32[2,8,4,128]{3,2,1,0:T(4,128)S(1)} %get-tuple-element.51), channel_id=1, source_target_pairs={{0,8},{1,9},{2,10},{3,11},{4,12},{5,13},{6,14},{7,15},{8,0},{9,1},... | collective-permute-start | bytes 98312 | tf_op jit(solution)/shard_map/ppermute | solution.py:500
  253.8 1.6 reverse_select_fusion.1
  255.4 3.5 %all-to-all-start = ((f32[16,8,128]{2,1,0:T(8,128)}), f32[16,8,128]{2,1,0:T(8,128)S(1)}, u32[]{:S(2)}, u32[]{:S(2)}) async-start(f32[16,8,128]{2,1,0:T(8,128)} %bitcast.8), calls=%async_computation | async-start | bytes 131072 | tf_op jit(solution)/shard_map/all_to_all | solution.py:507
  259.0 0.7 copy.13
  259.7 6.4 %all-to-all-done = f32[16,8,128]{2,1,0:T(8,128)S(1)} async-done(((f32[16,8,128]{2,1,0:T(8,128)}), f32[16,8,128]{2,1,0:T(8,128)S(1)}, u32[]{:S(2)}, u32[]{:S(2)}) %all-to-all-start) | async-done | bytes 65568 | tf_op jit(solution)/shard_map/all_to_all | solution.py:507
  266.1 0.2 reshape.26
  266.3 0.2 copy.14
  266.5 0.9 copy.15
  (43 shorter events, 0.2 us)
Async XLA Ops:
  0.6 9.0 %copy-start.1 = (bf16[32,16384]{1,0:T(8,128)(2,1)S(1)}, bf16[32,16384]{1,0:T(8,128)(2,1)}, u32[]{:S(2)}) copy-start(bf16[32,16384]{1,0:T(8,128)(2,1)} %x_ref.5) | copy-start | bytes 3145732
  0.6 10.7 %copy-start.9 = (s32[32,1]{0,1:T(1,128)S(1)}, s32[32,1]{0,1:T(1,128)}, u32[]{:S(2)}) copy-start(s32[32,1]{0,1:T(1,128)} %param.9) | copy-start | bytes 388
  2.9 54.9 %copy-start = (bf16[32,16384]{1,0:T(8,128)(2,1)}, bf16[32,16384]{1,0:T(8,128)(2,1)S(1)}, u32[]{:S(2)}) copy-start(bf16[32,16384]{1,0:T(8,128)(2,1)S(1)} %multiply_convert_fusion.w_ref) | copy-start | bytes 3145732
  2.9 84.0 %copy-start.8 = (s32[4,16384]{1,0:T(4,128)S(1)}, s32[4,16384]{1,0:T(4,128)}, u32[]{:S(2)}) copy-start(s32[4,16384]{1,0:T(4,128)} %param.8) | copy-start | bytes 786436
  2.9 51.9 %collective-permute-start.10 = (bf16[32,16384]{1,0:T(8,128)(2,1)S(1)}, bf16[32,16384]{1,0:T(8,128)(2,1)S(1)}, u32[]{:S(2)}, u32[]{:S(2)}) collective-permute-start(bf16[32,16384]{1,0:T(8,128)(2,1)S(1)} %multiply_convert_fusion.w_ref), channel_id=1, source_target_pairs={{8,16},{9,17},{10,18},{11,19},{12,20},{13,21},{14,22},{15,23},{16,... | collective-permute-start | bytes 3145736 | tf_op jit(solution)/shard_map/ppermute | solution.py:485
  3.8 51.0 %collective-permute-start.9 = (bf16[32,16384]{1,0:T(8,128)(2,1)S(1)}, bf16[32,16384]{1,0:T(8,128)(2,1)S(1)}, u32[]{:S(2)}, u32[]{:S(2)}) collective-permute-start(bf16[32,16384]{1,0:T(8,128)(2,1)S(1)} %multiply_convert_fusion.w_ref), channel_id=1, source_target_pairs={{0,8},{1,9},{2,10},{3,11},{4,12},{5,13},{6,14},{7,15},{8,0},{9,1},... | collective-permute-start | bytes 3145736 | tf_op jit(solution)/shard_map/ppermute | solution.py:484
  9.6 45.4 %collective-permute-start.7 = (bf16[32,16384]{1,0:T(8,128)(2,1)S(1)}, bf16[32,16384]{1,0:T(8,128)(2,1)S(1)}, u32[]{:S(2)}, u32[]{:S(2)}) collective-permute-start(bf16[32,16384]{1,0:T(8,128)(2,1)S(1)} %copy-done.1), channel_id=1, source_target_pairs={{0,8},{1,9},{2,10},{3,11},{4,12},{5,13},{6,14},{7,15},{8,0},{9,1},... | collective-permute-start | bytes 3145736 | tf_op jit(solution)/shard_map/ppermute | solution.py:480
  9.7 45.3 %collective-permute-start.8 = (bf16[32,16384]{1,0:T(8,128)(2,1)S(1)}, bf16[32,16384]{1,0:T(8,128)(2,1)}, u32[]{:S(2)}, u32[]{:S(2)}) collective-permute-start(bf16[32,16384]{1,0:T(8,128)(2,1)S(1)} %copy-done.1), channel_id=1, source_target_pairs={{8,16},{9,17},{10,18},{11,19},{12,20},{13,21},{14,22},{15,23},{16,... | collective-permute-start | bytes 3145736 | tf_op jit(solution)/shard_map/ppermute | solution.py:481
  11.4 43.4 %collective-permute-start.11 = (s32[32]{0:T(128)S(1)}, s32[32]{0:T(128)S(1)}, u32[]{:S(2)}, u32[]{:S(2)}) collective-permute-start(s32[32]{0:T(128)S(1)} %bitcast.27), channel_id=1, source_target_pairs={{0,16},{1,17},{2,18},{3,19},{4,20},{5,21},{6,22},{7,23},{8,24},{9,... | collective-permute-start | bytes 392 | tf_op jit(solution)/shard_map/ppermute | solution.py:482
  54.8 69.8 %copy-start.10 = (s32[32]{0:T(128)}, s32[32]{0:T(128)S(1)}, u32[]{:S(2)}) copy-start(s32[32]{0:T(128)S(1)} %collective-permute-done.11.pick_ref) | copy-start | bytes 388
  54.8 33.0 %copy-start.2 = (bf16[32,16384]{1,0:T(8,128)(2,1)}, bf16[32,16384]{1,0:T(8,128)(2,1)S(1)}, u32[]{:S(2)}) copy-start(bf16[32,16384]{1,0:T(8,128)(2,1)S(1)} %collective-permute-done.9.w1_ref) | copy-start | bytes 3145732
  55.0 32.7 %copy-start.3 = (bf16[32,16384]{1,0:T(8,128)(2,1)}, bf16[32,16384]{1,0:T(8,128)(2,1)S(1)}, u32[]{:S(2)}) copy-start(bf16[32,16384]{1,0:T(8,128)(2,1)S(1)} %collective-permute-done.7.x1_ref) | copy-start | bytes 3145732
  55.0 8.7 %collective-permute-start.14 = (bf16[32,16384]{1,0:T(8,128)(2,1)S(1)}, bf16[32,16384]{1,0:T(8,128)(2,1)S(1)}, u32[]{:S(2)}, u32[]{:S(2)}) collective-permute-start(bf16[32,16384]{1,0:T(8,128)(2,1)S(1)} %collective-permute-done.7.x1_ref), channel_id=1, source_target_pairs={{8,16},{9,17},{10,18},{11,19},{12,20},{13,21},{14,22},{15,23},{16,... | collective-permute-start | bytes 3145736 | tf_op jit(solution)/shard_map/ppermute | solution.py:489
  55.7 8.3 %collective-permute-start.15 = (bf16[32,16384]{1,0:T(8,128)(2,1)S(1)}, bf16[32,16384]{1,0:T(8,128)(2,1)S(1)}, u32[]{:S(2)}, u32[]{:S(2)}) collective-permute-start(bf16[32,16384]{1,0:T(8,128)(2,1)S(1)} %collective-permute-done.9.w1_ref), channel_id=1, source_target_pairs={{8,16},{9,17},{10,18},{11,19},{12,20},{13,21},{14,22},{15,23},{16,... | collective-permute-start | bytes 3145736 | tf_op jit(solution)/shard_map/ppermute | solution.py:491
  56.5 29.1 %collective-permute-start.12 = (bf16[32,16384]{1,0:T(8,128)(2,1)}, bf16[32,16384]{1,0:T(8,128)(2,1)S(1)}, u32[]{:S(2)}, u32[]{:S(2)}) collective-permute-start(bf16[32,16384]{1,0:T(8,128)(2,1)} %collective-permute-done.8), channel_id=1, source_target_pairs={{8,0},{9,1},{10,2},{11,3},{12,4},{13,5},{14,6},{15,7},{16,24},{17,... | collective-permute-start | bytes 3145736 | tf_op jit(solution)/shard_map/ppermute | solution.py:488
  62.0 72.6 %collective-permute-start = (bf16[2,8,16384]{2,1,0:T(8,128)(2,1)}, bf16[2,8,16384]{2,1,0:T(8,128)(2,1)}, u32[]{:S(2)}, u32[]{:S(2)}) collective-permute-start(bf16[2,8,16384]{2,1,0:T(8,128)(2,1)} %get-tuple-element.24), channel_id=1, source_target_pairs={{0,1},{1,0},{2,3},{3,2},{4,5},{5,4},{6,7},{7,6},{8,9},{9,8},{10,11... | collective-permute-start | bytes 1572872 | tf_op jit(solution)/shard_map/ppermute | solution.py:476
  62.1 74.0 %collective-permute-start.1 = (bf16[2,8,16384]{2,1,0:T(8,128)(2,1)}, bf16[2,8,16384]{2,1,0:T(8,128)(2,1)}, u32[]{:S(2)}, u32[]{:S(2)}) collective-permute-start(bf16[2,8,16384]{2,1,0:T(8,128)(2,1)} %get-tuple-element.25), channel_id=1, source_target_pairs={{0,2},{1,3},{2,0},{3,1},{4,6},{5,7},{6,4},{7,5},{8,10},{9,11},{10,... | collective-permute-start | bytes 1572872 | tf_op jit(solution)/shard_map/ppermute | solution.py:476
  63.7 60.9 %copy-start.4 = (bf16[32,16384]{1,0:T(8,128)(2,1)}, bf16[32,16384]{1,0:T(8,128)(2,1)S(1)}, u32[]{:S(2)}) copy-start(bf16[32,16384]{1,0:T(8,128)(2,1)S(1)} %collective-permute-done.14.xi_ref) | copy-start | bytes 3145732
  63.7 72.9 %collective-permute-start.2 = (bf16[2,8,16384]{2,1,0:T(8,128)(2,1)}, bf16[2,8,16384]{2,1,0:T(8,128)(2,1)}, u32[]{:S(2)}, u32[]{:S(2)}) collective-permute-start(bf16[2,8,16384]{2,1,0:T(8,128)(2,1)} %get-tuple-element.26), channel_id=1, source_target_pairs={{0,3},{1,2},{2,1},{3,0},{4,7},{5,6},{6,5},{7,4},{8,11},{9,10},{10,... | collective-permute-start | bytes 1572872 | tf_op jit(solution)/shard_map/ppermute | solution.py:476
  64.0 60.6 %copy-start.5 = (bf16[32,16384]{1,0:T(8,128)(2,1)}, bf16[32,16384]{1,0:T(8,128)(2,1)S(1)}, u32[]{:S(2)}) copy-start(bf16[32,16384]{1,0:T(8,128)(2,1)S(1)} %collective-permute-done.15.wi_ref) | copy-start | bytes 3145732
  64.0 73.8 %collective-permute-start.3 = (bf16[2,8,16384]{2,1,0:T(8,128)(2,1)}, bf16[2,8,16384]{2,1,0:T(8,128)(2,1)}, u32[]{:S(2)}, u32[]{:S(2)}) collective-permute-start(bf16[2,8,16384]{2,1,0:T(8,128)(2,1)} %get-tuple-element.27), channel_id=1, source_target_pairs={{0,4},{1,5},{2,6},{3,7},{4,0},{5,1},{6,2},{7,3},{8,12},{9,13},{10,... | collective-permute-start | bytes 1572872 | tf_op jit(solution)/shard_map/ppermute | solution.py:476
  85.6 39.0 %copy-start.6 = (bf16[32,16384]{1,0:T(8,128)(2,1)}, bf16[32,16384]{1,0:T(8,128)(2,1)S(1)}, u32[]{:S(2)}) copy-start(bf16[32,16384]{1,0:T(8,128)(2,1)S(1)} %collective-permute-done.12.xo_ref) | copy-start | bytes 3145732
  85.6 43.0 %collective-permute-start.13 = (bf16[32,16384]{1,0:T(8,128)(2,1)S(1)}, bf16[32,16384]{1,0:T(8,128)(2,1)S(1)}, u32[]{:S(2)}, u32[]{:S(2)}) collective-permute-start(bf16[32,16384]{1,0:T(8,128)(2,1)S(1)} %collective-permute-done.10), channel_id=1, source_target_pairs={{8,0},{9,1},{10,2},{11,3},{12,4},{13,5},{14,6},{15,7},{16,24},{17,... | collective-permute-start | bytes 3145736 | tf_op jit(solution)/shard_map/ppermute | solution.py:490
  128.5 1.0 copy-start.7
  128.5 6.1 %copy-start.18 = (bf16[2,8,16384]{2,1,0:T(8,128)(2,1)S(1)}, bf16[2,8,16384]{2,1,0:T(8,128)(2,1)}, u32[]{:S(2)}) copy-start(bf16[2,8,16384]{2,1,0:T(8,128)(2,1)} %get-tuple-element.29) | copy-start | bytes 1572868
  128.5 7.6 %copy-start.17 = (bf16[2,8,16384]{2,1,0:T(8,128)(2,1)S(1)}, bf16[2,8,16384]{2,1,0:T(8,128)(2,1)}, u32[]{:S(2)}) copy-start(bf16[2,8,16384]{2,1,0:T(8,128)(2,1)} %get-tuple-element.30) | copy-start | bytes 1572868
  128.6 36.0 %collective-permute-start.4 = (bf16[2,8,16384]{2,1,0:T(8,128)(2,1)}, bf16[2,8,16384]{2,1,0:T(8,128)(2,1)S(1)}, u32[]{:S(2)}, u32[]{:S(2)}) collective-permute-start(bf16[2,8,16384]{2,1,0:T(8,128)(2,1)} %get-tuple-element.28), channel_id=1, source_target_pairs={{0,5},{1,4},{2,7},{3,6},{4,1},{5,0},{6,3},{7,2},{8,13},{9,12},{10,... | collective-permute-start | bytes 1572872 | tf_op jit(solution)/shard_map/ppermute | solution.py:476
  134.6 30.2 %collective-permute-start.5 = (bf16[2,8,16384]{2,1,0:T(8,128)(2,1)S(1)}, bf16[2,8,16384]{2,1,0:T(8,128)(2,1)S(1)}, u32[]{:S(2)}, u32[]{:S(2)}) collective-permute-start(bf16[2,8,16384]{2,1,0:T(8,128)(2,1)S(1)} %copy-done.18), channel_id=1, source_target_pairs={{0,6},{1,7},{2,4},{3,5},{4,2},{5,3},{6,0},{7,1},{8,14},{9,15},{10,... | collective-permute-start | bytes 1572872 | tf_op jit(solution)/shard_map/ppermute | solution.py:476
  136.1 31.1 %collective-permute-start.6 = (bf16[2,8,16384]{2,1,0:T(8,128)(2,1)S(1)}, bf16[2,8,16384]{2,1,0:T(8,128)(2,1)S(1)}, u32[]{:S(2)}, u32[]{:S(2)}) collective-permute-start(bf16[2,8,16384]{2,1,0:T(8,128)(2,1)S(1)} %copy-done.17), channel_id=1, source_target_pairs={{0,7},{1,6},{2,5},{3,4},{4,3},{5,2},{6,1},{7,0},{8,15},{9,14},{10,... | collective-permute-start | bytes 1572872 | tf_op jit(solution)/shard_map/ppermute | solution.py:476
  136.5 30.9 %collective-permute-start.16 = (bf16[2,8,16384]{2,1,0:T(8,128)(2,1)}, bf16[2,8,16384]{2,1,0:T(8,128)(2,1)S(1)}, u32[]{:S(2)}, u32[]{:S(2)}) collective-permute-start(bf16[2,8,16384]{2,1,0:T(8,128)(2,1)} %get-tuple-element.37), channel_id=1, source_target_pairs={{0,1},{1,0},{2,3},{3,2},{4,5},{5,4},{6,7},{7,6},{8,9},{9,8},{10,11... | collective-permute-start | bytes 1572872 | tf_op jit(solution)/shard_map/ppermute | solution.py:476
  137.7 34.1 %collective-permute-start.17 = (bf16[2,8,16384]{2,1,0:T(8,128)(2,1)}, bf16[2,8,16384]{2,1,0:T(8,128)(2,1)S(1)}, u32[]{:S(2)}, u32[]{:S(2)}) collective-permute-start(bf16[2,8,16384]{2,1,0:T(8,128)(2,1)} %get-tuple-element.38), channel_id=1, source_target_pairs={{0,2},{1,3},{2,0},{3,1},{4,6},{5,7},{6,4},{7,5},{8,10},{9,11},{10,... | collective-permute-start | bytes 1572872 | tf_op jit(solution)/shard_map/ppermute | solution.py:476
  164.5 45.0 %copy-start.11 = (bf16[2,8,16384]{2,1,0:T(8,128)(2,1)}, bf16[2,8,16384]{2,1,0:T(8,128)(2,1)S(1)}, u32[]{:S(2)}) copy-start(bf16[2,8,16384]{2,1,0:T(8,128)(2,1)S(1)} %collective-permute-done.4.refs_5_) | copy-start | bytes 1572868
  164.5 45.0 %collective-permute-start.18 = (bf16[2,8,16384]{2,1,0:T(8,128)(2,1)}, bf16[2,8,16384]{2,1,0:T(8,128)(2,1)S(1)}, u32[]{:S(2)}, u32[]{:S(2)}) collective-permute-start(bf16[2,8,16384]{2,1,0:T(8,128)(2,1)} %get-tuple-element.39), channel_id=1, source_target_pairs={{0,3},{1,2},{2,1},{3,0},{4,7},{5,6},{6,5},{7,4},{8,11},{9,10},{10,... | collective-permute-start | bytes 1572872 | tf_op jit(solution)/shard_map/ppermute | solution.py:476
  164.8 44.7 %copy-start.12 = (bf16[2,8,16384]{2,1,0:T(8,128)(2,1)}, bf16[2,8,16384]{2,1,0:T(8,128)(2,1)S(1)}, u32[]{:S(2)}) copy-start(bf16[2,8,16384]{2,1,0:T(8,128)(2,1)S(1)} %collective-permute-done.5.refs_6_) | copy-start | bytes 1572868
  164.8 44.7 %collective-permute-start.19 = (bf16[2,8,16384]{2,1,0:T(8,128)(2,1)}, bf16[2,8,16384]{2,1,0:T(8,128)(2,1)}, u32[]{:S(2)}, u32[]{:S(2)}) collective-permute-start(bf16[2,8,16384]{2,1,0:T(8,128)(2,1)} %get-tuple-element.40), channel_id=1, source_target_pairs={{0,4},{1,5},{2,6},{3,7},{4,0},{5,1},{6,2},{7,3},{8,12},{9,13},{10,... | collective-permute-start | bytes 1572872 | tf_op jit(solution)/shard_map/ppermute | solution.py:476
  167.2 42.3 %copy-start.13 = (bf16[2,8,16384]{2,1,0:T(8,128)(2,1)}, bf16[2,8,16384]{2,1,0:T(8,128)(2,1)S(1)}, u32[]{:S(2)}) copy-start(bf16[2,8,16384]{2,1,0:T(8,128)(2,1)S(1)} %collective-permute-done.6.refs_7_) | copy-start | bytes 1572868
  167.2 46.8 %collective-permute-start.20 = (bf16[2,8,16384]{2,1,0:T(8,128)(2,1)}, bf16[2,8,16384]{2,1,0:T(8,128)(2,1)}, u32[]{:S(2)}, u32[]{:S(2)}) collective-permute-start(bf16[2,8,16384]{2,1,0:T(8,128)(2,1)} %get-tuple-element.41), channel_id=1, source_target_pairs={{0,5},{1,4},{2,7},{3,6},{4,1},{5,0},{6,3},{7,2},{8,13},{9,12},{10,... | collective-permute-start | bytes 1572872 | tf_op jit(solution)/shard_map/ppermute | solution.py:476
  167.5 42.0 %copy-start.14 = (bf16[2,8,16384]{2,1,0:T(8,128)(2,1)}, bf16[2,8,16384]{2,1,0:T(8,128)(2,1)S(1)}, u32[]{:S(2)}) copy-start(bf16[2,8,16384]{2,1,0:T(8,128)(2,1)S(1)} %collective-permute-done.16.refs_9_) | copy-start | bytes 1572868
  167.5 46.5 %collective-permute-start.21 = (bf16[2,8,16384]{2,1,0:T(8,128)(2,1)}, bf16[2,8,16384]{2,1,0:T(8,128)(2,1)}, u32[]{:S(2)}, u32[]{:S(2)}) collective-permute-start(bf16[2,8,16384]{2,1,0:T(8,128)(2,1)} %get-tuple-element.42), channel_id=1, source_target_pairs={{0,6},{1,7},{2,4},{3,5},{4,2},{5,3},{6,0},{7,1},{8,14},{9,15},{10,... | collective-permute-start | bytes 1572872 | tf_op jit(solution)/shard_map/ppermute | solution.py:476
  171.9 37.7 %copy-start.15 = (bf16[2,8,16384]{2,1,0:T(8,128)(2,1)}, bf16[2,8,16384]{2,1,0:T(8,128)(2,1)S(1)}, u32[]{:S(2)}) copy-start(bf16[2,8,16384]{2,1,0:T(8,128)(2,1)S(1)} %collective-permute-done.17.refs_10_) | copy-start | bytes 1572868
  171.9 42.1 %collective-permute-start.22 = (bf16[2,8,16384]{2,1,0:T(8,128)(2,1)}, bf16[2,8,16384]{2,1,0:T(8,128)(2,1)}, u32[]{:S(2)}, u32[]{:S(2)}) collective-permute-start(bf16[2,8,16384]{2,1,0:T(8,128)(2,1)} %get-tuple-element.43), channel_id=1, source_target_pairs={{0,7},{1,6},{2,5},{3,4},{4,3},{5,2},{6,1},{7,0},{8,15},{9,14},{10,... | collective-permute-start | bytes 1572872 | tf_op jit(solution)/shard_map/ppermute | solution.py:476
  209.5 4.5 %copy-start.16 = (bf16[2,8,16384]{2,1,0:T(8,128)(2,1)}, bf16[2,8,16384]{2,1,0:T(8,128)(2,1)S(1)}, u32[]{:S(2)}) copy-start(bf16[2,8,16384]{2,1,0:T(8,128)(2,1)S(1)} %collective-permute-done.18.refs_11_) | copy-start | bytes 1572868
  236.8 22.1 %collective-permute-start.23 = (f32[2,8,4,128]{3,2,1,0:T(4,128)S(1)}, f32[2,8,4,128]{3,2,1,0:T(4,128)S(1)}, u32[]{:S(2)}, u32[]{:S(2)}) collective-permute-start(f32[2,8,4,128]{3,2,1,0:T(4,128)S(1)} %get-tuple-element.51), channel_id=1, source_target_pairs={{0,8},{1,9},{2,10},{3,11},{4,12},{5,13},{6,14},{7,15},{8,0},{9,1},... | collective-permute-start | bytes 98312 | tf_op jit(solution)/shard_map/ppermute | solution.py:500
  255.4 10.7 %all-to-all-start = ((f32[16,8,128]{2,1,0:T(8,128)}), f32[16,8,128]{2,1,0:T(8,128)S(1)}, u32[]{:S(2)}, u32[]{:S(2)}) async-start(f32[16,8,128]{2,1,0:T(8,128)} %bitcast.8), calls=%async_computation | async-start | bytes 131072 | tf_op jit(solution)/shard_map/all_to_all | solution.py:507

commit v12 on v10

--- a/solution.py
+++ b/solution.py
@@ -389,9 +389,9 @@
     return numer / jnp.sqrt(var_x * var_y)
 
 
-def plane_sums_kernel(ended, got_ref, *refs):
-    moved_refs, before, outs, acc = refs[:4], refs[4 : 4 + ended], refs[4 + ended : -1], refs[-1]
-    rows, depth = got_ref.shape
+def plane_sums_kernel(own_ref, far_ref, *refs):
+    moved_refs, (mine_ref, near_ref, back_ref, acc) = refs[:4], refs[4:]
+    rows, depth = own_ref.shape
     step = min(1024, depth)
     half = LANES // 2
     slabs = rows // SLAB // 2
@@ -404,15 +404,19 @@
         cols = slice(i * step, (i + 1) * step)
         is_x = lax.broadcasted_iota(jnp.int32, (slabs, SLAB, step), 1) < SUB
         low = lax.broadcasted_iota(jnp.int32, (step, LANES), 1) < half
-        full = got_ref[:, cols].astype(jnp.float32).reshape(slabs, 2, SLAB, step)
+        fulls = [
+            ref[:, cols].astype(jnp.float32).reshape(slabs, 2, SLAB, step) for ref in (own_ref, far_ref)
+        ]
         for t in range(2):
-            wide = full[:, t]
-            rolled = pltpu.roll(wide, SUB, 1)
-            product = wide * rolled
-            both = jnp.where(is_x, product * wide, product).reshape(slabs * SLAB, step)
-            even = rolled.reshape(slabs // 2, 2, SLAB, step)[:, 0]
-            odd = wide.reshape(slabs // 2, 2, SLAB, step)[:, 1]
-            weights = jnp.where(is_x[: slabs // 2], even, odd).reshape(slabs // 2 * SLAB, step)
+            weights, products = [], []
+            for full in fulls:
+                wide = full[:, t]
+                rolled = pltpu.roll(wide, SUB, 1)
+                product = wide * rolled
+                products.append(jnp.where(is_x, product * wide, product).reshape(slabs * SLAB, step))
+                even = rolled.reshape(slabs // 2, 2, SLAB, step)[:, 0]
+                odd = wide.reshape(slabs // 2, 2, SLAB, step)[:, 1]
+                weights.append(jnp.where(is_x[: slabs // 2], even, odd).reshape(slabs // 2 * SLAB, step))
             linear, square = [], []
             for a in range(2):
                 values = moved_refs[2 * t + a][cols, :].astype(jnp.float32)
@@ -421,12 +425,12 @@
                 linear.append(jnp.where(low, product, values).astype(jnp.bfloat16))
                 square.append(product * (values if a == 0 else swapped))
             right = jnp.concatenate(linear + [jnp.where(low, *square).astype(jnp.bfloat16)], 1)
-            left = jnp.concatenate([weights, both], 0).astype(jnp.bfloat16)
+            left = jnp.concatenate(weights + products, 0).astype(jnp.bfloat16)
             acc[t] += jnp.dot(left, right, preferred_element_type=jnp.float32)
 
     @pl.when(pl.program_id(0) == pl.num_programs(0) - 1)
     def _():
-        count = slabs * SUB
+        count = 2 * slabs * SUB
         tiles = count // SLAB
         top = lax.broadcasted_iota(jnp.int32, (tiles, SLAB, LANES), 1) < SUB
         low = lax.broadcasted_iota(jnp.int32, (count, LANES), 1) < half
@@ -455,49 +459,40 @@
             straight = jnp.where(low, kept, pltpu.roll(got, half, 1))
             crossed = jnp.where(low, got, pltpu.roll(kept, half, 1))
             results.append(jnp.where(lax.rem(me, 2) == 0, straight, crossed))
-        if not ended:
-            for t in range(2):
-                outs[0][t] = results[t]
-            return
-        mine_ref, near_ref, back_ref = outs
+        mine, near = results
+        mine_ref[...] = mine
+        near_ref[...] = near
+        mine, near = mine.reshape(tiles, SLAB, LANES), near.reshape(tiles, SLAB, LANES)
+        even = jnp.where(top, mine, pltpu.roll(near, SUB, 1))
+        odd = jnp.where(top, pltpu.roll(mine, SUB, 1), near)
         upper = lax.div(me, 2 * PLANE)
-        for part, (mine, near) in enumerate(((before[0][0], before[0][1]), results)):
-            mine_ref[part] = mine
-            near_ref[part] = near
-            mine, near = mine.reshape(tiles, SLAB, LANES), near.reshape(tiles, SLAB, LANES)
+        for i in range(tiles):
+            part, c = 2 * i // slabs, 2 * i % slabs
             slot = part + upper - 2 * part * upper
-            even = jnp.where(top, mine, pltpu.roll(near, SUB, 1))
-            odd = jnp.where(top, pltpu.roll(mine, SUB, 1), near)
-            for i in range(tiles):
-                for twin in range(2):
-                    back_ref[slot, twin, 2 * i] = even[i]
-                    back_ref[slot, twin, 2 * i + 1] = odd[i]
-
-
-def plane_sums(got, moved, before):
-    rows, width = got.shape
+            back_ref[slot, c] = even[i]
+            back_ref[slot, c + 1] = odd[i]
+
+
+def plane_sums(own, far, moved):
+    rows, width = own.shape
     depth = min(2048, width)
-    ended = before is not None
-    count = rows // 4
+    count = rows // 2
+    part = pl.BlockSpec((rows, depth), lambda i: (0, i))
     placed = pl.BlockSpec((depth, LANES), lambda i: (i, 0))
-    result = (2, count, LANES)
-    shapes = (result, result, (2, 2, PLANE, SLAB, LANES)) if ended else (result,)
-    entire = [pl.BlockSpec(shape, lambda i, shape=shape: (0,) * len(shape)) for shape in shapes]
-    outs = pl.pallas_call(
-        functools.partial(plane_sums_kernel, ended),
+    shapes = ((count, LANES), (count, LANES), (2, PLANE, SLAB, LANES))
+    return pl.pallas_call(
+        plane_sums_kernel,
         grid=(width // depth,),
         out_shape=tuple(jax.ShapeDtypeStruct(shape, jnp.float32) for shape in shapes),
-        in_specs=[pl.BlockSpec((rows, depth), lambda i: (0, i)), placed, placed, placed, placed]
-        + ([entire[0]] if ended else []),
-        out_specs=tuple(entire),
+        in_specs=[part, part, placed, placed, placed, placed],
+        out_specs=tuple(pl.BlockSpec(shape, lambda i, shape=shape: (0,) * len(shape)) for shape in shapes),
         scratch_shapes=[pltpu.VMEM((2, 3 * count, 3 * LANES), jnp.float32)],
         compiler_params=params(),
         cost_estimate=pl.CostEstimate(
-            flops=9 * rows * width * LANES, bytes_accessed=width * (2 * rows + 8 * LANES), transcendentals=0
+            flops=18 * rows * width * LANES, bytes_accessed=width * (4 * rows + 8 * LANES), transcendentals=0
         ),
         name="plane_sums",
-    )(got, *moved, *((before,) if ended else ()))
-    return outs if ended else outs[0]
+    )(own, far, *moved)
 
 
 def shards_by_plane(intensities, observed, qweights, ops, pick):
@@ -509,6 +504,7 @@
     middle = [(i, 3 * PLANE + 2 * (i % PLANE) - i) for i in range(PLANE, 3 * PLANE)]
     outward = [(i, i - PLANE if i < 2 * PLANE else i + PLANE) for i in range(PLANE, 3 * PLANE)]
     rings = [[z * PLANE + c for c in range(PLANE)] for z in range(PLANES)]
+    couples = [[z * PLANE + c for z in (odd, odd + 2) for c in range(PLANE)] for odd in range(2)]
     plane = lax.axis_index("dp") // PLANE
     odd, upper = plane % 2 == 1, plane >= 2
 
@@ -536,11 +532,9 @@
     near_other = [lax.ppermute(rows, "dp", swap) for rows in near]
     keep, give = place(ops, near, near_other, own_pick, 256)
     far_send = far_pack(far_pick, outer, inner, keep)
-    far_send, give = lax.optimization_barrier((far_send, give))
     far_got = spread(far_send)
     moved = own_moved + [keep, lax.ppermute(give, "dp", swap)]
-    own_corr = plane_sums(own_got, moved, None)
-    ours, theirs, back = plane_sums(far_got, moved, own_corr)
+    ours, theirs, back = plane_sums(own_got, far_got, moved)
 
     from_near = lax.ppermute(theirs, "dp", beside)
     pair = [each.reshape(2, PLANE, SUB, NOPS * blk) for each in (ours, from_near)]
@@ -549,10 +543,10 @@
     pair = jnp.where(upper, pair[::-1], pair)
     corr = pair.reshape(groups * SUB, NOPS * blk).T.reshape(NOPS, blk, groups * SUB)
 
-    back = back.reshape(groups, 2 * SUB, NOPS * blk)
-    back = lax.all_to_all(back, "dp", split_axis=0, concat_axis=0, tiled=True)
-    back = back.reshape(2, 2, PLANE, 2, SUB, NOPS, blk)
-    back = jnp.where(odd, back[:, 1, :, ::-1], back[:, 0])
+    back = back.reshape(2 * PLANE, 2 * SUB, NOPS * blk)
+    back = lax.all_to_all(back, "dp", split_axis=0, concat_axis=0, axis_index_groups=couples, tiled=True)
+    back = back.reshape(2, PLANE, 2, SUB, NOPS, blk)
+    back = jnp.where(odd, back[:, :, ::-1], back)
     returned = jnp.transpose(back, (4, 0, 2, 1, 3, 5)).reshape(NOPS, 1, groups, SUB, blk)
     return (corr, returned)
 

time: 217 us -> 215 us (level)
  Pallas kernels: 132 us -> 118 us
  waiting for transfers between devices: 46.7 us -> 57.9 us
    all_to_all x2, waiting for transfers between devices: 30.9 us -> 49.1 us  [spread(): lax.all_to_all(send, 'dp', split_axis=0, concat_axis=0, axis_index_groups...]
    pallas_call x2 -> x1, Pallas kernels: 30.9 us -> 17.6 us  [plane_sums(): pl.pallas_call(plane_sums_kernel, grid=(width // depth,), out_shape=tuple...]
    ppermute x1, starting transfers between devices: 1.73 us -> 5.4 us  [shards_by_plane(): far_pick = lax.ppermute(own_pick, 'dp', across)]
    ppermute x2, starting transfers between devices: 6.03 us -> 2.92 us  [shards_by_plane(): near = [lax.ppermute(rows, 'dp', beside) for rows in mine]]
    ppermute x1, waiting for transfers between devices: 2.85 us -> 0.01 us  [shards_by_plane(): moved = own_moved + [keep, lax.ppermute(give, 'dp', swap)]]
    ppermute x2, waiting for transfers between devices: 2.76 us -> 0.01 us  [shards_by_plane(): other = [lax.ppermute(rows, 'dp', swap) for rows in mine]]
  transfers between devices with their start and end apart: 19 -> 19, of which waited for: 5 -> 3; matrix products, arithmetic and copies ran while one was open for 1% -> 1% of each run, Pallas kernels for 52% -> 45%
where the time goes in v12:
time: 215 us
  Pallas kernels  118 us (55%)
  waiting for transfers between devices  57.9 us (27%)
  starting transfers between devices  31.7 us (15%)
  local copies, waits for them, and re-layouts  4.02 us (2%)
    pallas_call x2, Pallas kernels, place(): pl.pallas_call(place_kernel, grid=(count, HALVES * chunks), out_shape=(ja...  84.2 us
    all_to_all x2, waiting for transfers between devices, spread(): lax.all_to_all(send, 'dp', split_axis=0, concat_axis=0, axis_index_groups...  49.1 us
    pallas_call x1, Pallas kernels, plane_sums(): pl.pallas_call(plane_sums_kernel, grid=(width // depth,), out_shape=tuple...  17.6 us
    pallas_call x2, Pallas kernels, pack_call(): pl.pallas_call(kernel, out_shape=jax.ShapeDtypeStruct((PLANE, 2, SLAB, wi...  9.33 us
    all_to_all x2, starting transfers between devices, spread(): lax.all_to_all(send, 'dp', split_axis=0, concat_axis=0, axis_index_groups...  9.29 us
    pallas_call x2, Pallas kernels, weigh(): pl.pallas_call(weigh_kernel, grid=(count,), out_shape=jax.ShapeDtypeStruc...  7.31 us
    all_to_all x1, waiting for transfers between devices, shards_by_plane(): lax.all_to_all(back, 'dp', split_axis=0, concat_axis=0, axis_index_groups...  5.7 us
    ppermute x1, starting transfers between devices, shards_by_plane(): far_pick = lax.ppermute(own_pick, 'dp', across)  5.4 us
  transfers between devices with their start and end apart: 19, of which 3 were waited for; matrix products, arithmetic and copies ran while one was open for 1% of the time, Pallas kernels for 45%

profile of v12, /device:TPU:0, one launch (start us, length us, event | category | flops | bytes accessed | tf_op | source)
XLA Modules:
  0.0 214.5 jit_solution(15738792874619307217)
XLA Ops:
  0.6 0.0 copy-start
  0.6 3.7 %weigh.2.refs_0_ = bf16[64,8192]{1,0:T(8,128)(2,1)} custom-call(bf16[32,16384]{1,0:T(8,128)(2,1)} %x_ref.3, s32[32,16384]{1,0:T(8,128)} %obs_ref.3, bf16[32,16384]{1,0:T(8,128)(2,1)} %qw_ref.3), custom_call_target="tpu_custom_call" | custom-call | flops 524288 | bytes 3145728 | tf_op jit(solution)/shard_map/weigh/pallas_call | solution.py:206
  4.3 0.5 collective-permute-start.5
  4.8 2.6 %collective-permute-start = (bf16[64,8192]{1,0:T(8,128)(2,1)}, bf16[64,8192]{1,0:T(8,128)(2,1)S(1)}, u32[]{:S(2)}, u32[]{:S(2)}) collective-permute-start(bf16[64,8192]{1,0:T(8,128)(2,1)} %weigh.2.refs_0_), channel_id=1, source_target_pairs={{0,8},{1,9},{2,10},{3,11},{4,12},{5,13},{6,14},{7,15},{8,0},{9,1},... | collective-permute-start | bytes 3145736 | tf_op jit(solution)/shard_map/ppermute | solution.py:519
  7.4 3.6 %weigh.3.refs_1_ = bf16[64,8192]{1,0:T(8,128)(2,1)} custom-call(bf16[32,16384]{1,0:T(8,128)(2,1)} %x_ref.3, s32[32,16384]{1,0:T(8,128)} %obs_ref.3, bf16[32,16384]{1,0:T(8,128)(2,1)} %qw_ref.3), custom_call_target="tpu_custom_call" | custom-call | flops 524288 | bytes 3145728 | tf_op jit(solution)/shard_map/weigh/pallas_call | solution.py:206
  11.0 0.2 collective-permute-start.6
  11.2 0.3 collective-permute-start.1
  11.5 0.0 copy-done.1
  11.5 1.6 collective-permute-start.2
  13.1 4.3 %own_pack.1 = bf16[8,2,8,16384]{3,2,1,0:T(8,128)(2,1)} custom-call(s32[32]{0:T(128)} %bitcast.23, bf16[64,8192]{1,0:T(8,128)(2,1)} %weigh.2.refs_0_, bf16[64,8192]{1,0:T(8,128)(2,1)} %weigh.3.refs_1_), custom_call_target="tpu_custom_call" | custom-call | flops 2097152 | bytes 6291456 | tf_op jit(solution)/shard_map/own_pack/pallas_call | solution.py:275
  17.5 0.0 copy-start.2
  17.5 0.0 copy-start.10
  17.5 4.7 %all-to-all-start = ((bf16[8,2,8,16384]{3,2,1,0:T(8,128)(2,1)}), bf16[8,2,8,16384]{3,2,1,0:T(8,128)(2,1)}, u32[]{:S(2)}, u32[]{:S(2)}) async-start(bf16[8,2,8,16384]{3,2,1,0:T(8,128)(2,1)} %own_pack.1), calls=%async_computation | async-start | bytes 8388608 | tf_op jit(solution)/shard_map/all_to_all | solution.py:512
  22.2 0.0 collective-permute-done.5.refs_2_
  22.2 0.0 copy-done.2
  22.2 1.6 collective-permute-start.3
  23.9 0.0 copy-done
  23.9 0.1 constant_dynamic-slice_fusion
  23.9 0.0 collective-permute-done.6.refs_3_
  24.0 5.4 %collective-permute-start.4 = (s32[32]{0:T(128)S(1)}, s32[32]{0:T(128)S(1)}, u32[]{:S(2)}, u32[]{:S(2)}) collective-permute-start(s32[32]{0:T(128)S(1)} %bitcast.26), channel_id=1, source_target_pairs={{0,16},{1,17},{2,18},{3,19},{4,20},{5,21},{6,22},{7,23},{8,24},{9,... | collective-permute-start | bytes 392 | tf_op jit(solution)/shard_map/ppermute | solution.py:522
  29.4 0.7 broadcast_in_dim.3.ops_ref
  30.1 42.1 %place.2 = (bf16[16384,128]{1,0:T(8,128)(2,1)}, bf16[16384,128]{1,0:T(8,128)(2,1)}) custom-call(s32[2,1,16384]{2,1,0:T(1,128)} %broadcast_in_dim.3.ops_ref, bf16[64,8192]{1,0:T(8,128)(2,1)} %weigh.2.refs_0_, bf16[64,8192]{1,0:T(8,128)(2,1)} %weigh.3.refs_1_, bf16[64,8192]{1,0:T(8,128)(2,1)} %collective-permute-done.5.refs_2_, ...), custom_call_target="tpu_custom_call" | custom-call | bytes 8388608 | tf_op jit(solution)/shard_map/place/pallas_call | solution.py:367
  72.2 0.0 collective-permute-done.4.pick_ref
  72.2 0.0 collective-permute-done.refs_0_
  72.2 0.0 copy-start.3
  72.2 0.0 collective-permute-done.1.refs_1_
  72.2 0.0 collective-permute-done.2
  72.2 0.0 collective-permute-done.3
  72.2 0.1 collective-permute-start.11
  72.3 0.5 collective-permute-start.12
  72.8 0.7 collective-permute-start.10
  73.5 1.3 collective-permute-start.7
  74.8 1.3 collective-permute-start.8
  76.1 0.0 collective-permute-done.11.refs_2_
  76.1 0.7 collective-permute-start.9
  76.9 0.0 collective-permute-done.12.refs_3_
  76.9 0.0 copy-start.9
  76.9 0.1 collective-permute-start.13
  77.1 0.1 copy-done.8
  77.1 0.8 copy-done.9
  77.9 42.1 %place.3 = (bf16[16384,128]{1,0:T(8,128)(2,1)}, bf16[16384,128]{1,0:T(8,128)(2,1)}) custom-call(s32[2,1,16384]{2,1,0:T(1,128)} %broadcast_in_dim.3.ops_ref, bf16[64,8192]{1,0:T(8,128)(2,1)} %copy-done.3, bf16[64,8192]{1,0:T(8,128)(2,1)} %collective-permute-done.1.refs_1_, bf16[64,8192]{1,0:T(8,128)(2,1)} %copy-done.8, bf16[64,8192]{1,0:T(8,128)(2,1)} %copy-done.9, ...), custom_call_target="tpu_custom_call" | custom-call | bytes 536870912 | tf_op jit(solution)/shard_map/place/pallas_call | solution.py:367
  120.0 0.0 collective-permute-done.10.refs_3_
  120.0 0.1 collective-permute-start.14
  120.2 0.0 collective-permute-done.7.refs_0_
  120.2 3.1 %collective-permute-done.8.refs_1_ = bf16[64,8192]{1,0:T(8,128)(2,1)S(1)} collective-permute-done((bf16[64,8192]{1,0:T(8,128)(2,1)}, bf16[64,8192]{1,0:T(8,128)(2,1)S(1)}, u32[]{:S(2)}, u32[]{:S(2)}) %collective-permute-start.8) | collective-permute-done | bytes 1048608 | tf_op jit(solution)/shard_map/ppermute | solution.py:530
  123.2 0.0 collective-permute-done.9.refs_2_
  123.3 0.9 copy-done.6
  124.2 0.4 copy-done.7
  124.6 5.0 %far_pack.1 = bf16[8,2,8,16384]{3,2,1,0:T(8,128)(2,1)} custom-call(s32[32]{0:T(128)} %copy-done.11, bf16[64,8192]{1,0:T(8,128)(2,1)} %copy-done.5, bf16[64,8192]{1,0:T(8,128)(2,1)} %copy-done.6, bf16[64,8192]{1,0:T(8,128)(2,1)} %copy-done.7, bf16[64,8192]{1,0:T(8,128)(2,1)} %copy-done.4, bf16[16384,128]{1,0:T(8,128)(2,1)} %get-tuple-element.21.refs_4_.refs_2_), custom_call_target="tpu_custom_call" | custom-call | flops 2097152 | bytes 6291456 | tf_op jit(solution)/shard_map/far_pack/pallas_call | solution.py:275
  129.6 0.0 all-to-all-done
  129.6 4.6 %all-to-all-start.1 = ((bf16[8,2,8,16384]{3,2,1,0:T(8,128)(2,1)}), bf16[8,2,8,16384]{3,2,1,0:T(8,128)(2,1)}, u32[]{:S(2)}, u32[]{:S(2)}) async-start(bf16[8,2,8,16384]{3,2,1,0:T(8,128)(2,1)} %far_pack.1), calls=%async_computation.1 | async-start | bytes 8388608 | tf_op jit(solution)/shard_map/all_to_all | solution.py:512
  134.3 0.0 collective-permute-done.13.refs_1_
  134.3 49.1 %all-to-all-done.1 = bf16[8,2,8,16384]{3,2,1,0:T(8,128)(2,1)} async-done(((bf16[8,2,8,16384]{3,2,1,0:T(8,128)(2,1)}), bf16[8,2,8,16384]{3,2,1,0:T(8,128)(2,1)}, u32[]{:S(2)}, u32[]{:S(2)}) %all-to-all-start.1) | async-done | bytes 4194336 | tf_op jit(solution)/shard_map/all_to_all | solution.py:512
  183.4 0.0 collective-permute-done.14.refs_3_
  183.4 17.6 %plane_sums.1 = (f32[64,128]{1,0:T(8,128)}, f32[64,128]{1,0:T(8,128)}, f32[2,8,8,128]{3,2,1,0:T(8,128)}) custom-call(bf16[128,16384]{1,0:T(8,128)(2,1)} %bitcast.1.own_ref, bf16[128,16384]{1,0:T(8,128)(2,1)} %bitcast.2.far_ref, bf16[16384,128]{1,0:T(8,128)(2,1)} %get-tuple-element.22.refs_0_, bf16[16384,128]{1,0:T(8,128)(2,1)} %collective-permute-done.13.refs_1_, ...), custom_call_target="tpu_custom_call" | custom-call | flops 4831838208 | bytes 25165824 | tf_op jit(solution)/shard_map/plane_sums/pallas_call | solution.py:483
  200.9 1.8 collective-permute-start.15
  202.7 3.5 %all-to-all-start.2 = ((f32[16,8,128]{2,1,0:T(8,128)}), f32[16,8,128]{2,1,0:T(8,128)S(1)}, u32[]{:S(2)}, u32[]{:S(2)}) async-start(f32[16,8,128]{2,1,0:T(8,128)} %bitcast.19), calls=%async_computation.2 | async-start | bytes 131072 | tf_op jit(solution)/shard_map/all_to_all | solution.py:547
  206.2 0.0 collective-permute-done.15
  206.3 0.8 pad_maximum_fusion
  207.1 0.7 copy.16
  207.8 5.7 %all-to-all-done.2 = f32[16,8,128]{2,1,0:T(8,128)S(1)} async-done(((f32[16,8,128]{2,1,0:T(8,128)}), f32[16,8,128]{2,1,0:T(8,128)S(1)}, u32[]{:S(2)}, u32[]{:S(2)}) %all-to-all-start.2) | async-done | bytes 65568 | tf_op jit(solution)/shard_map/all_to_all | solution.py:547
  213.5 0.2 reshape.30
  213.7 0.1 copy.17
  213.8 0.8 reverse_select_fusion
  (14 shorter events, 0.1 us)
Async XLA Ops:
  0.6 23.2 %copy-start = (s32[4,16384]{1,0:T(4,128)S(1)}, s32[4,16384]{1,0:T(4,128)}, u32[]{:S(2)}) copy-start(s32[4,16384]{1,0:T(4,128)} %param.8) | copy-start | bytes 786436
  4.3 7.2 %copy-start.1 = (bf16[64,8192]{1,0:T(8,128)(2,1)S(1)}, bf16[64,8192]{1,0:T(8,128)(2,1)}, u32[]{:S(2)}) copy-start(bf16[64,8192]{1,0:T(8,128)(2,1)} %weigh.2.refs_0_) | copy-start | bytes 3145732
  4.3 17.9 %collective-permute-start.5 = (bf16[64,8192]{1,0:T(8,128)(2,1)}, bf16[64,8192]{1,0:T(8,128)(2,1)}, u32[]{:S(2)}, u32[]{:S(2)}) collective-permute-start(bf16[64,8192]{1,0:T(8,128)(2,1)} %weigh.2.refs_0_), channel_id=1, source_target_pairs={{0,1},{1,0},{2,3},{3,2},{4,5},{5,4},{6,7},{7,6},{8,9},{9,8},{10,11... | collective-permute-start | bytes 3145736 | tf_op jit(solution)/shard_map/ppermute | solution.py:521
  4.8 67.4 %collective-permute-start = (bf16[64,8192]{1,0:T(8,128)(2,1)}, bf16[64,8192]{1,0:T(8,128)(2,1)S(1)}, u32[]{:S(2)}, u32[]{:S(2)}) collective-permute-start(bf16[64,8192]{1,0:T(8,128)(2,1)} %weigh.2.refs_0_), channel_id=1, source_target_pairs={{0,8},{1,9},{2,10},{3,11},{4,12},{5,13},{6,14},{7,15},{8,0},{9,1},... | collective-permute-start | bytes 3145736 | tf_op jit(solution)/shard_map/ppermute | solution.py:519
  11.0 12.9 %collective-permute-start.6 = (bf16[64,8192]{1,0:T(8,128)(2,1)}, bf16[64,8192]{1,0:T(8,128)(2,1)}, u32[]{:S(2)}, u32[]{:S(2)}) collective-permute-start(bf16[64,8192]{1,0:T(8,128)(2,1)} %weigh.3.refs_1_), channel_id=1, source_target_pairs={{0,1},{1,0},{2,3},{3,2},{4,5},{5,4},{6,7},{7,6},{8,9},{9,8},{10,11... | collective-permute-start | bytes 3145736 | tf_op jit(solution)/shard_map/ppermute | solution.py:521
  11.2 61.0 %collective-permute-start.1 = (bf16[64,8192]{1,0:T(8,128)(2,1)}, bf16[64,8192]{1,0:T(8,128)(2,1)}, u32[]{:S(2)}, u32[]{:S(2)}) collective-permute-start(bf16[64,8192]{1,0:T(8,128)(2,1)} %weigh.3.refs_1_), channel_id=1, source_target_pairs={{0,8},{1,9},{2,10},{3,11},{4,12},{5,13},{6,14},{7,15},{8,0},{9,1},... | collective-permute-start | bytes 3145736 | tf_op jit(solution)/shard_map/ppermute | solution.py:519
  11.5 60.7 %collective-permute-start.2 = (bf16[64,8192]{1,0:T(8,128)(2,1)S(1)}, bf16[64,8192]{1,0:T(8,128)(2,1)}, u32[]{:S(2)}, u32[]{:S(2)}) collective-permute-start(bf16[64,8192]{1,0:T(8,128)(2,1)S(1)} %copy-done.1), channel_id=1, source_target_pairs={{8,16},{9,17},{10,18},{11,19},{12,20},{13,21},{14,22},{15,23},{16,... | collective-permute-start | bytes 3145736 | tf_op jit(solution)/shard_map/ppermute | solution.py:520
  17.5 4.8 %copy-start.2 = (bf16[64,8192]{1,0:T(8,128)(2,1)S(1)}, bf16[64,8192]{1,0:T(8,128)(2,1)}, u32[]{:S(2)}) copy-start(bf16[64,8192]{1,0:T(8,128)(2,1)} %weigh.3.refs_1_) | copy-start | bytes 3145732
  17.5 6.5 %copy-start.10 = (s32[32,1]{0,1:T(1,128)S(1)}, s32[32,1]{0,1:T(1,128)}, u32[]{:S(2)}) copy-start(s32[32,1]{0,1:T(1,128)} %param.9) | copy-start | bytes 388
  17.5 112.1 %all-to-all-start = ((bf16[8,2,8,16384]{3,2,1,0:T(8,128)(2,1)}), bf16[8,2,8,16384]{3,2,1,0:T(8,128)(2,1)}, u32[]{:S(2)}, u32[]{:S(2)}) async-start(bf16[8,2,8,16384]{3,2,1,0:T(8,128)(2,1)} %own_pack.1), calls=%async_computation | async-start | bytes 8388608 | tf_op jit(solution)/shard_map/all_to_all | solution.py:512
  22.2 50.0 %collective-permute-start.3 = (bf16[64,8192]{1,0:T(8,128)(2,1)S(1)}, bf16[64,8192]{1,0:T(8,128)(2,1)}, u32[]{:S(2)}, u32[]{:S(2)}) collective-permute-start(bf16[64,8192]{1,0:T(8,128)(2,1)S(1)} %copy-done.2), channel_id=1, source_target_pairs={{8,16},{9,17},{10,18},{11,19},{12,20},{13,21},{14,22},{15,23},{16,... | collective-permute-start | bytes 3145736 | tf_op jit(solution)/shard_map/ppermute | solution.py:520
  24.0 48.2 %collective-permute-start.4 = (s32[32]{0:T(128)S(1)}, s32[32]{0:T(128)S(1)}, u32[]{:S(2)}, u32[]{:S(2)}) collective-permute-start(s32[32]{0:T(128)S(1)} %bitcast.26), channel_id=1, source_target_pairs={{0,16},{1,17},{2,18},{3,19},{4,20},{5,21},{6,22},{7,23},{8,24},{9,... | collective-permute-start | bytes 392 | tf_op jit(solution)/shard_map/ppermute | solution.py:522
  72.2 51.1 %copy-start.11 = (s32[32]{0:T(128)}, s32[32]{0:T(128)S(1)}, u32[]{:S(2)}) copy-start(s32[32]{0:T(128)S(1)} %collective-permute-done.4.pick_ref) | copy-start | bytes 388
  72.2 4.9 %copy-start.3 = (bf16[64,8192]{1,0:T(8,128)(2,1)}, bf16[64,8192]{1,0:T(8,128)(2,1)S(1)}, u32[]{:S(2)}) copy-start(bf16[64,8192]{1,0:T(8,128)(2,1)S(1)} %collective-permute-done.refs_0_) | copy-start | bytes 3145732
  72.2 3.9 %collective-permute-start.11 = (bf16[64,8192]{1,0:T(8,128)(2,1)S(1)}, bf16[64,8192]{1,0:T(8,128)(2,1)S(1)}, u32[]{:S(2)}, u32[]{:S(2)}) collective-permute-start(bf16[64,8192]{1,0:T(8,128)(2,1)S(1)} %collective-permute-done.refs_0_), channel_id=1, source_target_pairs={{0,1},{1,0},{2,3},{3,2},{4,5},{5,4},{6,7},{7,6},{8,9},{9,8},{10,11... | collective-permute-start | bytes 3145736 | tf_op jit(solution)/shard_map/ppermute | solution.py:532
  72.3 4.6 %collective-permute-start.12 = (bf16[64,8192]{1,0:T(8,128)(2,1)}, bf16[64,8192]{1,0:T(8,128)(2,1)S(1)}, u32[]{:S(2)}, u32[]{:S(2)}) collective-permute-start(bf16[64,8192]{1,0:T(8,128)(2,1)} %collective-permute-done.1.refs_1_), channel_id=1, source_target_pairs={{0,1},{1,0},{2,3},{3,2},{4,5},{5,4},{6,7},{7,6},{8,9},{9,8},{10,11... | collective-permute-start | bytes 3145736 | tf_op jit(solution)/shard_map/ppermute | solution.py:532
  72.8 47.2 %collective-permute-start.10 = (bf16[64,8192]{1,0:T(8,128)(2,1)}, bf16[64,8192]{1,0:T(8,128)(2,1)S(1)}, u32[]{:S(2)}, u32[]{:S(2)}) collective-permute-start(bf16[64,8192]{1,0:T(8,128)(2,1)} %collective-permute-done.1.refs_1_), channel_id=1, source_target_pairs={{8,16},{9,17},{10,18},{11,19},{12,20},{13,21},{14,22},{15,23},{16,... | collective-permute-start | bytes 3145736 | tf_op jit(solution)/shard_map/ppermute | solution.py:531
  73.5 46.6 %collective-permute-start.7 = (bf16[64,8192]{1,0:T(8,128)(2,1)}, bf16[64,8192]{1,0:T(8,128)(2,1)S(1)}, u32[]{:S(2)}, u32[]{:S(2)}) collective-permute-start(bf16[64,8192]{1,0:T(8,128)(2,1)} %collective-permute-done.2), channel_id=1, source_target_pairs={{8,0},{9,1},{10,2},{11,3},{12,4},{13,5},{14,6},{15,7},{16,24},{17,... | collective-permute-start | bytes 3145736 | tf_op jit(solution)/shard_map/ppermute | solution.py:530
  74.8 48.4 %collective-permute-start.8 = (bf16[64,8192]{1,0:T(8,128)(2,1)}, bf16[64,8192]{1,0:T(8,128)(2,1)S(1)}, u32[]{:S(2)}, u32[]{:S(2)}) collective-permute-start(bf16[64,8192]{1,0:T(8,128)(2,1)} %collective-permute-done.3), channel_id=1, source_target_pairs={{8,0},{9,1},{10,2},{11,3},{12,4},{13,5},{14,6},{15,7},{16,24},{17,... | collective-permute-start | bytes 3145736 | tf_op jit(solution)/shard_map/ppermute | solution.py:530
  76.1 1.0 copy-start.8
  76.1 47.1 %collective-permute-start.9 = (bf16[64,8192]{1,0:T(8,128)(2,1)S(1)}, bf16[64,8192]{1,0:T(8,128)(2,1)S(1)}, u32[]{:S(2)}, u32[]{:S(2)}) collective-permute-start(bf16[64,8192]{1,0:T(8,128)(2,1)S(1)} %collective-permute-done.refs_0_), channel_id=1, source_target_pairs={{8,16},{9,17},{10,18},{11,19},{12,20},{13,21},{14,22},{15,23},{16,... | collective-permute-start | bytes 3145736 | tf_op jit(solution)/shard_map/ppermute | solution.py:531
  76.9 1.0 copy-start.9
  76.9 57.4 %collective-permute-start.13 = (bf16[16384,128]{1,0:T(8,128)(2,1)}, bf16[16384,128]{1,0:T(8,128)(2,1)}, u32[]{:S(2)}, u32[]{:S(2)}) collective-permute-start(bf16[16384,128]{1,0:T(8,128)(2,1)} %get-tuple-element.23), channel_id=1, source_target_pairs={{0,1},{1,0},{2,3},{3,2},{4,5},{5,4},{6,7},{7,6},{8,9},{9,8},{10,11... | collective-permute-start | bytes 12582920 | tf_op jit(solution)/shard_map/ppermute | solution.py:526
  120.0 3.2 %copy-start.4 = (bf16[64,8192]{1,0:T(8,128)(2,1)}, bf16[64,8192]{1,0:T(8,128)(2,1)S(1)}, u32[]{:S(2)}) copy-start(bf16[64,8192]{1,0:T(8,128)(2,1)S(1)} %collective-permute-done.10.refs_3_) | copy-start | bytes 3145732
  120.0 63.4 %collective-permute-start.14 = (bf16[16384,128]{1,0:T(8,128)(2,1)}, bf16[16384,128]{1,0:T(8,128)(2,1)}, u32[]{:S(2)}, u32[]{:S(2)}) collective-permute-start(bf16[16384,128]{1,0:T(8,128)(2,1)} %get-tuple-element.24), channel_id=1, source_target_pairs={{0,1},{1,0},{2,3},{3,2},{4,5},{5,4},{6,7},{7,6},{8,9},{9,8},{10,11... | collective-permute-start | bytes 12582920 | tf_op jit(solution)/shard_map/ppermute | solution.py:536
  120.2 3.1 %copy-start.5 = (bf16[64,8192]{1,0:T(8,128)(2,1)}, bf16[64,8192]{1,0:T(8,128)(2,1)S(1)}, u32[]{:S(2)}) copy-start(bf16[64,8192]{1,0:T(8,128)(2,1)S(1)} %collective-permute-done.7.refs_0_) | copy-start | bytes 3145732
  123.2 1.0 copy-start.6
  123.2 1.4 copy-start.7
  129.6 53.7 %all-to-all-start.1 = ((bf16[8,2,8,16384]{3,2,1,0:T(8,128)(2,1)}), bf16[8,2,8,16384]{3,2,1,0:T(8,128)(2,1)}, u32[]{:S(2)}, u32[]{:S(2)}) async-start(bf16[8,2,8,16384]{3,2,1,0:T(8,128)(2,1)} %far_pack.1), calls=%async_computation.1 | async-start | bytes 8388608 | tf_op jit(solution)/shard_map/all_to_all | solution.py:512
  200.9 5.3 %collective-permute-start.15 = (f32[64,128]{1,0:T(8,128)}, f32[64,128]{1,0:T(8,128)S(1)}, u32[]{:S(2)}, u32[]{:S(2)}) collective-permute-start(f32[64,128]{1,0:T(8,128)} %get-tuple-element.26), channel_id=1, source_target_pairs={{0,8},{1,9},{2,10},{3,11},{4,12},{5,13},{6,14},{7,15},{8,0},{9,1},... | collective-permute-start | bytes 98312 | tf_op jit(solution)/shard_map/ppermute | solution.py:539
  202.7 10.8 %all-to-all-start.2 = ((f32[16,8,128]{2,1,0:T(8,128)}), f32[16,8,128]{2,1,0:T(8,128)S(1)}, u32[]{:S(2)}, u32[]{:S(2)}) async-start(f32[16,8,128]{2,1,0:T(8,128)} %bitcast.19), calls=%async_computation.2 | async-start | bytes 131072 | tf_op jit(solution)/shard_map/all_to_all | solution.py:547

commit v13 on v12

--- a/solution.py
+++ b/solution.py
@@ -532,8 +532,10 @@
     near_other = [lax.ppermute(rows, "dp", swap) for rows in near]
     keep, give = place(ops, near, near_other, own_pick, 256)
     far_send = far_pack(far_pick, outer, inner, keep)
+    near_moved = [keep, lax.ppermute(give, "dp", swap)]
+    far_send, own_moved[1], near_moved[1] = lax.optimization_barrier((far_send, own_moved[1], near_moved[1]))
     far_got = spread(far_send)
-    moved = own_moved + [keep, lax.ppermute(give, "dp", swap)]
+    moved = own_moved + near_moved
     ours, theirs, back = plane_sums(own_got, far_got, moved)
 
     from_near = lax.ppermute(theirs, "dp", beside)

time: 215 us -> 266 us (1.24)
  blocking collectives: 0 us -> 53.6 us
  starting transfers between devices: 31.7 us -> 27.6 us
    all_to_all x0 -> x1, blocking collectives: none -> 53.6 us  [spread(): lax.all_to_all(send, 'dp', split_axis=0, concat_axis=0, axis_index_groups...]
    all_to_all x2 -> x1, waiting for transfers between devices: 49.1 us -> 0.01 us  [spread(): lax.all_to_all(send, 'dp', split_axis=0, concat_axis=0, axis_index_groups...]
    ppermute x2, waiting for transfers between devices: 3.07 us -> 46.6 us  [shards_by_plane(): outer = [lax.ppermute(rows, 'dp', outward) for rows in mid]]
    ppermute x2, waiting for transfers between devices: 0.01 us -> 5.14 us  [shards_by_plane(): near_other = [lax.ppermute(rows, 'dp', swap) for rows in near]]
    all_to_all x2 -> x1, starting transfers between devices: 9.29 us -> 4.83 us  [spread(): lax.all_to_all(send, 'dp', split_axis=0, concat_axis=0, axis_index_groups...]
  transfers between devices with their start and end apart: 19 -> 18, of which waited for: 3 -> 6; matrix products, arithmetic and copies ran while one was open for 1% -> 1% of each run, Pallas kernels for 45% -> 37%
where the time goes in v13:
time: 266 us; the launch traced here: 265 us
  Pallas kernels  118 us (44%)
  waiting for transfers between devices  57.5 us (22%)
  blocking collectives  53.6 us (20%)
  starting transfers between devices  27.6 us (10%)
  local copies, waits for them, and re-layouts  5.27 us (2%)
    pallas_call x2, Pallas kernels, place(): pl.pallas_call(place_kernel, grid=(count, HALVES * chunks), out_shape=(ja...  84.2 us
    all_to_all x1, blocking collectives, spread(): lax.all_to_all(send, 'dp', split_axis=0, concat_axis=0, axis_index_groups...  53.6 us
    ppermute x2, waiting for transfers between devices, shards_by_plane(): outer = [lax.ppermute(rows, 'dp', outward) for rows in mid]  46.6 us
    pallas_call x1, Pallas kernels, plane_sums(): pl.pallas_call(plane_sums_kernel, grid=(width // depth,), out_shape=tuple...  17.6 us
    pallas_call x2, Pallas kernels, pack_call(): pl.pallas_call(kernel, out_shape=jax.ShapeDtypeStruct((PLANE, 2, SLAB, wi...  9.3 us
    pallas_call x2, Pallas kernels, weigh(): pl.pallas_call(weigh_kernel, grid=(count,), out_shape=jax.ShapeDtypeStruc...  7.34 us
    ppermute x1, starting transfers between devices, shards_by_plane(): far_pick = lax.ppermute(own_pick, 'dp', across)  6.24 us
    all_to_all x1, waiting for transfers between devices, shards_by_plane(): lax.all_to_all(back, 'dp', split_axis=0, concat_axis=0, axis_index_groups...  5.66 us
  transfers between devices with their start and end apart: 18, of which 6 were waited for; matrix products, arithmetic and copies ran while one was open for 1% of the time, Pallas kernels for 37%

profile of v13, /device:TPU:0, one launch (start us, length us, event | category | flops | bytes accessed | tf_op | source)
XLA Modules:
  0.0 264.9 jit_solution(7322352027147846550)
XLA Ops:
  0.6 0.0 copy-start
  0.6 0.0 copy-start.12
  0.7 3.7 %weigh.2.refs_0_ = bf16[64,8192]{1,0:T(8,128)(2,1)} custom-call(bf16[32,16384]{1,0:T(8,128)(2,1)} %x_ref.3, s32[32,16384]{1,0:T(8,128)} %obs_ref.3, bf16[32,16384]{1,0:T(8,128)(2,1)} %qw_ref.3), custom_call_target="tpu_custom_call" | custom-call | flops 524288 | bytes 3145728 | tf_op jit(solution)/shard_map/weigh/pallas_call | solution.py:206
  4.4 0.5 collective-permute-start.5
  4.8 2.6 collective-permute-start
  7.4 3.6 %weigh.3.refs_1_ = bf16[64,8192]{1,0:T(8,128)(2,1)} custom-call(bf16[32,16384]{1,0:T(8,128)(2,1)} %x_ref.3, s32[32,16384]{1,0:T(8,128)} %obs_ref.3, bf16[32,16384]{1,0:T(8,128)(2,1)} %qw_ref.3), custom_call_target="tpu_custom_call" | custom-call | flops 524288 | bytes 3145728 | tf_op jit(solution)/shard_map/weigh/pallas_call | solution.py:206
  11.1 0.2 collective-permute-start.6
  11.3 0.3 collective-permute-start.1
  11.5 0.0 copy-done.1
  11.5 1.6 collective-permute-start.2
  13.2 0.0 collective-permute-done.5.refs_2_
  13.2 0.7 collective-permute-start.3
  13.9 0.0 copy-done
  13.9 0.1 constant_dynamic-slice_fusion
  14.0 0.1 collective-permute-done.6.refs_3_
  14.1 0.0 copy-done.12
  14.1 6.2 %collective-permute-start.4 = (s32[32]{0:T(128)S(1)}, s32[32]{0:T(128)S(1)}, u32[]{:S(2)}, u32[]{:S(2)}) collective-permute-start(s32[32]{0:T(128)S(1)} %bitcast.27), channel_id=1, source_target_pairs={{0,16},{1,17},{2,18},{3,19},{4,20},{5,21},{6,22},{7,23},{8,24},{9,... | collective-permute-start | bytes 392 | tf_op jit(solution)/shard_map/ppermute | solution.py:522
  20.3 0.7 broadcast_in_dim.3.ops_ref
  21.1 42.1 %place.2 = (bf16[16384,128]{1,0:T(8,128)(2,1)}, bf16[16384,128]{1,0:T(8,128)(2,1)}) custom-call(s32[2,1,16384]{2,1,0:T(1,128)} %broadcast_in_dim.3.ops_ref, bf16[64,8192]{1,0:T(8,128)(2,1)} %weigh.2.refs_0_, bf16[64,8192]{1,0:T(8,128)(2,1)} %weigh.3.refs_1_, bf16[64,8192]{1,0:T(8,128)(2,1)} %collective-permute-done.5.refs_2_, ...), custom_call_target="tpu_custom_call" | custom-call | bytes 8388608 | tf_op jit(solution)/shard_map/place/pallas_call | solution.py:367
  63.2 0.0 collective-permute-done.4.pick_ref
  63.2 0.0 collective-permute-done.refs_0_
  63.2 0.0 copy-start.2
  63.2 0.0 collective-permute-done.1.refs_1_
  63.2 0.0 copy-start.4
  63.2 0.0 collective-permute-done.2
  63.3 0.0 collective-permute-done.3
  63.3 1.0 copy-done.14
  64.3 0.0 collective-permute-start.11
  64.3 0.5 collective-permute-start.12
  64.8 0.0 collective-permute-start.13
  64.8 2.1 collective-permute-done.11.refs_2_
  67.0 3.0 %collective-permute-done.12.refs_3_ = bf16[64,8192]{1,0:T(8,128)(2,1)S(1)} collective-permute-done((bf16[64,8192]{1,0:T(8,128)(2,1)S(1)}, bf16[64,8192]{1,0:T(8,128)(2,1)S(1)}, u32[]{:S(2)}, u32[]{:S(2)}) %collective-permute-start.12) | collective-permute-done | bytes 1048608 | tf_op jit(solution)/shard_map/ppermute | solution.py:532
  70.0 0.0 copy-start.11
  70.0 1.1 copy-done.11
  71.1 42.1 %place.3 = (bf16[16384,128]{1,0:T(8,128)(2,1)}, bf16[16384,128]{1,0:T(8,128)(2,1)}) custom-call(s32[2,1,16384]{2,1,0:T(1,128)} %broadcast_in_dim.3.ops_ref, bf16[64,8192]{1,0:T(8,128)(2,1)} %copy-done.2, bf16[64,8192]{1,0:T(8,128)(2,1)} %copy-done.4, bf16[64,8192]{1,0:T(8,128)(2,1)} %copy-done.9, bf16[64,8192]{1,0:T(8,128)(2,1)} %copy-done.11, s32[32]{0:T(128)} %bitcast.25), custom_call_target="tpu_custom_call" | custom-call | bytes 536870912 | tf_op jit(solution)/shard_map/place/pallas_call | solution.py:367
  113.2 0.1 collective-permute-start.14
  113.3 4.3 %own_pack.1 = bf16[8,2,8,16384]{3,2,1,0:T(8,128)(2,1)} custom-call(s32[32]{0:T(128)} %bitcast.26, bf16[64,8192]{1,0:T(8,128)(2,1)} %weigh.2.refs_0_, bf16[64,8192]{1,0:T(8,128)(2,1)} %weigh.3.refs_1_), custom_call_target="tpu_custom_call" | custom-call | flops 2097152 | bytes 6291456 | tf_op jit(solution)/shard_map/own_pack/pallas_call | solution.py:275
  117.6 4.8 %all-to-all-start = ((bf16[8,2,8,16384]{3,2,1,0:T(8,128)(2,1)}), bf16[8,2,8,16384]{3,2,1,0:T(8,128)(2,1)}, u32[]{:S(2)}, u32[]{:S(2)}) async-start(bf16[8,2,8,16384]{3,2,1,0:T(8,128)(2,1)} %own_pack.1), calls=%async_computation | async-start | bytes 8388608 | tf_op jit(solution)/shard_map/all_to_all | solution.py:512
  122.5 0.7 collective-permute-start.10
  123.2 1.3 collective-permute-start.7
  124.5 1.3 collective-permute-start.8
  125.8 0.0 collective-permute-done.10.refs_3_
  125.9 0.7 collective-permute-start.9
  126.6 24.7 %collective-permute-done.7.refs_0_ = bf16[64,8192]{1,0:T(8,128)(2,1)S(1)} collective-permute-done((bf16[64,8192]{1,0:T(8,128)(2,1)}, bf16[64,8192]{1,0:T(8,128)(2,1)S(1)}, u32[]{:S(2)}, u32[]{:S(2)}) %collective-permute-start.7) | collective-permute-done | bytes 1048608 | tf_op jit(solution)/shard_map/ppermute | solution.py:530
  151.3 21.9 %collective-permute-done.8.refs_1_ = bf16[64,8192]{1,0:T(8,128)(2,1)S(1)} collective-permute-done((bf16[64,8192]{1,0:T(8,128)(2,1)S(1)}, bf16[64,8192]{1,0:T(8,128)(2,1)S(1)}, u32[]{:S(2)}, u32[]{:S(2)}) %collective-permute-start.8) | collective-permute-done | bytes 1048608 | tf_op jit(solution)/shard_map/ppermute | solution.py:530
  173.2 0.0 collective-permute-done.9.refs_2_
  173.2 0.0 copy-done.6
  173.2 0.9 copy-done.8
  174.2 0.4 copy-done.10
  174.6 5.0 %far_pack.1 = bf16[8,2,8,16384]{3,2,1,0:T(8,128)(2,1)} custom-call(s32[32]{0:T(128)} %copy-done.13, bf16[64,8192]{1,0:T(8,128)(2,1)} %copy-done.7, bf16[64,8192]{1,0:T(8,128)(2,1)} %copy-done.8, bf16[64,8192]{1,0:T(8,128)(2,1)} %copy-done.10, bf16[64,8192]{1,0:T(8,128)(2,1)} %copy-done.6, bf16[16384,128]{1,0:T(8,128)(2,1)} %get-tuple-element.24.refs_4_.refs_2_), custom_call_target="tpu_custom_call" | custom-call | flops 2097152 | bytes 6291456 | tf_op jit(solution)/shard_map/far_pack/pallas_call | solution.py:275
  179.6 0.0 collective-permute-done.13.refs_1_
  179.6 0.0 collective-permute-done.14.refs_3_
  179.6 0.0 all-to-all-done
  179.6 53.6 %all_to_all.15 = bf16[8,2,8,16384]{3,2,1,0:T(8,128)(2,1)} all-to-all(bf16[8,2,8,16384]{3,2,1,0:T(8,128)(2,1)} %far_pack.1), channel_id=1, replica_groups={{0,1,2,3,4,5,6,7},{8,9,10,11,12,13,14,15},{16,17,18,19,20,21,22,23},{24..., dimensions={0} | all-to-all | bytes 8388608 | tf_op jit(solution)/shard_map/all_to_all | solution.py:512
  233.2 17.6 %plane_sums.1 = (f32[64,128]{1,0:T(8,128)}, f32[64,128]{1,0:T(8,128)}, f32[2,8,8,128]{3,2,1,0:T(8,128)}) custom-call(bf16[128,16384]{1,0:T(8,128)(2,1)} %bitcast.1.own_ref, bf16[128,16384]{1,0:T(8,128)(2,1)} %bitcast.17, bf16[16384,128]{1,0:T(8,128)(2,1)} %get-tuple-element.28.refs_0_, bf16[16384,128]{1,0:T(8,128)(2,1)} %collective-permute-done.13.refs_1_, ...), custom_call_target="tpu_custom_call" | custom-call | flops 4831838208 | bytes 25165824 | tf_op jit(solution)/shard_map/plane_sums/pallas_call | solution.py:483
  250.8 2.4 collective-permute-start.15
  253.2 3.5 %all-to-all-start.2 = ((f32[16,8,128]{2,1,0:T(8,128)}), f32[16,8,128]{2,1,0:T(8,128)S(1)}, u32[]{:S(2)}, u32[]{:S(2)}) async-start(f32[16,8,128]{2,1,0:T(8,128)} %bitcast.20), calls=%async_computation.2 | async-start | bytes 131072 | tf_op jit(solution)/shard_map/all_to_all | solution.py:549
  256.7 0.0 collective-permute-done.15
  256.7 0.8 pad_maximum_fusion
  257.6 0.7 copy.16
  258.3 5.7 %all-to-all-done.2 = f32[16,8,128]{2,1,0:T(8,128)S(1)} async-done(((f32[16,8,128]{2,1,0:T(8,128)}), f32[16,8,128]{2,1,0:T(8,128)S(1)}, u32[]{:S(2)}, u32[]{:S(2)}) %all-to-all-start.2) | async-done | bytes 65568 | tf_op jit(solution)/shard_map/all_to_all | solution.py:549
  263.9 0.2 reshape.30
  264.1 0.1 copy.17
  264.2 0.8 reverse_select_fusion
  (21 shorter events, 0.1 us)
Async XLA Ops:
  0.6 13.3 %copy-start = (s32[4,16384]{1,0:T(4,128)S(1)}, s32[4,16384]{1,0:T(4,128)}, u32[]{:S(2)}) copy-start(s32[4,16384]{1,0:T(4,128)} %param.8) | copy-start | bytes 786436
  0.6 13.4 %copy-start.12 = (s32[32,1]{0,1:T(1,128)S(1)}, s32[32,1]{0,1:T(1,128)}, u32[]{:S(2)}) copy-start(s32[32,1]{0,1:T(1,128)} %param.9) | copy-start | bytes 388
  4.3 7.2 %copy-start.1 = (bf16[64,8192]{1,0:T(8,128)(2,1)S(1)}, bf16[64,8192]{1,0:T(8,128)(2,1)}, u32[]{:S(2)}) copy-start(bf16[64,8192]{1,0:T(8,128)(2,1)} %weigh.2.refs_0_) | copy-start | bytes 3145732
  4.4 8.8 %collective-permute-start.5 = (bf16[64,8192]{1,0:T(8,128)(2,1)}, bf16[64,8192]{1,0:T(8,128)(2,1)}, u32[]{:S(2)}, u32[]{:S(2)}) collective-permute-start(bf16[64,8192]{1,0:T(8,128)(2,1)} %weigh.2.refs_0_), channel_id=1, source_target_pairs={{0,1},{1,0},{2,3},{3,2},{4,5},{5,4},{6,7},{7,6},{8,9},{9,8},{10,11... | collective-permute-start | bytes 3145736 | tf_op jit(solution)/shard_map/ppermute | solution.py:521
  4.8 58.4 %collective-permute-start = (bf16[64,8192]{1,0:T(8,128)(2,1)}, bf16[64,8192]{1,0:T(8,128)(2,1)S(1)}, u32[]{:S(2)}, u32[]{:S(2)}) collective-permute-start(bf16[64,8192]{1,0:T(8,128)(2,1)} %weigh.2.refs_0_), channel_id=1, source_target_pairs={{0,8},{1,9},{2,10},{3,11},{4,12},{5,13},{6,14},{7,15},{8,0},{9,1},... | collective-permute-start | bytes 3145736 | tf_op jit(solution)/shard_map/ppermute | solution.py:519
  11.1 3.0 %collective-permute-start.6 = (bf16[64,8192]{1,0:T(8,128)(2,1)}, bf16[64,8192]{1,0:T(8,128)(2,1)}, u32[]{:S(2)}, u32[]{:S(2)}) collective-permute-start(bf16[64,8192]{1,0:T(8,128)(2,1)} %weigh.3.refs_1_), channel_id=1, source_target_pairs={{0,1},{1,0},{2,3},{3,2},{4,5},{5,4},{6,7},{7,6},{8,9},{9,8},{10,11... | collective-permute-start | bytes 3145736 | tf_op jit(solution)/shard_map/ppermute | solution.py:521
  11.3 52.0 %collective-permute-start.1 = (bf16[64,8192]{1,0:T(8,128)(2,1)}, bf16[64,8192]{1,0:T(8,128)(2,1)S(1)}, u32[]{:S(2)}, u32[]{:S(2)}) collective-permute-start(bf16[64,8192]{1,0:T(8,128)(2,1)} %weigh.3.refs_1_), channel_id=1, source_target_pairs={{0,8},{1,9},{2,10},{3,11},{4,12},{5,13},{6,14},{7,15},{8,0},{9,1},... | collective-permute-start | bytes 3145736 | tf_op jit(solution)/shard_map/ppermute | solution.py:519
  11.5 51.7 %collective-permute-start.2 = (bf16[64,8192]{1,0:T(8,128)(2,1)S(1)}, bf16[64,8192]{1,0:T(8,128)(2,1)}, u32[]{:S(2)}, u32[]{:S(2)}) collective-permute-start(bf16[64,8192]{1,0:T(8,128)(2,1)S(1)} %copy-done.1), channel_id=1, source_target_pairs={{8,16},{9,17},{10,18},{11,19},{12,20},{13,21},{14,22},{15,23},{16,... | collective-permute-start | bytes 3145736 | tf_op jit(solution)/shard_map/ppermute | solution.py:520
  13.2 50.1 %collective-permute-start.3 = (bf16[64,8192]{1,0:T(8,128)(2,1)}, bf16[64,8192]{1,0:T(8,128)(2,1)S(1)}, u32[]{:S(2)}, u32[]{:S(2)}) collective-permute-start(bf16[64,8192]{1,0:T(8,128)(2,1)} %weigh.3.refs_1_), channel_id=1, source_target_pairs={{8,16},{9,17},{10,18},{11,19},{12,20},{13,21},{14,22},{15,23},{16,... | collective-permute-start | bytes 3145736 | tf_op jit(solution)/shard_map/ppermute | solution.py:520
  14.1 49.1 %collective-permute-start.4 = (s32[32]{0:T(128)S(1)}, s32[32]{0:T(128)S(1)}, u32[]{:S(2)}, u32[]{:S(2)}) collective-permute-start(s32[32]{0:T(128)S(1)} %bitcast.27), channel_id=1, source_target_pairs={{0,16},{1,17},{2,18},{3,19},{4,20},{5,21},{6,22},{7,23},{8,24},{9,... | collective-permute-start | bytes 392 | tf_op jit(solution)/shard_map/ppermute | solution.py:522
  63.2 54.4 %copy-start.13 = (s32[32]{0:T(128)}, s32[32]{0:T(128)S(1)}, u32[]{:S(2)}) copy-start(s32[32]{0:T(128)S(1)} %collective-permute-done.4.pick_ref) | copy-start | bytes 388
  63.2 6.8 %copy-start.2 = (bf16[64,8192]{1,0:T(8,128)(2,1)}, bf16[64,8192]{1,0:T(8,128)(2,1)S(1)}, u32[]{:S(2)}) copy-start(bf16[64,8192]{1,0:T(8,128)(2,1)S(1)} %collective-permute-done.refs_0_) | copy-start | bytes 3145732
  63.2 6.7 %copy-start.4 = (bf16[64,8192]{1,0:T(8,128)(2,1)}, bf16[64,8192]{1,0:T(8,128)(2,1)S(1)}, u32[]{:S(2)}) copy-start(bf16[64,8192]{1,0:T(8,128)(2,1)S(1)} %collective-permute-done.1.refs_1_) | copy-start | bytes 3145732
  63.3 1.0 copy-start.14
  64.3 2.7 %collective-permute-start.11 = (bf16[64,8192]{1,0:T(8,128)(2,1)S(1)}, bf16[64,8192]{1,0:T(8,128)(2,1)S(1)}, u32[]{:S(2)}, u32[]{:S(2)}) collective-permute-start(bf16[64,8192]{1,0:T(8,128)(2,1)S(1)} %collective-permute-done.refs_0_), channel_id=1, source_target_pairs={{0,1},{1,0},{2,3},{3,2},{4,5},{5,4},{6,7},{7,6},{8,9},{9,8},{10,11... | collective-permute-start | bytes 3145736 | tf_op jit(solution)/shard_map/ppermute | solution.py:532
  64.3 5.7 %collective-permute-start.12 = (bf16[64,8192]{1,0:T(8,128)(2,1)S(1)}, bf16[64,8192]{1,0:T(8,128)(2,1)S(1)}, u32[]{:S(2)}, u32[]{:S(2)}) collective-permute-start(bf16[64,8192]{1,0:T(8,128)(2,1)S(1)} %collective-permute-done.1.refs_1_), channel_id=1, source_target_pairs={{0,1},{1,0},{2,3},{3,2},{4,5},{5,4},{6,7},{7,6},{8,9},{9,8},{10,11... | collective-permute-start | bytes 3145736 | tf_op jit(solution)/shard_map/ppermute | solution.py:532
  64.8 114.8 %collective-permute-start.13 = (bf16[16384,128]{1,0:T(8,128)(2,1)}, bf16[16384,128]{1,0:T(8,128)(2,1)}, u32[]{:S(2)}, u32[]{:S(2)}) collective-permute-start(bf16[16384,128]{1,0:T(8,128)(2,1)} %get-tuple-element.25), channel_id=1, source_target_pairs={{0,1},{1,0},{2,3},{3,2},{4,5},{5,4},{6,7},{7,6},{8,9},{9,8},{10,11... | collective-permute-start | bytes 12582920 | tf_op jit(solution)/shard_map/ppermute | solution.py:526
  67.0 3.0 %copy-start.9 = (bf16[64,8192]{1,0:T(8,128)(2,1)}, bf16[64,8192]{1,0:T(8,128)(2,1)S(1)}, u32[]{:S(2)}) copy-start(bf16[64,8192]{1,0:T(8,128)(2,1)S(1)} %collective-permute-done.11.refs_2_) | copy-start | bytes 3145732
  70.0 1.1 copy-start.11
  113.2 66.5 %collective-permute-start.14 = (bf16[16384,128]{1,0:T(8,128)(2,1)}, bf16[16384,128]{1,0:T(8,128)(2,1)}, u32[]{:S(2)}, u32[]{:S(2)}) collective-permute-start(bf16[16384,128]{1,0:T(8,128)(2,1)} %get-tuple-element.26), channel_id=1, source_target_pairs={{0,1},{1,0},{2,3},{3,2},{4,5},{5,4},{6,7},{7,6},{8,9},{9,8},{10,11... | collective-permute-start | bytes 12582920 | tf_op jit(solution)/shard_map/ppermute | solution.py:535
  117.6 4.9 %copy-start.5 = (bf16[64,8192]{1,0:T(8,128)(2,1)S(1)}, bf16[64,8192]{1,0:T(8,128)(2,1)}, u32[]{:S(2)}) copy-start(bf16[64,8192]{1,0:T(8,128)(2,1)} %copy-done.4) | copy-start | bytes 3145732
  117.6 6.9 %copy-start.15 = (bf16[64,8192]{1,0:T(8,128)(2,1)S(1)}, bf16[64,8192]{1,0:T(8,128)(2,1)}, u32[]{:S(2)}) copy-start(bf16[64,8192]{1,0:T(8,128)(2,1)} %copy-done.14) | copy-start | bytes 3145732
  117.6 8.2 %copy-start.3 = (bf16[64,8192]{1,0:T(8,128)(2,1)S(1)}, bf16[64,8192]{1,0:T(8,128)(2,1)}, u32[]{:S(2)}) copy-start(bf16[64,8192]{1,0:T(8,128)(2,1)} %copy-done.2) | copy-start | bytes 3145732
  117.6 62.0 %all-to-all-start = ((bf16[8,2,8,16384]{3,2,1,0:T(8,128)(2,1)}), bf16[8,2,8,16384]{3,2,1,0:T(8,128)(2,1)}, u32[]{:S(2)}, u32[]{:S(2)}) async-start(bf16[8,2,8,16384]{3,2,1,0:T(8,128)(2,1)} %own_pack.1), calls=%async_computation | async-start | bytes 8388608 | tf_op jit(solution)/shard_map/all_to_all | solution.py:512
  122.5 3.3 %collective-permute-start.10 = (bf16[64,8192]{1,0:T(8,128)(2,1)S(1)}, bf16[64,8192]{1,0:T(8,128)(2,1)S(1)}, u32[]{:S(2)}, u32[]{:S(2)}) collective-permute-start(bf16[64,8192]{1,0:T(8,128)(2,1)S(1)} %copy-done.5), channel_id=1, source_target_pairs={{8,16},{9,17},{10,18},{11,19},{12,20},{13,21},{14,22},{15,23},{16,... | collective-permute-start | bytes 3145736 | tf_op jit(solution)/shard_map/ppermute | solution.py:531
  123.2 28.1 %collective-permute-start.7 = (bf16[64,8192]{1,0:T(8,128)(2,1)}, bf16[64,8192]{1,0:T(8,128)(2,1)S(1)}, u32[]{:S(2)}, u32[]{:S(2)}) collective-permute-start(bf16[64,8192]{1,0:T(8,128)(2,1)} %collective-permute-done.2), channel_id=1, source_target_pairs={{8,0},{9,1},{10,2},{11,3},{12,4},{13,5},{14,6},{15,7},{16,24},{17,... | collective-permute-start | bytes 3145736 | tf_op jit(solution)/shard_map/ppermute | solution.py:530
  124.5 48.7 %collective-permute-start.8 = (bf16[64,8192]{1,0:T(8,128)(2,1)S(1)}, bf16[64,8192]{1,0:T(8,128)(2,1)S(1)}, u32[]{:S(2)}, u32[]{:S(2)}) collective-permute-start(bf16[64,8192]{1,0:T(8,128)(2,1)S(1)} %copy-done.15), channel_id=1, source_target_pairs={{8,0},{9,1},{10,2},{11,3},{12,4},{13,5},{14,6},{15,7},{16,24},{17,... | collective-permute-start | bytes 3145736 | tf_op jit(solution)/shard_map/ppermute | solution.py:530
  125.8 47.4 %copy-start.6 = (bf16[64,8192]{1,0:T(8,128)(2,1)}, bf16[64,8192]{1,0:T(8,128)(2,1)S(1)}, u32[]{:S(2)}) copy-start(bf16[64,8192]{1,0:T(8,128)(2,1)S(1)} %collective-permute-done.10.refs_3_) | copy-start | bytes 3145732
  125.9 47.4 %collective-permute-start.9 = (bf16[64,8192]{1,0:T(8,128)(2,1)S(1)}, bf16[64,8192]{1,0:T(8,128)(2,1)S(1)}, u32[]{:S(2)}, u32[]{:S(2)}) collective-permute-start(bf16[64,8192]{1,0:T(8,128)(2,1)S(1)} %copy-done.3), channel_id=1, source_target_pairs={{8,16},{9,17},{10,18},{11,19},{12,20},{13,21},{14,22},{15,23},{16,... | collective-permute-start | bytes 3145736 | tf_op jit(solution)/shard_map/ppermute | solution.py:531
  151.3 21.9 %copy-start.7 = (bf16[64,8192]{1,0:T(8,128)(2,1)}, bf16[64,8192]{1,0:T(8,128)(2,1)S(1)}, u32[]{:S(2)}) copy-start(bf16[64,8192]{1,0:T(8,128)(2,1)S(1)} %collective-permute-done.7.refs_0_) | copy-start | bytes 3145732
  173.2 1.0 copy-start.8
  173.2 1.4 copy-start.10
  250.8 5.9 %collective-permute-start.15 = (f32[64,128]{1,0:T(8,128)}, f32[64,128]{1,0:T(8,128)S(1)}, u32[]{:S(2)}, u32[]{:S(2)}) collective-permute-start(f32[64,128]{1,0:T(8,128)} %get-tuple-element.32), channel_id=1, source_target_pairs={{0,8},{1,9},{2,10},{3,11},{4,12},{5,13},{6,14},{7,15},{8,0},{9,1},... | collective-permute-start | bytes 98312 | tf_op jit(solution)/shard_map/ppermute | solution.py:541
  253.2 10.7 %all-to-all-start.2 = ((f32[16,8,128]{2,1,0:T(8,128)}), f32[16,8,128]{2,1,0:T(8,128)S(1)}, u32[]{:S(2)}, u32[]{:S(2)}) async-start(f32[16,8,128]{2,1,0:T(8,128)} %bitcast.20), calls=%async_computation.2 | async-start | bytes 131072 | tf_op jit(solution)/shard_map/all_to_all | solution.py:549

commit v14 on v9

--- a/solution.py
+++ b/solution.py
@@ -322,8 +322,7 @@
             moved_ref[rows, :] = target[rows, :].astype(jnp.bfloat16)
 
 
-def place(ops, x, x1, w, w1, after):
-    count = ops.shape[0]
+def place(ops, first, count, x, x1, w, w1, after):
     blk, width = x.shape
     depth = min(2048, width)
     last = width // depth - 1
@@ -333,7 +332,7 @@
         grid=(count, width // depth),
         out_shape=jax.ShapeDtypeStruct((width, count * LANES), jnp.bfloat16),
         in_specs=[
-            pl.BlockSpec((1, 1, depth), lambda k, i: (k, 0, i), memory_space=pltpu.SMEM),
+            pl.BlockSpec((1, 1, depth), lambda k, i: (first + k, 0, i), memory_space=pltpu.SMEM),
             part,
             part,
             part,
@@ -347,7 +346,7 @@
             flops=0, bytes_accessed=count * width * LANES * 64, transcendentals=0
         ),
         name="place",
-    )(ops[:, None, :], x, x1, w, w1, after)
+    )(ops, x, x1, w, w1, after)
 
 
 def ratio(total_w, sum_x, sum_xx, sum_y, sum_xy, sum_yy):
@@ -400,7 +399,8 @@
     return result
 
 
-def own_sums_kernel(got_ref, first_ref, second_ref, out_ref, right_ref, acc):
+def plane_sums_kernel(ended, got_ref, first_ref, second_ref, *refs):
+    acc = refs[-1]
     depth = got_ref.shape[1]
     step = min(1024, depth)
     half = LANES // 2
@@ -425,36 +425,19 @@
                 else:
                     odd = product * swapped
             square.append(jnp.where(low, even, odd).astype(jnp.bfloat16))
-        right = jnp.concatenate(linear + square, 1)
-        right_ref[cols, :] = right
-        add_sums(acc, got_ref, cols, right)
+        add_sums(acc, got_ref, cols, jnp.concatenate(linear + square, 1))
 
     @pl.when(pl.program_id(0) == pl.num_programs(0) - 1)
     def _():
-        out_ref[...] = correlations(acc)
-
-
-def far_sums_kernel(got_ref, right_ref, own_ref, mine_ref, other_ref, back_ref, acc):
-    depth = got_ref.shape[1]
-    step = min(1024, depth)
-
-    @pl.when(pl.program_id(0) == 0)
-    def _():
-        acc[...] = jnp.zeros_like(acc)
-
-    for i in range(depth // step):
-        cols = slice(i * step, (i + 1) * step)
-        add_sums(acc, got_ref, cols, right_ref[cols, :])
-
-    @pl.when(pl.program_id(0) == pl.num_programs(0) - 1)
-    def _():
+        if not ended:
+            refs[0][...] = correlations(acc)
+            return
+        own_ref, mine_ref, other_ref, back_ref = refs[:-1]
         upper = lax.div(lax.axis_index("dp"), 2 * PLANE)
         count = own_ref.shape[0] // 2
         for part, result in enumerate((own_ref[...], correlations(acc))):
-            tiles = result.reshape(PLANE, SLAB, LANES)
             slot = part + upper - 2 * part * upper
-            for twin in range(2):
-                back_ref[slot, twin] = tiles
+            back_ref[slot] = result.reshape(PLANE, SLAB, LANES)
             pairs = result.reshape(PLANE // 2, 2, SLAB, LANES)
             even, odd = pairs[:, 0], pairs[:, 1]
             top = lax.broadcasted_iota(jnp.int32, even.shape, 1) < SUB
@@ -463,56 +446,29 @@
             other_ref[here, :] = jnp.where(top, pltpu.roll(even, SUB, 1), odd).reshape(count, LANES)
 
 
-def own_sums(got, first, second):
+def plane_sums(got, first, second, own):
     rows, width = got.shape
     depth = min(2048, width)
     lanes = (NOPS + NOPS // 2) * LANES
+    ended = own is not None
     moved = pl.BlockSpec((depth, 2 * LANES), lambda i: (i, 0))
-    return pl.pallas_call(
-        own_sums_kernel,
+    result = (rows // 2, LANES)
+    shapes = (result, result, (2, PLANE, SLAB, LANES)) if ended else (result,)
+    entire = [pl.BlockSpec(shape, lambda i, shape=shape: (0,) * len(shape)) for shape in shapes]
+    outs = pl.pallas_call(
+        functools.partial(plane_sums_kernel, ended),
         grid=(width // depth,),
-        out_shape=(
-            jax.ShapeDtypeStruct((rows // 2, LANES), jnp.float32),
-            jax.ShapeDtypeStruct((width, lanes), jnp.bfloat16),
-        ),
-        in_specs=[pl.BlockSpec((rows, depth), lambda i: (0, i)), moved, moved],
-        out_specs=(
-            pl.BlockSpec((rows // 2, LANES), lambda i: (0, 0)),
-            pl.BlockSpec((depth, lanes), lambda i: (i, 0)),
-        ),
+        out_shape=tuple(jax.ShapeDtypeStruct(shape, jnp.float32) for shape in shapes),
+        in_specs=[pl.BlockSpec((rows, depth), lambda i: (0, i)), moved, moved] + ([entire[0]] if ended else []),
+        out_specs=tuple(entire),
         scratch_shapes=[pltpu.VMEM((rows * 3 // 2, lanes), jnp.float32)],
         compiler_params=params(),
         cost_estimate=pl.CostEstimate(
-            flops=3 * rows * width * lanes,
-            bytes_accessed=2 * width * (rows + 4 * LANES + lanes),
-            transcendentals=0,
-        ),
-        name="own_sums",
-    )(got, first, second)
-
-
-def far_sums(got, right, own):
-    rows, width = got.shape
-    depth = min(2048, width)
-    lanes = right.shape[1]
-    shapes = (own.shape, own.shape, (2, 2, PLANE, SLAB, LANES))
-    return pl.pallas_call(
-        far_sums_kernel,
-        grid=(width // depth,),
-        out_shape=tuple(jax.ShapeDtypeStruct(shape, jnp.float32) for shape in shapes),
-        in_specs=[
-            pl.BlockSpec((rows, depth), lambda i: (0, i)),
-            pl.BlockSpec((depth, lanes), lambda i: (i, 0)),
-            pl.BlockSpec(own.shape, lambda i: (0, 0)),
-        ],
-        out_specs=tuple(pl.BlockSpec(shape, lambda i, shape=shape: (0,) * len(shape)) for shape in shapes),
-        scratch_shapes=[pltpu.VMEM((rows * 3 // 2, lanes), jnp.float32)],
-        compiler_params=params(),
-        cost_estimate=pl.CostEstimate(
-            flops=3 * rows * width * lanes, bytes_accessed=2 * width * (rows + lanes), transcendentals=0
-        ),
-        name="far_sums",
-    )(got, right, own)
+            flops=3 * rows * width * lanes, bytes_accessed=2 * width * (rows + 4 * LANES), transcendentals=0
+        ),
+        name="plane_sums",
+    )(got, first, second, *((own,) if ended else ()))
+    return outs if ended else outs[0]
 
 
 def shards_by_plane(intensities, observed, qweights, ops, pick):
@@ -523,6 +479,7 @@
     middle = [(i, 3 * PLANE + 2 * (i % PLANE) - i) for i in range(PLANE, 3 * PLANE)]
     outward = [(i, i - PLANE if i < 2 * PLANE else i + PLANE) for i in range(PLANE, 3 * PLANE)]
     rings = [[z * PLANE + c for c in range(PLANE)] for z in range(PLANES)]
+    couples = [[z * PLANE + c for z in (odd, odd + 2) for c in range(PLANE)] for odd in range(2)]
     plane = lax.axis_index("dp") // PLANE
     odd, upper = plane % 2 == 1, plane >= 2
 
@@ -531,6 +488,7 @@
         return got.reshape(PLANE * 2 * SLAB, width)
 
     own_pick = pick[:, 0]
+    ops = ops[:, None, :]
     near_x = lax.ppermute(intensities, "dp", near)
     mid_x = lax.ppermute(intensities, "dp", middle)
     far_pick = lax.ppermute(own_pick, "dp", far)
@@ -543,12 +501,12 @@
     inner_x = lax.ppermute(near_x, "dp", middle)
     outer_w = lax.ppermute(mid_w, "dp", outward)
     inner_w = lax.ppermute(near_w, "dp", middle)
-    first = place(ops[:2], intensities, near_x, own_w, near_w, own_pick)
+    first = place(ops, 0, 2, intensities, near_x, own_w, near_w, own_pick)
     far_send = far_pack(far_pick, outer_x, outer_w, inner_x, inner_w, first)
     far_got = spread(far_send)
-    second = place(ops[2:], intensities, near_x, own_w, near_w, far_send)
-    own_corr, right = own_sums(own_got, first, second)
-    mine, other, back = far_sums(far_got, right, own_corr)
+    second = place(ops, 2, 2, intensities, near_x, own_w, near_w, far_send)
+    own_corr = plane_sums(own_got, first, second, None)
+    mine, other, back = plane_sums(far_got, first, second, own_corr)
 
     from_near = lax.ppermute(other, "dp", near)
     pair = [each.reshape(2, PLANE, SUB, NOPS * blk) for each in (mine, from_near)]
@@ -557,10 +515,10 @@
     pair = jnp.where(upper, pair[::-1], pair)
     corr = pair.reshape(groups * SUB, NOPS * blk).T.reshape(NOPS, blk, groups * SUB)
 
-    back = back.reshape(groups, 2 * SUB, NOPS * blk)
-    back = lax.all_to_all(back, "dp", split_axis=0, concat_axis=0, tiled=True)
-    back = back.reshape(2, 2, PLANE, 2, SUB, NOPS, blk)
-    back = jnp.where(odd, back[:, 1, :, ::-1], back[:, 0])
+    back = back.reshape(2 * PLANE, 2 * SUB, NOPS * blk)
+    back = lax.all_to_all(back, "dp", split_axis=0, concat_axis=0, axis_index_groups=couples, tiled=True)
+    back = back.reshape(2, PLANE, 2, SUB, NOPS, blk)
+    back = jnp.where(odd, back[:, :, ::-1], back)
     returned = jnp.transpose(back, (4, 0, 2, 1, 3, 5)).reshape(NOPS, 1, groups, SUB, blk)
     return (corr, returned)
 

time: 208 us -> 214 us (1.029)
  waiting for transfers between devices: 49.2 us -> 57.9 us
  Pallas kernels: 119 us -> 115 us
    ppermute x1, waiting for transfers between devices: 32.1 us -> 41.7 us  [shards_by_plane(): far_pick = lax.ppermute(own_pick, 'dp', far)]
    pallas_call x2, Pallas kernels: 36.5 us -> 31.8 us  [plane_sums(): pl.pallas_call(functools.partial(plane_sums_kernel, ended), grid=(width /...]
  transfers between devices with their start and end apart: 13 -> 13, of which waited for: 3 -> 3; matrix products, arithmetic and copies ran while one was open for 2% -> 1% of each run, Pallas kernels for 51% -> 44%
where the time goes in v14:
time: 214 us; the launch traced here: 213 us
  Pallas kernels  115 us (54%)
  waiting for transfers between devices  57.9 us (27%)
  starting transfers between devices  31.6 us (15%)
  other arithmetic  4.75 us (2%)
  local copies, waits for them, and re-layouts  2.86 us (1%)
    pallas_call x2, Pallas kernels, place(): pl.pallas_call(place_kernel, grid=(count, width // depth), out_shape=jax....  73.6 us
    ppermute x1, waiting for transfers between devices, shards_by_plane(): far_pick = lax.ppermute(own_pick, 'dp', far)  41.7 us
    pallas_call x2, Pallas kernels, plane_sums(): pl.pallas_call(functools.partial(plane_sums_kernel, ended), grid=(width /...  31.8 us
    ppermute x1, waiting for transfers between devices, shards_by_plane(): outer_w = lax.ppermute(mid_w, 'dp', outward)  10.9 us
    all_to_all x2, starting transfers between devices, spread(): lax.all_to_all(send, 'dp', split_axis=0, concat_axis=0, axis_index_groups...  9.95 us
    pallas_call x2, Pallas kernels, pack_call(): pl.pallas_call(kernel, out_shape=jax.ShapeDtypeStruct((PLANE, 2, SLAB, wi...  9.31 us
    all_to_all x1, starting transfers between devices, shards_by_plane(): lax.all_to_all(back, 'dp', split_axis=0, concat_axis=0, axis_index_groups...  6.51 us
    all_to_all x1, waiting for transfers between devices, shards_by_plane(): lax.all_to_all(back, 'dp', split_axis=0, concat_axis=0, axis_index_groups...  5.31 us
  transfers between devices with their start and end apart: 13, of which 3 were waited for; matrix products, arithmetic and copies ran while one was open for 1% of the time, Pallas kernels for 44%

profile of v14, /device:TPU:0, one launch (start us, length us, event | category | flops | bytes accessed | tf_op | source)
XLA Modules:
  0.0 212.6 jit_solution(10862117346101144227)
XLA Ops:
  0.6 3.2 %multiply_convert_fusion.w_ref = bf16[32,16384]{1,0:T(8,128)(2,1)} fusion(bf16[32,16384]{1,0:T(8,128)(2,1)} %param.7, s32[32,16384]{1,0:T(8,128)} %param.6), kind=kLoop, calls=%fused_computation | loop fusion | flops 2097152 | bytes 4194304 | tf_op jit(solution)/shard_map/convert_element_type | solution.py:495
  3.8 4.3 %own_pack.1 = bf16[8,2,8,16384]{3,2,1,0:T(8,128)(2,1)} custom-call(s32[32]{0:T(128)} %bitcast.23, bf16[32,16384]{1,0:T(8,128)(2,1)} %x_ref.5, bf16[32,16384]{1,0:T(8,128)(2,1)} %multiply_convert_fusion.w_ref), custom_call_target="tpu_custom_call" | custom-call | flops 2097152 | bytes 6291456 | tf_op jit(solution)/shard_map/own_pack/pallas_call | solution.py:254
  8.1 0.0 copy-start
  8.1 0.0 copy-start.1
  8.2 0.0 copy-start.9
  8.2 0.0 copy-start.8
  8.2 5.3 %all-to-all-start.1 = ((bf16[8,2,8,16384]{3,2,1,0:T(8,128)(2,1)}), bf16[8,2,8,16384]{3,2,1,0:T(8,128)(2,1)}, u32[]{:S(2)}, u32[]{:S(2)}) async-start(bf16[8,2,8,16384]{3,2,1,0:T(8,128)(2,1)} %own_pack.1), calls=%async_computation.1 | async-start | bytes 8388608 | tf_op jit(solution)/shard_map/all_to_all | solution.py:487
  13.5 0.0 copy-done
  13.5 2.5 %collective-permute-start.2 = (bf16[32,16384]{1,0:T(8,128)(2,1)S(1)}, bf16[32,16384]{1,0:T(8,128)(2,1)S(1)}, u32[]{:S(2)}, u32[]{:S(2)}) collective-permute-start(bf16[32,16384]{1,0:T(8,128)(2,1)S(1)} %copy-done), channel_id=1, source_target_pairs={{0,8},{1,9},{2,10},{3,11},{4,12},{5,13},{6,14},{7,15},{8,0},{9,1},... | collective-permute-start | bytes 3145736 | tf_op jit(solution)/shard_map/ppermute | solution.py:496
  16.0 0.7 collective-permute-start.3
  16.7 0.0 copy-done.1
  16.7 4.4 %collective-permute-start = (bf16[32,16384]{1,0:T(8,128)(2,1)S(1)}, bf16[32,16384]{1,0:T(8,128)(2,1)S(1)}, u32[]{:S(2)}, u32[]{:S(2)}) collective-permute-start(bf16[32,16384]{1,0:T(8,128)(2,1)S(1)} %copy-done.1), channel_id=1, source_target_pairs={{0,8},{1,9},{2,10},{3,11},{4,12},{5,13},{6,14},{7,15},{8,0},{9,1},... | collective-permute-start | bytes 3145736 | tf_op jit(solution)/shard_map/ppermute | solution.py:492
  21.1 1.7 collective-permute-start.1
  22.8 0.0 copy-done.9
  22.8 1.8 collective-permute-start.4
  24.6 41.7 %collective-permute-done.4.pick_ref = s32[32]{0:T(128)S(1)} collective-permute-done((s32[32]{0:T(128)S(1)}, s32[32]{0:T(128)S(1)}, u32[]{:S(2)}, u32[]{:S(2)}) %collective-permute-start.4) | collective-permute-done | bytes 160 | tf_op jit(solution)/shard_map/ppermute | solution.py:494
  66.3 0.0 copy-start.10
  66.3 0.0 collective-permute-done.2.w1_ref
  66.3 0.0 copy-start.2
  66.3 0.0 collective-permute-done.3
  66.3 0.0 collective-permute-done.x1_ref
  66.3 0.0 copy-start.3
  66.3 0.0 collective-permute-done.1
  66.3 0.7 collective-permute-start.7
  67.1 0.7 collective-permute-start.8
  67.8 1.3 collective-permute-start.5
  69.1 1.3 collective-permute-start.6
  70.4 0.0 copy-done.8
  70.4 0.9 broadcast_in_dim.3.ops_ref
  71.3 0.0 copy-done.2
  71.3 0.0 copy-done.3
  71.3 36.8 %place.2.after_ref.first_ref = bf16[16384,256]{1,0:T(8,128)(2,1)} custom-call(s32[4,1,16384]{2,1,0:T(1,128)} %broadcast_in_dim.3.ops_ref, bf16[32,16384]{1,0:T(8,128)(2,1)} %x_ref.5, bf16[32,16384]{1,0:T(8,128)(2,1)} %copy-done.3, bf16[32,16384]{1,0:T(8,128)(2,1)} %multiply_convert_fusion.w_ref, bf16[32,16384]{1,0:T(8,128)(2,1)} %copy-done.2, s32[32]{0:T(128)} %bitcast.24), custom_call_target="tpu_custom_call" | custom-call | bytes 268435456 | tf_op jit(solution)/shard_map/place/pallas_call | solution.py:330
  108.1 0.0 copy-done.10
  108.1 0.0 collective-permute-done.7.xi
  108.1 0.0 copy-start.4
  108.1 0.0 collective-permute-done.8.wi
  108.1 0.0 copy-start.5
  108.1 0.0 collective-permute-done.5.xo
  108.1 0.0 copy-start.6
  108.2 10.9 %collective-permute-done.6.wo = bf16[32,16384]{1,0:T(8,128)(2,1)S(1)} collective-permute-done((bf16[32,16384]{1,0:T(8,128)(2,1)S(1)}, bf16[32,16384]{1,0:T(8,128)(2,1)S(1)}, u32[]{:S(2)}, u32[]{:S(2)}) %collective-permute-start.6) | collective-permute-done | bytes 1048608 | tf_op jit(solution)/shard_map/ppermute | solution.py:502
  119.0 0.0 copy-done.4
  119.0 0.0 copy-done.5
  119.0 0.0 copy-done.6
  119.0 0.0 copy-start.7
  119.0 1.0 copy-done.7
  120.0 5.0 %far_pack.1.after_ref = bf16[8,2,8,16384]{3,2,1,0:T(8,128)(2,1)} custom-call(s32[32]{0:T(128)} %copy-done.10, bf16[32,16384]{1,0:T(8,128)(2,1)} %copy-done.6, bf16[32,16384]{1,0:T(8,128)(2,1)} %copy-done.7, bf16[32,16384]{1,0:T(8,128)(2,1)} %copy-done.4, bf16[32,16384]{1,0:T(8,128)(2,1)} %copy-done.5, bf16[16384,256]{1,0:T(8,128)(2,1)} %place.2.after_ref.first_ref), custom_call_target="tpu_custom_call" | custom-call | flops 2097152 | bytes 6291456 | tf_op jit(solution)/shard_map/far_pack/pallas_call | solution.py:254
  125.0 0.0 all-to-all-done.1
  125.0 4.6 %all-to-all-start = ((bf16[8,2,8,16384]{3,2,1,0:T(8,128)(2,1)}), bf16[8,2,8,16384]{3,2,1,0:T(8,128)(2,1)}, u32[]{:S(2)}, u32[]{:S(2)}) async-start(bf16[8,2,8,16384]{3,2,1,0:T(8,128)(2,1)} %far_pack.1.after_ref), calls=%async_computation | async-start | bytes 8388608 | tf_op jit(solution)/shard_map/all_to_all | solution.py:487
  129.7 36.8 %place.3.second_ref = bf16[16384,256]{1,0:T(8,128)(2,1)} custom-call(s32[4,1,16384]{2,1,0:T(1,128)} %broadcast_in_dim.3.ops_ref, bf16[32,16384]{1,0:T(8,128)(2,1)} %x_ref.5, bf16[32,16384]{1,0:T(8,128)(2,1)} %copy-done.3, bf16[32,16384]{1,0:T(8,128)(2,1)} %multiply_convert_fusion.w_ref, bf16[32,16384]{1,0:T(8,128)(2,1)} %copy-done.2, ...), custom_call_target="tpu_custom_call" | custom-call | bytes 268435456 | tf_op jit(solution)/shard_map/place/pallas_call | solution.py:330
  166.4 15.8 %plane_sums.2.refs_0_ = f32[64,128]{1,0:T(8,128)} custom-call(bf16[128,16384]{1,0:T(8,128)(2,1)} %bitcast.2.got_ref, bf16[16384,256]{1,0:T(8,128)(2,1)} %place.2.after_ref.first_ref, bf16[16384,256]{1,0:T(8,128)(2,1)} %place.3.second_ref), custom_call_target="tpu_custom_call" | custom-call | flops 4831838208 | bytes 20971520 | tf_op jit(solution)/shard_map/plane_sums/pallas_call | solution.py:458
  182.2 0.0 all-to-all-done
  182.2 16.0 %plane_sums.3 = (f32[64,128]{1,0:T(8,128)}, f32[64,128]{1,0:T(8,128)}, f32[2,8,8,128]{3,2,1,0:T(8,128)}) custom-call(bf16[128,16384]{1,0:T(8,128)(2,1)} %bitcast.1.got_ref, bf16[16384,256]{1,0:T(8,128)(2,1)} %place.2.after_ref.first_ref, bf16[16384,256]{1,0:T(8,128)(2,1)} %place.3.second_ref, f32[64,128]{1,0:T(8,128)} %plane_sums.2.refs_0_), custom_call_target="tpu_custom_call" | custom-call | flops 4831838208 | bytes 20971520 | tf_op jit(solution)/shard_map/plane_sums/pallas_call | solution.py:458
  198.2 0.0 collective-permute-start.9
  198.2 6.5 %all-to-all-start.2 = ((f32[16,8,128]{2,1,0:T(8,128)}), f32[16,8,128]{2,1,0:T(8,128)S(1)}, u32[]{:S(2)}, u32[]{:S(2)}) async-start(f32[16,8,128]{2,1,0:T(8,128)} %bitcast.19), calls=%async_computation.2 | async-start | bytes 131072 | tf_op jit(solution)/shard_map/all_to_all | solution.py:519
  204.8 0.0 collective-permute-done.9
  204.8 0.8 pad_maximum_fusion
  205.6 0.7 copy.16
  206.3 5.3 %all-to-all-done.2 = f32[16,8,128]{2,1,0:T(8,128)S(1)} async-done(((f32[16,8,128]{2,1,0:T(8,128)}), f32[16,8,128]{2,1,0:T(8,128)S(1)}, u32[]{:S(2)}, u32[]{:S(2)}) %all-to-all-start.2) | async-done | bytes 65568 | tf_op jit(solution)/shard_map/all_to_all | solution.py:519
  211.6 0.2 reshape.30
  211.8 0.1 copy.17
  211.9 0.8 reverse_select_fusion
  (2 shorter events, 0.0 us)
Async XLA Ops:
  8.1 5.4 %copy-start = (bf16[32,16384]{1,0:T(8,128)(2,1)S(1)}, bf16[32,16384]{1,0:T(8,128)(2,1)}, u32[]{:S(2)}) copy-start(bf16[32,16384]{1,0:T(8,128)(2,1)} %multiply_convert_fusion.w_ref) | copy-start | bytes 3145732
  8.1 8.6 %copy-start.1 = (bf16[32,16384]{1,0:T(8,128)(2,1)S(1)}, bf16[32,16384]{1,0:T(8,128)(2,1)}, u32[]{:S(2)}) copy-start(bf16[32,16384]{1,0:T(8,128)(2,1)} %x_ref.5) | copy-start | bytes 3145732
  8.2 14.7 %copy-start.9 = (s32[32,1]{0,1:T(1,128)S(1)}, s32[32,1]{0,1:T(1,128)}, u32[]{:S(2)}) copy-start(s32[32,1]{0,1:T(1,128)} %param.9) | copy-start | bytes 388
  8.2 62.2 %copy-start.8 = (s32[4,16384]{1,0:T(4,128)S(1)}, s32[4,16384]{1,0:T(4,128)}, u32[]{:S(2)}) copy-start(s32[4,16384]{1,0:T(4,128)} %param.8) | copy-start | bytes 786436
  8.2 116.9 %all-to-all-start.1 = ((bf16[8,2,8,16384]{3,2,1,0:T(8,128)(2,1)}), bf16[8,2,8,16384]{3,2,1,0:T(8,128)(2,1)}, u32[]{:S(2)}, u32[]{:S(2)}) async-start(bf16[8,2,8,16384]{3,2,1,0:T(8,128)(2,1)} %own_pack.1), calls=%async_computation.1 | async-start | bytes 8388608 | tf_op jit(solution)/shard_map/all_to_all | solution.py:487
  13.5 52.8 %collective-permute-start.2 = (bf16[32,16384]{1,0:T(8,128)(2,1)S(1)}, bf16[32,16384]{1,0:T(8,128)(2,1)S(1)}, u32[]{:S(2)}, u32[]{:S(2)}) collective-permute-start(bf16[32,16384]{1,0:T(8,128)(2,1)S(1)} %copy-done), channel_id=1, source_target_pairs={{0,8},{1,9},{2,10},{3,11},{4,12},{5,13},{6,14},{7,15},{8,0},{9,1},... | collective-permute-start | bytes 3145736 | tf_op jit(solution)/shard_map/ppermute | solution.py:496
  16.0 50.3 %collective-permute-start.3 = (bf16[32,16384]{1,0:T(8,128)(2,1)S(1)}, bf16[32,16384]{1,0:T(8,128)(2,1)S(1)}, u32[]{:S(2)}, u32[]{:S(2)}) collective-permute-start(bf16[32,16384]{1,0:T(8,128)(2,1)S(1)} %copy-done), channel_id=1, source_target_pairs={{8,16},{9,17},{10,18},{11,19},{12,20},{13,21},{14,22},{15,23},{16,... | collective-permute-start | bytes 3145736 | tf_op jit(solution)/shard_map/ppermute | solution.py:497
  16.7 49.6 %collective-permute-start = (bf16[32,16384]{1,0:T(8,128)(2,1)S(1)}, bf16[32,16384]{1,0:T(8,128)(2,1)S(1)}, u32[]{:S(2)}, u32[]{:S(2)}) collective-permute-start(bf16[32,16384]{1,0:T(8,128)(2,1)S(1)} %copy-done.1), channel_id=1, source_target_pairs={{0,8},{1,9},{2,10},{3,11},{4,12},{5,13},{6,14},{7,15},{8,0},{9,1},... | collective-permute-start | bytes 3145736 | tf_op jit(solution)/shard_map/ppermute | solution.py:492
  21.1 45.2 %collective-permute-start.1 = (bf16[32,16384]{1,0:T(8,128)(2,1)S(1)}, bf16[32,16384]{1,0:T(8,128)(2,1)}, u32[]{:S(2)}, u32[]{:S(2)}) collective-permute-start(bf16[32,16384]{1,0:T(8,128)(2,1)S(1)} %copy-done.1), channel_id=1, source_target_pairs={{8,16},{9,17},{10,18},{11,19},{12,20},{13,21},{14,22},{15,23},{16,... | collective-permute-start | bytes 3145736 | tf_op jit(solution)/shard_map/ppermute | solution.py:493
  22.8 43.5 %collective-permute-start.4 = (s32[32]{0:T(128)S(1)}, s32[32]{0:T(128)S(1)}, u32[]{:S(2)}, u32[]{:S(2)}) collective-permute-start(s32[32]{0:T(128)S(1)} %bitcast.25), channel_id=1, source_target_pairs={{0,16},{1,17},{2,18},{3,19},{4,20},{5,21},{6,22},{7,23},{8,24},{9,... | collective-permute-start | bytes 392 | tf_op jit(solution)/shard_map/ppermute | solution.py:494
  66.3 41.8 %copy-start.10 = (s32[32]{0:T(128)}, s32[32]{0:T(128)S(1)}, u32[]{:S(2)}) copy-start(s32[32]{0:T(128)S(1)} %collective-permute-done.4.pick_ref) | copy-start | bytes 388
  66.3 5.0 %copy-start.2 = (bf16[32,16384]{1,0:T(8,128)(2,1)}, bf16[32,16384]{1,0:T(8,128)(2,1)S(1)}, u32[]{:S(2)}) copy-start(bf16[32,16384]{1,0:T(8,128)(2,1)S(1)} %collective-permute-done.2.w1_ref) | copy-start | bytes 3145732
  66.3 5.0 %copy-start.3 = (bf16[32,16384]{1,0:T(8,128)(2,1)}, bf16[32,16384]{1,0:T(8,128)(2,1)S(1)}, u32[]{:S(2)}) copy-start(bf16[32,16384]{1,0:T(8,128)(2,1)S(1)} %collective-permute-done.x1_ref) | copy-start | bytes 3145732
  66.3 41.8 %collective-permute-start.7 = (bf16[32,16384]{1,0:T(8,128)(2,1)S(1)}, bf16[32,16384]{1,0:T(8,128)(2,1)S(1)}, u32[]{:S(2)}, u32[]{:S(2)}) collective-permute-start(bf16[32,16384]{1,0:T(8,128)(2,1)S(1)} %collective-permute-done.x1_ref), channel_id=1, source_target_pairs={{8,16},{9,17},{10,18},{11,19},{12,20},{13,21},{14,22},{15,23},{16,... | collective-permute-start | bytes 3145736 | tf_op jit(solution)/shard_map/ppermute | solution.py:501
  67.1 41.1 %collective-permute-start.8 = (bf16[32,16384]{1,0:T(8,128)(2,1)S(1)}, bf16[32,16384]{1,0:T(8,128)(2,1)S(1)}, u32[]{:S(2)}, u32[]{:S(2)}) collective-permute-start(bf16[32,16384]{1,0:T(8,128)(2,1)S(1)} %collective-permute-done.2.w1_ref), channel_id=1, source_target_pairs={{8,16},{9,17},{10,18},{11,19},{12,20},{13,21},{14,22},{15,23},{16,... | collective-permute-start | bytes 3145736 | tf_op jit(solution)/shard_map/ppermute | solution.py:503
  67.8 40.3 %collective-permute-start.5 = (bf16[32,16384]{1,0:T(8,128)(2,1)}, bf16[32,16384]{1,0:T(8,128)(2,1)S(1)}, u32[]{:S(2)}, u32[]{:S(2)}) collective-permute-start(bf16[32,16384]{1,0:T(8,128)(2,1)} %collective-permute-done.1), channel_id=1, source_target_pairs={{8,0},{9,1},{10,2},{11,3},{12,4},{13,5},{14,6},{15,7},{16,24},{17,... | collective-permute-start | bytes 3145736 | tf_op jit(solution)/shard_map/ppermute | solution.py:500
  69.1 49.9 %collective-permute-start.6 = (bf16[32,16384]{1,0:T(8,128)(2,1)S(1)}, bf16[32,16384]{1,0:T(8,128)(2,1)S(1)}, u32[]{:S(2)}, u32[]{:S(2)}) collective-permute-start(bf16[32,16384]{1,0:T(8,128)(2,1)S(1)} %collective-permute-done.3), channel_id=1, source_target_pairs={{8,0},{9,1},{10,2},{11,3},{12,4},{13,5},{14,6},{15,7},{16,24},{17,... | collective-permute-start | bytes 3145736 | tf_op jit(solution)/shard_map/ppermute | solution.py:502
  108.1 10.9 %copy-start.4 = (bf16[32,16384]{1,0:T(8,128)(2,1)}, bf16[32,16384]{1,0:T(8,128)(2,1)S(1)}, u32[]{:S(2)}) copy-start(bf16[32,16384]{1,0:T(8,128)(2,1)S(1)} %collective-permute-done.7.xi) | copy-start | bytes 3145732
  108.1 10.9 %copy-start.5 = (bf16[32,16384]{1,0:T(8,128)(2,1)}, bf16[32,16384]{1,0:T(8,128)(2,1)S(1)}, u32[]{:S(2)}) copy-start(bf16[32,16384]{1,0:T(8,128)(2,1)S(1)} %collective-permute-done.8.wi) | copy-start | bytes 3145732
  108.1 10.9 %copy-start.6 = (bf16[32,16384]{1,0:T(8,128)(2,1)}, bf16[32,16384]{1,0:T(8,128)(2,1)S(1)}, u32[]{:S(2)}) copy-start(bf16[32,16384]{1,0:T(8,128)(2,1)S(1)} %collective-permute-done.5.xo) | copy-start | bytes 3145732
  119.0 1.0 copy-start.7
  125.0 57.2 %all-to-all-start = ((bf16[8,2,8,16384]{3,2,1,0:T(8,128)(2,1)}), bf16[8,2,8,16384]{3,2,1,0:T(8,128)(2,1)}, u32[]{:S(2)}, u32[]{:S(2)}) async-start(bf16[8,2,8,16384]{3,2,1,0:T(8,128)(2,1)} %far_pack.1.after_ref), calls=%async_computation | async-start | bytes 8388608 | tf_op jit(solution)/shard_map/all_to_all | solution.py:487
  198.2 6.5 %collective-permute-start.9 = (f32[64,128]{1,0:T(8,128)}, f32[64,128]{1,0:T(8,128)S(1)}, u32[]{:S(2)}, u32[]{:S(2)}) collective-permute-start(f32[64,128]{1,0:T(8,128)} %get-tuple-element.16), channel_id=1, source_target_pairs={{0,8},{1,9},{2,10},{3,11},{4,12},{5,13},{6,14},{7,15},{8,0},{9,1},... | collective-permute-start | bytes 98312 | tf_op jit(solution)/shard_map/ppermute | solution.py:511
  198.2 13.4 %all-to-all-start.2 = ((f32[16,8,128]{2,1,0:T(8,128)}), f32[16,8,128]{2,1,0:T(8,128)S(1)}, u32[]{:S(2)}, u32[]{:S(2)}) async-start(f32[16,8,128]{2,1,0:T(8,128)} %bitcast.19), calls=%async_computation.2 | async-start | bytes 131072 | tf_op jit(solution)/shard_map/all_to_all | solution.py:519

commit v15 on v14

--- a/solution.py
+++ b/solution.py
@@ -322,7 +322,8 @@
             moved_ref[rows, :] = target[rows, :].astype(jnp.bfloat16)
 
 
-def place(ops, first, count, x, x1, w, w1, after):
+def place(ops, x, x1, w, w1, after):
+    count = ops.shape[0]
     blk, width = x.shape
     depth = min(2048, width)
     last = width // depth - 1
@@ -332,7 +333,7 @@
         grid=(count, width // depth),
         out_shape=jax.ShapeDtypeStruct((width, count * LANES), jnp.bfloat16),
         in_specs=[
-            pl.BlockSpec((1, 1, depth), lambda k, i: (first + k, 0, i), memory_space=pltpu.SMEM),
+            pl.BlockSpec((1, 1, depth), lambda k, i: (k, 0, i), memory_space=pltpu.SMEM),
             part,
             part,
             part,
@@ -346,7 +347,7 @@
             flops=0, bytes_accessed=count * width * LANES * 64, transcendentals=0
         ),
         name="place",
-    )(ops, x, x1, w, w1, after)
+    )(ops[:, None, :], x, x1, w, w1, after)
 
 
 def ratio(total_w, sum_x, sum_xx, sum_y, sum_xy, sum_yy):
@@ -379,9 +380,10 @@
     top = lax.broadcasted_iota(jnp.int32, (tiles, SLAB, LANES), 1) < SUB
     lane = lax.broadcasted_iota(jnp.int32, (rows, LANES), 1)
     result = jnp.zeros((rows, LANES), jnp.float32)
-    for k in range(NOPS):
+    count = acc.shape[1] * 2 // 3 // LANES
+    for k in range(count):
         lanes = slice(k * LANES, (k + 1) * LANES)
-        squares = slice((NOPS + k // 2) * LANES, (NOPS + k // 2 + 1) * LANES)
+        squares = slice((count + k // 2) * LANES, (count + k // 2 + 1) * LANES)
         with_w = acc[:rows, lanes]
         with_y = acc[rows:, lanes].reshape(tiles, 2, SLAB, LANES)
         mine, partner = with_y[:, 0], with_y[:, 1]
@@ -399,8 +401,8 @@
     return result
 
 
-def plane_sums_kernel(ended, got_ref, first_ref, second_ref, *refs):
-    acc = refs[-1]
+def plane_sums_kernel(pairs, got_ref, *refs):
+    moved_refs, refs, acc = refs[:pairs], refs[pairs:-1], refs[-1]
     depth = got_ref.shape[1]
     step = min(1024, depth)
     half = LANES // 2
@@ -413,7 +415,7 @@
     for i in range(depth // step):
         cols = slice(i * step, (i + 1) * step)
         linear, square = [], []
-        for ref in (first_ref, second_ref):
+        for ref in moved_refs:
             even, odd = None, None
             for k in range(2):
                 values = ref[cols, k * LANES : (k + 1) * LANES].astype(jnp.float32)
@@ -429,13 +431,15 @@
 
     @pl.when(pl.program_id(0) == pl.num_programs(0) - 1)
     def _():
-        if not ended:
+        if len(refs) == 1:
             refs[0][...] = correlations(acc)
             return
-        own_ref, mine_ref, other_ref, back_ref = refs[:-1]
+        first_ref, second_ref, mine_ref, other_ref, back_ref = refs
         upper = lax.div(lax.axis_index("dp"), 2 * PLANE)
-        count = own_ref.shape[0] // 2
-        for part, result in enumerate((own_ref[...], correlations(acc))):
+        count = first_ref.shape[0] // 2
+        low = lax.broadcasted_iota(jnp.int32, first_ref.shape, 1) < half
+        own = jnp.where(low, first_ref[...], pltpu.roll(second_ref[...], half, 1))
+        for part, result in enumerate((own, correlations(acc))):
             slot = part + upper - 2 * part * upper
             back_ref[slot] = result.reshape(PLANE, SLAB, LANES)
             pairs = result.reshape(PLANE // 2, 2, SLAB, LANES)
@@ -446,28 +450,28 @@
             other_ref[here, :] = jnp.where(top, pltpu.roll(even, SUB, 1), odd).reshape(count, LANES)
 
 
-def plane_sums(got, first, second, own):
+def plane_sums(got, moved, own):
     rows, width = got.shape
     depth = min(2048, width)
-    lanes = (NOPS + NOPS // 2) * LANES
-    ended = own is not None
-    moved = pl.BlockSpec((depth, 2 * LANES), lambda i: (i, 0))
+    lanes = 3 * len(moved) * LANES
+    ended = len(own) > 0
+    placed = pl.BlockSpec((depth, 2 * LANES), lambda i: (i, 0))
     result = (rows // 2, LANES)
     shapes = (result, result, (2, PLANE, SLAB, LANES)) if ended else (result,)
     entire = [pl.BlockSpec(shape, lambda i, shape=shape: (0,) * len(shape)) for shape in shapes]
     outs = pl.pallas_call(
-        functools.partial(plane_sums_kernel, ended),
+        functools.partial(plane_sums_kernel, len(moved)),
         grid=(width // depth,),
         out_shape=tuple(jax.ShapeDtypeStruct(shape, jnp.float32) for shape in shapes),
-        in_specs=[pl.BlockSpec((rows, depth), lambda i: (0, i)), moved, moved] + ([entire[0]] if ended else []),
+        in_specs=[pl.BlockSpec((rows, depth), lambda i: (0, i))] + [placed] * len(moved) + [entire[0]] * len(own),
         out_specs=tuple(entire),
         scratch_shapes=[pltpu.VMEM((rows * 3 // 2, lanes), jnp.float32)],
         compiler_params=params(),
         cost_estimate=pl.CostEstimate(
-            flops=3 * rows * width * lanes, bytes_accessed=2 * width * (rows + 4 * LANES), transcendentals=0
+            flops=3 * rows * width * lanes, bytes_accessed=2 * width * (rows + 2 * len(moved) * LANES), transcendentals=0
         ),
         name="plane_sums",
-    )(got, first, second, *((own,) if ended else ()))
+    )(got, *moved, *own)
     return outs if ended else outs[0]
 
 
@@ -488,7 +492,6 @@
         return got.reshape(PLANE * 2 * SLAB, width)
 
     own_pick = pick[:, 0]
-    ops = ops[:, None, :]
     near_x = lax.ppermute(intensities, "dp", near)
     mid_x = lax.ppermute(intensities, "dp", middle)
     far_pick = lax.ppermute(own_pick, "dp", far)
@@ -501,12 +504,13 @@
     inner_x = lax.ppermute(near_x, "dp", middle)
     outer_w = lax.ppermute(mid_w, "dp", outward)
     inner_w = lax.ppermute(near_w, "dp", middle)
-    first = place(ops, 0, 2, intensities, near_x, own_w, near_w, own_pick)
-    far_send = far_pack(far_pick, outer_x, outer_w, inner_x, inner_w, first)
+    first = place(ops[:2], intensities, near_x, own_w, near_w, own_pick)
+    own_first = plane_sums(own_got, (first,), ())
+    far_send = far_pack(far_pick, outer_x, outer_w, inner_x, inner_w, own_first)
     far_got = spread(far_send)
-    second = place(ops, 2, 2, intensities, near_x, own_w, near_w, far_send)
-    own_corr = plane_sums(own_got, first, second, None)
-    mine, other, back = plane_sums(far_got, first, second, own_corr)
+    second = place(ops[2:], intensities, near_x, own_w, near_w, far_send)
+    own_second = plane_sums(own_got, (second,), ())
+    mine, other, back = plane_sums(far_got, (first, second), (own_first, own_second))
 
     from_near = lax.ppermute(other, "dp", near)
     pair = [each.reshape(2, PLANE, SUB, NOPS * blk) for each in (mine, from_near)]

time: 214 us -> 206 us (0.963)
  waiting for transfers between devices: 57.9 us -> 37.5 us
  Pallas kernels: 115 us -> 122 us
  starting transfers between devices: 31.6 us -> 36.7 us
    ppermute x1, waiting for transfers between devices: 10.9 us -> 0.01 us  [shards_by_plane(): outer_w = lax.ppermute(mid_w, 'dp', outward)]
    ppermute x1, waiting for transfers between devices: 41.7 us -> 32.2 us  [shards_by_plane(): far_pick = lax.ppermute(own_pick, 'dp', far)]
    pallas_call x2 -> x3, Pallas kernels: 31.8 us -> 39.1 us  [plane_sums(): pl.pallas_call(functools.partial(plane_sums_kernel, len(moved)), grid=(wi...]
    ppermute x1, starting transfers between devices: 0.01 us -> 6.98 us  [shards_by_plane(): from_near = lax.ppermute(other, 'dp', near)]
  transfers between devices with their start and end apart: 13 -> 13, of which waited for: 3 -> 3; matrix products, arithmetic and copies ran while one was open for 1% -> 2% of each run, Pallas kernels for 44% -> 49%
where the time goes in v15:
time: 206 us; the launch traced here: 205 us
  Pallas kernels  122 us (59%)
  waiting for transfers between devices  37.5 us (18%)
  starting transfers between devices  36.7 us (18%)
  local copies, waits for them, and re-layouts  3.96 us (2%)
  other arithmetic  3.8 us (2%)
    pallas_call x2, Pallas kernels, place(): pl.pallas_call(place_kernel, grid=(count, width // depth), out_shape=jax....  73.5 us
    pallas_call x3, Pallas kernels, plane_sums(): pl.pallas_call(functools.partial(plane_sums_kernel, len(moved)), grid=(wi...  39.1 us
    ppermute x1, waiting for transfers between devices, shards_by_plane(): far_pick = lax.ppermute(own_pick, 'dp', far)  32.2 us
    all_to_all x2, starting transfers between devices, spread(): lax.all_to_all(send, 'dp', split_axis=0, concat_axis=0, axis_index_groups...  9.32 us
    pallas_call x2, Pallas kernels, pack_call(): pl.pallas_call(kernel, out_shape=jax.ShapeDtypeStruct((PLANE, 2, SLAB, wi...  9.31 us
    ppermute x1, starting transfers between devices, shards_by_plane(): from_near = lax.ppermute(other, 'dp', near)  6.98 us
    all_to_all x1, waiting for transfers between devices, shards_by_plane(): lax.all_to_all(back, 'dp', split_axis=0, concat_axis=0, axis_index_groups...  5.15 us
    all_to_all x1, starting transfers between devices, shards_by_plane(): lax.all_to_all(back, 'dp', split_axis=0, concat_axis=0, axis_index_groups...  4.7 us
  transfers between devices with their start and end apart: 13, of which 3 were waited for; matrix products, arithmetic and copies ran while one was open for 2% of the time, Pallas kernels for 49%

profile of v15, /device:TPU:0, one launch (start us, length us, event | category | flops | bytes accessed | tf_op | source)
XLA Modules:
  0.0 204.7 jit_solution(14075813129529670532)
XLA Ops:
  0.6 0.0 copy-start.1
  0.6 2.2 %multiply_convert_fusion.w_ref = bf16[32,16384]{1,0:T(8,128)(2,1)S(1)} fusion(bf16[32,16384]{1,0:T(8,128)(2,1)} %param.7, s32[32,16384]{1,0:T(8,128)} %param.6), kind=kLoop, calls=%fused_computation | loop fusion | flops 2097152 | bytes 4194304 | tf_op jit(solution)/shard_map/convert_element_type | solution.py:498
  2.9 0.0 copy-start
  2.9 3.1 %collective-permute-start.2 = (bf16[32,16384]{1,0:T(8,128)(2,1)S(1)}, bf16[32,16384]{1,0:T(8,128)(2,1)S(1)}, u32[]{:S(2)}, u32[]{:S(2)}) collective-permute-start(bf16[32,16384]{1,0:T(8,128)(2,1)S(1)} %multiply_convert_fusion.w_ref), channel_id=1, source_target_pairs={{0,8},{1,9},{2,10},{3,11},{4,12},{5,13},{6,14},{7,15},{8,0},{9,1},... | collective-permute-start | bytes 3145736 | tf_op jit(solution)/shard_map/ppermute | solution.py:499
  6.0 1.7 collective-permute-start.3
  7.7 0.0 copy-done.1
  7.7 3.4 %collective-permute-start = (bf16[32,16384]{1,0:T(8,128)(2,1)S(1)}, bf16[32,16384]{1,0:T(8,128)(2,1)}, u32[]{:S(2)}, u32[]{:S(2)}) collective-permute-start(bf16[32,16384]{1,0:T(8,128)(2,1)S(1)} %copy-done.1), channel_id=1, source_target_pairs={{0,8},{1,9},{2,10},{3,11},{4,12},{5,13},{6,14},{7,15},{8,0},{9,1},... | collective-permute-start | bytes 3145736 | tf_op jit(solution)/shard_map/ppermute | solution.py:495
  11.1 1.6 collective-permute-start.1
  12.8 0.0 copy-done
  12.8 4.3 %own_pack.1 = bf16[8,2,8,16384]{3,2,1,0:T(8,128)(2,1)} custom-call(s32[32]{0:T(128)} %bitcast.23, bf16[32,16384]{1,0:T(8,128)(2,1)} %x_ref.5, bf16[32,16384]{1,0:T(8,128)(2,1)} %copy-done), custom_call_target="tpu_custom_call" | custom-call | flops 2097152 | bytes 6291456 | tf_op jit(solution)/shard_map/own_pack/pallas_call | solution.py:254
  17.1 0.0 copy-start.6
  17.1 0.0 copy-start.5
  17.1 4.7 %all-to-all-start = ((bf16[8,2,8,16384]{3,2,1,0:T(8,128)(2,1)}), bf16[8,2,8,16384]{3,2,1,0:T(8,128)(2,1)}, u32[]{:S(2)}, u32[]{:S(2)}) async-start(bf16[8,2,8,16384]{3,2,1,0:T(8,128)(2,1)} %own_pack.1), calls=%async_computation | async-start | bytes 8388608 | tf_op jit(solution)/shard_map/all_to_all | solution.py:491
  21.8 0.0 copy-done.6
  21.8 1.8 collective-permute-start.4
  23.6 32.2 %collective-permute-done.4.pick_ref = s32[32]{0:T(128)S(1)} collective-permute-done((s32[32]{0:T(128)S(1)}, s32[32]{0:T(128)S(1)}, u32[]{:S(2)}, u32[]{:S(2)}) %collective-permute-start.4) | collective-permute-done | bytes 160 | tf_op jit(solution)/shard_map/ppermute | solution.py:497
  55.8 0.0 copy-start.7
  55.8 0.0 collective-permute-done.2.w1_ref
  55.8 0.0 copy-start.2
  55.8 0.0 collective-permute-done.3
  55.8 0.0 collective-permute-done.x1_ref
  55.8 0.0 collective-permute-done.1
  55.8 0.7 collective-permute-start.7
  56.6 0.7 collective-permute-start.8
  57.3 1.3 collective-permute-start.5
  58.6 1.3 collective-permute-start.6
  59.9 0.0 copy-done.5
  59.9 0.1 fusion
  60.0 0.7 broadcast_in_dim.6.ops_ref
  60.8 0.0 copy-done.2
  60.8 36.8 %place.2.refs_0_ = bf16[16384,256]{1,0:T(8,128)(2,1)} custom-call(s32[2,1,16384]{2,1,0:T(1,128)} %broadcast_in_dim.6.ops_ref, bf16[32,16384]{1,0:T(8,128)(2,1)} %x_ref.5, bf16[32,16384]{1,0:T(8,128)(2,1)} %collective-permute-done.x1_ref, bf16[32,16384]{1,0:T(8,128)(2,1)} %copy-done, bf16[32,16384]{1,0:T(8,128)(2,1)} %copy-done.2, s32[32]{0:T(128)} %bitcast.24), custom_call_target="tpu_custom_call" | custom-call | bytes 268435456 | tf_op jit(solution)/shard_map/place/pallas_call | solution.py:331
  97.6 0.0 copy-done.7
  97.6 0.0 all-to-all-done
  97.6 11.5 %plane_sums.3.after_ref.refs_2_ = f32[64,128]{1,0:T(8,128)} custom-call(bf16[128,16384]{1,0:T(8,128)(2,1)} %bitcast.1.got_ref, bf16[16384,256]{1,0:T(8,128)(2,1)} %place.2.refs_0_), custom_call_target="tpu_custom_call" | custom-call | flops 2415919104 | bytes 12582912 | tf_op jit(solution)/shard_map/plane_sums/pallas_call | solution.py:462
  109.1 0.0 collective-permute-done.7.xi
  109.1 0.0 copy-start.3
  109.1 0.0 collective-permute-done.8.wi
  109.1 0.0 copy-start.4
  109.1 0.0 collective-permute-done.5.xo
  109.1 0.0 collective-permute-done.6.wo
  109.1 1.0 copy-done.3
  110.2 0.3 copy-done.4
  110.5 5.0 %far_pack.1.after_ref = bf16[8,2,8,16384]{3,2,1,0:T(8,128)(2,1)} custom-call(s32[32]{0:T(128)} %copy-done.7, bf16[32,16384]{1,0:T(8,128)(2,1)} %collective-permute-done.5.xo, bf16[32,16384]{1,0:T(8,128)(2,1)} %collective-permute-done.6.wo, bf16[32,16384]{1,0:T(8,128)(2,1)} %copy-done.3, bf16[32,16384]{1,0:T(8,128)(2,1)} %copy-done.4, ...), custom_call_target="tpu_custom_call" | custom-call | flops 2097152 | bytes 6291456 | tf_op jit(solution)/shard_map/far_pack/pallas_call | solution.py:254
  115.5 4.6 %all-to-all-start.1 = ((bf16[8,2,8,16384]{3,2,1,0:T(8,128)(2,1)}), bf16[8,2,8,16384]{3,2,1,0:T(8,128)(2,1)}, u32[]{:S(2)}, u32[]{:S(2)}) async-start(bf16[8,2,8,16384]{3,2,1,0:T(8,128)(2,1)} %far_pack.1.after_ref), calls=%async_computation.1 | async-start | bytes 8388608 | tf_op jit(solution)/shard_map/all_to_all | solution.py:491
  120.1 0.7 broadcast_in_dim.7.ops_ref
  120.9 36.7 %place.3.refs_0_.refs_1_ = bf16[16384,256]{1,0:T(8,128)(2,1)} custom-call(s32[2,1,16384]{2,1,0:T(1,128)} %broadcast_in_dim.7.ops_ref, bf16[32,16384]{1,0:T(8,128)(2,1)} %x_ref.5, bf16[32,16384]{1,0:T(8,128)(2,1)} %collective-permute-done.x1_ref, bf16[32,16384]{1,0:T(8,128)(2,1)} %copy-done, bf16[32,16384]{1,0:T(8,128)(2,1)} %copy-done.2, ...), custom_call_target="tpu_custom_call" | custom-call | bytes 268435456 | tf_op jit(solution)/shard_map/place/pallas_call | solution.py:331
  157.6 11.5 %plane_sums.4.refs_3_ = f32[64,128]{1,0:T(8,128)} custom-call(bf16[128,16384]{1,0:T(8,128)(2,1)} %bitcast.1.got_ref, bf16[16384,256]{1,0:T(8,128)(2,1)} %place.3.refs_0_.refs_1_), custom_call_target="tpu_custom_call" | custom-call | flops 2415919104 | bytes 12582912 | tf_op jit(solution)/shard_map/plane_sums/pallas_call | solution.py:462
  169.1 0.1 all-to-all-done.1
  169.3 16.0 %plane_sums.5 = (f32[64,128]{1,0:T(8,128)}, f32[64,128]{1,0:T(8,128)}, f32[2,8,8,128]{3,2,1,0:T(8,128)}) custom-call(bf16[128,16384]{1,0:T(8,128)(2,1)} %bitcast.2.got_ref, bf16[16384,256]{1,0:T(8,128)(2,1)} %place.2.refs_0_, bf16[16384,256]{1,0:T(8,128)(2,1)} %place.3.refs_0_.refs_1_, f32[64,128]{1,0:T(8,128)} %plane_sums.3.after_ref.refs_2_, ...), custom_call_target="tpu_custom_call" | custom-call | flops 4831838208 | bytes 20971520 | tf_op jit(solution)/shard_map/plane_sums/pallas_call | solution.py:462
  185.3 7.0 %collective-permute-start.9 = (f32[64,128]{1,0:T(8,128)}, f32[64,128]{1,0:T(8,128)S(1)}, u32[]{:S(2)}, u32[]{:S(2)}) collective-permute-start(f32[64,128]{1,0:T(8,128)} %get-tuple-element.16), channel_id=1, source_target_pairs={{0,8},{1,9},{2,10},{3,11},{4,12},{5,13},{6,14},{7,15},{8,0},{9,1},... | collective-permute-start | bytes 98312 | tf_op jit(solution)/shard_map/ppermute | solution.py:515
  192.3 4.7 %all-to-all-start.2 = ((f32[16,8,128]{2,1,0:T(8,128)}), f32[16,8,128]{2,1,0:T(8,128)S(1)}, u32[]{:S(2)}, u32[]{:S(2)}) async-start(f32[16,8,128]{2,1,0:T(8,128)} %bitcast.19), calls=%async_computation.2 | async-start | bytes 131072 | tf_op jit(solution)/shard_map/all_to_all | solution.py:523
  197.0 0.0 collective-permute-done.9
  197.0 0.8 pad_maximum_fusion
  197.8 0.7 copy.16
  198.6 5.2 %all-to-all-done.2 = f32[16,8,128]{2,1,0:T(8,128)S(1)} async-done(((f32[16,8,128]{2,1,0:T(8,128)}), f32[16,8,128]{2,1,0:T(8,128)S(1)}, u32[]{:S(2)}, u32[]{:S(2)}) %all-to-all-start.2) | async-done | bytes 65568 | tf_op jit(solution)/shard_map/all_to_all | solution.py:523
  203.7 0.2 reshape.30
  203.9 0.1 copy.17
  204.0 0.8 reverse_select_fusion
  (2 shorter events, 0.0 us)
Async XLA Ops:
  0.6 7.0 %copy-start.1 = (bf16[32,16384]{1,0:T(8,128)(2,1)S(1)}, bf16[32,16384]{1,0:T(8,128)(2,1)}, u32[]{:S(2)}) copy-start(bf16[32,16384]{1,0:T(8,128)(2,1)} %x_ref.5) | copy-start | bytes 3145732
  2.9 9.9 %copy-start = (bf16[32,16384]{1,0:T(8,128)(2,1)}, bf16[32,16384]{1,0:T(8,128)(2,1)S(1)}, u32[]{:S(2)}) copy-start(bf16[32,16384]{1,0:T(8,128)(2,1)S(1)} %multiply_convert_fusion.w_ref) | copy-start | bytes 3145732
  2.9 52.9 %collective-permute-start.2 = (bf16[32,16384]{1,0:T(8,128)(2,1)S(1)}, bf16[32,16384]{1,0:T(8,128)(2,1)S(1)}, u32[]{:S(2)}, u32[]{:S(2)}) collective-permute-start(bf16[32,16384]{1,0:T(8,128)(2,1)S(1)} %multiply_convert_fusion.w_ref), channel_id=1, source_target_pairs={{0,8},{1,9},{2,10},{3,11},{4,12},{5,13},{6,14},{7,15},{8,0},{9,1},... | collective-permute-start | bytes 3145736 | tf_op jit(solution)/shard_map/ppermute | solution.py:499
  6.0 49.8 %collective-permute-start.3 = (bf16[32,16384]{1,0:T(8,128)(2,1)S(1)}, bf16[32,16384]{1,0:T(8,128)(2,1)}, u32[]{:S(2)}, u32[]{:S(2)}) collective-permute-start(bf16[32,16384]{1,0:T(8,128)(2,1)S(1)} %multiply_convert_fusion.w_ref), channel_id=1, source_target_pairs={{8,16},{9,17},{10,18},{11,19},{12,20},{13,21},{14,22},{15,23},{16,... | collective-permute-start | bytes 3145736 | tf_op jit(solution)/shard_map/ppermute | solution.py:500
  7.7 48.1 %collective-permute-start = (bf16[32,16384]{1,0:T(8,128)(2,1)S(1)}, bf16[32,16384]{1,0:T(8,128)(2,1)}, u32[]{:S(2)}, u32[]{:S(2)}) collective-permute-start(bf16[32,16384]{1,0:T(8,128)(2,1)S(1)} %copy-done.1), channel_id=1, source_target_pairs={{0,8},{1,9},{2,10},{3,11},{4,12},{5,13},{6,14},{7,15},{8,0},{9,1},... | collective-permute-start | bytes 3145736 | tf_op jit(solution)/shard_map/ppermute | solution.py:495
  11.1 44.7 %collective-permute-start.1 = (bf16[32,16384]{1,0:T(8,128)(2,1)S(1)}, bf16[32,16384]{1,0:T(8,128)(2,1)}, u32[]{:S(2)}, u32[]{:S(2)}) collective-permute-start(bf16[32,16384]{1,0:T(8,128)(2,1)S(1)} %copy-done.1), channel_id=1, source_target_pairs={{8,16},{9,17},{10,18},{11,19},{12,20},{13,21},{14,22},{15,23},{16,... | collective-permute-start | bytes 3145736 | tf_op jit(solution)/shard_map/ppermute | solution.py:496
  17.1 4.7 %copy-start.6 = (s32[32,1]{0,1:T(1,128)S(1)}, s32[32,1]{0,1:T(1,128)}, u32[]{:S(2)}) copy-start(s32[32,1]{0,1:T(1,128)} %param.9) | copy-start | bytes 388
  17.1 42.8 %copy-start.5 = (s32[4,16384]{1,0:T(4,128)S(1)}, s32[4,16384]{1,0:T(4,128)}, u32[]{:S(2)}) copy-start(s32[4,16384]{1,0:T(4,128)} %param.8) | copy-start | bytes 786436
  17.1 80.5 %all-to-all-start = ((bf16[8,2,8,16384]{3,2,1,0:T(8,128)(2,1)}), bf16[8,2,8,16384]{3,2,1,0:T(8,128)(2,1)}, u32[]{:S(2)}, u32[]{:S(2)}) async-start(bf16[8,2,8,16384]{3,2,1,0:T(8,128)(2,1)} %own_pack.1), calls=%async_computation | async-start | bytes 8388608 | tf_op jit(solution)/shard_map/all_to_all | solution.py:491
  21.8 34.0 %collective-permute-start.4 = (s32[32]{0:T(128)S(1)}, s32[32]{0:T(128)S(1)}, u32[]{:S(2)}, u32[]{:S(2)}) collective-permute-start(s32[32]{0:T(128)S(1)} %bitcast.25), channel_id=1, source_target_pairs={{0,16},{1,17},{2,18},{3,19},{4,20},{5,21},{6,22},{7,23},{8,24},{9,... | collective-permute-start | bytes 392 | tf_op jit(solution)/shard_map/ppermute | solution.py:497
  55.8 41.8 %copy-start.7 = (s32[32]{0:T(128)}, s32[32]{0:T(128)S(1)}, u32[]{:S(2)}) copy-start(s32[32]{0:T(128)S(1)} %collective-permute-done.4.pick_ref) | copy-start | bytes 388
  55.8 5.0 %copy-start.2 = (bf16[32,16384]{1,0:T(8,128)(2,1)}, bf16[32,16384]{1,0:T(8,128)(2,1)S(1)}, u32[]{:S(2)}) copy-start(bf16[32,16384]{1,0:T(8,128)(2,1)S(1)} %collective-permute-done.2.w1_ref) | copy-start | bytes 3145732
  55.8 53.3 %collective-permute-start.7 = (bf16[32,16384]{1,0:T(8,128)(2,1)}, bf16[32,16384]{1,0:T(8,128)(2,1)S(1)}, u32[]{:S(2)}, u32[]{:S(2)}) collective-permute-start(bf16[32,16384]{1,0:T(8,128)(2,1)} %collective-permute-done.x1_ref), channel_id=1, source_target_pairs={{8,16},{9,17},{10,18},{11,19},{12,20},{13,21},{14,22},{15,23},{16,... | collective-permute-start | bytes 3145736 | tf_op jit(solution)/shard_map/ppermute | solution.py:504
  56.6 52.5 %collective-permute-start.8 = (bf16[32,16384]{1,0:T(8,128)(2,1)S(1)}, bf16[32,16384]{1,0:T(8,128)(2,1)S(1)}, u32[]{:S(2)}, u32[]{:S(2)}) collective-permute-start(bf16[32,16384]{1,0:T(8,128)(2,1)S(1)} %collective-permute-done.2.w1_ref), channel_id=1, source_target_pairs={{8,16},{9,17},{10,18},{11,19},{12,20},{13,21},{14,22},{15,23},{16,... | collective-permute-start | bytes 3145736 | tf_op jit(solution)/shard_map/ppermute | solution.py:506
  57.3 51.8 %collective-permute-start.5 = (bf16[32,16384]{1,0:T(8,128)(2,1)}, bf16[32,16384]{1,0:T(8,128)(2,1)}, u32[]{:S(2)}, u32[]{:S(2)}) collective-permute-start(bf16[32,16384]{1,0:T(8,128)(2,1)} %collective-permute-done.1), channel_id=1, source_target_pairs={{8,0},{9,1},{10,2},{11,3},{12,4},{13,5},{14,6},{15,7},{16,24},{17,... | collective-permute-start | bytes 3145736 | tf_op jit(solution)/shard_map/ppermute | solution.py:503
  58.6 50.5 %collective-permute-start.6 = (bf16[32,16384]{1,0:T(8,128)(2,1)}, bf16[32,16384]{1,0:T(8,128)(2,1)}, u32[]{:S(2)}, u32[]{:S(2)}) collective-permute-start(bf16[32,16384]{1,0:T(8,128)(2,1)} %collective-permute-done.3), channel_id=1, source_target_pairs={{8,0},{9,1},{10,2},{11,3},{12,4},{13,5},{14,6},{15,7},{16,24},{17,... | collective-permute-start | bytes 3145736 | tf_op jit(solution)/shard_map/ppermute | solution.py:505
  109.1 1.1 copy-start.3
  109.1 1.4 copy-start.4
  115.5 53.8 %all-to-all-start.1 = ((bf16[8,2,8,16384]{3,2,1,0:T(8,128)(2,1)}), bf16[8,2,8,16384]{3,2,1,0:T(8,128)(2,1)}, u32[]{:S(2)}, u32[]{:S(2)}) async-start(bf16[8,2,8,16384]{3,2,1,0:T(8,128)(2,1)} %far_pack.1.after_ref), calls=%async_computation.1 | async-start | bytes 8388608 | tf_op jit(solution)/shard_map/all_to_all | solution.py:491
  185.3 11.7 %collective-permute-start.9 = (f32[64,128]{1,0:T(8,128)}, f32[64,128]{1,0:T(8,128)S(1)}, u32[]{:S(2)}, u32[]{:S(2)}) collective-permute-start(f32[64,128]{1,0:T(8,128)} %get-tuple-element.16), channel_id=1, source_target_pairs={{0,8},{1,9},{2,10},{3,11},{4,12},{5,13},{6,14},{7,15},{8,0},{9,1},... | collective-permute-start | bytes 98312 | tf_op jit(solution)/shard_map/ppermute | solution.py:515
  192.3 11.4 %all-to-all-start.2 = ((f32[16,8,128]{2,1,0:T(8,128)}), f32[16,8,128]{2,1,0:T(8,128)S(1)}, u32[]{:S(2)}, u32[]{:S(2)}) async-start(f32[16,8,128]{2,1,0:T(8,128)} %bitcast.19), calls=%async_computation.2 | async-start | bytes 131072 | tf_op jit(solution)/shard_map/all_to_all | solution.py:523

commit v16 on v15

--- a/solution.py
+++ b/solution.py
@@ -190,18 +190,17 @@
     return numer / jnp.sqrt(var_x * var_y)
 
 
-def fill_slabs(slabs, x_ref, w_ref):
-    blk, width = x_ref.shape
+def fill_slabs(slabs, xw_ref):
+    blk, width = xw_ref.shape[0] // 2, xw_ref.shape[1]
     step = min(512, width)
 
     @pl.loop(0, width // step)
     def _(i):
         cols = pl.ds(pl.multiple_of(i * step, step), step)
-        wide_x = x_ref[:, cols].astype(jnp.float32)
-        wide_w = w_ref[:, cols].astype(jnp.float32)
+        wide = xw_ref[:, cols].astype(jnp.float32)
         for g in range(blk // SUB):
             rows = slice(g * SUB, (g + 1) * SUB)
-            slab = jnp.concatenate([wide_x[rows], wide_w[rows]], 0)
+            slab = jnp.concatenate([wide[:blk][rows], wide[blk:][rows]], 0)
             slabs[g, :, cols] = slab.astype(jnp.bfloat16)
 
 
@@ -219,34 +218,29 @@
         copy.wait()
 
 
-def own_pack_kernel(pick_ref, x_ref, w_ref, send_ref, slabs, sems):
-    fill_slabs(slabs, x_ref, w_ref)
+def own_pack_kernel(pick_ref, xw_ref, send_ref, slabs, sems):
+    fill_slabs(slabs, xw_ref)
     send_slabs(slabs, pick_ref, send_ref, sems)
 
 
-def far_pack_kernel(pick_ref, xo_ref, wo_ref, xi_ref, wi_ref, after_ref, send_ref, x_buf, w_buf, slabs, sems, in_sems):
+def far_pack_kernel(pick_ref, outer_ref, inner_ref, after_ref, send_ref, buf, in_sem, slabs, sems):
     plane = lax.div(lax.axis_index("dp"), PLANE)
-    inner = (plane == 1) | (plane == 2)
-
-    def fetch(x_ref, w_ref):
-        copies = (
-            pltpu.make_async_copy(x_ref, x_buf, in_sems.at[0]),
-            pltpu.make_async_copy(w_ref, w_buf, in_sems.at[1]),
-        )
-        for copy in copies:
-            copy.start()
-        for copy in copies:
-            copy.wait()
-
-    @pl.when(inner)
-    def _():
-        fetch(xi_ref, wi_ref)
-
-    @pl.when(jnp.logical_not(inner))
-    def _():
-        fetch(xo_ref, wo_ref)
-
-    fill_slabs(slabs, x_buf, w_buf)
+    is_inner = (plane == 1) | (plane == 2)
+
+    def fetch(ref):
+        copy = pltpu.make_async_copy(ref, buf, in_sem)
+        copy.start()
+        copy.wait()
+
+    @pl.when(is_inner)
+    def _():
+        fetch(inner_ref)
+
+    @pl.when(jnp.logical_not(is_inner))
+    def _():
+        fetch(outer_ref)
+
+    fill_slabs(slabs, buf)
     send_slabs(slabs, pick_ref, send_ref, sems)
 
 
@@ -266,27 +260,21 @@
     )(*operands)
 
 
-def own_pack(pick, x, w):
-    specs = [pl.BlockSpec(memory_space=pltpu.VMEM)] * 2
-    return pack_call(own_pack_kernel, "own_pack", specs, [], *x.shape, pick, x, w)
-
-
-def far_pack(pick, x_outer, w_outer, x_inner, w_inner, after):
-    blk, width = x_outer.shape
-    buf = pltpu.VMEM((blk, width), jnp.bfloat16)
-
-    def kernel(pick_ref, xo, wo, xi, wi, after_ref, send_ref, x_buf, w_buf, in_sems, slabs, sems):
-        far_pack_kernel(pick_ref, xo, wo, xi, wi, after_ref, send_ref, x_buf, w_buf, slabs, sems, in_sems)
-
-    return pack_call(
-        kernel, "far_pack", [pl.BlockSpec(memory_space=pl.ANY)] * 5,
-        [buf, buf, pltpu.SemaphoreType.DMA((2,))], blk, width,
-        pick, x_outer, w_outer, x_inner, w_inner, after,
-    )
-
-
-def place_kernel(ops_ref, x_ref, x1_ref, w_ref, w1_ref, after_ref, moved_ref, table, target):
-    depth = x_ref.shape[1]
+def own_pack(pick, xw):
+    rows, width = xw.shape
+    specs = [pl.BlockSpec(memory_space=pltpu.VMEM)]
+    return pack_call(own_pack_kernel, "own_pack", specs, [], rows // 2, width, pick, xw)
+
+
+def far_pack(pick, outer, inner, after):
+    rows, width = outer.shape
+    scratch = [pltpu.VMEM((rows, width), jnp.bfloat16), pltpu.SemaphoreType.DMA]
+    specs = [pl.BlockSpec(memory_space=pl.ANY)] * 3
+    return pack_call(far_pack_kernel, "far_pack", specs, scratch, rows // 2, width, pick, outer, inner, after)
+
+
+def place_kernel(ops_ref, mine_ref, near_ref, after_ref, moved_ref, table, target):
+    blk, depth = mine_ref.shape[0] // 2, mine_ref.shape[1]
     width = target.shape[0]
     part = pl.multiple_of(pl.program_id(1) * depth, depth)
 
@@ -299,7 +287,8 @@
         identity = jnp.where(diagonal, 1.0, 0.0).astype(jnp.bfloat16)
         for i in range(depth // step):
             cols = slice(i * step, (i + 1) * step)
-            rows = jnp.concatenate([x_ref[:, cols], x1_ref[:, cols], w_ref[:, cols], w1_ref[:, cols]], 0)
+            pair = (mine_ref, near_ref)
+            rows = jnp.concatenate([ref[:blk, cols] for ref in pair] + [ref[blk:, cols] for ref in pair], 0)
             table[pl.ds(part + i * step, step), :] = lax.dot_general(
                 identity, rows, (((1,), (1,)), ((), ())), preferred_element_type=jnp.float32
             )
@@ -322,20 +311,18 @@
             moved_ref[rows, :] = target[rows, :].astype(jnp.bfloat16)
 
 
-def place(ops, x, x1, w, w1, after):
+def place(ops, mine, near, after):
     count = ops.shape[0]
-    blk, width = x.shape
+    rows, width = mine.shape
     depth = min(2048, width)
     last = width // depth - 1
-    part = pl.BlockSpec((blk, depth), lambda k, i: (0, jnp.where(k == 0, i, last)))
+    part = pl.BlockSpec((rows, depth), lambda k, i: (0, jnp.where(k == 0, i, last)))
     return pl.pallas_call(
         place_kernel,
         grid=(count, width // depth),
         out_shape=jax.ShapeDtypeStruct((width, count * LANES), jnp.bfloat16),
         in_specs=[
             pl.BlockSpec((1, 1, depth), lambda k, i: (k, 0, i), memory_space=pltpu.SMEM),
-            part,
-            part,
             part,
             part,
             pl.BlockSpec(memory_space=pl.ANY),
@@ -347,7 +334,7 @@
             flops=0, bytes_accessed=count * width * LANES * 64, transcendentals=0
         ),
         name="place",
-    )(ops[:, None, :], x, x1, w, w1, after)
+    )(ops[:, None, :], mine, near, after)
 
 
 def ratio(total_w, sum_x, sum_xx, sum_y, sum_xy, sum_yy):
@@ -492,23 +479,20 @@
         return got.reshape(PLANE * 2 * SLAB, width)
 
     own_pick = pick[:, 0]
-    near_x = lax.ppermute(intensities, "dp", near)
-    mid_x = lax.ppermute(intensities, "dp", middle)
+    own_w = (observed.astype(jnp.float32) * qweights.astype(jnp.float32)).astype(jnp.bfloat16)
+    mine_xw = jnp.concatenate([intensities, own_w], 0)
+    near_xw = lax.ppermute(mine_xw, "dp", near)
+    mid_xw = lax.ppermute(mine_xw, "dp", middle)
     far_pick = lax.ppermute(own_pick, "dp", far)
-    own_w = (observed.astype(jnp.float32) * qweights.astype(jnp.float32)).astype(jnp.bfloat16)
-    near_w = lax.ppermute(own_w, "dp", near)
-    mid_w = lax.ppermute(own_w, "dp", middle)
-    own_got = spread(own_pack(own_pick, intensities, own_w))
-    near_x, mid_x, near_w, mid_w, far_pick = lax.optimization_barrier((near_x, mid_x, near_w, mid_w, far_pick))
-    outer_x = lax.ppermute(mid_x, "dp", outward)
-    inner_x = lax.ppermute(near_x, "dp", middle)
-    outer_w = lax.ppermute(mid_w, "dp", outward)
-    inner_w = lax.ppermute(near_w, "dp", middle)
-    first = place(ops[:2], intensities, near_x, own_w, near_w, own_pick)
+    own_got = spread(own_pack(own_pick, mine_xw))
+    near_xw, mid_xw, far_pick = lax.optimization_barrier((near_xw, mid_xw, far_pick))
+    outer_xw = lax.ppermute(mid_xw, "dp", outward)
+    inner_xw = lax.ppermute(near_xw, "dp", middle)
+    first = place(ops[:2], mine_xw, near_xw, own_pick)
     own_first = plane_sums(own_got, (first,), ())
-    far_send = far_pack(far_pick, outer_x, outer_w, inner_x, inner_w, own_first)
+    far_send = far_pack(far_pick, outer_xw, inner_xw, own_first)
     far_got = spread(far_send)
-    second = place(ops[2:], intensities, near_x, own_w, near_w, far_send)
+    second = place(ops[2:], mine_xw, near_xw, far_send)
     own_second = plane_sums(own_got, (second,), ())
     mine, other, back = plane_sums(far_got, (first, second), (own_first, own_second))
 

time: 206 us -> 202 us (0.981)
  starting transfers between devices: 36.7 us -> 28 us
  waiting for transfers between devices: 37.5 us -> 41.3 us
    ppermute x8 -> x4, starting transfers between devices: 13.9 us -> 7.19 us  [the longest x1 3.09 us: shards_by_plane(): near_xw = lax.ppermute(mine_xw, 'dp', near)]
    ppermute x1, waiting for transfers between devices: 32.2 us -> 36.1 us  [shards_by_plane(): far_pick = lax.ppermute(own_pick, 'dp', far)]
    ppermute x1, starting transfers between devices: 6.98 us -> 4.82 us  [shards_by_plane(): from_near = lax.ppermute(other, 'dp', near)]
  transfers between devices with their start and end apart: 13 -> 9, of which waited for: 3 -> 2; matrix products, arithmetic and copies ran while one was open for 2% -> 2% of each run, Pallas kernels for 49% -> 51%
where the time goes in v16:
time: 202 us; the launch traced here: 201 us
  Pallas kernels  123 us (61%)
  waiting for transfers between devices  41.3 us (20%)
  starting transfers between devices  28 us (14%)
  local copies, waits for them, and re-layouts  3.96 us (2%)
  other arithmetic  3.94 us (2%)
    pallas_call x2, Pallas kernels, place(): pl.pallas_call(place_kernel, grid=(count, width // depth), out_shape=jax....  74.5 us
    pallas_call x3, Pallas kernels, plane_sums(): pl.pallas_call(functools.partial(plane_sums_kernel, len(moved)), grid=(wi...  39.1 us
    ppermute x1, waiting for transfers between devices, shards_by_plane(): far_pick = lax.ppermute(own_pick, 'dp', far)  36.1 us
    pallas_call x2, Pallas kernels, pack_call(): pl.pallas_call(kernel, out_shape=jax.ShapeDtypeStruct((PLANE, 2, SLAB, wi...  9.36 us
    all_to_all x2, starting transfers between devices, spread(): lax.all_to_all(send, 'dp', split_axis=0, concat_axis=0, axis_index_groups...  9.26 us
    all_to_all x1, waiting for transfers between devices, shards_by_plane(): lax.all_to_all(back, 'dp', split_axis=0, concat_axis=0, axis_index_groups...  5.15 us
    ppermute x1, starting transfers between devices, shards_by_plane(): from_near = lax.ppermute(other, 'dp', near)  4.82 us
    all_to_all x1, starting transfers between devices, shards_by_plane(): lax.all_to_all(back, 'dp', split_axis=0, concat_axis=0, axis_index_groups...  4.19 us
  transfers between devices with their start and end apart: 9, of which 2 were waited for; matrix products, arithmetic and copies ran while one was open for 2% of the time, Pallas kernels for 51%

profile of v16, /device:TPU:0, one launch (start us, length us, event | category | flops | bytes accessed | tf_op | source)
XLA Modules:
  0.0 201.0 jit_solution(15436836496036547366)
XLA Ops:
  0.6 0.0 copy-start.2
  0.6 2.2 %multiply_convert_fusion = bf16[32,16384]{1,0:T(8,128)(2,1)S(1)} fusion(bf16[32,16384]{1,0:T(8,128)(2,1)} %param.7, s32[32,16384]{1,0:T(8,128)} %param.6), kind=kLoop, calls=%fused_computation.1 | loop fusion | flops 2097152 | bytes 4194304 | tf_op jit(solution)/shard_map/convert_element_type | solution.py:482
  2.9 0.0 copy-done.2
  2.9 0.1 pad_maximum_fusion.xw_ref.mine_ref
  3.0 0.0 copy-start
  3.0 3.1 %collective-permute-start = (bf16[64,16384]{1,0:T(8,128)(2,1)S(1)}, bf16[64,16384]{1,0:T(8,128)(2,1)}, u32[]{:S(2)}, u32[]{:S(2)}) collective-permute-start(bf16[64,16384]{1,0:T(8,128)(2,1)S(1)} %pad_maximum_fusion.xw_ref.mine_ref), channel_id=1, source_target_pairs={{0,8},{1,9},{2,10},{3,11},{4,12},{5,13},{6,14},{7,15},{8,0},{9,1},... | collective-permute-start | bytes 6291464 | tf_op jit(solution)/shard_map/ppermute | solution.py:484
  6.1 2.0 %collective-permute-start.1 = (bf16[64,16384]{1,0:T(8,128)(2,1)S(1)}, bf16[64,16384]{1,0:T(8,128)(2,1)}, u32[]{:S(2)}, u32[]{:S(2)}) collective-permute-start(bf16[64,16384]{1,0:T(8,128)(2,1)S(1)} %pad_maximum_fusion.xw_ref.mine_ref), channel_id=1, source_target_pairs={{8,16},{9,17},{10,18},{11,19},{12,20},{13,21},{14,22},{15,23},{16,... | collective-permute-start | bytes 6291464 | tf_op jit(solution)/shard_map/ppermute | solution.py:485
  8.2 0.0 copy-done
  8.2 4.3 %own_pack.1 = bf16[8,2,8,16384]{3,2,1,0:T(8,128)(2,1)} custom-call(s32[32]{0:T(128)} %bitcast.23, bf16[64,16384]{1,0:T(8,128)(2,1)} %copy-done), custom_call_target="tpu_custom_call" | custom-call | flops 2097152 | bytes 6291456 | tf_op jit(solution)/shard_map/own_pack/pallas_call | solution.py:248
  12.5 0.0 copy-start.4
  12.5 0.0 copy-start.3
  12.5 4.7 %all-to-all-start = ((bf16[8,2,8,16384]{3,2,1,0:T(8,128)(2,1)}), bf16[8,2,8,16384]{3,2,1,0:T(8,128)(2,1)}, u32[]{:S(2)}, u32[]{:S(2)}) async-start(bf16[8,2,8,16384]{3,2,1,0:T(8,128)(2,1)} %own_pack.1), calls=%async_computation | async-start | bytes 8388608 | tf_op jit(solution)/shard_map/all_to_all | solution.py:478
  17.2 0.0 copy-done.4
  17.3 2.6 %collective-permute-start.2 = (s32[32]{0:T(128)S(1)}, s32[32]{0:T(128)S(1)}, u32[]{:S(2)}, u32[]{:S(2)}) collective-permute-start(s32[32]{0:T(128)S(1)} %bitcast.25), channel_id=1, source_target_pairs={{0,16},{1,17},{2,18},{3,19},{4,20},{5,21},{6,22},{7,23},{8,24},{9,... | collective-permute-start | bytes 392 | tf_op jit(solution)/shard_map/ppermute | solution.py:486
  19.8 36.1 %collective-permute-done.2.pick_ref = s32[32]{0:T(128)S(1)} collective-permute-done((s32[32]{0:T(128)S(1)}, s32[32]{0:T(128)S(1)}, u32[]{:S(2)}, u32[]{:S(2)}) %collective-permute-start.2) | collective-permute-done | bytes 160 | tf_op jit(solution)/shard_map/ppermute | solution.py:486
  56.0 0.0 copy-start.5
  56.0 0.0 collective-permute-done.near_ref
  56.0 0.0 collective-permute-done.1
  56.0 0.8 collective-permute-start.4
  56.8 1.3 collective-permute-start.3
  58.1 0.0 copy-done.3
  58.1 0.1 fusion
  58.2 0.7 broadcast_in_dim.6.ops_ref
  58.9 37.3 %place.2.refs_0_ = bf16[16384,256]{1,0:T(8,128)(2,1)} custom-call(s32[2,1,16384]{2,1,0:T(1,128)} %broadcast_in_dim.6.ops_ref, bf16[64,16384]{1,0:T(8,128)(2,1)} %copy-done, bf16[64,16384]{1,0:T(8,128)(2,1)} %collective-permute-done.near_ref, s32[32]{0:T(128)} %bitcast.24), custom_call_target="tpu_custom_call" | custom-call | bytes 268435456 | tf_op jit(solution)/shard_map/place/pallas_call | solution.py:320
  96.2 0.0 copy-done.5
  96.2 0.0 all-to-all-done
  96.2 11.5 %plane_sums.3.after_ref.refs_2_ = f32[64,128]{1,0:T(8,128)} custom-call(bf16[128,16384]{1,0:T(8,128)(2,1)} %bitcast.1.got_ref, bf16[16384,256]{1,0:T(8,128)(2,1)} %place.2.refs_0_), custom_call_target="tpu_custom_call" | custom-call | flops 2415919104 | bytes 12582912 | tf_op jit(solution)/shard_map/plane_sums/pallas_call | solution.py:449
  107.7 0.0 collective-permute-done.4.inner_ref
  107.7 0.0 copy-start.1
  107.7 0.0 collective-permute-done.3.outer_ref
  107.7 1.4 copy-done.1
  109.1 5.0 %far_pack.1.after_ref = bf16[8,2,8,16384]{3,2,1,0:T(8,128)(2,1)} custom-call(s32[32]{0:T(128)} %copy-done.5, bf16[64,16384]{1,0:T(8,128)(2,1)} %collective-permute-done.3.outer_ref, bf16[64,16384]{1,0:T(8,128)(2,1)} %copy-done.1, f32[64,128]{1,0:T(8,128)} %plane_sums.3.after_ref.refs_2_), custom_call_target="tpu_custom_call" | custom-call | flops 2097152 | bytes 6291456 | tf_op jit(solution)/shard_map/far_pack/pallas_call | solution.py:248
  114.1 4.6 %all-to-all-start.1 = ((bf16[8,2,8,16384]{3,2,1,0:T(8,128)(2,1)}), bf16[8,2,8,16384]{3,2,1,0:T(8,128)(2,1)}, u32[]{:S(2)}, u32[]{:S(2)}) async-start(bf16[8,2,8,16384]{3,2,1,0:T(8,128)(2,1)} %far_pack.1.after_ref), calls=%async_computation.1 | async-start | bytes 8388608 | tf_op jit(solution)/shard_map/all_to_all | solution.py:478
  118.7 0.7 broadcast_in_dim.7.ops_ref
  119.5 37.2 %place.3.refs_0_.refs_1_ = bf16[16384,256]{1,0:T(8,128)(2,1)} custom-call(s32[2,1,16384]{2,1,0:T(1,128)} %broadcast_in_dim.7.ops_ref, bf16[64,16384]{1,0:T(8,128)(2,1)} %copy-done, bf16[64,16384]{1,0:T(8,128)(2,1)} %collective-permute-done.near_ref, bf16[8,2,8,16384]{3,2,1,0:T(8,128)(2,1)} %far_pack.1.after_ref), custom_call_target="tpu_custom_call" | custom-call | bytes 268435456 | tf_op jit(solution)/shard_map/place/pallas_call | solution.py:320
  156.7 11.5 %plane_sums.4.refs_3_ = f32[64,128]{1,0:T(8,128)} custom-call(bf16[128,16384]{1,0:T(8,128)(2,1)} %bitcast.1.got_ref, bf16[16384,256]{1,0:T(8,128)(2,1)} %place.3.refs_0_.refs_1_), custom_call_target="tpu_custom_call" | custom-call | flops 2415919104 | bytes 12582912 | tf_op jit(solution)/shard_map/plane_sums/pallas_call | solution.py:449
  168.2 0.0 all-to-all-done.1
  168.2 16.1 %plane_sums.5 = (f32[64,128]{1,0:T(8,128)}, f32[64,128]{1,0:T(8,128)}, f32[2,8,8,128]{3,2,1,0:T(8,128)}) custom-call(bf16[128,16384]{1,0:T(8,128)(2,1)} %bitcast.2.got_ref, bf16[16384,256]{1,0:T(8,128)(2,1)} %place.2.refs_0_, bf16[16384,256]{1,0:T(8,128)(2,1)} %place.3.refs_0_.refs_1_, f32[64,128]{1,0:T(8,128)} %plane_sums.3.after_ref.refs_2_, ...), custom_call_target="tpu_custom_call" | custom-call | flops 4831838208 | bytes 20971520 | tf_op jit(solution)/shard_map/plane_sums/pallas_call | solution.py:449
  184.2 4.8 %collective-permute-start.5 = (f32[64,128]{1,0:T(8,128)}, f32[64,128]{1,0:T(8,128)S(1)}, u32[]{:S(2)}, u32[]{:S(2)}) collective-permute-start(f32[64,128]{1,0:T(8,128)} %get-tuple-element.12), channel_id=1, source_target_pairs={{0,8},{1,9},{2,10},{3,11},{4,12},{5,13},{6,14},{7,15},{8,0},{9,1},... | collective-permute-start | bytes 98312 | tf_op jit(solution)/shard_map/ppermute | solution.py:499
  189.1 4.2 %all-to-all-start.2 = ((f32[16,8,128]{2,1,0:T(8,128)}), f32[16,8,128]{2,1,0:T(8,128)S(1)}, u32[]{:S(2)}, u32[]{:S(2)}) async-start(f32[16,8,128]{2,1,0:T(8,128)} %bitcast.19), calls=%async_computation.2 | async-start | bytes 131072 | tf_op jit(solution)/shard_map/all_to_all | solution.py:507
  193.3 0.0 collective-permute-done.5
  193.3 0.8 pad_maximum_fusion.1
  194.1 0.7 copy.16
  194.8 5.2 %all-to-all-done.2 = f32[16,8,128]{2,1,0:T(8,128)S(1)} async-done(((f32[16,8,128]{2,1,0:T(8,128)}), f32[16,8,128]{2,1,0:T(8,128)S(1)}, u32[]{:S(2)}, u32[]{:S(2)}) %all-to-all-start.2) | async-done | bytes 65568 | tf_op jit(solution)/shard_map/all_to_all | solution.py:507
  200.0 0.2 reshape.30
  200.2 0.1 copy.17
  200.2 0.8 reverse_select_fusion
  (2 shorter events, 0.0 us)
Async XLA Ops:
  0.6 2.2 %copy-start.2 = (bf16[32,16384]{1,0:T(8,128)(2,1)S(1)}, bf16[32,16384]{1,0:T(8,128)(2,1)}, u32[]{:S(2)}) copy-start(bf16[32,16384]{1,0:T(8,128)(2,1)} %param.5) | copy-start | bytes 3145732
  3.0 5.1 %copy-start = (bf16[64,16384]{1,0:T(8,128)(2,1)}, bf16[64,16384]{1,0:T(8,128)(2,1)S(1)}, u32[]{:S(2)}) copy-start(bf16[64,16384]{1,0:T(8,128)(2,1)S(1)} %pad_maximum_fusion.xw_ref.mine_ref) | copy-start | bytes 6291460
  3.0 52.9 %collective-permute-start = (bf16[64,16384]{1,0:T(8,128)(2,1)S(1)}, bf16[64,16384]{1,0:T(8,128)(2,1)}, u32[]{:S(2)}, u32[]{:S(2)}) collective-permute-start(bf16[64,16384]{1,0:T(8,128)(2,1)S(1)} %pad_maximum_fusion.xw_ref.mine_ref), channel_id=1, source_target_pairs={{0,8},{1,9},{2,10},{3,11},{4,12},{5,13},{6,14},{7,15},{8,0},{9,1},... | collective-permute-start | bytes 6291464 | tf_op jit(solution)/shard_map/ppermute | solution.py:484
  6.1 49.8 %collective-permute-start.1 = (bf16[64,16384]{1,0:T(8,128)(2,1)S(1)}, bf16[64,16384]{1,0:T(8,128)(2,1)}, u32[]{:S(2)}, u32[]{:S(2)}) collective-permute-start(bf16[64,16384]{1,0:T(8,128)(2,1)S(1)} %pad_maximum_fusion.xw_ref.mine_ref), channel_id=1, source_target_pairs={{8,16},{9,17},{10,18},{11,19},{12,20},{13,21},{14,22},{15,23},{16,... | collective-permute-start | bytes 6291464 | tf_op jit(solution)/shard_map/ppermute | solution.py:485
  12.5 4.7 %copy-start.4 = (s32[32,1]{0,1:T(1,128)S(1)}, s32[32,1]{0,1:T(1,128)}, u32[]{:S(2)}) copy-start(s32[32,1]{0,1:T(1,128)} %param.9) | copy-start | bytes 388
  12.5 45.6 %copy-start.3 = (s32[4,16384]{1,0:T(4,128)S(1)}, s32[4,16384]{1,0:T(4,128)}, u32[]{:S(2)}) copy-start(s32[4,16384]{1,0:T(4,128)} %param.8) | copy-start | bytes 786436
  12.5 83.7 %all-to-all-start = ((bf16[8,2,8,16384]{3,2,1,0:T(8,128)(2,1)}), bf16[8,2,8,16384]{3,2,1,0:T(8,128)(2,1)}, u32[]{:S(2)}, u32[]{:S(2)}) async-start(bf16[8,2,8,16384]{3,2,1,0:T(8,128)(2,1)} %own_pack.1), calls=%async_computation | async-start | bytes 8388608 | tf_op jit(solution)/shard_map/all_to_all | solution.py:478
  17.3 38.7 %collective-permute-start.2 = (s32[32]{0:T(128)S(1)}, s32[32]{0:T(128)S(1)}, u32[]{:S(2)}, u32[]{:S(2)}) collective-permute-start(s32[32]{0:T(128)S(1)} %bitcast.25), channel_id=1, source_target_pairs={{0,16},{1,17},{2,18},{3,19},{4,20},{5,21},{6,22},{7,23},{8,24},{9,... | collective-permute-start | bytes 392 | tf_op jit(solution)/shard_map/ppermute | solution.py:486
  56.0 40.3 %copy-start.5 = (s32[32]{0:T(128)}, s32[32]{0:T(128)S(1)}, u32[]{:S(2)}) copy-start(s32[32]{0:T(128)S(1)} %collective-permute-done.2.pick_ref) | copy-start | bytes 388
  56.0 51.8 %collective-permute-start.4 = (bf16[64,16384]{1,0:T(8,128)(2,1)}, bf16[64,16384]{1,0:T(8,128)(2,1)S(1)}, u32[]{:S(2)}, u32[]{:S(2)}) collective-permute-start(bf16[64,16384]{1,0:T(8,128)(2,1)} %collective-permute-done.near_ref), channel_id=1, source_target_pairs={{8,16},{9,17},{10,18},{11,19},{12,20},{13,21},{14,22},{15,23},{16,... | collective-permute-start | bytes 6291464 | tf_op jit(solution)/shard_map/ppermute | solution.py:490
  56.8 51.0 %collective-permute-start.3 = (bf16[64,16384]{1,0:T(8,128)(2,1)}, bf16[64,16384]{1,0:T(8,128)(2,1)}, u32[]{:S(2)}, u32[]{:S(2)}) collective-permute-start(bf16[64,16384]{1,0:T(8,128)(2,1)} %collective-permute-done.1), channel_id=1, source_target_pairs={{8,0},{9,1},{10,2},{11,3},{12,4},{13,5},{14,6},{15,7},{16,24},{17,... | collective-permute-start | bytes 6291464 | tf_op jit(solution)/shard_map/ppermute | solution.py:489
  107.7 1.4 copy-start.1
  114.1 54.1 %all-to-all-start.1 = ((bf16[8,2,8,16384]{3,2,1,0:T(8,128)(2,1)}), bf16[8,2,8,16384]{3,2,1,0:T(8,128)(2,1)}, u32[]{:S(2)}, u32[]{:S(2)}) async-start(bf16[8,2,8,16384]{3,2,1,0:T(8,128)(2,1)} %far_pack.1.after_ref), calls=%async_computation.1 | async-start | bytes 8388608 | tf_op jit(solution)/shard_map/all_to_all | solution.py:478
  184.2 9.0 %collective-permute-start.5 = (f32[64,128]{1,0:T(8,128)}, f32[64,128]{1,0:T(8,128)S(1)}, u32[]{:S(2)}, u32[]{:S(2)}) collective-permute-start(f32[64,128]{1,0:T(8,128)} %get-tuple-element.12), channel_id=1, source_target_pairs={{0,8},{1,9},{2,10},{3,11},{4,12},{5,13},{6,14},{7,15},{8,0},{9,1},... | collective-permute-start | bytes 98312 | tf_op jit(solution)/shard_map/ppermute | solution.py:499
  189.1 10.9 %all-to-all-start.2 = ((f32[16,8,128]{2,1,0:T(8,128)}), f32[16,8,128]{2,1,0:T(8,128)S(1)}, u32[]{:S(2)}, u32[]{:S(2)}) async-start(f32[16,8,128]{2,1,0:T(8,128)} %bitcast.19), calls=%async_computation.2 | async-start | bytes 131072 | tf_op jit(solution)/shard_map/all_to_all | solution.py:507

commit v17 on v16

--- a/solution.py
+++ b/solution.py
@@ -15,6 +15,7 @@
 PLANES = 4
 PLANE = 8
 UNROLL = 64
+PARTS = 4
 
 
 def params():
@@ -190,13 +191,13 @@
     return numer / jnp.sqrt(var_x * var_y)
 
 
-def fill_slabs(slabs, xw_ref):
-    blk, width = xw_ref.shape[0] // 2, xw_ref.shape[1]
+def fill_slabs(slabs, xw_ref, offset, width):
+    blk = xw_ref.shape[0] // 2
     step = min(512, width)
 
     @pl.loop(0, width // step)
     def _(i):
-        cols = pl.ds(pl.multiple_of(i * step, step), step)
+        cols = pl.ds(pl.multiple_of(offset + i * step, step), step)
         wide = xw_ref[:, cols].astype(jnp.float32)
         for g in range(blk // SUB):
             rows = slice(g * SUB, (g + 1) * SUB)
@@ -204,44 +205,52 @@
             slabs[g, :, cols] = slab.astype(jnp.bfloat16)
 
 
-def send_slabs(slabs, pick_ref, send_ref, sems):
+def send_slabs(xw_ref, pick_ref, send_ref, slabs, sems, ready):
     mine = lax.div(lax.axis_index("dp"), PLANE)
     partner = mine + 1 - 2 * lax.rem(mine, 2)
+    span = xw_ref.shape[1] // PARTS
     copies = []
-    for c in range(PLANE):
-        for t, plane in enumerate((mine, partner)):
-            group = pick_ref[plane * PLANE + c]
-            copies.append(pltpu.make_async_copy(slabs.at[group], send_ref.at[c, t], sems.at[c, t]))
-    for copy in copies:
-        copy.start()
+    for part in range(PARTS):
+        ready(part)
+        fill_slabs(slabs, xw_ref, part * span, span)
+        cols = pl.ds(part * span, span)
+        for c in range(PLANE):
+            for t, plane in enumerate((mine, partner)):
+                group = pick_ref[plane * PLANE + c]
+                copy = pltpu.make_async_copy(
+                    slabs.at[group, :, cols], send_ref.at[c, t, :, cols], sems.at[c, t, part]
+                )
+                copy.start()
+                copies.append(copy)
     for copy in copies:
         copy.wait()
 
 
 def own_pack_kernel(pick_ref, xw_ref, send_ref, slabs, sems):
-    fill_slabs(slabs, xw_ref)
-    send_slabs(slabs, pick_ref, send_ref, sems)
-
-
-def far_pack_kernel(pick_ref, outer_ref, inner_ref, after_ref, send_ref, buf, in_sem, slabs, sems):
+    send_slabs(xw_ref, pick_ref, send_ref, slabs, sems, lambda part: None)
+
+
+def far_pack_kernel(pick_ref, outer_ref, inner_ref, after_ref, send_ref, buf, in_sems, slabs, sems):
     plane = lax.div(lax.axis_index("dp"), PLANE)
     is_inner = (plane == 1) | (plane == 2)
-
-    def fetch(ref):
-        copy = pltpu.make_async_copy(ref, buf, in_sem)
-        copy.start()
-        copy.wait()
+    span = buf.shape[1] // PARTS
+
+    def forward(ref):
+        fetches = []
+        for part in range(PARTS):
+            cols = pl.ds(part * span, span)
+            fetches.append(pltpu.make_async_copy(ref.at[:, cols], buf.at[:, cols], in_sems.at[part]))
+        for fetch in fetches:
+            fetch.start()
+        send_slabs(buf, pick_ref, send_ref, slabs, sems, lambda part: fetches[part].wait())
 
     @pl.when(is_inner)
     def _():
-        fetch(inner_ref)
+        forward(inner_ref)
 
     @pl.when(jnp.logical_not(is_inner))
     def _():
-        fetch(outer_ref)
-
-    fill_slabs(slabs, buf)
-    send_slabs(slabs, pick_ref, send_ref, sems)
+        forward(outer_ref)
 
 
 def pack_call(kernel, name, specs, scratch, blk, width, *operands):
@@ -251,7 +260,7 @@
         in_specs=[pl.BlockSpec(memory_space=pltpu.SMEM)] + specs,
         out_specs=pl.BlockSpec(memory_space=pl.ANY),
         scratch_shapes=scratch
-        + [pltpu.VMEM((blk // SUB, SLAB, width), jnp.bfloat16), pltpu.SemaphoreType.DMA((PLANE, 2))],
+        + [pltpu.VMEM((blk // SUB, SLAB, width), jnp.bfloat16), pltpu.SemaphoreType.DMA((PLANE, 2, PARTS))],
         compiler_params=params(),
         cost_estimate=pl.CostEstimate(
             flops=blk * width * 4, bytes_accessed=(PLANE * 2 * SLAB * 2 + blk * 4) * width, transcendentals=0
@@ -268,7 +277,7 @@
 
 def far_pack(pick, outer, inner, after):
     rows, width = outer.shape
-    scratch = [pltpu.VMEM((rows, width), jnp.bfloat16), pltpu.SemaphoreType.DMA]
+    scratch = [pltpu.VMEM((rows, width), jnp.bfloat16), pltpu.SemaphoreType.DMA((PARTS,))]
     specs = [pl.BlockSpec(memory_space=pl.ANY)] * 3
     return pack_call(far_pack_kernel, "far_pack", specs, scratch, rows // 2, width, pick, outer, inner, after)
 
@@ -439,7 +448,7 @@
 
 def plane_sums(got, moved, own):
     rows, width = got.shape
-    depth = min(2048, width)
+    depth = min(4096, width)
     lanes = 3 * len(moved) * LANES
     ended = len(own) > 0
     placed = pl.BlockSpec((depth, 2 * LANES), lambda i: (i, 0))

time: 202 us -> 199 us (0.985)
  Pallas kernels: 123 us -> 120 us
  transfers between devices with their start and end apart: 9 -> 9, of which waited for: 2 -> 3; matrix products, arithmetic and copies ran while one was open for 2% -> 2% of each run, Pallas kernels for 51% -> 50%
where the time goes in v17:
time: 199 us
  Pallas kernels  120 us (60%)
  waiting for transfers between devices  42.3 us (21%)
  starting transfers between devices  27.3 us (14%)
  local copies, waits for them, and re-layouts  3.96 us (2%)
  other arithmetic  3.94 us (2%)
    pallas_call x2, Pallas kernels, place(): pl.pallas_call(place_kernel, grid=(count, width // depth), out_shape=jax....  74.5 us
    pallas_call x3, Pallas kernels, plane_sums(): pl.pallas_call(functools.partial(plane_sums_kernel, len(moved)), grid=(wi...  37.1 us
    ppermute x1, waiting for transfers between devices, shards_by_plane(): far_pick = lax.ppermute(own_pick, 'dp', far)  36.2 us
    all_to_all x2, starting transfers between devices, spread(): lax.all_to_all(send, 'dp', split_axis=0, concat_axis=0, axis_index_groups...  9.26 us
    pallas_call x2, Pallas kernels, pack_call(): pl.pallas_call(kernel, out_shape=jax.ShapeDtypeStruct((PLANE, 2, SLAB, wi...  8.7 us
    all_to_all x1, waiting for transfers between devices, shards_by_plane(): lax.all_to_all(back, 'dp', split_axis=0, concat_axis=0, axis_index_groups...  5.12 us
    ppermute x1, starting transfers between devices, shards_by_plane(): from_near = lax.ppermute(other, 'dp', near)  4.79 us
  transfers between devices with their start and end apart: 9, of which 3 were waited for; matrix products, arithmetic and copies ran while one was open for 2% of the time, Pallas kernels for 50%

profile of v17, /device:TPU:0, one launch (start us, length us, event | category | flops | bytes accessed | tf_op | source)
XLA Modules:
  0.0 198.6 jit_solution(7786959444413608216)
XLA Ops:
  0.6 0.0 copy-start.2
  0.6 2.2 %multiply_convert_fusion = bf16[32,16384]{1,0:T(8,128)(2,1)S(1)} fusion(bf16[32,16384]{1,0:T(8,128)(2,1)} %param.7, s32[32,16384]{1,0:T(8,128)} %param.6), kind=kLoop, calls=%fused_computation.1 | loop fusion | flops 2097152 | bytes 4194304 | tf_op jit(solution)/shard_map/convert_element_type | solution.py:491
  2.9 0.0 copy-done.2
  2.9 0.1 pad_maximum_fusion.xw_ref.mine_ref
  3.0 0.0 copy-start
  3.0 3.1 %collective-permute-start = (bf16[64,16384]{1,0:T(8,128)(2,1)S(1)}, bf16[64,16384]{1,0:T(8,128)(2,1)}, u32[]{:S(2)}, u32[]{:S(2)}) collective-permute-start(bf16[64,16384]{1,0:T(8,128)(2,1)S(1)} %pad_maximum_fusion.xw_ref.mine_ref), channel_id=1, source_target_pairs={{0,8},{1,9},{2,10},{3,11},{4,12},{5,13},{6,14},{7,15},{8,0},{9,1},... | collective-permute-start | bytes 6291464 | tf_op jit(solution)/shard_map/ppermute | solution.py:493
  6.1 2.0 %collective-permute-start.1 = (bf16[64,16384]{1,0:T(8,128)(2,1)S(1)}, bf16[64,16384]{1,0:T(8,128)(2,1)}, u32[]{:S(2)}, u32[]{:S(2)}) collective-permute-start(bf16[64,16384]{1,0:T(8,128)(2,1)S(1)} %pad_maximum_fusion.xw_ref.mine_ref), channel_id=1, source_target_pairs={{8,16},{9,17},{10,18},{11,19},{12,20},{13,21},{14,22},{15,23},{16,... | collective-permute-start | bytes 6291464 | tf_op jit(solution)/shard_map/ppermute | solution.py:494
  8.2 0.0 copy-done
  8.2 4.3 %own_pack.1 = bf16[8,2,8,16384]{3,2,1,0:T(8,128)(2,1)} custom-call(s32[32]{0:T(128)} %bitcast.23, bf16[64,16384]{1,0:T(8,128)(2,1)} %copy-done), custom_call_target="tpu_custom_call" | custom-call | flops 2097152 | bytes 6291456 | tf_op jit(solution)/shard_map/own_pack/pallas_call | solution.py:257
  12.4 0.0 copy-start.4
  12.5 0.0 copy-start.3
  12.5 4.7 %all-to-all-start = ((bf16[8,2,8,16384]{3,2,1,0:T(8,128)(2,1)}), bf16[8,2,8,16384]{3,2,1,0:T(8,128)(2,1)}, u32[]{:S(2)}, u32[]{:S(2)}) async-start(bf16[8,2,8,16384]{3,2,1,0:T(8,128)(2,1)} %own_pack.1), calls=%async_computation | async-start | bytes 8388608 | tf_op jit(solution)/shard_map/all_to_all | solution.py:487
  17.2 0.0 copy-done.4
  17.2 2.6 %collective-permute-start.2 = (s32[32]{0:T(128)S(1)}, s32[32]{0:T(128)S(1)}, u32[]{:S(2)}, u32[]{:S(2)}) collective-permute-start(s32[32]{0:T(128)S(1)} %bitcast.25), channel_id=1, source_target_pairs={{0,16},{1,17},{2,18},{3,19},{4,20},{5,21},{6,22},{7,23},{8,24},{9,... | collective-permute-start | bytes 392 | tf_op jit(solution)/shard_map/ppermute | solution.py:495
  19.8 36.2 %collective-permute-done.2.pick_ref = s32[32]{0:T(128)S(1)} collective-permute-done((s32[32]{0:T(128)S(1)}, s32[32]{0:T(128)S(1)}, u32[]{:S(2)}, u32[]{:S(2)}) %collective-permute-start.2) | collective-permute-done | bytes 160 | tf_op jit(solution)/shard_map/ppermute | solution.py:495
  56.0 0.0 copy-start.5
  56.0 0.0 collective-permute-done.near_ref
  56.0 0.0 collective-permute-done.1
  56.0 0.8 collective-permute-start.4
  56.8 1.3 collective-permute-start.3
  58.1 0.0 copy-done.3
  58.1 0.1 fusion
  58.2 0.7 broadcast_in_dim.6.ops_ref
  58.9 37.3 %place.2.refs_0_ = bf16[16384,256]{1,0:T(8,128)(2,1)} custom-call(s32[2,1,16384]{2,1,0:T(1,128)} %broadcast_in_dim.6.ops_ref, bf16[64,16384]{1,0:T(8,128)(2,1)} %copy-done, bf16[64,16384]{1,0:T(8,128)(2,1)} %collective-permute-done.near_ref, s32[32]{0:T(128)} %bitcast.24), custom_call_target="tpu_custom_call" | custom-call | bytes 268435456 | tf_op jit(solution)/shard_map/place/pallas_call | solution.py:329
  96.2 0.0 copy-done.5
  96.2 0.0 all-to-all-done
  96.2 10.2 %plane_sums.3.after_ref.refs_2_ = f32[64,128]{1,0:T(8,128)} custom-call(bf16[128,16384]{1,0:T(8,128)(2,1)} %bitcast.1.got_ref, bf16[16384,256]{1,0:T(8,128)(2,1)} %place.2.refs_0_), custom_call_target="tpu_custom_call" | custom-call | flops 2415919104 | bytes 12582912 | tf_op jit(solution)/shard_map/plane_sums/pallas_call | solution.py:458
  106.4 0.0 collective-permute-done.4.inner_ref
  106.4 0.0 copy-start.1
  106.4 0.0 collective-permute-done.3.outer_ref
  106.4 1.4 copy-done.1
  107.8 4.4 %far_pack.1.after_ref = bf16[8,2,8,16384]{3,2,1,0:T(8,128)(2,1)} custom-call(s32[32]{0:T(128)} %copy-done.5, bf16[64,16384]{1,0:T(8,128)(2,1)} %collective-permute-done.3.outer_ref, bf16[64,16384]{1,0:T(8,128)(2,1)} %copy-done.1, f32[64,128]{1,0:T(8,128)} %plane_sums.3.after_ref.refs_2_), custom_call_target="tpu_custom_call" | custom-call | flops 2097152 | bytes 6291456 | tf_op jit(solution)/shard_map/far_pack/pallas_call | solution.py:257
  112.2 4.6 %all-to-all-start.1 = ((bf16[8,2,8,16384]{3,2,1,0:T(8,128)(2,1)}), bf16[8,2,8,16384]{3,2,1,0:T(8,128)(2,1)}, u32[]{:S(2)}, u32[]{:S(2)}) async-start(bf16[8,2,8,16384]{3,2,1,0:T(8,128)(2,1)} %far_pack.1.after_ref), calls=%async_computation.1 | async-start | bytes 8388608 | tf_op jit(solution)/shard_map/all_to_all | solution.py:487
  116.8 0.7 broadcast_in_dim.7.ops_ref
  117.5 37.2 %place.3.refs_0_.refs_1_ = bf16[16384,256]{1,0:T(8,128)(2,1)} custom-call(s32[2,1,16384]{2,1,0:T(1,128)} %broadcast_in_dim.7.ops_ref, bf16[64,16384]{1,0:T(8,128)(2,1)} %copy-done, bf16[64,16384]{1,0:T(8,128)(2,1)} %collective-permute-done.near_ref, bf16[8,2,8,16384]{3,2,1,0:T(8,128)(2,1)} %far_pack.1.after_ref), custom_call_target="tpu_custom_call" | custom-call | bytes 268435456 | tf_op jit(solution)/shard_map/place/pallas_call | solution.py:329
  154.8 10.2 %plane_sums.4.refs_3_ = f32[64,128]{1,0:T(8,128)} custom-call(bf16[128,16384]{1,0:T(8,128)(2,1)} %bitcast.1.got_ref, bf16[16384,256]{1,0:T(8,128)(2,1)} %place.3.refs_0_.refs_1_), custom_call_target="tpu_custom_call" | custom-call | flops 2415919104 | bytes 12582912 | tf_op jit(solution)/shard_map/plane_sums/pallas_call | solution.py:458
  164.9 1.0 all-to-all-done.1
  165.9 16.7 %plane_sums.5 = (f32[64,128]{1,0:T(8,128)}, f32[64,128]{1,0:T(8,128)}, f32[2,8,8,128]{3,2,1,0:T(8,128)}) custom-call(bf16[128,16384]{1,0:T(8,128)(2,1)} %bitcast.2.got_ref, bf16[16384,256]{1,0:T(8,128)(2,1)} %place.2.refs_0_, bf16[16384,256]{1,0:T(8,128)(2,1)} %place.3.refs_0_.refs_1_, f32[64,128]{1,0:T(8,128)} %plane_sums.3.after_ref.refs_2_, ...), custom_call_target="tpu_custom_call" | custom-call | flops 4831838208 | bytes 20971520 | tf_op jit(solution)/shard_map/plane_sums/pallas_call | solution.py:458
  182.6 4.8 %collective-permute-start.5 = (f32[64,128]{1,0:T(8,128)}, f32[64,128]{1,0:T(8,128)S(1)}, u32[]{:S(2)}, u32[]{:S(2)}) collective-permute-start(f32[64,128]{1,0:T(8,128)} %get-tuple-element.12), channel_id=1, source_target_pairs={{0,8},{1,9},{2,10},{3,11},{4,12},{5,13},{6,14},{7,15},{8,0},{9,1},... | collective-permute-start | bytes 98312 | tf_op jit(solution)/shard_map/ppermute | solution.py:508
  187.4 3.5 %all-to-all-start.2 = ((f32[16,8,128]{2,1,0:T(8,128)}), f32[16,8,128]{2,1,0:T(8,128)S(1)}, u32[]{:S(2)}, u32[]{:S(2)}) async-start(f32[16,8,128]{2,1,0:T(8,128)} %bitcast.19), calls=%async_computation.2 | async-start | bytes 131072 | tf_op jit(solution)/shard_map/all_to_all | solution.py:516
  190.9 0.0 collective-permute-done.5
  190.9 0.8 pad_maximum_fusion.1
  191.8 0.7 copy.16
  192.5 5.1 %all-to-all-done.2 = f32[16,8,128]{2,1,0:T(8,128)S(1)} async-done(((f32[16,8,128]{2,1,0:T(8,128)}), f32[16,8,128]{2,1,0:T(8,128)S(1)}, u32[]{:S(2)}, u32[]{:S(2)}) %all-to-all-start.2) | async-done | bytes 65568 | tf_op jit(solution)/shard_map/all_to_all | solution.py:516
  197.6 0.2 reshape.30
  197.8 0.1 copy.17
  197.8 0.8 reverse_select_fusion
  (2 shorter events, 0.0 us)
Async XLA Ops:
  0.6 2.2 %copy-start.2 = (bf16[32,16384]{1,0:T(8,128)(2,1)S(1)}, bf16[32,16384]{1,0:T(8,128)(2,1)}, u32[]{:S(2)}) copy-start(bf16[32,16384]{1,0:T(8,128)(2,1)} %param.5) | copy-start | bytes 3145732
  3.0 5.1 %copy-start = (bf16[64,16384]{1,0:T(8,128)(2,1)}, bf16[64,16384]{1,0:T(8,128)(2,1)S(1)}, u32[]{:S(2)}) copy-start(bf16[64,16384]{1,0:T(8,128)(2,1)S(1)} %pad_maximum_fusion.xw_ref.mine_ref) | copy-start | bytes 6291460
  3.0 52.9 %collective-permute-start = (bf16[64,16384]{1,0:T(8,128)(2,1)S(1)}, bf16[64,16384]{1,0:T(8,128)(2,1)}, u32[]{:S(2)}, u32[]{:S(2)}) collective-permute-start(bf16[64,16384]{1,0:T(8,128)(2,1)S(1)} %pad_maximum_fusion.xw_ref.mine_ref), channel_id=1, source_target_pairs={{0,8},{1,9},{2,10},{3,11},{4,12},{5,13},{6,14},{7,15},{8,0},{9,1},... | collective-permute-start | bytes 6291464 | tf_op jit(solution)/shard_map/ppermute | solution.py:493
  6.1 49.8 %collective-permute-start.1 = (bf16[64,16384]{1,0:T(8,128)(2,1)S(1)}, bf16[64,16384]{1,0:T(8,128)(2,1)}, u32[]{:S(2)}, u32[]{:S(2)}) collective-permute-start(bf16[64,16384]{1,0:T(8,128)(2,1)S(1)} %pad_maximum_fusion.xw_ref.mine_ref), channel_id=1, source_target_pairs={{8,16},{9,17},{10,18},{11,19},{12,20},{13,21},{14,22},{15,23},{16,... | collective-permute-start | bytes 6291464 | tf_op jit(solution)/shard_map/ppermute | solution.py:494
  12.4 4.7 %copy-start.4 = (s32[32,1]{0,1:T(1,128)S(1)}, s32[32,1]{0,1:T(1,128)}, u32[]{:S(2)}) copy-start(s32[32,1]{0,1:T(1,128)} %param.9) | copy-start | bytes 388
  12.5 45.6 %copy-start.3 = (s32[4,16384]{1,0:T(4,128)S(1)}, s32[4,16384]{1,0:T(4,128)}, u32[]{:S(2)}) copy-start(s32[4,16384]{1,0:T(4,128)} %param.8) | copy-start | bytes 786436
  12.5 83.7 %all-to-all-start = ((bf16[8,2,8,16384]{3,2,1,0:T(8,128)(2,1)}), bf16[8,2,8,16384]{3,2,1,0:T(8,128)(2,1)}, u32[]{:S(2)}, u32[]{:S(2)}) async-start(bf16[8,2,8,16384]{3,2,1,0:T(8,128)(2,1)} %own_pack.1), calls=%async_computation | async-start | bytes 8388608 | tf_op jit(solution)/shard_map/all_to_all | solution.py:487
  17.2 38.8 %collective-permute-start.2 = (s32[32]{0:T(128)S(1)}, s32[32]{0:T(128)S(1)}, u32[]{:S(2)}, u32[]{:S(2)}) collective-permute-start(s32[32]{0:T(128)S(1)} %bitcast.25), channel_id=1, source_target_pairs={{0,16},{1,17},{2,18},{3,19},{4,20},{5,21},{6,22},{7,23},{8,24},{9,... | collective-permute-start | bytes 392 | tf_op jit(solution)/shard_map/ppermute | solution.py:495
  56.0 40.3 %copy-start.5 = (s32[32]{0:T(128)}, s32[32]{0:T(128)S(1)}, u32[]{:S(2)}) copy-start(s32[32]{0:T(128)S(1)} %collective-permute-done.2.pick_ref) | copy-start | bytes 388
  56.0 50.4 %collective-permute-start.4 = (bf16[64,16384]{1,0:T(8,128)(2,1)}, bf16[64,16384]{1,0:T(8,128)(2,1)S(1)}, u32[]{:S(2)}, u32[]{:S(2)}) collective-permute-start(bf16[64,16384]{1,0:T(8,128)(2,1)} %collective-permute-done.near_ref), channel_id=1, source_target_pairs={{8,16},{9,17},{10,18},{11,19},{12,20},{13,21},{14,22},{15,23},{16,... | collective-permute-start | bytes 6291464 | tf_op jit(solution)/shard_map/ppermute | solution.py:499
  56.8 49.6 %collective-permute-start.3 = (bf16[64,16384]{1,0:T(8,128)(2,1)}, bf16[64,16384]{1,0:T(8,128)(2,1)}, u32[]{:S(2)}, u32[]{:S(2)}) collective-permute-start(bf16[64,16384]{1,0:T(8,128)(2,1)} %collective-permute-done.1), channel_id=1, source_target_pairs={{8,0},{9,1},{10,2},{11,3},{12,4},{13,5},{14,6},{15,7},{16,24},{17,... | collective-permute-start | bytes 6291464 | tf_op jit(solution)/shard_map/ppermute | solution.py:498
  106.4 1.4 copy-start.1
  112.2 53.7 %all-to-all-start.1 = ((bf16[8,2,8,16384]{3,2,1,0:T(8,128)(2,1)}), bf16[8,2,8,16384]{3,2,1,0:T(8,128)(2,1)}, u32[]{:S(2)}, u32[]{:S(2)}) async-start(bf16[8,2,8,16384]{3,2,1,0:T(8,128)(2,1)} %far_pack.1.after_ref), calls=%async_computation.1 | async-start | bytes 8388608 | tf_op jit(solution)/shard_map/all_to_all | solution.py:487
  182.6 8.3 %collective-permute-start.5 = (f32[64,128]{1,0:T(8,128)}, f32[64,128]{1,0:T(8,128)S(1)}, u32[]{:S(2)}, u32[]{:S(2)}) collective-permute-start(f32[64,128]{1,0:T(8,128)} %get-tuple-element.12), channel_id=1, source_target_pairs={{0,8},{1,9},{2,10},{3,11},{4,12},{5,13},{6,14},{7,15},{8,0},{9,1},... | collective-permute-start | bytes 98312 | tf_op jit(solution)/shard_map/ppermute | solution.py:508
  187.4 10.2 %all-to-all-start.2 = ((f32[16,8,128]{2,1,0:T(8,128)}), f32[16,8,128]{2,1,0:T(8,128)S(1)}, u32[]{:S(2)}, u32[]{:S(2)}) async-start(f32[16,8,128]{2,1,0:T(8,128)} %bitcast.19), calls=%async_computation.2 | async-start | bytes 131072 | tf_op jit(solution)/shard_map/all_to_all | solution.py:516

commit v18 on v17

--- a/solution.py
+++ b/solution.py
@@ -14,7 +14,7 @@
 VMEM_LIMIT = 56 * 1024 * 1024
 PLANES = 4
 PLANE = 8
-UNROLL = 64
+UNROLL = 128
 PARTS = 4
 
 
@@ -400,7 +400,7 @@
 def plane_sums_kernel(pairs, got_ref, *refs):
     moved_refs, refs, acc = refs[:pairs], refs[pairs:-1], refs[-1]
     depth = got_ref.shape[1]
-    step = min(1024, depth)
+    step = min(2048, depth)
     half = LANES // 2
 
     @pl.when(pl.program_id(0) == 0)

time: 199 us -> 198 us (level)
  Pallas kernels: 120 us -> 117 us
  waiting for transfers between devices: 42.3 us -> 44.7 us
    pallas_call x2, Pallas kernels: 74.5 us -> 72 us  [place(): pl.pallas_call(place_kernel, grid=(count, width // depth), out_shape=jax....]
  transfers between devices with their start and end apart: 9 -> 9, of which waited for: 3 -> 4; matrix products, arithmetic and copies ran while one was open for 2% -> 2% of each run, Pallas kernels for 50% -> 49%
where the time goes in v18:
time: 198 us; the launch traced here: 197 us
  Pallas kernels  117 us (59%)
  waiting for transfers between devices  44.7 us (23%)
  starting transfers between devices  27.3 us (14%)
  other arithmetic  3.94 us (2%)
  local copies, waits for them, and re-layouts  3.04 us (2%)
    pallas_call x2, Pallas kernels, place(): pl.pallas_call(place_kernel, grid=(count, width // depth), out_shape=jax....  72 us
    pallas_call x3, Pallas kernels, plane_sums(): pl.pallas_call(functools.partial(plane_sums_kernel, len(moved)), grid=(wi...  36.8 us
    ppermute x1, waiting for transfers between devices, shards_by_plane(): far_pick = lax.ppermute(own_pick, 'dp', far)  36.2 us
    all_to_all x2, starting transfers between devices, spread(): lax.all_to_all(send, 'dp', split_axis=0, concat_axis=0, axis_index_groups...  9.26 us
    pallas_call x2, Pallas kernels, pack_call(): pl.pallas_call(kernel, out_shape=jax.ShapeDtypeStruct((PLANE, 2, SLAB, wi...  8.7 us
    all_to_all x1, waiting for transfers between devices, shards_by_plane(): lax.all_to_all(back, 'dp', split_axis=0, concat_axis=0, axis_index_groups...  5.33 us
    ppermute x1, starting transfers between devices, shards_by_plane(): from_near = lax.ppermute(other, 'dp', near)  4.79 us
  transfers between devices with their start and end apart: 9, of which 4 were waited for; matrix products, arithmetic and copies ran while one was open for 2% of the time, Pallas kernels for 49%

profile of v18, /device:TPU:0, one launch (start us, length us, event | category | flops | bytes accessed | tf_op | source)
XLA Modules:
  0.0 197.3 jit_solution(11023582030008159410)
XLA Ops:
  0.6 0.0 copy-start.2
  0.6 2.2 %multiply_convert_fusion = bf16[32,16384]{1,0:T(8,128)(2,1)S(1)} fusion(bf16[32,16384]{1,0:T(8,128)(2,1)} %param.7, s32[32,16384]{1,0:T(8,128)} %param.6), kind=kLoop, calls=%fused_computation.1 | loop fusion | flops 2097152 | bytes 4194304 | tf_op jit(solution)/shard_map/convert_element_type | solution.py:491
  2.9 0.0 copy-done.2
  2.9 0.1 pad_maximum_fusion.xw_ref.mine_ref
  3.0 0.0 copy-start
  3.0 3.1 %collective-permute-start = (bf16[64,16384]{1,0:T(8,128)(2,1)S(1)}, bf16[64,16384]{1,0:T(8,128)(2,1)}, u32[]{:S(2)}, u32[]{:S(2)}) collective-permute-start(bf16[64,16384]{1,0:T(8,128)(2,1)S(1)} %pad_maximum_fusion.xw_ref.mine_ref), channel_id=1, source_target_pairs={{0,8},{1,9},{2,10},{3,11},{4,12},{5,13},{6,14},{7,15},{8,0},{9,1},... | collective-permute-start | bytes 6291464 | tf_op jit(solution)/shard_map/ppermute | solution.py:493
  6.1 2.0 %collective-permute-start.1 = (bf16[64,16384]{1,0:T(8,128)(2,1)S(1)}, bf16[64,16384]{1,0:T(8,128)(2,1)}, u32[]{:S(2)}, u32[]{:S(2)}) collective-permute-start(bf16[64,16384]{1,0:T(8,128)(2,1)S(1)} %pad_maximum_fusion.xw_ref.mine_ref), channel_id=1, source_target_pairs={{8,16},{9,17},{10,18},{11,19},{12,20},{13,21},{14,22},{15,23},{16,... | collective-permute-start | bytes 6291464 | tf_op jit(solution)/shard_map/ppermute | solution.py:494
  8.2 0.0 copy-done
  8.2 4.3 %own_pack.1 = bf16[8,2,8,16384]{3,2,1,0:T(8,128)(2,1)} custom-call(s32[32]{0:T(128)} %bitcast.23, bf16[64,16384]{1,0:T(8,128)(2,1)} %copy-done), custom_call_target="tpu_custom_call" | custom-call | flops 2097152 | bytes 6291456 | tf_op jit(solution)/shard_map/own_pack/pallas_call | solution.py:257
  12.4 0.0 copy-start.4
  12.5 0.0 copy-start.3
  12.5 4.7 %all-to-all-start = ((bf16[8,2,8,16384]{3,2,1,0:T(8,128)(2,1)}), bf16[8,2,8,16384]{3,2,1,0:T(8,128)(2,1)}, u32[]{:S(2)}, u32[]{:S(2)}) async-start(bf16[8,2,8,16384]{3,2,1,0:T(8,128)(2,1)} %own_pack.1), calls=%async_computation | async-start | bytes 8388608 | tf_op jit(solution)/shard_map/all_to_all | solution.py:487
  17.2 0.0 copy-done.4
  17.2 2.6 %collective-permute-start.2 = (s32[32]{0:T(128)S(1)}, s32[32]{0:T(128)S(1)}, u32[]{:S(2)}, u32[]{:S(2)}) collective-permute-start(s32[32]{0:T(128)S(1)} %bitcast.25), channel_id=1, source_target_pairs={{0,16},{1,17},{2,18},{3,19},{4,20},{5,21},{6,22},{7,23},{8,24},{9,... | collective-permute-start | bytes 392 | tf_op jit(solution)/shard_map/ppermute | solution.py:495
  19.8 36.2 %collective-permute-done.2.pick_ref = s32[32]{0:T(128)S(1)} collective-permute-done((s32[32]{0:T(128)S(1)}, s32[32]{0:T(128)S(1)}, u32[]{:S(2)}, u32[]{:S(2)}) %collective-permute-start.2) | collective-permute-done | bytes 160 | tf_op jit(solution)/shard_map/ppermute | solution.py:495
  56.0 0.0 copy-start.5
  56.0 0.0 collective-permute-done.near_ref
  56.0 0.0 collective-permute-done.1
  56.0 0.8 collective-permute-start.4
  56.8 1.3 collective-permute-start.3
  58.1 0.0 copy-done.3
  58.1 0.1 fusion
  58.2 0.7 broadcast_in_dim.6.ops_ref
  58.9 36.0 %place.2.refs_0_ = bf16[16384,256]{1,0:T(8,128)(2,1)} custom-call(s32[2,1,16384]{2,1,0:T(1,128)} %broadcast_in_dim.6.ops_ref, bf16[64,16384]{1,0:T(8,128)(2,1)} %copy-done, bf16[64,16384]{1,0:T(8,128)(2,1)} %collective-permute-done.near_ref, s32[32]{0:T(128)} %bitcast.24), custom_call_target="tpu_custom_call" | custom-call | bytes 268435456 | tf_op jit(solution)/shard_map/place/pallas_call | solution.py:329
  94.9 0.0 copy-done.5
  95.0 0.0 all-to-all-done
  95.0 10.1 %plane_sums.3.after_ref.refs_2_ = f32[64,128]{1,0:T(8,128)} custom-call(bf16[128,16384]{1,0:T(8,128)(2,1)} %bitcast.1.got_ref, bf16[16384,256]{1,0:T(8,128)(2,1)} %place.2.refs_0_), custom_call_target="tpu_custom_call" | custom-call | flops 2415919104 | bytes 12582912 | tf_op jit(solution)/shard_map/plane_sums/pallas_call | solution.py:458
  105.1 0.0 collective-permute-done.4.inner_ref
  105.1 0.0 copy-start.1
  105.1 0.9 collective-permute-done.3.outer_ref
  106.0 0.5 copy-done.1
  106.5 4.4 %far_pack.1.after_ref = bf16[8,2,8,16384]{3,2,1,0:T(8,128)(2,1)} custom-call(s32[32]{0:T(128)} %copy-done.5, bf16[64,16384]{1,0:T(8,128)(2,1)} %collective-permute-done.3.outer_ref, bf16[64,16384]{1,0:T(8,128)(2,1)} %copy-done.1, f32[64,128]{1,0:T(8,128)} %plane_sums.3.after_ref.refs_2_), custom_call_target="tpu_custom_call" | custom-call | flops 2097152 | bytes 6291456 | tf_op jit(solution)/shard_map/far_pack/pallas_call | solution.py:257
  110.9 4.6 %all-to-all-start.1 = ((bf16[8,2,8,16384]{3,2,1,0:T(8,128)(2,1)}), bf16[8,2,8,16384]{3,2,1,0:T(8,128)(2,1)}, u32[]{:S(2)}, u32[]{:S(2)}) async-start(bf16[8,2,8,16384]{3,2,1,0:T(8,128)(2,1)} %far_pack.1.after_ref), calls=%async_computation.1 | async-start | bytes 8388608 | tf_op jit(solution)/shard_map/all_to_all | solution.py:487
  115.5 0.7 broadcast_in_dim.7.ops_ref
  116.2 36.0 %place.3.refs_0_.refs_1_ = bf16[16384,256]{1,0:T(8,128)(2,1)} custom-call(s32[2,1,16384]{2,1,0:T(1,128)} %broadcast_in_dim.7.ops_ref, bf16[64,16384]{1,0:T(8,128)(2,1)} %copy-done, bf16[64,16384]{1,0:T(8,128)(2,1)} %collective-permute-done.near_ref, bf16[8,2,8,16384]{3,2,1,0:T(8,128)(2,1)} %far_pack.1.after_ref), custom_call_target="tpu_custom_call" | custom-call | bytes 268435456 | tf_op jit(solution)/shard_map/place/pallas_call | solution.py:329
  152.2 10.1 %plane_sums.4.refs_3_ = f32[64,128]{1,0:T(8,128)} custom-call(bf16[128,16384]{1,0:T(8,128)(2,1)} %bitcast.1.got_ref, bf16[16384,256]{1,0:T(8,128)(2,1)} %place.3.refs_0_.refs_1_), custom_call_target="tpu_custom_call" | custom-call | flops 2415919104 | bytes 12582912 | tf_op jit(solution)/shard_map/plane_sums/pallas_call | solution.py:458
  162.3 2.3 %all-to-all-done.1 = bf16[8,2,8,16384]{3,2,1,0:T(8,128)(2,1)} async-done(((bf16[8,2,8,16384]{3,2,1,0:T(8,128)(2,1)}), bf16[8,2,8,16384]{3,2,1,0:T(8,128)(2,1)}, u32[]{:S(2)}, u32[]{:S(2)}) %all-to-all-start.1) | async-done | bytes 4194336 | tf_op jit(solution)/shard_map/all_to_all | solution.py:487
  164.6 16.5 %plane_sums.5 = (f32[64,128]{1,0:T(8,128)}, f32[64,128]{1,0:T(8,128)}, f32[2,8,8,128]{3,2,1,0:T(8,128)}) custom-call(bf16[128,16384]{1,0:T(8,128)(2,1)} %bitcast.2.got_ref, bf16[16384,256]{1,0:T(8,128)(2,1)} %place.2.refs_0_, bf16[16384,256]{1,0:T(8,128)(2,1)} %place.3.refs_0_.refs_1_, f32[64,128]{1,0:T(8,128)} %plane_sums.3.after_ref.refs_2_, ...), custom_call_target="tpu_custom_call" | custom-call | flops 4831838208 | bytes 20971520 | tf_op jit(solution)/shard_map/plane_sums/pallas_call | solution.py:458
  181.1 4.8 %collective-permute-start.5 = (f32[64,128]{1,0:T(8,128)}, f32[64,128]{1,0:T(8,128)S(1)}, u32[]{:S(2)}, u32[]{:S(2)}) collective-permute-start(f32[64,128]{1,0:T(8,128)} %get-tuple-element.12), channel_id=1, source_target_pairs={{0,8},{1,9},{2,10},{3,11},{4,12},{5,13},{6,14},{7,15},{8,0},{9,1},... | collective-permute-start | bytes 98312 | tf_op jit(solution)/shard_map/ppermute | solution.py:508
  185.9 3.5 %all-to-all-start.2 = ((f32[16,8,128]{2,1,0:T(8,128)}), f32[16,8,128]{2,1,0:T(8,128)S(1)}, u32[]{:S(2)}, u32[]{:S(2)}) async-start(f32[16,8,128]{2,1,0:T(8,128)} %bitcast.19), calls=%async_computation.2 | async-start | bytes 131072 | tf_op jit(solution)/shard_map/all_to_all | solution.py:516
  189.4 0.0 collective-permute-done.5
  189.4 0.8 pad_maximum_fusion.1
  190.3 0.7 copy.16
  191.0 5.3 %all-to-all-done.2 = f32[16,8,128]{2,1,0:T(8,128)S(1)} async-done(((f32[16,8,128]{2,1,0:T(8,128)}), f32[16,8,128]{2,1,0:T(8,128)S(1)}, u32[]{:S(2)}, u32[]{:S(2)}) %all-to-all-start.2) | async-done | bytes 65568 | tf_op jit(solution)/shard_map/all_to_all | solution.py:516
  196.3 0.2 reshape.30
  196.5 0.1 copy.17
  196.6 0.8 reverse_select_fusion
  (2 shorter events, 0.0 us)
Async XLA Ops:
  0.6 2.2 %copy-start.2 = (bf16[32,16384]{1,0:T(8,128)(2,1)S(1)}, bf16[32,16384]{1,0:T(8,128)(2,1)}, u32[]{:S(2)}) copy-start(bf16[32,16384]{1,0:T(8,128)(2,1)} %param.5) | copy-start | bytes 3145732
  3.0 5.1 %copy-start = (bf16[64,16384]{1,0:T(8,128)(2,1)}, bf16[64,16384]{1,0:T(8,128)(2,1)S(1)}, u32[]{:S(2)}) copy-start(bf16[64,16384]{1,0:T(8,128)(2,1)S(1)} %pad_maximum_fusion.xw_ref.mine_ref) | copy-start | bytes 6291460
  3.0 52.9 %collective-permute-start = (bf16[64,16384]{1,0:T(8,128)(2,1)S(1)}, bf16[64,16384]{1,0:T(8,128)(2,1)}, u32[]{:S(2)}, u32[]{:S(2)}) collective-permute-start(bf16[64,16384]{1,0:T(8,128)(2,1)S(1)} %pad_maximum_fusion.xw_ref.mine_ref), channel_id=1, source_target_pairs={{0,8},{1,9},{2,10},{3,11},{4,12},{5,13},{6,14},{7,15},{8,0},{9,1},... | collective-permute-start | bytes 6291464 | tf_op jit(solution)/shard_map/ppermute | solution.py:493
  6.1 49.8 %collective-permute-start.1 = (bf16[64,16384]{1,0:T(8,128)(2,1)S(1)}, bf16[64,16384]{1,0:T(8,128)(2,1)}, u32[]{:S(2)}, u32[]{:S(2)}) collective-permute-start(bf16[64,16384]{1,0:T(8,128)(2,1)S(1)} %pad_maximum_fusion.xw_ref.mine_ref), channel_id=1, source_target_pairs={{8,16},{9,17},{10,18},{11,19},{12,20},{13,21},{14,22},{15,23},{16,... | collective-permute-start | bytes 6291464 | tf_op jit(solution)/shard_map/ppermute | solution.py:494
  12.4 4.7 %copy-start.4 = (s32[32,1]{0,1:T(1,128)S(1)}, s32[32,1]{0,1:T(1,128)}, u32[]{:S(2)}) copy-start(s32[32,1]{0,1:T(1,128)} %param.9) | copy-start | bytes 388
  12.5 45.6 %copy-start.3 = (s32[4,16384]{1,0:T(4,128)S(1)}, s32[4,16384]{1,0:T(4,128)}, u32[]{:S(2)}) copy-start(s32[4,16384]{1,0:T(4,128)} %param.8) | copy-start | bytes 786436
  12.5 82.5 %all-to-all-start = ((bf16[8,2,8,16384]{3,2,1,0:T(8,128)(2,1)}), bf16[8,2,8,16384]{3,2,1,0:T(8,128)(2,1)}, u32[]{:S(2)}, u32[]{:S(2)}) async-start(bf16[8,2,8,16384]{3,2,1,0:T(8,128)(2,1)} %own_pack.1), calls=%async_computation | async-start | bytes 8388608 | tf_op jit(solution)/shard_map/all_to_all | solution.py:487
  17.2 38.8 %collective-permute-start.2 = (s32[32]{0:T(128)S(1)}, s32[32]{0:T(128)S(1)}, u32[]{:S(2)}, u32[]{:S(2)}) collective-permute-start(s32[32]{0:T(128)S(1)} %bitcast.25), channel_id=1, source_target_pairs={{0,16},{1,17},{2,18},{3,19},{4,20},{5,21},{6,22},{7,23},{8,24},{9,... | collective-permute-start | bytes 392 | tf_op jit(solution)/shard_map/ppermute | solution.py:495
  56.0 39.0 %copy-start.5 = (s32[32]{0:T(128)}, s32[32]{0:T(128)S(1)}, u32[]{:S(2)}) copy-start(s32[32]{0:T(128)S(1)} %collective-permute-done.2.pick_ref) | copy-start | bytes 388
  56.0 49.1 %collective-permute-start.4 = (bf16[64,16384]{1,0:T(8,128)(2,1)}, bf16[64,16384]{1,0:T(8,128)(2,1)S(1)}, u32[]{:S(2)}, u32[]{:S(2)}) collective-permute-start(bf16[64,16384]{1,0:T(8,128)(2,1)} %collective-permute-done.near_ref), channel_id=1, source_target_pairs={{8,16},{9,17},{10,18},{11,19},{12,20},{13,21},{14,22},{15,23},{16,... | collective-permute-start | bytes 6291464 | tf_op jit(solution)/shard_map/ppermute | solution.py:499
  56.8 49.3 %collective-permute-start.3 = (bf16[64,16384]{1,0:T(8,128)(2,1)}, bf16[64,16384]{1,0:T(8,128)(2,1)}, u32[]{:S(2)}, u32[]{:S(2)}) collective-permute-start(bf16[64,16384]{1,0:T(8,128)(2,1)} %collective-permute-done.1), channel_id=1, source_target_pairs={{8,0},{9,1},{10,2},{11,3},{12,4},{13,5},{14,6},{15,7},{16,24},{17,... | collective-permute-start | bytes 6291464 | tf_op jit(solution)/shard_map/ppermute | solution.py:498
  105.1 1.4 copy-start.1
  110.9 53.7 %all-to-all-start.1 = ((bf16[8,2,8,16384]{3,2,1,0:T(8,128)(2,1)}), bf16[8,2,8,16384]{3,2,1,0:T(8,128)(2,1)}, u32[]{:S(2)}, u32[]{:S(2)}) async-start(bf16[8,2,8,16384]{3,2,1,0:T(8,128)(2,1)} %far_pack.1.after_ref), calls=%async_computation.1 | async-start | bytes 8388608 | tf_op jit(solution)/shard_map/all_to_all | solution.py:487
  181.1 8.3 %collective-permute-start.5 = (f32[64,128]{1,0:T(8,128)}, f32[64,128]{1,0:T(8,128)S(1)}, u32[]{:S(2)}, u32[]{:S(2)}) collective-permute-start(f32[64,128]{1,0:T(8,128)} %get-tuple-element.12), channel_id=1, source_target_pairs={{0,8},{1,9},{2,10},{3,11},{4,12},{5,13},{6,14},{7,15},{8,0},{9,1},... | collective-permute-start | bytes 98312 | tf_op jit(solution)/shard_map/ppermute | solution.py:508
  185.9 10.4 %all-to-all-start.2 = ((f32[16,8,128]{2,1,0:T(8,128)}), f32[16,8,128]{2,1,0:T(8,128)S(1)}, u32[]{:S(2)}, u32[]{:S(2)}) async-start(f32[16,8,128]{2,1,0:T(8,128)} %bitcast.19), calls=%async_computation.2 | async-start | bytes 131072 | tf_op jit(solution)/shard_map/all_to_all | solution.py:516

commit v19 on v18

--- a/solution.py
+++ b/solution.py
@@ -323,7 +323,7 @@
 def place(ops, mine, near, after):
     count = ops.shape[0]
     rows, width = mine.shape
-    depth = min(2048, width)
+    depth = min(4096, width)
     last = width // depth - 1
     part = pl.BlockSpec((rows, depth), lambda k, i: (0, jnp.where(k == 0, i, last)))
     return pl.pallas_call(

time: 198 us -> 197 us (level)
  waiting for transfers between devices: 44.7 us -> 47.3 us
  Pallas kernels: 117 us -> 115 us
    pallas_call x2, Pallas kernels: 72 us -> 69.5 us  [place(): pl.pallas_call(place_kernel, grid=(count, width // depth), out_shape=jax....]
  transfers between devices with their start and end apart: 9 -> 9, of which waited for: 4 -> 4; matrix products, arithmetic and copies ran while one was open for 2% -> 2% of each run, Pallas kernels for 49% -> 48%
where the time goes in v19:
time: 197 us; the launch traced here: 196 us
  Pallas kernels  115 us (58%)
  waiting for transfers between devices  47.3 us (24%)
  starting transfers between devices  26.5 us (13%)
  other arithmetic  3.94 us (2%)
  local copies, waits for them, and re-layouts  2.59 us (1%)
    pallas_call x2, Pallas kernels, place(): pl.pallas_call(place_kernel, grid=(count, width // depth), out_shape=jax....  69.5 us
    pallas_call x3, Pallas kernels, plane_sums(): pl.pallas_call(functools.partial(plane_sums_kernel, len(moved)), grid=(wi...  36.8 us
    ppermute x1, waiting for transfers between devices, shards_by_plane(): far_pick = lax.ppermute(own_pick, 'dp', far)  36.2 us
    all_to_all x2, starting transfers between devices, spread(): lax.all_to_all(send, 'dp', split_axis=0, concat_axis=0, axis_index_groups...  9.26 us
    pallas_call x2, Pallas kernels, pack_call(): pl.pallas_call(kernel, out_shape=jax.ShapeDtypeStruct((PLANE, 2, SLAB, wi...  8.71 us
    all_to_all x1, waiting for transfers between devices, shards_by_plane(): lax.all_to_all(back, 'dp', split_axis=0, concat_axis=0, axis_index_groups...  5.33 us
    ppermute x1, starting transfers between devices, shards_by_plane(): from_near = lax.ppermute(other, 'dp', near)  3.99 us
  transfers between devices with their start and end apart: 9, of which 4 were waited for; matrix products, arithmetic and copies ran while one was open for 2% of the time, Pallas kernels for 48%

profile of v19, /device:TPU:0, one launch (start us, length us, event | category | flops | bytes accessed | tf_op | source)
XLA Modules:
  0.0 196.1 jit_solution(6326744296411669338)
XLA Ops:
  0.6 0.0 copy-start.2
  0.6 2.2 %multiply_convert_fusion = bf16[32,16384]{1,0:T(8,128)(2,1)S(1)} fusion(bf16[32,16384]{1,0:T(8,128)(2,1)} %param.7, s32[32,16384]{1,0:T(8,128)} %param.6), kind=kLoop, calls=%fused_computation.1 | loop fusion | flops 2097152 | bytes 4194304 | tf_op jit(solution)/shard_map/convert_element_type | solution.py:491
  2.9 0.0 copy-done.2
  2.9 0.1 pad_maximum_fusion.xw_ref.mine_ref
  3.0 0.0 copy-start
  3.0 3.1 %collective-permute-start = (bf16[64,16384]{1,0:T(8,128)(2,1)S(1)}, bf16[64,16384]{1,0:T(8,128)(2,1)}, u32[]{:S(2)}, u32[]{:S(2)}) collective-permute-start(bf16[64,16384]{1,0:T(8,128)(2,1)S(1)} %pad_maximum_fusion.xw_ref.mine_ref), channel_id=1, source_target_pairs={{0,8},{1,9},{2,10},{3,11},{4,12},{5,13},{6,14},{7,15},{8,0},{9,1},... | collective-permute-start | bytes 6291464 | tf_op jit(solution)/shard_map/ppermute | solution.py:493
  6.1 2.0 %collective-permute-start.1 = (bf16[64,16384]{1,0:T(8,128)(2,1)S(1)}, bf16[64,16384]{1,0:T(8,128)(2,1)}, u32[]{:S(2)}, u32[]{:S(2)}) collective-permute-start(bf16[64,16384]{1,0:T(8,128)(2,1)S(1)} %pad_maximum_fusion.xw_ref.mine_ref), channel_id=1, source_target_pairs={{8,16},{9,17},{10,18},{11,19},{12,20},{13,21},{14,22},{15,23},{16,... | collective-permute-start | bytes 6291464 | tf_op jit(solution)/shard_map/ppermute | solution.py:494
  8.2 0.0 copy-done
  8.2 4.3 %own_pack.1 = bf16[8,2,8,16384]{3,2,1,0:T(8,128)(2,1)} custom-call(s32[32]{0:T(128)} %bitcast.23, bf16[64,16384]{1,0:T(8,128)(2,1)} %copy-done), custom_call_target="tpu_custom_call" | custom-call | flops 2097152 | bytes 6291456 | tf_op jit(solution)/shard_map/own_pack/pallas_call | solution.py:257
  12.4 0.0 copy-start.4
  12.5 0.0 copy-start.3
  12.5 4.7 %all-to-all-start = ((bf16[8,2,8,16384]{3,2,1,0:T(8,128)(2,1)}), bf16[8,2,8,16384]{3,2,1,0:T(8,128)(2,1)}, u32[]{:S(2)}, u32[]{:S(2)}) async-start(bf16[8,2,8,16384]{3,2,1,0:T(8,128)(2,1)} %own_pack.1), calls=%async_computation | async-start | bytes 8388608 | tf_op jit(solution)/shard_map/all_to_all | solution.py:487
  17.2 0.0 copy-done.4
  17.2 2.6 %collective-permute-start.2 = (s32[32]{0:T(128)S(1)}, s32[32]{0:T(128)S(1)}, u32[]{:S(2)}, u32[]{:S(2)}) collective-permute-start(s32[32]{0:T(128)S(1)} %bitcast.25), channel_id=1, source_target_pairs={{0,16},{1,17},{2,18},{3,19},{4,20},{5,21},{6,22},{7,23},{8,24},{9,... | collective-permute-start | bytes 392 | tf_op jit(solution)/shard_map/ppermute | solution.py:495
  19.8 36.2 %collective-permute-done.2.pick_ref = s32[32]{0:T(128)S(1)} collective-permute-done((s32[32]{0:T(128)S(1)}, s32[32]{0:T(128)S(1)}, u32[]{:S(2)}, u32[]{:S(2)}) %collective-permute-start.2) | collective-permute-done | bytes 160 | tf_op jit(solution)/shard_map/ppermute | solution.py:495
  56.0 0.0 copy-start.5
  56.0 0.0 collective-permute-done.near_ref
  56.0 0.0 collective-permute-done.1
  56.0 0.8 collective-permute-start.4
  56.8 1.3 collective-permute-start.3
  58.1 0.0 copy-done.3
  58.1 0.1 fusion
  58.2 0.7 broadcast_in_dim.6.ops_ref
  58.9 34.8 %place.2.refs_0_ = bf16[16384,256]{1,0:T(8,128)(2,1)} custom-call(s32[2,1,16384]{2,1,0:T(1,128)} %broadcast_in_dim.6.ops_ref, bf16[64,16384]{1,0:T(8,128)(2,1)} %copy-done, bf16[64,16384]{1,0:T(8,128)(2,1)} %collective-permute-done.near_ref, s32[32]{0:T(128)} %bitcast.24), custom_call_target="tpu_custom_call" | custom-call | bytes 268435456 | tf_op jit(solution)/shard_map/place/pallas_call | solution.py:329
  93.7 0.0 copy-done.5
  93.7 0.0 all-to-all-done
  93.7 10.2 %plane_sums.3.after_ref.refs_2_ = f32[64,128]{1,0:T(8,128)} custom-call(bf16[128,16384]{1,0:T(8,128)(2,1)} %bitcast.1.got_ref, bf16[16384,256]{1,0:T(8,128)(2,1)} %place.2.refs_0_), custom_call_target="tpu_custom_call" | custom-call | flops 2415919104 | bytes 12582912 | tf_op jit(solution)/shard_map/plane_sums/pallas_call | solution.py:458
  103.9 0.0 collective-permute-done.4.inner_ref
  103.9 0.0 copy-start.1
  103.9 2.2 %collective-permute-done.3.outer_ref = bf16[64,16384]{1,0:T(8,128)(2,1)} collective-permute-done((bf16[64,16384]{1,0:T(8,128)(2,1)}, bf16[64,16384]{1,0:T(8,128)(2,1)}, u32[]{:S(2)}, u32[]{:S(2)}) %collective-permute-start.3) | collective-permute-done | bytes 2097184 | tf_op jit(solution)/shard_map/ppermute | solution.py:498
  106.0 0.0 copy-done.1
  106.0 4.4 %far_pack.1.after_ref = bf16[8,2,8,16384]{3,2,1,0:T(8,128)(2,1)} custom-call(s32[32]{0:T(128)} %copy-done.5, bf16[64,16384]{1,0:T(8,128)(2,1)} %collective-permute-done.3.outer_ref, bf16[64,16384]{1,0:T(8,128)(2,1)} %copy-done.1, f32[64,128]{1,0:T(8,128)} %plane_sums.3.after_ref.refs_2_), custom_call_target="tpu_custom_call" | custom-call | flops 2097152 | bytes 6291456 | tf_op jit(solution)/shard_map/far_pack/pallas_call | solution.py:257
  110.5 4.6 %all-to-all-start.1 = ((bf16[8,2,8,16384]{3,2,1,0:T(8,128)(2,1)}), bf16[8,2,8,16384]{3,2,1,0:T(8,128)(2,1)}, u32[]{:S(2)}, u32[]{:S(2)}) async-start(bf16[8,2,8,16384]{3,2,1,0:T(8,128)(2,1)} %far_pack.1.after_ref), calls=%async_computation.1 | async-start | bytes 8388608 | tf_op jit(solution)/shard_map/all_to_all | solution.py:487
  115.0 0.7 broadcast_in_dim.7.ops_ref
  115.8 34.7 %place.3.refs_0_.refs_1_ = bf16[16384,256]{1,0:T(8,128)(2,1)} custom-call(s32[2,1,16384]{2,1,0:T(1,128)} %broadcast_in_dim.7.ops_ref, bf16[64,16384]{1,0:T(8,128)(2,1)} %copy-done, bf16[64,16384]{1,0:T(8,128)(2,1)} %collective-permute-done.near_ref, bf16[8,2,8,16384]{3,2,1,0:T(8,128)(2,1)} %far_pack.1.after_ref), custom_call_target="tpu_custom_call" | custom-call | bytes 268435456 | tf_op jit(solution)/shard_map/place/pallas_call | solution.py:329
  150.5 10.1 %plane_sums.4.refs_3_ = f32[64,128]{1,0:T(8,128)} custom-call(bf16[128,16384]{1,0:T(8,128)(2,1)} %bitcast.1.got_ref, bf16[16384,256]{1,0:T(8,128)(2,1)} %place.3.refs_0_.refs_1_), custom_call_target="tpu_custom_call" | custom-call | flops 2415919104 | bytes 12582912 | tf_op jit(solution)/shard_map/plane_sums/pallas_call | solution.py:458
  160.6 3.5 %all-to-all-done.1 = bf16[8,2,8,16384]{3,2,1,0:T(8,128)(2,1)} async-done(((bf16[8,2,8,16384]{3,2,1,0:T(8,128)(2,1)}), bf16[8,2,8,16384]{3,2,1,0:T(8,128)(2,1)}, u32[]{:S(2)}, u32[]{:S(2)}) %all-to-all-start.1) | async-done | bytes 4194336 | tf_op jit(solution)/shard_map/all_to_all | solution.py:487
  164.2 16.5 %plane_sums.5 = (f32[64,128]{1,0:T(8,128)}, f32[64,128]{1,0:T(8,128)}, f32[2,8,8,128]{3,2,1,0:T(8,128)}) custom-call(bf16[128,16384]{1,0:T(8,128)(2,1)} %bitcast.2.got_ref, bf16[16384,256]{1,0:T(8,128)(2,1)} %place.2.refs_0_, bf16[16384,256]{1,0:T(8,128)(2,1)} %place.3.refs_0_.refs_1_, f32[64,128]{1,0:T(8,128)} %plane_sums.3.after_ref.refs_2_, ...), custom_call_target="tpu_custom_call" | custom-call | flops 4831838208 | bytes 20971520 | tf_op jit(solution)/shard_map/plane_sums/pallas_call | solution.py:458
  180.7 4.0 %collective-permute-start.5 = (f32[64,128]{1,0:T(8,128)}, f32[64,128]{1,0:T(8,128)S(1)}, u32[]{:S(2)}, u32[]{:S(2)}) collective-permute-start(f32[64,128]{1,0:T(8,128)} %get-tuple-element.12), channel_id=1, source_target_pairs={{0,8},{1,9},{2,10},{3,11},{4,12},{5,13},{6,14},{7,15},{8,0},{9,1},... | collective-permute-start | bytes 98312 | tf_op jit(solution)/shard_map/ppermute | solution.py:508
  184.7 3.5 %all-to-all-start.2 = ((f32[16,8,128]{2,1,0:T(8,128)}), f32[16,8,128]{2,1,0:T(8,128)S(1)}, u32[]{:S(2)}, u32[]{:S(2)}) async-start(f32[16,8,128]{2,1,0:T(8,128)} %bitcast.19), calls=%async_computation.2 | async-start | bytes 131072 | tf_op jit(solution)/shard_map/all_to_all | solution.py:516
  188.2 0.0 collective-permute-done.5
  188.2 0.8 pad_maximum_fusion.1
  189.0 0.7 copy.16
  189.7 5.3 %all-to-all-done.2 = f32[16,8,128]{2,1,0:T(8,128)S(1)} async-done(((f32[16,8,128]{2,1,0:T(8,128)}), f32[16,8,128]{2,1,0:T(8,128)S(1)}, u32[]{:S(2)}, u32[]{:S(2)}) %all-to-all-start.2) | async-done | bytes 65568 | tf_op jit(solution)/shard_map/all_to_all | solution.py:516
  195.1 0.2 reshape.30
  195.2 0.1 copy.17
  195.3 0.8 reverse_select_fusion
  (2 shorter events, 0.0 us)
Async XLA Ops:
  0.6 2.2 %copy-start.2 = (bf16[32,16384]{1,0:T(8,128)(2,1)S(1)}, bf16[32,16384]{1,0:T(8,128)(2,1)}, u32[]{:S(2)}) copy-start(bf16[32,16384]{1,0:T(8,128)(2,1)} %param.5) | copy-start | bytes 3145732
  3.0 5.1 %copy-start = (bf16[64,16384]{1,0:T(8,128)(2,1)}, bf16[64,16384]{1,0:T(8,128)(2,1)S(1)}, u32[]{:S(2)}) copy-start(bf16[64,16384]{1,0:T(8,128)(2,1)S(1)} %pad_maximum_fusion.xw_ref.mine_ref) | copy-start | bytes 6291460
  3.0 52.9 %collective-permute-start = (bf16[64,16384]{1,0:T(8,128)(2,1)S(1)}, bf16[64,16384]{1,0:T(8,128)(2,1)}, u32[]{:S(2)}, u32[]{:S(2)}) collective-permute-start(bf16[64,16384]{1,0:T(8,128)(2,1)S(1)} %pad_maximum_fusion.xw_ref.mine_ref), channel_id=1, source_target_pairs={{0,8},{1,9},{2,10},{3,11},{4,12},{5,13},{6,14},{7,15},{8,0},{9,1},... | collective-permute-start | bytes 6291464 | tf_op jit(solution)/shard_map/ppermute | solution.py:493
  6.1 49.8 %collective-permute-start.1 = (bf16[64,16384]{1,0:T(8,128)(2,1)S(1)}, bf16[64,16384]{1,0:T(8,128)(2,1)}, u32[]{:S(2)}, u32[]{:S(2)}) collective-permute-start(bf16[64,16384]{1,0:T(8,128)(2,1)S(1)} %pad_maximum_fusion.xw_ref.mine_ref), channel_id=1, source_target_pairs={{8,16},{9,17},{10,18},{11,19},{12,20},{13,21},{14,22},{15,23},{16,... | collective-permute-start | bytes 6291464 | tf_op jit(solution)/shard_map/ppermute | solution.py:494
  12.4 4.7 %copy-start.4 = (s32[32,1]{0,1:T(1,128)S(1)}, s32[32,1]{0,1:T(1,128)}, u32[]{:S(2)}) copy-start(s32[32,1]{0,1:T(1,128)} %param.9) | copy-start | bytes 388
  12.5 45.6 %copy-start.3 = (s32[4,16384]{1,0:T(4,128)S(1)}, s32[4,16384]{1,0:T(4,128)}, u32[]{:S(2)}) copy-start(s32[4,16384]{1,0:T(4,128)} %param.8) | copy-start | bytes 786436
  12.5 81.2 %all-to-all-start = ((bf16[8,2,8,16384]{3,2,1,0:T(8,128)(2,1)}), bf16[8,2,8,16384]{3,2,1,0:T(8,128)(2,1)}, u32[]{:S(2)}, u32[]{:S(2)}) async-start(bf16[8,2,8,16384]{3,2,1,0:T(8,128)(2,1)} %own_pack.1), calls=%async_computation | async-start | bytes 8388608 | tf_op jit(solution)/shard_map/all_to_all | solution.py:487
  17.2 38.8 %collective-permute-start.2 = (s32[32]{0:T(128)S(1)}, s32[32]{0:T(128)S(1)}, u32[]{:S(2)}, u32[]{:S(2)}) collective-permute-start(s32[32]{0:T(128)S(1)} %bitcast.25), channel_id=1, source_target_pairs={{0,16},{1,17},{2,18},{3,19},{4,20},{5,21},{6,22},{7,23},{8,24},{9,... | collective-permute-start | bytes 392 | tf_op jit(solution)/shard_map/ppermute | solution.py:495
  56.0 37.7 %copy-start.5 = (s32[32]{0:T(128)}, s32[32]{0:T(128)S(1)}, u32[]{:S(2)}) copy-start(s32[32]{0:T(128)S(1)} %collective-permute-done.2.pick_ref) | copy-start | bytes 388
  56.0 47.9 %collective-permute-start.4 = (bf16[64,16384]{1,0:T(8,128)(2,1)}, bf16[64,16384]{1,0:T(8,128)(2,1)S(1)}, u32[]{:S(2)}, u32[]{:S(2)}) collective-permute-start(bf16[64,16384]{1,0:T(8,128)(2,1)} %collective-permute-done.near_ref), channel_id=1, source_target_pairs={{8,16},{9,17},{10,18},{11,19},{12,20},{13,21},{14,22},{15,23},{16,... | collective-permute-start | bytes 6291464 | tf_op jit(solution)/shard_map/ppermute | solution.py:499
  56.8 49.3 %collective-permute-start.3 = (bf16[64,16384]{1,0:T(8,128)(2,1)}, bf16[64,16384]{1,0:T(8,128)(2,1)}, u32[]{:S(2)}, u32[]{:S(2)}) collective-permute-start(bf16[64,16384]{1,0:T(8,128)(2,1)} %collective-permute-done.1), channel_id=1, source_target_pairs={{8,0},{9,1},{10,2},{11,3},{12,4},{13,5},{14,6},{15,7},{16,24},{17,... | collective-permute-start | bytes 6291464 | tf_op jit(solution)/shard_map/ppermute | solution.py:498
  103.9 2.2 %copy-start.1 = (bf16[64,16384]{1,0:T(8,128)(2,1)}, bf16[64,16384]{1,0:T(8,128)(2,1)S(1)}, u32[]{:S(2)}) copy-start(bf16[64,16384]{1,0:T(8,128)(2,1)S(1)} %collective-permute-done.4.inner_ref) | copy-start | bytes 6291460
  110.5 53.7 %all-to-all-start.1 = ((bf16[8,2,8,16384]{3,2,1,0:T(8,128)(2,1)}), bf16[8,2,8,16384]{3,2,1,0:T(8,128)(2,1)}, u32[]{:S(2)}, u32[]{:S(2)}) async-start(bf16[8,2,8,16384]{3,2,1,0:T(8,128)(2,1)} %far_pack.1.after_ref), calls=%async_computation.1 | async-start | bytes 8388608 | tf_op jit(solution)/shard_map/all_to_all | solution.py:487
  180.7 7.5 %collective-permute-start.5 = (f32[64,128]{1,0:T(8,128)}, f32[64,128]{1,0:T(8,128)S(1)}, u32[]{:S(2)}, u32[]{:S(2)}) collective-permute-start(f32[64,128]{1,0:T(8,128)} %get-tuple-element.12), channel_id=1, source_target_pairs={{0,8},{1,9},{2,10},{3,11},{4,12},{5,13},{6,14},{7,15},{8,0},{9,1},... | collective-permute-start | bytes 98312 | tf_op jit(solution)/shard_map/ppermute | solution.py:508
  184.7 10.4 %all-to-all-start.2 = ((f32[16,8,128]{2,1,0:T(8,128)}), f32[16,8,128]{2,1,0:T(8,128)S(1)}, u32[]{:S(2)}, u32[]{:S(2)}) async-start(f32[16,8,128]{2,1,0:T(8,128)} %bitcast.19), calls=%async_computation.2 | async-start | bytes 131072 | tf_op jit(solution)/shard_map/all_to_all | solution.py:516

commit v20 on v19

--- a/solution.py
+++ b/solution.py
@@ -323,7 +323,7 @@
 def place(ops, mine, near, after):
     count = ops.shape[0]
     rows, width = mine.shape
-    depth = min(4096, width)
+    depth = min(8192, width)
     last = width // depth - 1
     part = pl.BlockSpec((rows, depth), lambda k, i: (0, jnp.where(k == 0, i, last)))
     return pl.pallas_call(

time: 197 us -> 196 us (level)
  no operation moved by 1% of the time
where the time goes in v20:
time: 196 us
  Pallas kernels  114 us (58%)
  waiting for transfers between devices  47.5 us (24%)
  starting transfers between devices  26.5 us (14%)
  other arithmetic  3.94 us (2%)
  local copies, waits for them, and re-layouts  2.59 us (1%)
    pallas_call x2, Pallas kernels, place(): pl.pallas_call(place_kernel, grid=(count, width // depth), out_shape=jax....  69 us
    pallas_call x3, Pallas kernels, plane_sums(): pl.pallas_call(functools.partial(plane_sums_kernel, len(moved)), grid=(wi...  36.8 us
    ppermute x1, waiting for transfers between devices, shards_by_plane(): far_pick = lax.ppermute(own_pick, 'dp', far)  36.2 us
    all_to_all x2, starting transfers between devices, spread(): lax.all_to_all(send, 'dp', split_axis=0, concat_axis=0, axis_index_groups...  9.44 us
    pallas_call x2, Pallas kernels, pack_call(): pl.pallas_call(kernel, out_shape=jax.ShapeDtypeStruct((PLANE, 2, SLAB, wi...  8.71 us
    all_to_all x1, waiting for transfers between devices, shards_by_plane(): lax.all_to_all(back, 'dp', split_axis=0, concat_axis=0, axis_index_groups...  5.33 us
  transfers between devices with their start and end apart: 9, of which 4 were waited for; matrix products, arithmetic and copies ran while one was open for 2% of the time, Pallas kernels for 48%

profile of v20, /device:TPU:0, one launch (start us, length us, event | category | flops | bytes accessed | tf_op | source)
XLA Modules:
  0.0 195.8 jit_solution(5942214445300904822)
XLA Ops:
  0.6 0.0 copy-start.2
  0.6 2.2 %multiply_convert_fusion = bf16[32,16384]{1,0:T(8,128)(2,1)S(1)} fusion(bf16[32,16384]{1,0:T(8,128)(2,1)} %param.7, s32[32,16384]{1,0:T(8,128)} %param.6), kind=kLoop, calls=%fused_computation.1 | loop fusion | flops 2097152 | bytes 4194304 | tf_op jit(solution)/shard_map/convert_element_type | solution.py:491
  2.9 0.0 copy-done.2
  2.9 0.1 pad_maximum_fusion.xw_ref.mine_ref
  3.0 0.0 copy-start
  3.0 3.1 %collective-permute-start = (bf16[64,16384]{1,0:T(8,128)(2,1)S(1)}, bf16[64,16384]{1,0:T(8,128)(2,1)}, u32[]{:S(2)}, u32[]{:S(2)}) collective-permute-start(bf16[64,16384]{1,0:T(8,128)(2,1)S(1)} %pad_maximum_fusion.xw_ref.mine_ref), channel_id=1, source_target_pairs={{0,8},{1,9},{2,10},{3,11},{4,12},{5,13},{6,14},{7,15},{8,0},{9,1},... | collective-permute-start | bytes 6291464 | tf_op jit(solution)/shard_map/ppermute | solution.py:493
  6.1 2.0 %collective-permute-start.1 = (bf16[64,16384]{1,0:T(8,128)(2,1)S(1)}, bf16[64,16384]{1,0:T(8,128)(2,1)}, u32[]{:S(2)}, u32[]{:S(2)}) collective-permute-start(bf16[64,16384]{1,0:T(8,128)(2,1)S(1)} %pad_maximum_fusion.xw_ref.mine_ref), channel_id=1, source_target_pairs={{8,16},{9,17},{10,18},{11,19},{12,20},{13,21},{14,22},{15,23},{16,... | collective-permute-start | bytes 6291464 | tf_op jit(solution)/shard_map/ppermute | solution.py:494
  8.2 0.0 copy-done
  8.2 4.3 %own_pack.1 = bf16[8,2,8,16384]{3,2,1,0:T(8,128)(2,1)} custom-call(s32[32]{0:T(128)} %bitcast.23, bf16[64,16384]{1,0:T(8,128)(2,1)} %copy-done), custom_call_target="tpu_custom_call" | custom-call | flops 2097152 | bytes 6291456 | tf_op jit(solution)/shard_map/own_pack/pallas_call | solution.py:257
  12.4 0.0 copy-start.4
  12.5 0.0 copy-start.3
  12.5 4.7 %all-to-all-start = ((bf16[8,2,8,16384]{3,2,1,0:T(8,128)(2,1)}), bf16[8,2,8,16384]{3,2,1,0:T(8,128)(2,1)}, u32[]{:S(2)}, u32[]{:S(2)}) async-start(bf16[8,2,8,16384]{3,2,1,0:T(8,128)(2,1)} %own_pack.1), calls=%async_computation | async-start | bytes 8388608 | tf_op jit(solution)/shard_map/all_to_all | solution.py:487
  17.2 0.0 copy-done.4
  17.2 2.6 %collective-permute-start.2 = (s32[32]{0:T(128)S(1)}, s32[32]{0:T(128)S(1)}, u32[]{:S(2)}, u32[]{:S(2)}) collective-permute-start(s32[32]{0:T(128)S(1)} %bitcast.25), channel_id=1, source_target_pairs={{0,16},{1,17},{2,18},{3,19},{4,20},{5,21},{6,22},{7,23},{8,24},{9,... | collective-permute-start | bytes 392 | tf_op jit(solution)/shard_map/ppermute | solution.py:495
  19.8 36.2 %collective-permute-done.2.pick_ref = s32[32]{0:T(128)S(1)} collective-permute-done((s32[32]{0:T(128)S(1)}, s32[32]{0:T(128)S(1)}, u32[]{:S(2)}, u32[]{:S(2)}) %collective-permute-start.2) | collective-permute-done | bytes 160 | tf_op jit(solution)/shard_map/ppermute | solution.py:495
  56.0 0.0 copy-start.5
  56.0 0.0 collective-permute-done.near_ref
  56.0 0.0 collective-permute-done.1
  56.0 0.8 collective-permute-start.4
  56.8 1.3 collective-permute-start.3
  58.1 0.0 copy-done.3
  58.1 0.1 fusion
  58.2 0.7 broadcast_in_dim.6.ops_ref
  58.9 34.5 %place.2.refs_0_ = bf16[16384,256]{1,0:T(8,128)(2,1)} custom-call(s32[2,1,16384]{2,1,0:T(1,128)} %broadcast_in_dim.6.ops_ref, bf16[64,16384]{1,0:T(8,128)(2,1)} %copy-done, bf16[64,16384]{1,0:T(8,128)(2,1)} %collective-permute-done.near_ref, s32[32]{0:T(128)} %bitcast.24), custom_call_target="tpu_custom_call" | custom-call | bytes 268435456 | tf_op jit(solution)/shard_map/place/pallas_call | solution.py:329
  93.5 0.0 copy-done.5
  93.5 0.0 all-to-all-done
  93.5 10.2 %plane_sums.3.after_ref.refs_2_ = f32[64,128]{1,0:T(8,128)} custom-call(bf16[128,16384]{1,0:T(8,128)(2,1)} %bitcast.1.got_ref, bf16[16384,256]{1,0:T(8,128)(2,1)} %place.2.refs_0_), custom_call_target="tpu_custom_call" | custom-call | flops 2415919104 | bytes 12582912 | tf_op jit(solution)/shard_map/plane_sums/pallas_call | solution.py:458
  103.6 0.0 collective-permute-done.4.inner_ref
  103.6 0.0 copy-start.1
  103.6 2.4 %collective-permute-done.3.outer_ref = bf16[64,16384]{1,0:T(8,128)(2,1)} collective-permute-done((bf16[64,16384]{1,0:T(8,128)(2,1)}, bf16[64,16384]{1,0:T(8,128)(2,1)}, u32[]{:S(2)}, u32[]{:S(2)}) %collective-permute-start.3) | collective-permute-done | bytes 2097184 | tf_op jit(solution)/shard_map/ppermute | solution.py:498
  106.0 0.0 copy-done.1
  106.0 4.4 %far_pack.1.after_ref = bf16[8,2,8,16384]{3,2,1,0:T(8,128)(2,1)} custom-call(s32[32]{0:T(128)} %copy-done.5, bf16[64,16384]{1,0:T(8,128)(2,1)} %collective-permute-done.3.outer_ref, bf16[64,16384]{1,0:T(8,128)(2,1)} %copy-done.1, f32[64,128]{1,0:T(8,128)} %plane_sums.3.after_ref.refs_2_), custom_call_target="tpu_custom_call" | custom-call | flops 2097152 | bytes 6291456 | tf_op jit(solution)/shard_map/far_pack/pallas_call | solution.py:257
  110.5 4.7 %all-to-all-start.1 = ((bf16[8,2,8,16384]{3,2,1,0:T(8,128)(2,1)}), bf16[8,2,8,16384]{3,2,1,0:T(8,128)(2,1)}, u32[]{:S(2)}, u32[]{:S(2)}) async-start(bf16[8,2,8,16384]{3,2,1,0:T(8,128)(2,1)} %far_pack.1.after_ref), calls=%async_computation.1 | async-start | bytes 8388608 | tf_op jit(solution)/shard_map/all_to_all | solution.py:487
  115.2 0.7 broadcast_in_dim.7.ops_ref
  116.0 34.5 %place.3.refs_0_.refs_1_ = bf16[16384,256]{1,0:T(8,128)(2,1)} custom-call(s32[2,1,16384]{2,1,0:T(1,128)} %broadcast_in_dim.7.ops_ref, bf16[64,16384]{1,0:T(8,128)(2,1)} %copy-done, bf16[64,16384]{1,0:T(8,128)(2,1)} %collective-permute-done.near_ref, bf16[8,2,8,16384]{3,2,1,0:T(8,128)(2,1)} %far_pack.1.after_ref), custom_call_target="tpu_custom_call" | custom-call | bytes 268435456 | tf_op jit(solution)/shard_map/place/pallas_call | solution.py:329
  150.4 10.1 %plane_sums.4.refs_3_ = f32[64,128]{1,0:T(8,128)} custom-call(bf16[128,16384]{1,0:T(8,128)(2,1)} %bitcast.1.got_ref, bf16[16384,256]{1,0:T(8,128)(2,1)} %place.3.refs_0_.refs_1_), custom_call_target="tpu_custom_call" | custom-call | flops 2415919104 | bytes 12582912 | tf_op jit(solution)/shard_map/plane_sums/pallas_call | solution.py:458
  160.6 3.6 %all-to-all-done.1 = bf16[8,2,8,16384]{3,2,1,0:T(8,128)(2,1)} async-done(((bf16[8,2,8,16384]{3,2,1,0:T(8,128)(2,1)}), bf16[8,2,8,16384]{3,2,1,0:T(8,128)(2,1)}, u32[]{:S(2)}, u32[]{:S(2)}) %all-to-all-start.1) | async-done | bytes 4194336 | tf_op jit(solution)/shard_map/all_to_all | solution.py:487
  164.2 16.5 %plane_sums.5 = (f32[64,128]{1,0:T(8,128)}, f32[64,128]{1,0:T(8,128)}, f32[2,8,8,128]{3,2,1,0:T(8,128)}) custom-call(bf16[128,16384]{1,0:T(8,128)(2,1)} %bitcast.2.got_ref, bf16[16384,256]{1,0:T(8,128)(2,1)} %place.2.refs_0_, bf16[16384,256]{1,0:T(8,128)(2,1)} %place.3.refs_0_.refs_1_, f32[64,128]{1,0:T(8,128)} %plane_sums.3.after_ref.refs_2_, ...), custom_call_target="tpu_custom_call" | custom-call | flops 4831838208 | bytes 20971520 | tf_op jit(solution)/shard_map/plane_sums/pallas_call | solution.py:458
  180.7 3.8 %collective-permute-start.5 = (f32[64,128]{1,0:T(8,128)}, f32[64,128]{1,0:T(8,128)S(1)}, u32[]{:S(2)}, u32[]{:S(2)}) collective-permute-start(f32[64,128]{1,0:T(8,128)} %get-tuple-element.12), channel_id=1, source_target_pairs={{0,8},{1,9},{2,10},{3,11},{4,12},{5,13},{6,14},{7,15},{8,0},{9,1},... | collective-permute-start | bytes 98312 | tf_op jit(solution)/shard_map/ppermute | solution.py:508
  184.4 3.5 %all-to-all-start.2 = ((f32[16,8,128]{2,1,0:T(8,128)}), f32[16,8,128]{2,1,0:T(8,128)S(1)}, u32[]{:S(2)}, u32[]{:S(2)}) async-start(f32[16,8,128]{2,1,0:T(8,128)} %bitcast.19), calls=%async_computation.2 | async-start | bytes 131072 | tf_op jit(solution)/shard_map/all_to_all | solution.py:516
  187.9 0.0 collective-permute-done.5
  187.9 0.8 pad_maximum_fusion.1
  188.8 0.7 copy.16
  189.5 5.3 %all-to-all-done.2 = f32[16,8,128]{2,1,0:T(8,128)S(1)} async-done(((f32[16,8,128]{2,1,0:T(8,128)}), f32[16,8,128]{2,1,0:T(8,128)S(1)}, u32[]{:S(2)}, u32[]{:S(2)}) %all-to-all-start.2) | async-done | bytes 65568 | tf_op jit(solution)/shard_map/all_to_all | solution.py:516
  194.8 0.2 reshape.30
  195.0 0.1 copy.17
  195.1 0.8 reverse_select_fusion
  (2 shorter events, 0.0 us)
Async XLA Ops:
  0.6 2.2 %copy-start.2 = (bf16[32,16384]{1,0:T(8,128)(2,1)S(1)}, bf16[32,16384]{1,0:T(8,128)(2,1)}, u32[]{:S(2)}) copy-start(bf16[32,16384]{1,0:T(8,128)(2,1)} %param.5) | copy-start | bytes 3145732
  3.0 5.1 %copy-start = (bf16[64,16384]{1,0:T(8,128)(2,1)}, bf16[64,16384]{1,0:T(8,128)(2,1)S(1)}, u32[]{:S(2)}) copy-start(bf16[64,16384]{1,0:T(8,128)(2,1)S(1)} %pad_maximum_fusion.xw_ref.mine_ref) | copy-start | bytes 6291460
  3.0 52.9 %collective-permute-start = (bf16[64,16384]{1,0:T(8,128)(2,1)S(1)}, bf16[64,16384]{1,0:T(8,128)(2,1)}, u32[]{:S(2)}, u32[]{:S(2)}) collective-permute-start(bf16[64,16384]{1,0:T(8,128)(2,1)S(1)} %pad_maximum_fusion.xw_ref.mine_ref), channel_id=1, source_target_pairs={{0,8},{1,9},{2,10},{3,11},{4,12},{5,13},{6,14},{7,15},{8,0},{9,1},... | collective-permute-start | bytes 6291464 | tf_op jit(solution)/shard_map/ppermute | solution.py:493
  6.1 49.8 %collective-permute-start.1 = (bf16[64,16384]{1,0:T(8,128)(2,1)S(1)}, bf16[64,16384]{1,0:T(8,128)(2,1)}, u32[]{:S(2)}, u32[]{:S(2)}) collective-permute-start(bf16[64,16384]{1,0:T(8,128)(2,1)S(1)} %pad_maximum_fusion.xw_ref.mine_ref), channel_id=1, source_target_pairs={{8,16},{9,17},{10,18},{11,19},{12,20},{13,21},{14,22},{15,23},{16,... | collective-permute-start | bytes 6291464 | tf_op jit(solution)/shard_map/ppermute | solution.py:494
  12.4 4.7 %copy-start.4 = (s32[32,1]{0,1:T(1,128)S(1)}, s32[32,1]{0,1:T(1,128)}, u32[]{:S(2)}) copy-start(s32[32,1]{0,1:T(1,128)} %param.9) | copy-start | bytes 388
  12.5 45.6 %copy-start.3 = (s32[4,16384]{1,0:T(4,128)S(1)}, s32[4,16384]{1,0:T(4,128)}, u32[]{:S(2)}) copy-start(s32[4,16384]{1,0:T(4,128)} %param.8) | copy-start | bytes 786436
  12.5 81.0 %all-to-all-start = ((bf16[8,2,8,16384]{3,2,1,0:T(8,128)(2,1)}), bf16[8,2,8,16384]{3,2,1,0:T(8,128)(2,1)}, u32[]{:S(2)}, u32[]{:S(2)}) async-start(bf16[8,2,8,16384]{3,2,1,0:T(8,128)(2,1)} %own_pack.1), calls=%async_computation | async-start | bytes 8388608 | tf_op jit(solution)/shard_map/all_to_all | solution.py:487
  17.2 38.8 %collective-permute-start.2 = (s32[32]{0:T(128)S(1)}, s32[32]{0:T(128)S(1)}, u32[]{:S(2)}, u32[]{:S(2)}) collective-permute-start(s32[32]{0:T(128)S(1)} %bitcast.25), channel_id=1, source_target_pairs={{0,16},{1,17},{2,18},{3,19},{4,20},{5,21},{6,22},{7,23},{8,24},{9,... | collective-permute-start | bytes 392 | tf_op jit(solution)/shard_map/ppermute | solution.py:495
  56.0 37.5 %copy-start.5 = (s32[32]{0:T(128)}, s32[32]{0:T(128)S(1)}, u32[]{:S(2)}) copy-start(s32[32]{0:T(128)S(1)} %collective-permute-done.2.pick_ref) | copy-start | bytes 388
  56.0 47.7 %collective-permute-start.4 = (bf16[64,16384]{1,0:T(8,128)(2,1)}, bf16[64,16384]{1,0:T(8,128)(2,1)S(1)}, u32[]{:S(2)}, u32[]{:S(2)}) collective-permute-start(bf16[64,16384]{1,0:T(8,128)(2,1)} %collective-permute-done.near_ref), channel_id=1, source_target_pairs={{8,16},{9,17},{10,18},{11,19},{12,20},{13,21},{14,22},{15,23},{16,... | collective-permute-start | bytes 6291464 | tf_op jit(solution)/shard_map/ppermute | solution.py:499
  56.8 49.3 %collective-permute-start.3 = (bf16[64,16384]{1,0:T(8,128)(2,1)}, bf16[64,16384]{1,0:T(8,128)(2,1)}, u32[]{:S(2)}, u32[]{:S(2)}) collective-permute-start(bf16[64,16384]{1,0:T(8,128)(2,1)} %collective-permute-done.1), channel_id=1, source_target_pairs={{8,0},{9,1},{10,2},{11,3},{12,4},{13,5},{14,6},{15,7},{16,24},{17,... | collective-permute-start | bytes 6291464 | tf_op jit(solution)/shard_map/ppermute | solution.py:498
  103.6 2.4 %copy-start.1 = (bf16[64,16384]{1,0:T(8,128)(2,1)}, bf16[64,16384]{1,0:T(8,128)(2,1)S(1)}, u32[]{:S(2)}) copy-start(bf16[64,16384]{1,0:T(8,128)(2,1)S(1)} %collective-permute-done.4.inner_ref) | copy-start | bytes 6291460
  110.5 53.7 %all-to-all-start.1 = ((bf16[8,2,8,16384]{3,2,1,0:T(8,128)(2,1)}), bf16[8,2,8,16384]{3,2,1,0:T(8,128)(2,1)}, u32[]{:S(2)}, u32[]{:S(2)}) async-start(bf16[8,2,8,16384]{3,2,1,0:T(8,128)(2,1)} %far_pack.1.after_ref), calls=%async_computation.1 | async-start | bytes 8388608 | tf_op jit(solution)/shard_map/all_to_all | solution.py:487
  180.7 7.3 %collective-permute-start.5 = (f32[64,128]{1,0:T(8,128)}, f32[64,128]{1,0:T(8,128)S(1)}, u32[]{:S(2)}, u32[]{:S(2)}) collective-permute-start(f32[64,128]{1,0:T(8,128)} %get-tuple-element.12), channel_id=1, source_target_pairs={{0,8},{1,9},{2,10},{3,11},{4,12},{5,13},{6,14},{7,15},{8,0},{9,1},... | collective-permute-start | bytes 98312 | tf_op jit(solution)/shard_map/ppermute | solution.py:508
  184.4 10.4 %all-to-all-start.2 = ((f32[16,8,128]{2,1,0:T(8,128)}), f32[16,8,128]{2,1,0:T(8,128)S(1)}, u32[]{:S(2)}, u32[]{:S(2)}) async-start(f32[16,8,128]{2,1,0:T(8,128)} %bitcast.19), calls=%async_computation.2 | async-start | bytes 131072 | tf_op jit(solution)/shard_map/all_to_all | solution.py:516
